TPU v7x, 128 devices: a whole 4x4x4 slice. The times are simulated.
128 devices in a mesh: batch: 4 (over z_hi, core), hidden: 32 (over z_lo, y, x).
Axes of the slice: x: 4, y: 4, z: 4 (z_hi: 2, z_lo: 2; z = z_hi * 2 + z_lo), core: 2. Of those that a mesh axis runs over, the one named last changes fastest.
Arguments:
- codes: bfloat16 [640, 9216], P('batch', 'hidden'), may hold values from -6 to 6
- exponents: int32 [640], P('batch'), may hold values from -2 to 2
- w_in: bfloat16 [9216, 36864], P('batch', 'hidden'), may hold values from -0.0625 to 0.0625
- w_out: bfloat16 [36864, 9216], P('hidden', 'batch'), may hold values from -0.0625 to 0.0625
Outputs:
- mixed: float32 [640, 9216], P(None, ('batch', 'hidden'))
All inputs are finite; a program needn't handle non-finite values.
Results may differ from a plain program's by a relative error of at most 0.0029.
Values may be sent and summed in bfloat16 or wider, within the bound.
No kernel may reach another device: no remote copies, remote signals or barrier semaphores. Data moves between devices by JAX's collectives and lax.ppermute only.
A program may use at most 128 MiB of HBM per device.

v0:
```python
import jax
import jax.numpy as jnp
from jax import lax
from jax.sharding import PartitionSpec as P


def shards(codes, exponents, w_in, w_out):
    gathered = lax.all_gather(codes, "hidden", axis=1, tiled=True)
    tok_rows = gathered.shape[0]
    width = gathered.shape[1]
    batch_count = lax.axis_size("batch")
    hidden_count = lax.axis_size("hidden")
    narrow = width // (batch_count * hidden_count)
    row_scale = jnp.exp2(exponents.astype(jnp.float32))[:, None]
    preact = jnp.dot(
        gathered,
        lax.all_gather(w_in, "batch", axis=0, tiled=True),
        preferred_element_type=jnp.float32,
    )
    activ = jax.nn.gelu(preact * row_scale, approximate=True).astype(jnp.bfloat16)
    partial_out = jnp.dot(
        activ,
        lax.all_gather(w_out, "batch", axis=1, tiled=True),
        preferred_element_type=jnp.float32,
    )
    partial_out = partial_out.reshape(tok_rows, batch_count, hidden_count, narrow)
    summed = lax.psum_scatter(partial_out, "hidden", scatter_dimension=2, tiled=True)
    summed = summed.reshape(tok_rows, batch_count, narrow)
    spread = lax.all_to_all(summed, "batch", split_axis=1, concat_axis=0, tiled=True)
    return spread.reshape(tok_rows * batch_count, narrow)


def solution(mesh):
    placed = (P("batch", "hidden"), P("batch"), P("batch", "hidden"), P("hidden", "batch"))
    return jax.shard_map(
        shards, mesh=mesh, in_specs=placed, out_specs=P(None, ("batch", "hidden")), check_vma=False
    )
```

profile of v0, /device:TPU:1, one launch (start us, length us, event | category | flops | bytes accessed | tf_op | source)
XLA Modules:
  0.0 695.6 jit_solution(8589030831387373959)
XLA Ops:
  6.5 0.0 copy-start
  6.5 0.0 all-gather.9.cloned.1.call-start
  6.5 0.7 all-gather.9.cloned.1.call-update
  7.3 0.0 all-gather.5.cloned.1.call-start
  7.3 0.7 all-gather.5.cloned.1.call-update
  8.0 0.0 all-gather.7.cloned.1.call-start
  8.1 0.7 all-gather.7.cloned.1.call-update
  8.7 0.0 reduce-scatter.2.cloned.1.call-start
  8.8 0.0 copy-done
  8.8 139.8 %all-gather.9.cloned.1.call-done = bf16[32,288,160]{1,2,0:T(8,128)(2,1)} async-done(((bf16[1,288,160]{1,2,0:T(8,128)(2,1)}), bf16[32,288,160]{1,2,0:T(8,128)(2,1)}) %all-gather.9.cloned.1.call-update) | async-done | bytes 2949136 | tf_op jit(solution)/shard_map/all_gather | solution.py:8
  148.7 5.4 copy.9
  154.0 6.4 reshape.15
  160.4 148.5 %all-gather.5.cloned.1.call-done = bf16[9216,1152]{1,0:T(8,128)(2,1)} async-done(((bf16[2304,1152]{1,0:T(8,128)(2,1)}), bf16[9216,1152]{1,0:T(8,128)(2,1)}) %all-gather.5.cloned.1.call-update) | async-done | bytes 21233680 | tf_op jit(solution)/shard_map/all_gather | solution.py:17
  309.0 138.1 %all-gather.7.cloned.1.call-done = bf16[1152,9216]{1,0:T(8,128)(2,1)} async-done(((bf16[1152,2304]{1,0:T(8,128)(2,1)}), bf16[1152,9216]{1,0:T(8,128)(2,1)}) %all-gather.7.cloned.1.call-update) | async-done | bytes 21233680 | tf_op jit(solution)/shard_map/all_gather | solution.py:23
  447.1 23.6 %fusion.8 = f32[160,9216]{1,0:T(8,128)} fusion(bf16[1152,9216]{1,0:T(8,128)(2,1)} %all-gather.7.cloned.1.call-done, bf16[9216,160]{0,1:T(8,128)(2,1)S(1)} %reshape.15, bf16[9216,1152]{1,0:T(8,128)(2,1)} %all-gather.5.cloned.1.call-done, f32[160]{0:T(256)S(1)} %multiply_exponential_fusion), kind=kOutput, calls=%fused_computation.10 | convolution fusion | flops 6796615680 | bytes 51315328 | tf_op jit(solution)/shard_map/dot_general | solution.py:21
  470.7 13.0 %reshape.11 = f32[160,4,32,72]{3,2,1,0:T(8,128)} reshape(f32[160,9216]{1,0:T(8,128)} %fusion.8) | data formatting | bytes 11796480 | tf_op jit(solution)/shard_map/reshape | solution.py:26
  483.7 12.1 %copy.10 = f32[160,4,32,72]{0,3,1,2:T(8,128)} copy(f32[160,4,32,72]{3,2,1,0:T(8,128)} %reshape.11) | data formatting | bytes 11796480 | tf_op jit(solution)/shard_map/reshape | solution.py:26
  495.8 0.0 reduce-scatter.2.cloned.1.call-update
  495.8 157.5 %reduce-scatter.2.cloned.1.call-done = f32[160,4,1,72]{0,3,1,2:T(8,128)} async-done(((f32[160,4,32,72]{0,3,1,2:T(8,128)}), f32[160,4,1,72]{0,3,1,2:T(8,128)}) %reduce-scatter.2.cloned.1.call-update) | async-done | bytes 184336 | tf_op jit(solution)/shard_map/reduce_scatter | solution.py:27
  653.3 34.8 %all_to_all.15 = f32[160,4,72]{0,2,1:T(8,128)S(1)} all-to-all(f32[160,4,72]{0,2,1:T(8,128)} %bitcast.15), channel_id=1, replica_groups=mesh['batch'=4,'hidden'=32] {'batch'}, dimensions={1} | all-to-all | bytes 368640 | tf_op jit(solution)/shard_map/all_to_all | solution.py:29
  688.1 0.1 copy.11
  688.2 0.9 reshape.13
  (1 shorter events, 0.0 us)
Async XLA Ops:
  6.5 2.3 copy-start
  6.5 142.1 %all-gather.9.cloned.1.call-start = ((), (), s32[]{:S(2)}) async-start(), calls=%async_computation.5 | async-start | bytes 4055040 | tf_op jit(solution)/shard_map/all_gather | solution.py:8
  7.3 301.7 %all-gather.5.cloned.1.call-start = ((), (), s32[]{:S(2)}) async-start(), calls=%async_computation.2 | async-start | bytes 26542080 | tf_op jit(solution)/shard_map/all_gather | solution.py:17
  8.0 439.1 %all-gather.7.cloned.1.call-start = ((), (), s32[]{:S(2)}) async-start(), calls=%async_computation.3 | async-start | bytes 26542080 | tf_op jit(solution)/shard_map/all_gather | solution.py:23
  8.7 644.6 %reduce-scatter.2.cloned.1.call-start = ((), (), s32[]{:S(2)}) async-start(), calls=%async_computation.4 | async-start | bytes 9732096 | tf_op jit(solution)/shard_map/reduce_scatter | solution.py:27
Sparse Core Ops, SparseCore 0:
  9.0 139.6 all-gather.8
  150.3 158.5 all-gather.4
  310.7 136.4 all-gather.6
  495.9 157.3 reduce-scatter.1
where the time goes:
time: 696 us
  waiting for transfers between devices  586 us (84%)
  local copies, waits for them, and re-layouts  37.9 us (5%)
  blocking collectives  34.8 us (5%)
  matrix products  23.6 us (3%)
  between operations  13.2 us (2%)
    reduce_scatter x1, waiting for transfers between devices, shards(): lax.psum_scatter(partial_out, 'hidden', scatter_dimension=2, tiled=True)  158 us
    all_gather x1, waiting for transfers between devices, shards(): lax.all_gather(w_in, 'batch', axis=0, tiled=True)  149 us
    all_gather x1, waiting for transfers between devices, shards(): gathered = lax.all_gather(codes, 'hidden', axis=1, tiled=True)  140 us
    all_gather x1, waiting for transfers between devices, shards(): lax.all_gather(w_out, 'batch', axis=1, tiled=True)  138 us
    all_to_all x1, blocking collectives, shards(): lax.all_to_all(summed, 'batch', split_axis=1, concat_axis=0, tiled=True)  34.8 us
    reshape x2, local copies, waits for them, and re-layouts, shards(): partial_out.reshape(tok_rows, batch_count, hidden_count, narrow)  25.1 us
    dot_general x1, matrix products, shards(): jnp.dot(activ, lax.all_gather(w_out, 'batch', axis=1, tiled=True), prefer...  23.6 us
  transfers between devices with their start and end apart: 4, of which 4 were waited for; matrix products, arithmetic and copies ran while one was open for 2% of the time, Pallas kernels for 0%

commit v1 on v0

v1 whole, which is shorter than its diff:
```python
import jax
import jax.numpy as jnp
from jax import lax
from jax.experimental import pallas as pl
from jax.experimental.pallas import tpu as pltpu
from jax.sharding import Mesh, PartitionSpec as P

BF, F32 = jnp.bfloat16, jnp.float32
QT = 160
PIECE = 288
UNITS = 1152
CHIP_COLS = 72
VMEM = pl.BlockSpec(memory_space=pltpu.VMEM)
ANY = pl.BlockSpec(memory_space=pl.ANY)
YX = ("c", "y", "x")


def first_axis(step):
    pairs = []
    for y in range(4):
        for x in range(4):
            pairs.append((y * 4 + x, y * 4 + (x + step) % 4))
            pairs.append((16 + y * 4 + x, 16 + (y + step) % 4 * 4 + x))
    return pairs


def second_axis(step):
    pairs = []
    for y in range(4):
        for x in range(4):
            pairs.append((y * 4 + x, (y + step) % 4 * 4 + x))
            pairs.append((16 + y * 4 + x, 16 + y * 4 + (x + step) % 4))
    return pairs


def call(kernel, outs, ins, scratch=(), flops=0, nbytes=0, name=None):
    return pl.pallas_call(
        kernel,
        out_shape=outs,
        in_specs=ins,
        out_specs=jax.tree.map(lambda _: VMEM, outs),
        scratch_shapes=list(scratch),
        compiler_params=pltpu.CompilerParams(vmem_limit_bytes=50 * 2**20),
        cost_estimate=pl.CostEstimate(flops=flops, bytes_accessed=nbytes, transcendentals=0),
        name=name,
    )


def dot(a, b):
    return jnp.dot(a, b, preferred_element_type=F32)


def pack_codes(x_ref, o_ref):
    o_ref[0:QT] = x_ref[:, 0:128]
    o_ref[QT : 2 * QT] = x_ref[:, 128:256]
    tail = x_ref[:, 256:288]
    src = lax.broadcasted_iota(jnp.int32, (32, 128), 0)
    dst = lax.broadcasted_iota(jnp.int32, (32, 128), 1)
    total = jnp.zeros((40, 128), F32)
    for j in range(4):
        place = jnp.where(dst == src + 32 * j, 1.0, 0.0).astype(BF)
        total += dot(tail, place)[40 * j : 40 * j + 40]
    o_ref[2 * QT : 360] = total.astype(BF)


def merge_codes(a_ref, b_ref, c_ref, d_ref, o_ref):
    pieces = (a_ref, b_ref, c_ref, d_ref)
    src = lax.broadcasted_iota(jnp.int32, (512, 128), 0)
    dst = lax.broadcasted_iota(jnp.int32, (512, 128), 1)
    for q in range(2):
        rows = slice(q * QT, (q + 1) * QT)
        for j, ref in enumerate(pieces):
            o_ref[rows, 256 * j : 256 * j + 128] = ref[q, 0:QT]
            o_ref[rows, 256 * j + 128 : 256 * j + 256] = ref[q, QT : 2 * QT]
        tails = jnp.concatenate([ref[q, 2 * QT : 360] for ref in pieces], axis=1)
        groups = []
        for j in range(4):
            place = (src // 128 == dst // 32) & (src % 128 == 32 * j + dst % 32)
            groups.append(dot(tails, jnp.where(place, 1.0, 0.0).astype(BF)))
        o_ref[rows, 1024:1152] = jnp.concatenate(groups, axis=0).astype(BF)


def own_place():
    c, y, x = lax.axis_index("c"), lax.axis_index("y"), lax.axis_index("x")
    return c, jnp.where(c == 0, x, y), jnp.where(c == 0, y, x)


def project_in(m0, m1, m2, m3, own_ref, other_ref, o_ref, w_ref, sems):
    c, first, second = own_place()
    for i in range(4):
        s = lax.rem(second + 4 - i, 4)
        for j in range(4):
            f = lax.rem(first + 4 - j, 4)
            y, x = jnp.where(c == 0, s, f), jnp.where(c == 0, f, s)
            row = lax.rem(y, 2) * UNITS + x * PIECE
            for ref, here in ((own_ref, lax.div(y, 2) == c), (other_ref, lax.div(y, 2) != c)):

                @pl.when(here)
                def _(ref=ref):
                    for at, to, n in ((0, 256 * j, 256), (256, 1024 + 32 * j, 32)):
                        pltpu.make_async_copy(
                            ref.at[pl.ds(pl.multiple_of(row + at, 32), n)], w_ref.at[i, to : to + n], sems.at[i]
                        ).start()

    for i, m in enumerate((m0, m1, m2, m3)):
        pltpu.make_async_copy(w_ref.at[i], w_ref.at[i], sems.at[i]).wait()
        part = dot(m[...], w_ref[i])
        o_ref[...] = part if i == 0 else o_ref[...] + part


def project_out(a_ref, own_ref, other_ref, o0, o1, o2, o3, w_ref, t_ref, tail_ref, sems):
    copies = []
    for g in range(4):
        src = own_ref if g < 2 else other_ref
        copy = pltpu.make_async_copy(src.at[:, (g % 2) * UNITS : (g % 2 + 1) * UNITS], w_ref.at[g], sems.at[g])
        copy.start()
        copies.append(copy)
    for g in range(4):
        copies[g].wait()
        part = dot(a_ref[...], w_ref[g])
        for q in range(2):
            t_ref[5 * q + g] = part[q * QT : q * QT + 128].T.reshape(16, CHIP_COLS, 128)
            tail_ref[q, 32 * g : 32 * g + 32] = part[q * QT + 128 : (q + 1) * QT]
    for q in range(2):
        t_ref[5 * q + 4] = tail_ref[q].T.reshape(16, CHIP_COLS, 128)
    c, first, _ = own_place()
    for rel, o in enumerate((o0, o1, o2, o3)):
        f = lax.rem(first + rel, 4)
        for s in range(4):
            yx = jnp.where(c == 0, s * 4 + f, f * 4 + s)
            for p in range(5):
                both = jnp.concatenate([t_ref[2 * p, yx], t_ref[2 * p + 1, yx]], axis=0)
                o[s, 144 * p : 144 * p + 144] = both.astype(o.dtype)


def add_first(a, b, c, d, o0, o1, o2, o3):
    _, _, second = own_place()
    for rel, o in enumerate((o0, o1, o2, o3)):
        s = lax.rem(second + rel, 4)
        total = a[s] + b[s].astype(F32) + c[s].astype(F32) + d[s].astype(F32)
        o[...] = total.astype(o.dtype)


def add_second(a, b, c, d, keep, to_zl, to_c, to_czl):
    total = a[...] + b[...].astype(F32) + c[...].astype(F32) + d[...].astype(F32)
    zl = lax.axis_index("zl")
    tiles = total.reshape(10, CHIP_COLS, 128)
    lane = lax.broadcasted_iota(jnp.int32, (CHIP_COLS, 128), 1)

    def share(crel, z):
        g = 2 * crel + z
        tail = jnp.where(lane < 32, pltpu.roll(tiles[4], (128 - 32 * g) % 128, 1), pltpu.roll(tiles[9], (160 - 32 * g) % 128, 1))
        return tiles[g], tiles[5 + g], tail

    for crel, same, swapped in ((0, keep, to_zl), (1, to_c, to_czl)):
        for i, (lo, hi) in enumerate(zip(share(crel, 0), share(crel, 1))):
            same[i] = jnp.where(zl == 0, lo, hi)
            swapped[i] = jnp.where(zl == 0, hi, lo)


def finish(keep, from_zl, from_c, from_czl, o_ref):
    c = lax.axis_index("c")
    for core, a, b in ((c, keep, from_zl), (1 - c, from_c, from_czl)):
        tail = (a[2] + b[2]).T
        for q in range(2):
            row = (2 * q + core) * QT
            o_ref[pl.ds(pl.multiple_of(row, 8), 128)] = (a[q] + b[q]).T
            o_ref[pl.ds(pl.multiple_of(row + 128, 8), 32)] = tail[32 * q : 32 * q + 32]


def shape(dims, dtype):
    return jax.ShapeDtypeStruct(dims, dtype)


def shards(codes, exponents, w_in, w_out):
    zh, zl = lax.axis_index("zh"), lax.axis_index("zl")
    swap = [(0, 1), (1, 0)]
    z = ("zh", "zl")
    w_in_other = lax.ppermute(w_in, "c", swap)
    w_out_other = lax.ppermute(w_out, "c", swap)

    packed = call(pack_codes, shape((360, 128), BF), [VMEM], name="pack_codes")(codes)
    one = lax.ppermute(packed, z, [(0, 1), (1, 2), (2, 0), (3, 3)])
    two = lax.ppermute(packed, z, [(2, 1), (3, 2), (1, 3), (0, 0)])
    piece = jnp.stack([jnp.where(zh == zl, two, one), jnp.where(zh == zl, one, two)])

    around = [lax.ppermute(piece, YX, first_axis(k)) for k in (1, 2, 3)]
    merged = call(merge_codes, shape((2 * QT, UNITS), BF), [VMEM] * 4, name="merge_codes")(piece, *around)
    around = [lax.ppermute(merged, YX, second_axis(k)) for k in (1, 2, 3)]
    preact = call(
        project_in,
        shape((2 * QT, UNITS), F32),
        [VMEM] * 4 + [ANY] * 2,
        [pltpu.VMEM((4, UNITS, UNITS), BF), pltpu.SemaphoreType.DMA((4,))],
        flops=2 * 320 * 4608 * 1152,
        nbytes=4608 * 1152 * 2,
        name="project_in",
    )(merged, *around, w_in, w_in_other)

    most = jnp.max(jnp.abs(preact))
    up = jnp.clip(13.0 - jnp.ceil(jnp.log2(jnp.maximum(most, 1e-30))), -100.0, 100.0)
    sent = (preact * jnp.exp2(up)).astype(jnp.float16)
    got = lax.ppermute(sent, "zh", swap)
    got_up = lax.ppermute(jnp.full((8, 128), up), "zh", swap)[0, 0]
    other_exponents = lax.ppermute(exponents, "zh", swap)
    powers = jnp.stack([jnp.where(zh == 0, exponents, other_exponents), jnp.where(zh == 0, other_exponents, exponents)])
    row_scale = jnp.exp2(powers.reshape(2 * QT).astype(F32))[:, None]
    summed = (preact + got.astype(F32) * jnp.exp2(-got_up)) * row_scale
    activ = jax.nn.gelu(summed, approximate=True).astype(BF)

    part = (4, 720, 128)
    mine, *away = call(
        project_out,
        [shape(part, F32)] + [shape(part, BF)] * 3,
        [VMEM] + [ANY] * 2,
        [
            pltpu.VMEM((4, UNITS, UNITS), BF),
            pltpu.VMEM((10, 16, CHIP_COLS, 128), F32),
            pltpu.VMEM((2, 128, UNITS), F32),
            pltpu.SemaphoreType.DMA((4,)),
        ],
        flops=2 * 320 * 4608 * 1152,
        nbytes=4608 * 1152 * 2,
        name="project_out",
    )(activ, w_out, w_out_other)
    away = [lax.ppermute(v, YX, first_axis(k)) for k, v in zip((1, 2, 3), away)]
    part = (720, 128)
    mine, *away = call(add_first, [shape(part, F32)] + [shape(part, BF)] * 3, [VMEM] * 4, name="add_first")(mine, *away)
    away = [lax.ppermute(v, YX, second_axis(k)) for k, v in zip((1, 2, 3), away)]
    keep, to_zl, to_c, to_czl = call(add_second, [shape((3, CHIP_COLS, 128), F32)] * 4, [VMEM] * 4, name="add_second")(mine, *away)
    from_zl = lax.ppermute(to_zl, "zl", swap)
    from_c = lax.ppermute(to_c, "c", swap)
    from_czl = lax.ppermute(to_czl, ("c", "zl"), [(0, 3), (1, 2), (2, 1), (3, 0)])
    return call(finish, shape((4 * QT, CHIP_COLS), F32), [VMEM] * 4, name="finish")(keep, from_zl, from_c, from_czl)


def solution(mesh):
    split = Mesh(mesh.devices.reshape(2, 2, 2, 4, 4), ("zh", "c", "zl", "y", "x"))
    batch, hidden = ("zh", "c"), ("zl", "y", "x")
    placed = (P(batch, hidden), P(batch), P(batch, hidden), P(hidden, batch))
    return jax.shard_map(shards, mesh=split, in_specs=placed, out_specs=P(None, batch + hidden), check_vma=False)
```

time: 696 us -> 133 us (0.19)
  waiting for transfers between devices: 586 us -> 60.7 us
  starting transfers between devices: 0.12 us -> 44 us
  local copies, waits for them, and re-layouts: 37.9 us -> 2.33 us
  blocking collectives: 34.8 us -> 0 us
  matrix products: 23.6 us -> 0 us
  Pallas kernels: 0 us -> 19.8 us
  between operations: 13.2 us -> 1.61 us
    all_gather x3 -> x0, waiting for transfers between devices: 427 us -> none  [the longest x1 149 us: shards(): lax.all_gather(w_in, 'batch', axis=0, tiled=True)]
    reduce_scatter x1 -> x0, waiting for transfers between devices: 158 us -> none  [shards(): lax.psum_scatter(partial_out, 'hidden', scatter_dimension=2, tiled=True)]
    ppermute x0 -> x22, waiting for transfers between devices: none -> 60.7 us  [the longest x3 15.9 us: shards(): away = [lax.ppermute(v, YX, first_axis(k)) for k, v in zip((1, 2, 3), away)]]
    ppermute x0 -> x22, starting transfers between devices: none -> 44 us  [the longest x1 8.39 us: shards(): from_c = lax.ppermute(to_c, 'c', swap)]
    all_to_all x1 -> x0, blocking collectives: 34.8 us -> none  [shards(): lax.all_to_all(summed, 'batch', split_axis=1, concat_axis=0, tiled=True)]
    reshape x3 -> x0, local copies, waits for them, and re-layouts: 26 us -> none  [the longest x2 25.1 us: shards(): partial_out.reshape(tok_rows, batch_count, hidden_count, narrow)]
    dot_general x1 -> x0, matrix products: 23.6 us -> none  [shards(): jnp.dot(activ, lax.all_gather(w_out, 'batch', axis=1, tiled=True), prefer...]
    pallas_call x0 -> x7, Pallas kernels: none -> 19.8 us  [the longest x1 9 us: shards(): call(project_out, [shape(part, F32)] + [shape(part, BF)] * 3, [VMEM] + [A...]
  transfers between devices with their start and end apart: 4 -> 22, of which waited for: 4 -> 14; matrix products, arithmetic and copies ran while one was open for 2% -> 3% of each run, Pallas kernels for 0% -> 7%
where the time goes in v1:
time: 133 us; the launch traced here: 132 us
  waiting for transfers between devices  60.7 us (46%)
  starting transfers between devices  44 us (33%)
  Pallas kernels  19.8 us (15%)
  other arithmetic  3.09 us (2%)
  local copies, waits for them, and re-layouts  2.33 us (2%)
  between operations  1.61 us (1%)
    ppermute x3, waiting for transfers between devices, shards(): away = [lax.ppermute(v, YX, first_axis(k)) for k, v in zip((1, 2, 3), away)]  15.9 us
    ppermute x3, waiting for transfers between devices, shards(): around = [lax.ppermute(merged, YX, second_axis(k)) for k in (1, 2, 3)]  15.9 us
    ppermute x1, waiting for transfers between devices, shards(): other_exponents = lax.ppermute(exponents, 'zh', swap)  13 us
    pallas_call x1, Pallas kernels, shards(): call(project_out, [shape(part, F32)] + [shape(part, BF)] * 3, [VMEM] + [A...  9 us
    ppermute x1, starting transfers between devices, shards(): from_c = lax.ppermute(to_c, 'c', swap)  8.39 us
    pallas_call x1, Pallas kernels, shards(): call(project_in, shape((2 * QT, UNITS), F32), [VMEM] * 4 + [ANY] * 2, [pl...  8.17 us
    ppermute x1, starting transfers between devices, shards(): one = lax.ppermute(packed, z, [(0, 1), (1, 2), (2, 0), (3, 3)])  7.57 us
    ppermute x3, starting transfers between devices, shards(): around = [lax.ppermute(piece, YX, first_axis(k)) for k in (1, 2, 3)]  5.05 us
  transfers between devices with their start and end apart: 22, of which 14 were waited for; matrix products, arithmetic and copies ran while one was open for 3% of the time, Pallas kernels for 7%

profile of v1, /device:TPU:1, one launch (start us, length us, event | category | flops | bytes accessed | tf_op | source)
XLA Modules:
  0.0 131.6 jit_solution(7725339013024080593)
XLA Ops:
  0.0 1.4 %collective-permute-start.8 = (bf16[2304,1152]{1,0:T(8,128)(2,1)}, bf16[2304,1152]{1,0:T(8,128)(2,1)}, u32[]{:S(2)}, u32[]{:S(2)}) collective-permute-start(bf16[2304,1152]{1,0:T(8,128)(2,1)} %own_ref.2), channel_id=1, source_target_pairs={{0,32},{32,0},{1,33},{33,1},{2,34},{34,2},{3,35},{35,3},{4,36},{36... | collective-permute-start | bytes 15925256 | tf_op jit(solution)/shard_map/ppermute | solution.py:179
  1.4 0.0 collective-permute-start.12
  1.4 0.0 copy-start
  1.4 0.9 copy-done
  2.3 0.2 pack_codes.1
  2.5 0.7 collective-permute-start
  3.2 7.6 %collective-permute-start.1 = (bf16[360,128]{1,0:T(8,128)(2,1)S(1)}, bf16[360,128]{1,0:T(8,128)(2,1)S(1)}, u32[]{:S(2)}, u32[]{:S(2)}) collective-permute-start(bf16[360,128]{1,0:T(8,128)(2,1)S(1)} %pack_codes.1), channel_id=1, source_target_pairs={{0,16},{16,64},{64,0},{80,80},{1,17},{17,65},{65,1},{81,81},{2,18}... | collective-permute-start | bytes 276488 | tf_op jit(solution)/shard_map/ppermute | solution.py:183
  10.8 0.0 collective-permute-done
  10.8 1.7 %collective-permute-done.1 = bf16[360,128]{1,0:T(8,128)(2,1)S(1)} collective-permute-done((bf16[360,128]{1,0:T(8,128)(2,1)S(1)}, bf16[360,128]{1,0:T(8,128)(2,1)S(1)}, u32[]{:S(2)}, u32[]{:S(2)}) %collective-permute-start.1) | collective-permute-done | bytes 92192 | tf_op jit(solution)/shard_map/ppermute | solution.py:183
  12.6 1.4 %collective-permute-start.2 = (bf16[2,360,128]{2,1,0:T(8,128)(2,1)S(1)}, bf16[2,360,128]{2,1,0:T(8,128)(2,1)S(1)}, u32[]{:S(2)}, u32[]{:S(2)}) collective-permute-start(bf16[2,360,128]{2,1,0:T(8,128)(2,1)S(1)} %pad_maximum_fusion.a_ref), channel_id=1, source_target_pairs={{0,1},{32,36},{1,2},{33,37},{2,3},{34,38},{3,0},{35,39},{4,5},{36,... | collective-permute-start | bytes 552968 | tf_op jit(solution)/shard_map/ppermute | solution.py:187
  13.9 2.6 %collective-permute-start.3 = (bf16[2,360,128]{2,1,0:T(8,128)(2,1)S(1)}, bf16[2,360,128]{2,1,0:T(8,128)(2,1)S(1)}, u32[]{:S(2)}, u32[]{:S(2)}) collective-permute-start(bf16[2,360,128]{2,1,0:T(8,128)(2,1)S(1)} %pad_maximum_fusion.a_ref), channel_id=1, source_target_pairs={{0,2},{32,40},{1,3},{33,41},{2,0},{34,42},{3,1},{35,43},{4,6},{36,... | collective-permute-start | bytes 552968 | tf_op jit(solution)/shard_map/ppermute | solution.py:187
  16.5 1.1 collective-permute-start.4
  17.6 1.0 collective-permute-done.2.b_ref
  18.6 3.2 %collective-permute-done.3.c_ref = bf16[2,360,128]{2,1,0:T(8,128)(2,1)S(1)} collective-permute-done((bf16[2,360,128]{2,1,0:T(8,128)(2,1)S(1)}, bf16[2,360,128]{2,1,0:T(8,128)(2,1)S(1)}, u32[]{:S(2)}, u32[]{:S(2)}) %collective-permute-start.3) | collective-permute-done | bytes 184352 | tf_op jit(solution)/shard_map/ppermute | solution.py:187
  21.7 0.0 collective-permute-done.4.d_ref
  21.7 0.4 merge_codes.1.m0
  22.2 1.0 collective-permute-start.5
  23.1 2.4 %collective-permute-start.6 = (bf16[320,1152]{1,0:T(8,128)(2,1)S(1)}, bf16[320,1152]{1,0:T(8,128)(2,1)S(1)}, u32[]{:S(2)}, u32[]{:S(2)}) collective-permute-start(bf16[320,1152]{1,0:T(8,128)(2,1)S(1)} %merge_codes.1.m0), channel_id=1, source_target_pairs={{0,8},{32,34},{1,9},{33,35},{2,10},{34,32},{3,11},{35,33},{4,12},{... | collective-permute-start | bytes 2211848 | tf_op jit(solution)/shard_map/ppermute | solution.py:189
  25.6 1.2 collective-permute-start.7
  26.8 7.3 %collective-permute-done.5.m1 = bf16[320,1152]{1,0:T(8,128)(2,1)S(1)} collective-permute-done((bf16[320,1152]{1,0:T(8,128)(2,1)S(1)}, bf16[320,1152]{1,0:T(8,128)(2,1)S(1)}, u32[]{:S(2)}, u32[]{:S(2)}) %collective-permute-start.5) | collective-permute-done | bytes 737312 | tf_op jit(solution)/shard_map/ppermute | solution.py:189
  34.0 8.6 %collective-permute-done.6.m2 = bf16[320,1152]{1,0:T(8,128)(2,1)S(1)} collective-permute-done((bf16[320,1152]{1,0:T(8,128)(2,1)S(1)}, bf16[320,1152]{1,0:T(8,128)(2,1)S(1)}, u32[]{:S(2)}, u32[]{:S(2)}) %collective-permute-start.6) | collective-permute-done | bytes 737312 | tf_op jit(solution)/shard_map/ppermute | solution.py:189
  42.6 0.0 collective-permute-done.7.m3
  42.6 0.0 collective-permute-done.8.other_ref
  42.6 8.2 %project_in.1 = f32[320,1152]{1,0:T(8,128)} custom-call(bf16[320,1152]{1,0:T(8,128)(2,1)S(1)} %merge_codes.1.m0, bf16[320,1152]{1,0:T(8,128)(2,1)S(1)} %collective-permute-done.5.m1, bf16[320,1152]{1,0:T(8,128)(2,1)S(1)} %collective-permute-done.6.m2, bf16[320,1152]{1,0:T(8,128)(2,1)S(1)} %collective-permute-done.7.m3, bf16[2304,1152]{1,0:T(8,128)(2,1)} %own_ref.2, ...), custom_call_target="tpu_custom_call" | custom-call | flops 3397386240 | bytes 10616832 | tf_op jit(solution)/shard_map/project_in/pallas_call | solution.py:190
  50.8 0.0 copy-start.1
  50.8 2.2 %abs_reduce_fusion = f32[]{:T(128)} fusion(f32[320,1152]{1,0:T(8,128)} %project_in.1), kind=kLoop, calls=%fused_computation.10 | loop fusion | flops 737279 | bytes 1474564 | tf_op jit(solution)/shard_map/reduce_max | solution.py:200
  53.0 0.0 copy-start.2
  53.8 0.0 copy-done.1
  53.8 0.1 multiply_convert_fusion
  53.9 2.4 %collective-permute-start.9 = (f16[320,1152]{1,0:T(8,128)(2,1)S(1)}, f16[320,1152]{1,0:T(8,128)(2,1)S(1)}, u32[]{:S(2)}, u32[]{:S(2)}) collective-permute-start(f16[320,1152]{1,0:T(8,128)(2,1)S(1)} %multiply_convert_fusion), channel_id=1, source_target_pairs={{0,64},{64,0},{1,65},{65,1},{2,66},{66,2},{3,67},{67,3},{4,68},{68... | collective-permute-start | bytes 2211848 | tf_op jit(solution)/shard_map/ppermute | solution.py:203
  56.3 0.0 copy-done.2
  56.3 0.7 collective-permute-start.11
  57.0 13.0 %collective-permute-done.11 = s32[160]{0:T(256)S(1)} collective-permute-done((s32[160]{0:T(256)S(1)}, s32[160]{0:T(256)S(1)}, u32[]{:S(2)}, u32[]{:S(2)}) %collective-permute-start.11) | collective-permute-done | bytes 672 | tf_op jit(solution)/shard_map/ppermute | solution.py:205
  70.0 2.4 %collective-permute-start.10 = (f32[8,128]{1,0:T(8,128)S(1)}, f32[8,128]{1,0:T(8,128)S(1)}, u32[]{:S(2)}, u32[]{:S(2)}) collective-permute-start(f32[8,128]{1,0:T(8,128)S(1)} %broadcast_in_dim.4), channel_id=1, source_target_pairs={{0,64},{64,0},{1,65},{65,1},{2,66},{66,2},{3,67},{67,3},{4,68},{68... | collective-permute-start | bytes 12296 | tf_op jit(solution)/shard_map/ppermute | solution.py:204
  72.4 0.1 exp2.45
  72.5 1.5 %collective-permute-done.10 = f32[8,128]{1,0:T(8,128)S(1)} collective-permute-done((f32[8,128]{1,0:T(8,128)S(1)}, f32[8,128]{1,0:T(8,128)S(1)}, u32[]{:S(2)}, u32[]{:S(2)}) %collective-permute-start.10) | collective-permute-done | bytes 4128 | tf_op jit(solution)/shard_map/ppermute | solution.py:204
  74.0 0.5 slice.3
  75.2 0.0 collective-permute-done.9
  75.2 0.7 fusion.7.a_ref
  76.0 0.0 collective-permute-done.12.other_ref
  76.0 9.0 %project_out.1 = (f32[4,720,128]{2,1,0:T(8,128)}, bf16[4,720,128]{2,1,0:T(8,128)(2,1)S(1)}, bf16[4,720,128]{2,1,0:T(8,128)(2,1)S(1)}, bf16[4,720,128]{2,1,0:T(8,128)(2,1)S(1)}) custom-call(bf16[320,1152]{1,0:T(8,128)(2,1)S(1)} %fusion.7.a_ref, bf16[1152,2304]{1,0:T(8,128)(2,1)} %own_ref.3, bf16[1152,2304]{1,0:T(8,128)(2,1)} %collective-permute-done.12.other_ref), custom_call_target="tpu_custom_call" | custom-call | flops 3397386240 | bytes 10616832 | tf_op jit(solution)/shard_map/project_out/pallas_call | solution.py:212
  85.0 0.9 collective-permute-start.13
  85.9 2.2 %collective-permute-start.14 = (bf16[4,720,128]{2,1,0:T(8,128)(2,1)S(1)}, bf16[4,720,128]{2,1,0:T(8,128)(2,1)S(1)}, u32[]{:S(2)}, u32[]{:S(2)}) collective-permute-start(bf16[4,720,128]{2,1,0:T(8,128)(2,1)S(1)} %get-tuple-element.19), channel_id=1, source_target_pairs={{0,2},{32,40},{1,3},{33,41},{2,0},{34,42},{3,1},{35,43},{4,6},{36,... | collective-permute-start | bytes 2211848 | tf_op jit(solution)/shard_map/ppermute | solution.py:226
  88.1 1.3 %collective-permute-start.15 = (bf16[4,720,128]{2,1,0:T(8,128)(2,1)S(1)}, bf16[4,720,128]{2,1,0:T(8,128)(2,1)S(1)}, u32[]{:S(2)}, u32[]{:S(2)}) collective-permute-start(bf16[4,720,128]{2,1,0:T(8,128)(2,1)S(1)} %get-tuple-element.20), channel_id=1, source_target_pairs={{0,3},{32,44},{1,0},{33,45},{2,1},{34,46},{3,2},{35,47},{4,7},{36,... | collective-permute-start | bytes 2211848 | tf_op jit(solution)/shard_map/ppermute | solution.py:226
  89.4 7.4 %collective-permute-done.13.b = bf16[4,720,128]{2,1,0:T(8,128)(2,1)S(1)} collective-permute-done((bf16[4,720,128]{2,1,0:T(8,128)(2,1)S(1)}, bf16[4,720,128]{2,1,0:T(8,128)(2,1)S(1)}, u32[]{:S(2)}, u32[]{:S(2)}) %collective-permute-start.13) | collective-permute-done | bytes 737312 | tf_op jit(solution)/shard_map/ppermute | solution.py:226
  96.9 8.3 %collective-permute-done.14.c = bf16[4,720,128]{2,1,0:T(8,128)(2,1)S(1)} collective-permute-done((bf16[4,720,128]{2,1,0:T(8,128)(2,1)S(1)}, bf16[4,720,128]{2,1,0:T(8,128)(2,1)S(1)}, u32[]{:S(2)}, u32[]{:S(2)}) %collective-permute-start.14) | collective-permute-done | bytes 737312 | tf_op jit(solution)/shard_map/ppermute | solution.py:226
  105.1 0.2 collective-permute-done.15.d
  105.4 1.7 %add_first.1 = (f32[720,128]{1,0:T(8,128)S(1)}, bf16[720,128]{1,0:T(8,128)(2,1)S(1)}, bf16[720,128]{1,0:T(8,128)(2,1)S(1)}, bf16[720,128]{1,0:T(8,128)(2,1)S(1)}) custom-call(f32[4,720,128]{2,1,0:T(8,128)} %get-tuple-element.17.a, bf16[4,720,128]{2,1,0:T(8,128)(2,1)S(1)} %collective-permute-done.13.b, bf16[4,720,128]{2,1,0:T(8,128)(2,1)S(1)} %collective-permute-done.14.c, ...), custom_call_target="tpu_custom_call" | custom-call | tf_op jit(solution)/shard_map/add_first/pallas_call | solution.py:228
  107.1 1.4 %collective-permute-start.16 = (bf16[720,128]{1,0:T(8,128)(2,1)S(1)}, bf16[720,128]{1,0:T(8,128)(2,1)S(1)}, u32[]{:S(2)}, u32[]{:S(2)}) collective-permute-start(bf16[720,128]{1,0:T(8,128)(2,1)S(1)} %get-tuple-element.22), channel_id=1, source_target_pairs={{0,4},{32,33},{1,5},{33,34},{2,6},{34,35},{3,7},{35,32},{4,8},{36,... | collective-permute-start | bytes 552968 | tf_op jit(solution)/shard_map/ppermute | solution.py:229
  108.5 2.1 %collective-permute-start.17 = (bf16[720,128]{1,0:T(8,128)(2,1)S(1)}, bf16[720,128]{1,0:T(8,128)(2,1)S(1)}, u32[]{:S(2)}, u32[]{:S(2)}) collective-permute-start(bf16[720,128]{1,0:T(8,128)(2,1)S(1)} %get-tuple-element.23), channel_id=1, source_target_pairs={{0,8},{32,34},{1,9},{33,35},{2,10},{34,32},{3,11},{35,33},{4,12},{... | collective-permute-start | bytes 552968 | tf_op jit(solution)/shard_map/ppermute | solution.py:229
  110.6 1.0 collective-permute-start.18
  111.6 1.6 %collective-permute-done.16.b = bf16[720,128]{1,0:T(8,128)(2,1)S(1)} collective-permute-done((bf16[720,128]{1,0:T(8,128)(2,1)S(1)}, bf16[720,128]{1,0:T(8,128)(2,1)S(1)}, u32[]{:S(2)}, u32[]{:S(2)}) %collective-permute-start.16) | collective-permute-done | bytes 184352 | tf_op jit(solution)/shard_map/ppermute | solution.py:229
  113.2 2.3 %collective-permute-done.17.c = bf16[720,128]{1,0:T(8,128)(2,1)S(1)} collective-permute-done((bf16[720,128]{1,0:T(8,128)(2,1)S(1)}, bf16[720,128]{1,0:T(8,128)(2,1)S(1)}, u32[]{:S(2)}, u32[]{:S(2)}) %collective-permute-start.17) | collective-permute-done | bytes 184352 | tf_op jit(solution)/shard_map/ppermute | solution.py:229
  115.5 0.0 collective-permute-done.18.d
  115.5 0.2 add_second.1
  115.7 1.8 %collective-permute-start.19 = (f32[3,72,128]{2,1,0:T(8,128)S(1)}, f32[3,72,128]{2,1,0:T(8,128)S(1)}, u32[]{:S(2)}, u32[]{:S(2)}) collective-permute-start(f32[3,72,128]{2,1,0:T(8,128)S(1)} %get-tuple-element.26), channel_id=1, source_target_pairs={{0,16},{16,0},{1,17},{17,1},{2,18},{18,2},{3,19},{19,3},{4,20},{20... | collective-permute-start | bytes 331784 | tf_op jit(solution)/shard_map/ppermute | solution.py:231
  117.5 8.4 %collective-permute-start.20 = (f32[3,72,128]{2,1,0:T(8,128)S(1)}, f32[3,72,128]{2,1,0:T(8,128)S(1)}, u32[]{:S(2)}, u32[]{:S(2)}) collective-permute-start(f32[3,72,128]{2,1,0:T(8,128)S(1)} %get-tuple-element.27), channel_id=1, source_target_pairs={{0,32},{32,0},{1,33},{33,1},{2,34},{34,2},{3,35},{35,3},{4,36},{36... | collective-permute-start | bytes 331784 | tf_op jit(solution)/shard_map/ppermute | solution.py:232
  125.9 0.0 collective-permute-start.21
  125.9 0.0 collective-permute-done.19.from_zl
  125.9 1.0 collective-permute-done.20.from_c
  126.9 3.7 %collective-permute-done.21.from_czl = f32[3,72,128]{2,1,0:T(8,128)S(1)} collective-permute-done((f32[3,72,128]{2,1,0:T(8,128)S(1)}, f32[3,72,128]{2,1,0:T(8,128)S(1)}, u32[]{:S(2)}, u32[]{:S(2)}) %collective-permute-start.21) | collective-permute-done | bytes 110624 | tf_op jit(solution)/shard_map/ppermute | solution.py:233
  130.6 0.2 finish.1
  130.7 0.8 copy.5
  (5 shorter events, 0.1 us)
Async XLA Ops:
  0.0 42.6 %collective-permute-start.8 = (bf16[2304,1152]{1,0:T(8,128)(2,1)}, bf16[2304,1152]{1,0:T(8,128)(2,1)}, u32[]{:S(2)}, u32[]{:S(2)}) collective-permute-start(bf16[2304,1152]{1,0:T(8,128)(2,1)} %own_ref.2), channel_id=1, source_target_pairs={{0,32},{32,0},{1,33},{33,1},{2,34},{34,2},{3,35},{35,3},{4,36},{36... | collective-permute-start | bytes 15925256 | tf_op jit(solution)/shard_map/ppermute | solution.py:179
  1.4 74.5 %collective-permute-start.12 = (bf16[1152,2304]{1,0:T(8,128)(2,1)}, bf16[1152,2304]{1,0:T(8,128)(2,1)}, u32[]{:S(2)}, u32[]{:S(2)}) collective-permute-start(bf16[1152,2304]{1,0:T(8,128)(2,1)} %own_ref.3), channel_id=1, source_target_pairs={{0,32},{32,0},{1,33},{33,1},{2,34},{34,2},{3,35},{35,3},{4,36},{36... | collective-permute-start | bytes 15925256 | tf_op jit(solution)/shard_map/ppermute | solution.py:180
  1.4 0.9 copy-start
  2.5 8.3 %collective-permute-start = (bf16[360,128]{1,0:T(8,128)(2,1)S(1)}, bf16[360,128]{1,0:T(8,128)(2,1)S(1)}, u32[]{:S(2)}, u32[]{:S(2)}) collective-permute-start(bf16[360,128]{1,0:T(8,128)(2,1)S(1)} %pack_codes.1), channel_id=1, source_target_pairs={{64,16},{80,64},{16,80},{0,0},{65,17},{81,65},{17,81},{1,1},{66,18... | collective-permute-start | bytes 276488 | tf_op jit(solution)/shard_map/ppermute | solution.py:184
  3.2 9.3 %collective-permute-start.1 = (bf16[360,128]{1,0:T(8,128)(2,1)S(1)}, bf16[360,128]{1,0:T(8,128)(2,1)S(1)}, u32[]{:S(2)}, u32[]{:S(2)}) collective-permute-start(bf16[360,128]{1,0:T(8,128)(2,1)S(1)} %pack_codes.1), channel_id=1, source_target_pairs={{0,16},{16,64},{64,0},{80,80},{1,17},{17,65},{65,1},{81,81},{2,18}... | collective-permute-start | bytes 276488 | tf_op jit(solution)/shard_map/ppermute | solution.py:183
  12.6 6.0 %collective-permute-start.2 = (bf16[2,360,128]{2,1,0:T(8,128)(2,1)S(1)}, bf16[2,360,128]{2,1,0:T(8,128)(2,1)S(1)}, u32[]{:S(2)}, u32[]{:S(2)}) collective-permute-start(bf16[2,360,128]{2,1,0:T(8,128)(2,1)S(1)} %pad_maximum_fusion.a_ref), channel_id=1, source_target_pairs={{0,1},{32,36},{1,2},{33,37},{2,3},{34,38},{3,0},{35,39},{4,5},{36,... | collective-permute-start | bytes 552968 | tf_op jit(solution)/shard_map/ppermute | solution.py:187
  13.9 7.8 %collective-permute-start.3 = (bf16[2,360,128]{2,1,0:T(8,128)(2,1)S(1)}, bf16[2,360,128]{2,1,0:T(8,128)(2,1)S(1)}, u32[]{:S(2)}, u32[]{:S(2)}) collective-permute-start(bf16[2,360,128]{2,1,0:T(8,128)(2,1)S(1)} %pad_maximum_fusion.a_ref), channel_id=1, source_target_pairs={{0,2},{32,40},{1,3},{33,41},{2,0},{34,42},{3,1},{35,43},{4,6},{36,... | collective-permute-start | bytes 552968 | tf_op jit(solution)/shard_map/ppermute | solution.py:187
  16.5 5.2 %collective-permute-start.4 = (bf16[2,360,128]{2,1,0:T(8,128)(2,1)S(1)}, bf16[2,360,128]{2,1,0:T(8,128)(2,1)S(1)}, u32[]{:S(2)}, u32[]{:S(2)}) collective-permute-start(bf16[2,360,128]{2,1,0:T(8,128)(2,1)S(1)} %pad_maximum_fusion.a_ref), channel_id=1, source_target_pairs={{0,3},{32,44},{1,0},{33,45},{2,1},{34,46},{3,2},{35,47},{4,7},{36,... | collective-permute-start | bytes 552968 | tf_op jit(solution)/shard_map/ppermute | solution.py:187
  22.2 11.9 %collective-permute-start.5 = (bf16[320,1152]{1,0:T(8,128)(2,1)S(1)}, bf16[320,1152]{1,0:T(8,128)(2,1)S(1)}, u32[]{:S(2)}, u32[]{:S(2)}) collective-permute-start(bf16[320,1152]{1,0:T(8,128)(2,1)S(1)} %merge_codes.1.m0), channel_id=1, source_target_pairs={{0,4},{32,33},{1,5},{33,34},{2,6},{34,35},{3,7},{35,32},{4,8},{36,... | collective-permute-start | bytes 2211848 | tf_op jit(solution)/shard_map/ppermute | solution.py:189
  23.1 19.5 %collective-permute-start.6 = (bf16[320,1152]{1,0:T(8,128)(2,1)S(1)}, bf16[320,1152]{1,0:T(8,128)(2,1)S(1)}, u32[]{:S(2)}, u32[]{:S(2)}) collective-permute-start(bf16[320,1152]{1,0:T(8,128)(2,1)S(1)} %merge_codes.1.m0), channel_id=1, source_target_pairs={{0,8},{32,34},{1,9},{33,35},{2,10},{34,32},{3,11},{35,33},{4,12},{... | collective-permute-start | bytes 2211848 | tf_op jit(solution)/shard_map/ppermute | solution.py:189
  25.6 17.0 %collective-permute-start.7 = (bf16[320,1152]{1,0:T(8,128)(2,1)S(1)}, bf16[320,1152]{1,0:T(8,128)(2,1)S(1)}, u32[]{:S(2)}, u32[]{:S(2)}) collective-permute-start(bf16[320,1152]{1,0:T(8,128)(2,1)S(1)} %merge_codes.1.m0), channel_id=1, source_target_pairs={{0,12},{32,35},{1,13},{33,32},{2,14},{34,33},{3,15},{35,34},{4,0},... | collective-permute-start | bytes 2211848 | tf_op jit(solution)/shard_map/ppermute | solution.py:189
  50.8 3.0 %copy-start.1 = (f32[320,1152]{1,0:T(8,128)S(1)}, f32[320,1152]{1,0:T(8,128)}, u32[]{:S(2)}) copy-start(f32[320,1152]{1,0:T(8,128)} %project_in.1) | copy-start | bytes 4423684
  53.0 3.3 %copy-start.2 = (s32[160]{0:T(256)S(1)}, s32[160]{0:T(256)}, u32[]{:S(2)}) copy-start(s32[160]{0:T(256)} %param.5) | copy-start | bytes 1924
  53.9 21.3 %collective-permute-start.9 = (f16[320,1152]{1,0:T(8,128)(2,1)S(1)}, f16[320,1152]{1,0:T(8,128)(2,1)S(1)}, u32[]{:S(2)}, u32[]{:S(2)}) collective-permute-start(f16[320,1152]{1,0:T(8,128)(2,1)S(1)} %multiply_convert_fusion), channel_id=1, source_target_pairs={{0,64},{64,0},{1,65},{65,1},{2,66},{66,2},{3,67},{67,3},{4,68},{68... | collective-permute-start | bytes 2211848 | tf_op jit(solution)/shard_map/ppermute | solution.py:203
  56.3 13.7 %collective-permute-start.11 = (s32[160]{0:T(256)S(1)}, s32[160]{0:T(256)S(1)}, u32[]{:S(2)}, u32[]{:S(2)}) collective-permute-start(s32[160]{0:T(256)S(1)} %copy-done.2), channel_id=1, source_target_pairs={{0,64},{64,0},{1,65},{65,1},{2,66},{66,2},{3,67},{67,3},{4,68},{68... | collective-permute-start | bytes 1928 | tf_op jit(solution)/shard_map/ppermute | solution.py:205
  70.0 4.0 %collective-permute-start.10 = (f32[8,128]{1,0:T(8,128)S(1)}, f32[8,128]{1,0:T(8,128)S(1)}, u32[]{:S(2)}, u32[]{:S(2)}) collective-permute-start(f32[8,128]{1,0:T(8,128)S(1)} %broadcast_in_dim.4), channel_id=1, source_target_pairs={{0,64},{64,0},{1,65},{65,1},{2,66},{66,2},{3,67},{67,3},{4,68},{68... | collective-permute-start | bytes 12296 | tf_op jit(solution)/shard_map/ppermute | solution.py:204
  85.0 11.9 %collective-permute-start.13 = (bf16[4,720,128]{2,1,0:T(8,128)(2,1)S(1)}, bf16[4,720,128]{2,1,0:T(8,128)(2,1)S(1)}, u32[]{:S(2)}, u32[]{:S(2)}) collective-permute-start(bf16[4,720,128]{2,1,0:T(8,128)(2,1)S(1)} %get-tuple-element.18), channel_id=1, source_target_pairs={{0,1},{32,36},{1,2},{33,37},{2,3},{34,38},{3,0},{35,39},{4,5},{36,... | collective-permute-start | bytes 2211848 | tf_op jit(solution)/shard_map/ppermute | solution.py:226
  85.9 19.2 %collective-permute-start.14 = (bf16[4,720,128]{2,1,0:T(8,128)(2,1)S(1)}, bf16[4,720,128]{2,1,0:T(8,128)(2,1)S(1)}, u32[]{:S(2)}, u32[]{:S(2)}) collective-permute-start(bf16[4,720,128]{2,1,0:T(8,128)(2,1)S(1)} %get-tuple-element.19), channel_id=1, source_target_pairs={{0,2},{32,40},{1,3},{33,41},{2,0},{34,42},{3,1},{35,43},{4,6},{36,... | collective-permute-start | bytes 2211848 | tf_op jit(solution)/shard_map/ppermute | solution.py:226
  88.1 17.3 %collective-permute-start.15 = (bf16[4,720,128]{2,1,0:T(8,128)(2,1)S(1)}, bf16[4,720,128]{2,1,0:T(8,128)(2,1)S(1)}, u32[]{:S(2)}, u32[]{:S(2)}) collective-permute-start(bf16[4,720,128]{2,1,0:T(8,128)(2,1)S(1)} %get-tuple-element.20), channel_id=1, source_target_pairs={{0,3},{32,44},{1,0},{33,45},{2,1},{34,46},{3,2},{35,47},{4,7},{36,... | collective-permute-start | bytes 2211848 | tf_op jit(solution)/shard_map/ppermute | solution.py:226
  107.1 6.1 %collective-permute-start.16 = (bf16[720,128]{1,0:T(8,128)(2,1)S(1)}, bf16[720,128]{1,0:T(8,128)(2,1)S(1)}, u32[]{:S(2)}, u32[]{:S(2)}) collective-permute-start(bf16[720,128]{1,0:T(8,128)(2,1)S(1)} %get-tuple-element.22), channel_id=1, source_target_pairs={{0,4},{32,33},{1,5},{33,34},{2,6},{34,35},{3,7},{35,32},{4,8},{36,... | collective-permute-start | bytes 552968 | tf_op jit(solution)/shard_map/ppermute | solution.py:229
  108.5 7.0 %collective-permute-start.17 = (bf16[720,128]{1,0:T(8,128)(2,1)S(1)}, bf16[720,128]{1,0:T(8,128)(2,1)S(1)}, u32[]{:S(2)}, u32[]{:S(2)}) collective-permute-start(bf16[720,128]{1,0:T(8,128)(2,1)S(1)} %get-tuple-element.23), channel_id=1, source_target_pairs={{0,8},{32,34},{1,9},{33,35},{2,10},{34,32},{3,11},{35,33},{4,12},{... | collective-permute-start | bytes 552968 | tf_op jit(solution)/shard_map/ppermute | solution.py:229
  110.6 4.9 %collective-permute-start.18 = (bf16[720,128]{1,0:T(8,128)(2,1)S(1)}, bf16[720,128]{1,0:T(8,128)(2,1)S(1)}, u32[]{:S(2)}, u32[]{:S(2)}) collective-permute-start(bf16[720,128]{1,0:T(8,128)(2,1)S(1)} %get-tuple-element.24), channel_id=1, source_target_pairs={{0,12},{32,35},{1,13},{33,32},{2,14},{34,33},{3,15},{35,34},{4,0},... | collective-permute-start | bytes 552968 | tf_op jit(solution)/shard_map/ppermute | solution.py:229
  115.7 10.2 %collective-permute-start.19 = (f32[3,72,128]{2,1,0:T(8,128)S(1)}, f32[3,72,128]{2,1,0:T(8,128)S(1)}, u32[]{:S(2)}, u32[]{:S(2)}) collective-permute-start(f32[3,72,128]{2,1,0:T(8,128)S(1)} %get-tuple-element.26), channel_id=1, source_target_pairs={{0,16},{16,0},{1,17},{17,1},{2,18},{18,2},{3,19},{19,3},{4,20},{20... | collective-permute-start | bytes 331784 | tf_op jit(solution)/shard_map/ppermute | solution.py:231
  117.5 9.4 %collective-permute-start.20 = (f32[3,72,128]{2,1,0:T(8,128)S(1)}, f32[3,72,128]{2,1,0:T(8,128)S(1)}, u32[]{:S(2)}, u32[]{:S(2)}) collective-permute-start(f32[3,72,128]{2,1,0:T(8,128)S(1)} %get-tuple-element.27), channel_id=1, source_target_pairs={{0,32},{32,0},{1,33},{33,1},{2,34},{34,2},{3,35},{35,3},{4,36},{36... | collective-permute-start | bytes 331784 | tf_op jit(solution)/shard_map/ppermute | solution.py:232
  125.9 4.7 %collective-permute-start.21 = (f32[3,72,128]{2,1,0:T(8,128)S(1)}, f32[3,72,128]{2,1,0:T(8,128)S(1)}, u32[]{:S(2)}, u32[]{:S(2)}) collective-permute-start(f32[3,72,128]{2,1,0:T(8,128)S(1)} %get-tuple-element.28), channel_id=1, source_target_pairs={{0,48},{16,32},{32,16},{48,0},{1,49},{17,33},{33,17},{49,1},{2,50}... | collective-permute-start | bytes 331784 | tf_op jit(solution)/shard_map/ppermute | solution.py:233

commit v2 on v1

v2 whole, which is shorter than its diff:
```python
import jax
import jax.numpy as jnp
from jax import lax
from jax.experimental import pallas as pl
from jax.experimental.pallas import tpu as pltpu
from jax.sharding import Mesh, PartitionSpec as P

BF, F32 = jnp.bfloat16, jnp.float32
QT = 160
PIECE = 288
UNITS = 1152
CHIP_COLS = 72
VMEM = pl.BlockSpec(memory_space=pltpu.VMEM)
ANY = pl.BlockSpec(memory_space=pl.ANY)
YX = ("c", "y", "x")
STEPS = (0, 2, 1, 3)


def first_axis(step):
    pairs = []
    for y in range(4):
        for x in range(4):
            pairs.append((y * 4 + x, y * 4 + (x + step) % 4))
            pairs.append((16 + y * 4 + x, 16 + (y + step) % 4 * 4 + x))
    return pairs


def second_axis(step):
    pairs = []
    for y in range(4):
        for x in range(4):
            pairs.append((y * 4 + x, (y + step) % 4 * 4 + x))
            pairs.append((16 + y * 4 + x, 16 + y * 4 + (x + step) % 4))
    return pairs


def call(kernel, outs, ins, scratch=(), flops=0, nbytes=0, vmem=8, name=None):
    return pl.pallas_call(
        kernel,
        out_shape=outs,
        in_specs=ins,
        out_specs=jax.tree.map(lambda _: VMEM, outs),
        scratch_shapes=list(scratch),
        compiler_params=pltpu.CompilerParams(vmem_limit_bytes=vmem * 2**20),
        cost_estimate=pl.CostEstimate(flops=flops, bytes_accessed=nbytes, transcendentals=0),
        name=name,
    )


def dot(a, b):
    return jnp.dot(a, b, preferred_element_type=F32)


def pack_codes(x_ref, o_ref):
    o_ref[0:QT] = x_ref[:, 0:128]
    o_ref[QT : 2 * QT] = x_ref[:, 128:256]
    tail = x_ref[:, 256:288]
    src = lax.broadcasted_iota(jnp.int32, (32, 128), 0)
    dst = lax.broadcasted_iota(jnp.int32, (32, 128), 1)
    total = jnp.zeros((40, 128), F32)
    for j in range(4):
        place = jnp.where(dst == src + 32 * j, 1.0, 0.0).astype(BF)
        total += dot(tail, place)[40 * j : 40 * j + 40]
    o_ref[2 * QT : 360] = total.astype(BF)


def merge_codes(a_ref, b_ref, c_ref, d_ref, *outs):
    pieces = (a_ref, b_ref, c_ref, d_ref)
    src = lax.broadcasted_iota(jnp.int32, (512, 128), 0)
    dst = lax.broadcasted_iota(jnp.int32, (512, 128), 1)
    for q, o_ref in enumerate(outs):
        for j, ref in enumerate(pieces):
            o_ref[:, 256 * j : 256 * j + 128] = ref[q, 0:QT]
            o_ref[:, 256 * j + 128 : 256 * j + 256] = ref[q, QT : 2 * QT]
        tails = jnp.concatenate([ref[q, 2 * QT : 360] for ref in pieces], axis=1)
        groups = []
        for j in range(4):
            place = (src // 128 == dst // 32) & (src % 128 == 32 * j + dst % 32)
            groups.append(dot(tails, jnp.where(place, 1.0, 0.0).astype(BF)))
        o_ref[:, 1024:1152] = jnp.concatenate(groups, axis=0).astype(BF)


def own_place():
    c, y, x = lax.axis_index("c"), lax.axis_index("y"), lax.axis_index("x")
    return c, jnp.where(c == 0, x, y), jnp.where(c == 0, y, x)


def arrange_rows(own_ref, other_ref, w_ref, sem):
    c, first, second = own_place()
    for i in range(4):
        s = lax.rem(second + 4 - STEPS[i], 4)
        for j in range(4):
            f = lax.rem(first + 4 - STEPS[j], 4)
            y, x = jnp.where(c == 0, s, f), jnp.where(c == 0, f, s)
            row = lax.rem(y, 2) * UNITS + x * PIECE
            for ref, here in ((own_ref, lax.div(y, 2) == c), (other_ref, lax.div(y, 2) != c)):

                @pl.when(here)
                def _(ref=ref):
                    for at, to, n in ((0, 256 * j, 256), (256, 1024 + 32 * j, 32)):
                        pltpu.make_async_copy(
                            ref.at[pl.ds(pl.multiple_of(row + at, 32), n)], w_ref.at[pl.ds(i * UNITS + to, n)], sem
                        ).start()

    pltpu.make_async_copy(w_ref, w_ref, sem).wait()


def project_in(m0, m1, m2, m3, w_ref, o_ref, scale_ref, power_ref, x_ref):
    for i, m in enumerate((m0, m1, m2, m3)):
        x_ref[:, i * UNITS : (i + 1) * UNITS] = m[...]
    most = jnp.zeros((QT, 128), F32)
    for n in range(0, UNITS, 256):
        to = min(n + 256, UNITS)
        part = dot(x_ref[...], w_ref[:, n:to])
        o_ref[:, n:to] = part
        for k in range(0, to - n, 128):
            most = jnp.maximum(most, jnp.abs(part[:, k : k + 128]))
    most = jnp.full((8, UNITS), jnp.max(most))
    power = 13.0 - jnp.ceil(jnp.log(jnp.maximum(most, 1e-30)) * 1.4426950408889634)
    power_ref[...] = power
    scale_ref[...] = jnp.exp2(power)


def project_out(a_ref, own_ref, other_ref, o0, o1, o2, o3, t_ref, tail_ref):
    for g in range(4):
        w_ref = own_ref if g < 2 else other_ref
        for n in range(0, UNITS, 256):
            to = min(n + 256, UNITS)
            part = dot(a_ref[...], w_ref[:, g % 2 * UNITS + n : g % 2 * UNITS + to])
            t_ref[g, n:to] = part[:128].T
            tail_ref[32 * g : 32 * g + 32, n:to] = part[128:]
    t_ref[4] = tail_ref[...].T
    c, first, _ = own_place()
    for rel, o in zip((0,) + STEPS[1:], (o0, o1, o2, o3)):
        f = lax.rem(first + rel, 4)
        for s in range(4):
            at = pl.ds(pl.multiple_of(jnp.where(c == 0, s * 4 + f, f * 4 + s) * CHIP_COLS, 8), CHIP_COLS)
            for p in range(2):
                both = jnp.concatenate([t_ref[2 * p, at], t_ref[2 * p + 1, at]], axis=0)
                o[s, 144 * p : 144 * p + 144] = both.astype(o.dtype)
            o[s, 288:360] = t_ref[4, at].astype(o.dtype)


def add_first(a0, b0, c0, d0, a1, b1, c1, d1, o0, o1, o2, o3):
    _, _, second = own_place()
    for rel, o in zip(STEPS, (o0, o1, o2, o3)):
        s = lax.rem(second + rel, 4)
        total = [
            a[s] + b[s].astype(F32) + c[s].astype(F32) + d[s].astype(F32) for a, b, c, d in ((a0, b0, c0, d0), (a1, b1, c1, d1))
        ]
        o[...] = jnp.concatenate(total, axis=0).astype(o.dtype)


def add_second(a, b, c, d, keep, to_zl, to_c, to_czl):
    total = a[...] + b[...].astype(F32) + c[...].astype(F32) + d[...].astype(F32)
    zl = lax.axis_index("zl")
    tiles = total.reshape(10, CHIP_COLS, 128)
    lane = lax.broadcasted_iota(jnp.int32, (CHIP_COLS, 128), 1)

    def share(crel, z):
        g = 2 * crel + z
        tail = jnp.where(lane < 32, pltpu.roll(tiles[4], (128 - 32 * g) % 128, 1), pltpu.roll(tiles[9], (160 - 32 * g) % 128, 1))
        return tiles[g], tiles[5 + g], tail

    for crel, same, swapped in ((0, keep, to_zl), (1, to_c, to_czl)):
        for i, (lo, hi) in enumerate(zip(share(crel, 0), share(crel, 1))):
            same[i] = jnp.where(zl == 0, lo, hi)
            swapped[i] = jnp.where(zl == 0, hi, lo)


def finish(keep, from_zl, from_c, from_czl, o_ref):
    c = lax.axis_index("c")
    for core, a, b in ((c, keep, from_zl), (1 - c, from_c, from_czl)):
        tail = (a[2] + b[2]).T
        for q in range(2):
            row = (2 * q + core) * QT
            o_ref[pl.ds(pl.multiple_of(row, 8), 128)] = (a[q] + b[q]).T
            o_ref[pl.ds(pl.multiple_of(row + 128, 8), 32)] = tail[32 * q : 32 * q + 32]


def shape(dims, dtype):
    return jax.ShapeDtypeStruct(dims, dtype)


def shards(codes, exponents, w_in, w_out):
    zh, zl = lax.axis_index("zh"), lax.axis_index("zl")
    swap = [(0, 1), (1, 0)]
    z = ("zh", "zl")
    w_in_other = lax.ppermute(w_in, "c", swap)
    w_out_other = lax.ppermute(w_out, "c", swap)

    packed = call(pack_codes, shape((360, 128), BF), [VMEM], name="pack_codes")(codes)
    one = lax.ppermute(packed, z, [(0, 1), (1, 2), (2, 0), (3, 3)])
    two = lax.ppermute(packed, z, [(2, 1), (3, 2), (1, 3), (0, 0)])
    piece = jnp.stack([jnp.where(zh == zl, two, one), jnp.where(zh == zl, one, two)])

    around = [lax.ppermute(piece, YX, first_axis(k)) for k in STEPS[1:]]
    quarter = shape((QT, UNITS), BF)
    merged = call(merge_codes, [quarter] * 2, [VMEM] * 4, name="merge_codes")(piece, *around)
    around = [[lax.ppermute(m, YX, second_axis(k)) for k in STEPS[1:]] for m in merged]
    weights = call(
        arrange_rows,
        shape((4 * UNITS, UNITS), BF),
        [ANY] * 2,
        [pltpu.SemaphoreType.DMA],
        nbytes=2 * 4608 * 1152 * 2,
        name="arrange_rows",
    )(w_in, w_in_other)
    other_exponents = lax.ppermute(exponents, "zh", swap)
    powers = [jnp.where(zh == 0, exponents, other_exponents), jnp.where(zh == 0, other_exponents, exponents)]

    scattered = []
    for m, others, power in zip(merged, around, powers):
        preact, scale, scale_power = call(
            project_in,
            [shape((QT, UNITS), F32)] + [shape((8, UNITS), F32)] * 2,
            [VMEM] * 5,
            [pltpu.VMEM((QT, 4 * UNITS), BF)],
            flops=2 * QT * 4608 * 1152,
            nbytes=4608 * 1152 * 2,
            name="project_in",
        )(m, *others, weights)
        sent = jnp.concatenate([(preact * scale[:1]).astype(jnp.float16), scale_power.astype(jnp.float16)])
        got = lax.ppermute(sent, "zh", swap).astype(F32)
        row_scale = jnp.exp2(power.astype(F32))[:, None]
        summed = (preact + got[:QT] * jnp.exp2(-got[QT : QT + 1])) * row_scale
        activ = jax.nn.gelu(summed, approximate=True).astype(BF)
        part = (4, 360, 128)
        mine, *away = call(
            project_out,
            [shape(part, F32)] + [shape(part, BF)] * 3,
            [VMEM] * 3,
            [pltpu.VMEM((5, UNITS, 128), F32), pltpu.VMEM((128, UNITS), F32)],
            flops=2 * QT * 4608 * 1152,
            nbytes=4608 * 1152 * 2,
            vmem=12,
            name="project_out",
        )(activ, w_out, w_out_other)
        scattered += [mine] + [lax.ppermute(v, YX, first_axis(k)) for k, v in zip(STEPS[1:], away)]
    part = (720, 128)
    mine, *away = call(add_first, [shape(part, F32)] + [shape(part, BF)] * 3, [VMEM] * 8, name="add_first")(*scattered)
    away = [lax.ppermute(v, YX, second_axis(k)) for k, v in zip(STEPS[1:], away)]
    keep, to_zl, to_c, to_czl = call(add_second, [shape((3, CHIP_COLS, 128), F32)] * 4, [VMEM] * 4, name="add_second")(mine, *away)
    from_zl = lax.ppermute(to_zl, "zl", swap)
    from_c = lax.ppermute(to_c, "c", swap)
    from_czl = lax.ppermute(to_czl, ("c", "zl"), [(0, 3), (1, 2), (2, 1), (3, 0)])
    return call(finish, shape((4 * QT, CHIP_COLS), F32), [VMEM] * 4, name="finish")(keep, from_zl, from_c, from_czl)


def solution(mesh):
    split = Mesh(mesh.devices.reshape(2, 2, 2, 4, 4), ("zh", "c", "zl", "y", "x"))
    batch, hidden = ("zh", "c"), ("zl", "y", "x")
    placed = (P(batch, hidden), P(batch), P(batch, hidden), P(hidden, batch))
    return jax.shard_map(shards, mesh=split, in_specs=placed, out_specs=P(None, batch + hidden), check_vma=False)
```

time: 133 us -> 113 us (0.85); the launches traced: 132 us -> 113 us
  waiting for transfers between devices: 60.7 us -> 32.3 us
  starting transfers between devices: 44 us -> 51.7 us
  local copies, waits for them, and re-layouts: 2.33 us -> 6.79 us
  between operations: 1.61 us -> 0.26 us
    ppermute x11 -> x17, waiting for transfers between devices: 37.5 us -> 13.1 us  [the longest x6 9.14 us: shards(): lax.ppermute(v, YX, first_axis(k))]
    ppermute x11 -> x17, starting transfers between devices: 18.9 us -> 25.7 us  [the longest x6 7.91 us: shards(): lax.ppermute(m, YX, second_axis(k))]
    unnamed x6 -> x12, local copies, waits for them, and re-layouts: 0.91 us -> 5.92 us
    ppermute x1, waiting for transfers between devices: 13 us -> 9.79 us  [shards(): other_exponents = lax.ppermute(exponents, 'zh', swap)]
    reduce_max x1 -> x0, other arithmetic: 2.19 us -> none  [shards(): most = jnp.max(jnp.abs(preact))]
    concatenate x0 -> x2, other arithmetic: none -> 1.7 us  [shards(): jnp.concatenate([(preact * scale[:1]).astype(jnp.float16), scale_power.as...]
    pallas_call x4 -> x7, Pallas kernels: 19.3 us -> 18.7 us  [the longest x2 10.3 us: shards(): call(project_out, [shape(part, F32)] + [shape(part, BF)] * 3, [VMEM] * 3,...]
  transfers between devices with their start and end apart: 22 -> 28, of which waited for: 14 -> 13; matrix products, arithmetic and copies ran while one was open for 3% -> 2% of each run, Pallas kernels for 7% -> 12%
where the time goes in v2:
time: 113 us
  starting transfers between devices  51.7 us (46%)
  waiting for transfers between devices  32.3 us (29%)
  Pallas kernels  19.2 us (17%)
  local copies, waits for them, and re-layouts  6.79 us (6%)
  other arithmetic  2.78 us (2%)
    pallas_call x2, Pallas kernels, shards(): call(project_out, [shape(part, F32)] + [shape(part, BF)] * 3, [VMEM] * 3,...  10.3 us
    ppermute x1, waiting for transfers between devices, shards(): other_exponents = lax.ppermute(exponents, 'zh', swap)  9.79 us
    ppermute x6, waiting for transfers between devices, shards(): lax.ppermute(v, YX, first_axis(k))  9.14 us
    ppermute x1, starting transfers between devices, shards(): from_c = lax.ppermute(to_c, 'c', swap)  8.94 us
    ppermute x6, starting transfers between devices, shards(): lax.ppermute(m, YX, second_axis(k))  7.91 us
    ppermute x1, starting transfers between devices, shards(): one = lax.ppermute(packed, z, [(0, 1), (1, 2), (2, 0), (3, 3)])  7.57 us
    ppermute x6, starting transfers between devices, shards(): lax.ppermute(v, YX, first_axis(k))  7.32 us
    unnamed x12, local copies, waits for them, and re-layouts  5.92 us
  transfers between devices with their start and end apart: 28, of which 13 were waited for; matrix products, arithmetic and copies ran while one was open for 2% of the time, Pallas kernels for 12%

profile of v2, /device:TPU:1, one launch (start us, length us, event | category | flops | bytes accessed | tf_op | source)
XLA Modules:
  0.0 113.0 jit_solution(17379577922831121996)
XLA Ops:
  0.0 1.4 %collective-permute-start.8 = (bf16[2304,1152]{1,0:T(8,128)(2,1)}, bf16[2304,1152]{1,0:T(8,128)(2,1)}, u32[]{:S(2)}, u32[]{:S(2)}) collective-permute-start(bf16[2304,1152]{1,0:T(8,128)(2,1)} %own_ref.3), channel_id=1, source_target_pairs={{0,32},{32,0},{1,33},{33,1},{2,34},{34,2},{3,35},{35,3},{4,36},{36... | collective-permute-start | bytes 15925256 | tf_op jit(solution)/shard_map/ppermute | solution.py:189
  1.4 0.0 collective-permute-start.11
  1.4 0.9 copy-done.2
  2.3 0.2 pack_codes.1
  2.5 0.7 collective-permute-start
  3.2 7.6 %collective-permute-start.1 = (bf16[360,128]{1,0:T(8,128)(2,1)S(1)}, bf16[360,128]{1,0:T(8,128)(2,1)S(1)}, u32[]{:S(2)}, u32[]{:S(2)}) collective-permute-start(bf16[360,128]{1,0:T(8,128)(2,1)S(1)} %pack_codes.1), channel_id=1, source_target_pairs={{0,16},{16,64},{64,0},{80,80},{1,17},{17,65},{65,1},{81,81},{2,18}... | collective-permute-start | bytes 276488 | tf_op jit(solution)/shard_map/ppermute | solution.py:193
  10.8 0.0 collective-permute-done
  10.8 1.7 %collective-permute-done.1 = bf16[360,128]{1,0:T(8,128)(2,1)S(1)} collective-permute-done((bf16[360,128]{1,0:T(8,128)(2,1)S(1)}, bf16[360,128]{1,0:T(8,128)(2,1)S(1)}, u32[]{:S(2)}, u32[]{:S(2)}) %collective-permute-start.1) | collective-permute-done | bytes 92192 | tf_op jit(solution)/shard_map/ppermute | solution.py:193
  12.6 3.0 %collective-permute-start.2 = (bf16[2,360,128]{2,1,0:T(8,128)(2,1)S(1)}, bf16[2,360,128]{2,1,0:T(8,128)(2,1)S(1)}, u32[]{:S(2)}, u32[]{:S(2)}) collective-permute-start(bf16[2,360,128]{2,1,0:T(8,128)(2,1)S(1)} %pad_maximum_fusion.2.a_ref), channel_id=1, source_target_pairs={{0,2},{32,40},{1,3},{33,41},{2,0},{34,42},{3,1},{35,43},{4,6},{36,... | collective-permute-start | bytes 552968 | tf_op jit(solution)/shard_map/ppermute | solution.py:197
  15.6 0.4 collective-permute-start.3
  15.9 2.3 %collective-permute-start.4 = (bf16[2,360,128]{2,1,0:T(8,128)(2,1)S(1)}, bf16[2,360,128]{2,1,0:T(8,128)(2,1)S(1)}, u32[]{:S(2)}, u32[]{:S(2)}) collective-permute-start(bf16[2,360,128]{2,1,0:T(8,128)(2,1)S(1)} %pad_maximum_fusion.2.a_ref), channel_id=1, source_target_pairs={{0,3},{32,44},{1,0},{33,45},{2,1},{34,46},{3,2},{35,47},{4,7},{36,... | collective-permute-start | bytes 552968 | tf_op jit(solution)/shard_map/ppermute | solution.py:197
  18.2 0.6 collective-permute-done.2.b_ref
  18.8 2.3 %collective-permute-done.3.c_ref = bf16[2,360,128]{2,1,0:T(8,128)(2,1)S(1)} collective-permute-done((bf16[2,360,128]{2,1,0:T(8,128)(2,1)S(1)}, bf16[2,360,128]{2,1,0:T(8,128)(2,1)S(1)}, u32[]{:S(2)}, u32[]{:S(2)}) %collective-permute-start.3) | collective-permute-done | bytes 184352 | tf_op jit(solution)/shard_map/ppermute | solution.py:197
  21.2 0.4 merge_codes.1
  21.6 2.8 %collective-permute-start.15 = (bf16[160,1152]{1,0:T(8,128)(2,1)S(1)}, bf16[160,1152]{1,0:T(8,128)(2,1)S(1)}, u32[]{:S(2)}, u32[]{:S(2)}) collective-permute-start(bf16[160,1152]{1,0:T(8,128)(2,1)S(1)} %get-tuple-element.37.m0), channel_id=1, source_target_pairs={{0,8},{32,34},{1,9},{33,35},{2,10},{34,32},{3,11},{35,33},{4,12},{... | collective-permute-start | bytes 1105928 | tf_op jit(solution)/shard_map/ppermute | solution.py:200
  24.4 0.3 collective-permute-start.16
  24.7 2.4 %collective-permute-start.17 = (bf16[160,1152]{1,0:T(8,128)(2,1)S(1)}, bf16[160,1152]{1,0:T(8,128)(2,1)S(1)}, u32[]{:S(2)}, u32[]{:S(2)}) collective-permute-start(bf16[160,1152]{1,0:T(8,128)(2,1)S(1)} %get-tuple-element.37.m0), channel_id=1, source_target_pairs={{0,12},{32,35},{1,13},{33,32},{2,14},{34,33},{3,15},{35,34},{4,0},... | collective-permute-start | bytes 1105928 | tf_op jit(solution)/shard_map/ppermute | solution.py:200
  27.1 0.0 collective-permute-done.8.other_ref
  27.1 2.5 %copy-done.1 = bf16[2304,1152]{1,0:T(8,128)(2,1)S(1)} copy-done((bf16[2304,1152]{1,0:T(8,128)(2,1)S(1)}, bf16[2304,1152]{1,0:T(8,128)(2,1)}, u32[]{:S(2)}) %copy-start.1) | copy-done | bytes 5308440
  29.6 3.2 %arrange_rows.1.w_ref = bf16[4608,1152]{1,0:T(8,128)(2,1)S(1)} custom-call(bf16[2304,1152]{1,0:T(8,128)(2,1)S(1)} %copy-done.1, bf16[2304,1152]{1,0:T(8,128)(2,1)} %collective-permute-done.8.other_ref), custom_call_target="tpu_custom_call" | custom-call | bytes 21233664 | tf_op jit(solution)/shard_map/arrange_rows/pallas_call | solution.py:201
  32.8 0.6 collective-permute-start.6
  33.4 0.3 collective-permute-done.16.m2
  33.8 1.8 %collective-permute-start.7 = (bf16[160,1152]{1,0:T(8,128)(2,1)S(1)}, bf16[160,1152]{1,0:T(8,128)(2,1)S(1)}, u32[]{:S(2)}, u32[]{:S(2)}) collective-permute-start(bf16[160,1152]{1,0:T(8,128)(2,1)S(1)} %get-tuple-element.29.m0), channel_id=1, source_target_pairs={{0,12},{32,35},{1,13},{33,32},{2,14},{34,33},{3,15},{35,34},{4,0},... | collective-permute-start | bytes 1105928 | tf_op jit(solution)/shard_map/ppermute | solution.py:200
  35.5 2.2 %project_in.3 = (f32[160,1152]{1,0:T(8,128)S(1)}, f32[8,1152]{1,0:T(8,128)S(1)}, f32[8,1152]{1,0:T(8,128)S(1)}) custom-call(bf16[160,1152]{1,0:T(8,128)(2,1)S(1)} %get-tuple-element.37.m0, bf16[160,1152]{1,0:T(8,128)(2,1)S(1)} %collective-permute-done.15.m1, bf16[160,1152]{1,0:T(8,128)(2,1)S(1)} %collective-permute-done.16.m2, ...), custom_call_target="tpu_custom_call" | custom-call | flops 1698693120 | bytes 10616832 | tf_op jit(solution)/shard_map/project_in/pallas_call | solution.py:214
  37.8 0.1 multiply_convert_fusion
  37.9 0.8 pad_maximum_fusion.1
  38.7 2.3 %collective-permute-start.18 = (f16[168,1152]{1,0:T(8,128)(2,1)}, f16[168,1152]{1,0:T(8,128)(2,1)S(1)}, u32[]{:S(2)}, u32[]{:S(2)}) collective-permute-start(f16[168,1152]{1,0:T(8,128)(2,1)} %pad_maximum_fusion.1), channel_id=1, source_target_pairs={{0,64},{64,0},{1,65},{65,1},{2,66},{66,2},{3,67},{67,3},{4,68},{68... | collective-permute-start | bytes 1161224 | tf_op jit(solution)/shard_map/ppermute | solution.py:224
  41.0 0.6 collective-permute-done.6.m2
  41.7 0.1 collective-permute-done.7.m3
  41.7 2.2 %project_in.2 = (f32[160,1152]{1,0:T(8,128)S(1)}, f32[8,1152]{1,0:T(8,128)S(1)}, f32[8,1152]{1,0:T(8,128)S(1)}) custom-call(bf16[160,1152]{1,0:T(8,128)(2,1)S(1)} %get-tuple-element.29.m0, bf16[160,1152]{1,0:T(8,128)(2,1)S(1)} %collective-permute-done.5.m1, bf16[160,1152]{1,0:T(8,128)(2,1)S(1)} %collective-permute-done.6.m2, ...), custom_call_target="tpu_custom_call" | custom-call | flops 1698693120 | bytes 10616832 | tf_op jit(solution)/shard_map/project_in/pallas_call | solution.py:214
  44.0 0.1 multiply_convert_fusion.1
  44.1 0.0 slice-start
  44.1 0.8 pad_maximum_fusion
  45.0 2.5 %collective-permute-start.9 = (f16[168,1152]{1,0:T(8,128)(2,1)}, f16[168,1152]{1,0:T(8,128)(2,1)S(1)}, u32[]{:S(2)}, u32[]{:S(2)}) collective-permute-start(f16[168,1152]{1,0:T(8,128)(2,1)} %pad_maximum_fusion), channel_id=1, source_target_pairs={{0,64},{64,0},{1,65},{65,1},{2,66},{66,2},{3,67},{67,3},{4,68},{68... | collective-permute-start | bytes 1161224 | tf_op jit(solution)/shard_map/ppermute | solution.py:224
  47.5 0.4 collective-permute-start.10
  47.9 9.8 %collective-permute-done.10 = s32[160]{0:T(256)S(1)} collective-permute-done((s32[160]{0:T(256)S(1)}, s32[160]{0:T(256)S(1)}, u32[]{:S(2)}, u32[]{:S(2)}) %collective-permute-start.10) | collective-permute-done | bytes 672 | tf_op jit(solution)/shard_map/ppermute | solution.py:209
  57.8 0.1 convert_element_type.37
  57.8 0.1 convert_element_type.32
  58.0 0.7 fusion.7
  58.7 0.0 copy-start
  58.7 2.5 %copy-done = bf16[1152,2304]{1,0:T(8,128)(2,1)S(1)} copy-done((bf16[1152,2304]{1,0:T(8,128)(2,1)S(1)}, bf16[1152,2304]{1,0:T(8,128)(2,1)}, u32[]{:S(2)}) %copy-start) | copy-done | bytes 5308440
  61.2 5.2 %project_out.2 = (f32[4,360,128]{2,1,0:T(8,128)S(1)}, bf16[4,360,128]{2,1,0:T(8,128)(2,1)S(1)}, bf16[4,360,128]{2,1,0:T(8,128)(2,1)S(1)}, bf16[4,360,128]{2,1,0:T(8,128)(2,1)S(1)}) custom-call(bf16[160,1152]{1,0:T(8,128)(2,1)S(1)} %get-tuple-element.57.a_ref, bf16[1152,2304]{1,0:T(8,128)(2,1)S(1)} %copy-done, ...), custom_call_target="tpu_custom_call" | custom-call | flops 1698693120 | bytes 10616832 | tf_op jit(solution)/shard_map/project_out/pallas_call | solution.py:229
  66.4 1.8 %collective-permute-start.12 = (bf16[4,360,128]{2,1,0:T(8,128)(2,1)S(1)}, bf16[4,360,128]{2,1,0:T(8,128)(2,1)S(1)}, u32[]{:S(2)}, u32[]{:S(2)}) collective-permute-start(bf16[4,360,128]{2,1,0:T(8,128)(2,1)S(1)} %get-tuple-element.34), channel_id=1, source_target_pairs={{0,2},{32,40},{1,3},{33,41},{2,0},{34,42},{3,1},{35,43},{4,6},{36,... | collective-permute-start | bytes 1105928 | tf_op jit(solution)/shard_map/ppermute | solution.py:239
  68.2 1.0 collective-permute-start.13
  69.2 1.7 %collective-permute-start.14 = (bf16[4,360,128]{2,1,0:T(8,128)(2,1)S(1)}, bf16[4,360,128]{2,1,0:T(8,128)(2,1)S(1)}, u32[]{:S(2)}, u32[]{:S(2)}) collective-permute-start(bf16[4,360,128]{2,1,0:T(8,128)(2,1)S(1)} %get-tuple-element.36), channel_id=1, source_target_pairs={{0,3},{32,44},{1,0},{33,45},{2,1},{34,46},{3,2},{35,47},{4,7},{36,... | collective-permute-start | bytes 1105928 | tf_op jit(solution)/shard_map/ppermute | solution.py:239
  70.9 5.0 %project_out.3 = (f32[4,360,128]{2,1,0:T(8,128)S(1)}, bf16[4,360,128]{2,1,0:T(8,128)(2,1)S(1)}, bf16[4,360,128]{2,1,0:T(8,128)(2,1)S(1)}, bf16[4,360,128]{2,1,0:T(8,128)(2,1)S(1)}) custom-call(bf16[160,1152]{1,0:T(8,128)(2,1)S(1)} %get-tuple-element.58.a_ref, bf16[1152,2304]{1,0:T(8,128)(2,1)S(1)} %bitcast.5, ...), custom_call_target="tpu_custom_call" | custom-call | flops 1698693120 | bytes 10616832 | tf_op jit(solution)/shard_map/project_out/pallas_call | solution.py:229
  76.0 0.1 collective-permute-start.19
  76.1 0.5 collective-permute-start.20
  76.6 2.2 %collective-permute-start.21 = (bf16[4,360,128]{2,1,0:T(8,128)(2,1)S(1)}, bf16[4,360,128]{2,1,0:T(8,128)(2,1)S(1)}, u32[]{:S(2)}, u32[]{:S(2)}) collective-permute-start(bf16[4,360,128]{2,1,0:T(8,128)(2,1)S(1)} %get-tuple-element.44), channel_id=1, source_target_pairs={{0,3},{32,44},{1,0},{33,45},{2,1},{34,46},{3,2},{35,47},{4,7},{36,... | collective-permute-start | bytes 1105928 | tf_op jit(solution)/shard_map/ppermute | solution.py:239
  78.8 5.2 %collective-permute-done.19.b1 = bf16[4,360,128]{2,1,0:T(8,128)(2,1)S(1)} collective-permute-done((bf16[4,360,128]{2,1,0:T(8,128)(2,1)S(1)}, bf16[4,360,128]{2,1,0:T(8,128)(2,1)S(1)}, u32[]{:S(2)}, u32[]{:S(2)}) %collective-permute-start.19) | collective-permute-done | bytes 368672 | tf_op jit(solution)/shard_map/ppermute | solution.py:239
  84.0 3.9 %collective-permute-done.20.c1 = bf16[4,360,128]{2,1,0:T(8,128)(2,1)S(1)} collective-permute-done((bf16[4,360,128]{2,1,0:T(8,128)(2,1)S(1)}, bf16[4,360,128]{2,1,0:T(8,128)(2,1)S(1)}, u32[]{:S(2)}, u32[]{:S(2)}) %collective-permute-start.20) | collective-permute-done | bytes 368672 | tf_op jit(solution)/shard_map/ppermute | solution.py:239
  88.0 0.4 add_first.1
  88.3 2.3 %collective-permute-start.22 = (bf16[720,128]{1,0:T(8,128)(2,1)S(1)}, bf16[720,128]{1,0:T(8,128)(2,1)S(1)}, u32[]{:S(2)}, u32[]{:S(2)}) collective-permute-start(bf16[720,128]{1,0:T(8,128)(2,1)S(1)} %get-tuple-element.46), channel_id=1, source_target_pairs={{0,8},{32,34},{1,9},{33,35},{2,10},{34,32},{3,11},{35,33},{4,12},{... | collective-permute-start | bytes 552968 | tf_op jit(solution)/shard_map/ppermute | solution.py:242
  90.6 0.6 collective-permute-start.23
  91.2 2.1 %collective-permute-start.24 = (bf16[720,128]{1,0:T(8,128)(2,1)S(1)}, bf16[720,128]{1,0:T(8,128)(2,1)S(1)}, u32[]{:S(2)}, u32[]{:S(2)}) collective-permute-start(bf16[720,128]{1,0:T(8,128)(2,1)S(1)} %get-tuple-element.48), channel_id=1, source_target_pairs={{0,12},{32,35},{1,13},{33,32},{2,14},{34,33},{3,15},{35,34},{4,0},... | collective-permute-start | bytes 552968 | tf_op jit(solution)/shard_map/ppermute | solution.py:242
  93.3 1.0 collective-permute-done.22.b
  94.3 2.0 %collective-permute-done.23.c = bf16[720,128]{1,0:T(8,128)(2,1)S(1)} collective-permute-done((bf16[720,128]{1,0:T(8,128)(2,1)S(1)}, bf16[720,128]{1,0:T(8,128)(2,1)S(1)}, u32[]{:S(2)}, u32[]{:S(2)}) %collective-permute-start.23) | collective-permute-done | bytes 184352 | tf_op jit(solution)/shard_map/ppermute | solution.py:242
  96.3 0.2 add_second.1
  96.5 2.0 %collective-permute-start.25 = (f32[3,72,128]{2,1,0:T(8,128)S(1)}, f32[3,72,128]{2,1,0:T(8,128)S(1)}, u32[]{:S(2)}, u32[]{:S(2)}) collective-permute-start(f32[3,72,128]{2,1,0:T(8,128)S(1)} %get-tuple-element.50), channel_id=1, source_target_pairs={{0,16},{16,0},{1,17},{17,1},{2,18},{18,2},{3,19},{19,3},{4,20},{20... | collective-permute-start | bytes 331784 | tf_op jit(solution)/shard_map/ppermute | solution.py:244
  98.4 8.9 %collective-permute-start.26 = (f32[3,72,128]{2,1,0:T(8,128)S(1)}, f32[3,72,128]{2,1,0:T(8,128)S(1)}, u32[]{:S(2)}, u32[]{:S(2)}) collective-permute-start(f32[3,72,128]{2,1,0:T(8,128)S(1)} %get-tuple-element.51), channel_id=1, source_target_pairs={{0,32},{32,0},{1,33},{33,1},{2,34},{34,2},{3,35},{35,3},{4,36},{36... | collective-permute-start | bytes 331784 | tf_op jit(solution)/shard_map/ppermute | solution.py:245
  107.4 1.0 collective-permute-done.26.from_c
  108.3 3.7 %collective-permute-done.27.from_czl = f32[3,72,128]{2,1,0:T(8,128)S(1)} collective-permute-done((f32[3,72,128]{2,1,0:T(8,128)S(1)}, f32[3,72,128]{2,1,0:T(8,128)S(1)}, u32[]{:S(2)}, u32[]{:S(2)}) %collective-permute-start.27) | collective-permute-done | bytes 110624 | tf_op jit(solution)/shard_map/ppermute | solution.py:246
  112.0 0.2 finish.1
  112.2 0.8 copy.5
  (32 shorter events, 0.2 us)
Async XLA Ops:
  0.0 27.1 %collective-permute-start.8 = (bf16[2304,1152]{1,0:T(8,128)(2,1)}, bf16[2304,1152]{1,0:T(8,128)(2,1)}, u32[]{:S(2)}, u32[]{:S(2)}) collective-permute-start(bf16[2304,1152]{1,0:T(8,128)(2,1)} %own_ref.3), channel_id=1, source_target_pairs={{0,32},{32,0},{1,33},{33,1},{2,34},{34,2},{3,35},{35,3},{4,36},{36... | collective-permute-start | bytes 15925256 | tf_op jit(solution)/shard_map/ppermute | solution.py:189
  1.4 57.2 %collective-permute-start.11 = (bf16[1152,2304]{1,0:T(8,128)(2,1)}, bf16[1152,2304]{1,0:T(8,128)(2,1)}, u32[]{:S(2)}, u32[]{:S(2)}) collective-permute-start(bf16[1152,2304]{1,0:T(8,128)(2,1)} %own_ref.5), channel_id=1, source_target_pairs={{0,32},{32,0},{1,33},{33,1},{2,34},{34,2},{3,35},{35,3},{4,36},{36... | collective-permute-start | bytes 15925256 | tf_op jit(solution)/shard_map/ppermute | solution.py:190
  1.4 0.9 copy-start.2
  2.5 8.3 %collective-permute-start = (bf16[360,128]{1,0:T(8,128)(2,1)S(1)}, bf16[360,128]{1,0:T(8,128)(2,1)S(1)}, u32[]{:S(2)}, u32[]{:S(2)}) collective-permute-start(bf16[360,128]{1,0:T(8,128)(2,1)S(1)} %pack_codes.1), channel_id=1, source_target_pairs={{64,16},{80,64},{16,80},{0,0},{65,17},{81,65},{17,81},{1,1},{66,18... | collective-permute-start | bytes 276488 | tf_op jit(solution)/shard_map/ppermute | solution.py:194
  3.2 9.3 %collective-permute-start.1 = (bf16[360,128]{1,0:T(8,128)(2,1)S(1)}, bf16[360,128]{1,0:T(8,128)(2,1)S(1)}, u32[]{:S(2)}, u32[]{:S(2)}) collective-permute-start(bf16[360,128]{1,0:T(8,128)(2,1)S(1)} %pack_codes.1), channel_id=1, source_target_pairs={{0,16},{16,64},{64,0},{80,80},{1,17},{17,65},{65,1},{81,81},{2,18}... | collective-permute-start | bytes 276488 | tf_op jit(solution)/shard_map/ppermute | solution.py:193
  12.6 6.3 %collective-permute-start.2 = (bf16[2,360,128]{2,1,0:T(8,128)(2,1)S(1)}, bf16[2,360,128]{2,1,0:T(8,128)(2,1)S(1)}, u32[]{:S(2)}, u32[]{:S(2)}) collective-permute-start(bf16[2,360,128]{2,1,0:T(8,128)(2,1)S(1)} %pad_maximum_fusion.2.a_ref), channel_id=1, source_target_pairs={{0,2},{32,40},{1,3},{33,41},{2,0},{34,42},{3,1},{35,43},{4,6},{36,... | collective-permute-start | bytes 552968 | tf_op jit(solution)/shard_map/ppermute | solution.py:197
  15.6 5.6 %collective-permute-start.3 = (bf16[2,360,128]{2,1,0:T(8,128)(2,1)S(1)}, bf16[2,360,128]{2,1,0:T(8,128)(2,1)S(1)}, u32[]{:S(2)}, u32[]{:S(2)}) collective-permute-start(bf16[2,360,128]{2,1,0:T(8,128)(2,1)S(1)} %pad_maximum_fusion.2.a_ref), channel_id=1, source_target_pairs={{0,1},{32,36},{1,2},{33,37},{2,3},{34,38},{3,0},{35,39},{4,5},{36,... | collective-permute-start | bytes 552968 | tf_op jit(solution)/shard_map/ppermute | solution.py:197
  15.9 5.2 %collective-permute-start.4 = (bf16[2,360,128]{2,1,0:T(8,128)(2,1)S(1)}, bf16[2,360,128]{2,1,0:T(8,128)(2,1)S(1)}, u32[]{:S(2)}, u32[]{:S(2)}) collective-permute-start(bf16[2,360,128]{2,1,0:T(8,128)(2,1)S(1)} %pad_maximum_fusion.2.a_ref), channel_id=1, source_target_pairs={{0,3},{32,44},{1,0},{33,45},{2,1},{34,46},{3,2},{35,47},{4,7},{36,... | collective-permute-start | bytes 552968 | tf_op jit(solution)/shard_map/ppermute | solution.py:197
  21.6 11.2 %collective-permute-start.15 = (bf16[160,1152]{1,0:T(8,128)(2,1)S(1)}, bf16[160,1152]{1,0:T(8,128)(2,1)S(1)}, u32[]{:S(2)}, u32[]{:S(2)}) collective-permute-start(bf16[160,1152]{1,0:T(8,128)(2,1)S(1)} %get-tuple-element.37.m0), channel_id=1, source_target_pairs={{0,8},{32,34},{1,9},{33,35},{2,10},{34,32},{3,11},{35,33},{4,12},{... | collective-permute-start | bytes 1105928 | tf_op jit(solution)/shard_map/ppermute | solution.py:200
  24.4 9.4 %collective-permute-start.16 = (bf16[160,1152]{1,0:T(8,128)(2,1)S(1)}, bf16[160,1152]{1,0:T(8,128)(2,1)S(1)}, u32[]{:S(2)}, u32[]{:S(2)}) collective-permute-start(bf16[160,1152]{1,0:T(8,128)(2,1)S(1)} %get-tuple-element.37.m0), channel_id=1, source_target_pairs={{0,4},{32,33},{1,5},{33,34},{2,6},{34,35},{3,7},{35,32},{4,8},{36,... | collective-permute-start | bytes 1105928 | tf_op jit(solution)/shard_map/ppermute | solution.py:200
  24.7 10.8 %collective-permute-start.17 = (bf16[160,1152]{1,0:T(8,128)(2,1)S(1)}, bf16[160,1152]{1,0:T(8,128)(2,1)S(1)}, u32[]{:S(2)}, u32[]{:S(2)}) collective-permute-start(bf16[160,1152]{1,0:T(8,128)(2,1)S(1)} %get-tuple-element.37.m0), channel_id=1, source_target_pairs={{0,12},{32,35},{1,13},{33,32},{2,14},{34,33},{3,15},{35,34},{4,0},... | collective-permute-start | bytes 1105928 | tf_op jit(solution)/shard_map/ppermute | solution.py:200
  27.1 13.9 %collective-permute-start.5 = (bf16[160,1152]{1,0:T(8,128)(2,1)S(1)}, bf16[160,1152]{1,0:T(8,128)(2,1)S(1)}, u32[]{:S(2)}, u32[]{:S(2)}) collective-permute-start(bf16[160,1152]{1,0:T(8,128)(2,1)S(1)} %get-tuple-element.29.m0), channel_id=1, source_target_pairs={{0,8},{32,34},{1,9},{33,35},{2,10},{34,32},{3,11},{35,33},{4,12},{... | collective-permute-start | bytes 1105928 | tf_op jit(solution)/shard_map/ppermute | solution.py:200
  27.1 2.5 %copy-start.1 = (bf16[2304,1152]{1,0:T(8,128)(2,1)S(1)}, bf16[2304,1152]{1,0:T(8,128)(2,1)}, u32[]{:S(2)}) copy-start(bf16[2304,1152]{1,0:T(8,128)(2,1)} %own_ref.3) | copy-start | bytes 15925252
  32.8 8.9 %collective-permute-start.6 = (bf16[160,1152]{1,0:T(8,128)(2,1)S(1)}, bf16[160,1152]{1,0:T(8,128)(2,1)S(1)}, u32[]{:S(2)}, u32[]{:S(2)}) collective-permute-start(bf16[160,1152]{1,0:T(8,128)(2,1)S(1)} %get-tuple-element.29.m0), channel_id=1, source_target_pairs={{0,4},{32,33},{1,5},{33,34},{2,6},{34,35},{3,7},{35,32},{4,8},{36,... | collective-permute-start | bytes 1105928 | tf_op jit(solution)/shard_map/ppermute | solution.py:200
  33.8 8.0 %collective-permute-start.7 = (bf16[160,1152]{1,0:T(8,128)(2,1)S(1)}, bf16[160,1152]{1,0:T(8,128)(2,1)S(1)}, u32[]{:S(2)}, u32[]{:S(2)}) collective-permute-start(bf16[160,1152]{1,0:T(8,128)(2,1)S(1)} %get-tuple-element.29.m0), channel_id=1, source_target_pairs={{0,12},{32,35},{1,13},{33,32},{2,14},{34,33},{3,15},{35,34},{4,0},... | collective-permute-start | bytes 1105928 | tf_op jit(solution)/shard_map/ppermute | solution.py:200
  38.7 8.8 %copy-start.3 = (s32[160]{0:T(256)S(1)}, s32[160]{0:T(256)}, u32[]{:S(2)}) copy-start(s32[160]{0:T(256)} %param.5) | copy-start | bytes 1924
  38.7 19.0 %collective-permute-start.18 = (f16[168,1152]{1,0:T(8,128)(2,1)}, f16[168,1152]{1,0:T(8,128)(2,1)S(1)}, u32[]{:S(2)}, u32[]{:S(2)}) collective-permute-start(f16[168,1152]{1,0:T(8,128)(2,1)} %pad_maximum_fusion.1), channel_id=1, source_target_pairs={{0,64},{64,0},{1,65},{65,1},{2,66},{66,2},{3,67},{67,3},{4,68},{68... | collective-permute-start | bytes 1161224 | tf_op jit(solution)/shard_map/ppermute | solution.py:224
  44.1 26.8 %slice-start = ((s8[5308416]{0:T(1024)(128)(4,1)}), s8[1114112]{0:T(1024)(128)(4,1)S(1)}, s32[]{:S(2)}) async-start(s8[5308416]{0:T(1024)(128)(4,1)} %bitcast.4), calls=%async_computation | async-start | bytes 2228224
  45.0 12.8 %collective-permute-start.9 = (f16[168,1152]{1,0:T(8,128)(2,1)}, f16[168,1152]{1,0:T(8,128)(2,1)S(1)}, u32[]{:S(2)}, u32[]{:S(2)}) collective-permute-start(f16[168,1152]{1,0:T(8,128)(2,1)} %pad_maximum_fusion), channel_id=1, source_target_pairs={{0,64},{64,0},{1,65},{65,1},{2,66},{66,2},{3,67},{67,3},{4,68},{68... | collective-permute-start | bytes 1161224 | tf_op jit(solution)/shard_map/ppermute | solution.py:224
  47.5 10.2 %collective-permute-start.10 = (s32[160]{0:T(256)S(1)}, s32[160]{0:T(256)S(1)}, u32[]{:S(2)}, u32[]{:S(2)}) collective-permute-start(s32[160]{0:T(256)S(1)} %copy-done.3), channel_id=1, source_target_pairs={{0,64},{64,0},{1,65},{65,1},{2,66},{66,2},{3,67},{67,3},{4,68},{68... | collective-permute-start | bytes 1928 | tf_op jit(solution)/shard_map/ppermute | solution.py:209
  58.7 2.5 %copy-start = (bf16[1152,2304]{1,0:T(8,128)(2,1)S(1)}, bf16[1152,2304]{1,0:T(8,128)(2,1)}, u32[]{:S(2)}) copy-start(bf16[1152,2304]{1,0:T(8,128)(2,1)} %own_ref.5) | copy-start | bytes 15925252
  61.2 9.7 %slice-start.1 = ((s8[5308416]{0:T(1024)(128)(4,1)}), s8[4194304]{0:T(1024)(128)(4,1)S(1)}, s32[]{:S(2)}) async-start(s8[5308416]{0:T(1024)(128)(4,1)} %bitcast.4), calls=%async_computation.1 | async-start | bytes 8388608
  66.4 10.2 %collective-permute-start.12 = (bf16[4,360,128]{2,1,0:T(8,128)(2,1)S(1)}, bf16[4,360,128]{2,1,0:T(8,128)(2,1)S(1)}, u32[]{:S(2)}, u32[]{:S(2)}) collective-permute-start(bf16[4,360,128]{2,1,0:T(8,128)(2,1)S(1)} %get-tuple-element.34), channel_id=1, source_target_pairs={{0,2},{32,40},{1,3},{33,41},{2,0},{34,42},{3,1},{35,43},{4,6},{36,... | collective-permute-start | bytes 1105928 | tf_op jit(solution)/shard_map/ppermute | solution.py:239
  68.2 10.6 %collective-permute-start.13 = (bf16[4,360,128]{2,1,0:T(8,128)(2,1)S(1)}, bf16[4,360,128]{2,1,0:T(8,128)(2,1)S(1)}, u32[]{:S(2)}, u32[]{:S(2)}) collective-permute-start(bf16[4,360,128]{2,1,0:T(8,128)(2,1)S(1)} %get-tuple-element.35), channel_id=1, source_target_pairs={{0,1},{32,36},{1,2},{33,37},{2,3},{34,38},{3,0},{35,39},{4,5},{36,... | collective-permute-start | bytes 1105928 | tf_op jit(solution)/shard_map/ppermute | solution.py:239
  69.2 9.6 %collective-permute-start.14 = (bf16[4,360,128]{2,1,0:T(8,128)(2,1)S(1)}, bf16[4,360,128]{2,1,0:T(8,128)(2,1)S(1)}, u32[]{:S(2)}, u32[]{:S(2)}) collective-permute-start(bf16[4,360,128]{2,1,0:T(8,128)(2,1)S(1)} %get-tuple-element.36), channel_id=1, source_target_pairs={{0,3},{32,44},{1,0},{33,45},{2,1},{34,46},{3,2},{35,47},{4,7},{36,... | collective-permute-start | bytes 1105928 | tf_op jit(solution)/shard_map/ppermute | solution.py:239
  76.0 8.1 %collective-permute-start.19 = (bf16[4,360,128]{2,1,0:T(8,128)(2,1)S(1)}, bf16[4,360,128]{2,1,0:T(8,128)(2,1)S(1)}, u32[]{:S(2)}, u32[]{:S(2)}) collective-permute-start(bf16[4,360,128]{2,1,0:T(8,128)(2,1)S(1)} %get-tuple-element.42), channel_id=1, source_target_pairs={{0,2},{32,40},{1,3},{33,41},{2,0},{34,42},{3,1},{35,43},{4,6},{36,... | collective-permute-start | bytes 1105928 | tf_op jit(solution)/shard_map/ppermute | solution.py:239
  76.1 11.8 %collective-permute-start.20 = (bf16[4,360,128]{2,1,0:T(8,128)(2,1)S(1)}, bf16[4,360,128]{2,1,0:T(8,128)(2,1)S(1)}, u32[]{:S(2)}, u32[]{:S(2)}) collective-permute-start(bf16[4,360,128]{2,1,0:T(8,128)(2,1)S(1)} %get-tuple-element.43), channel_id=1, source_target_pairs={{0,1},{32,36},{1,2},{33,37},{2,3},{34,38},{3,0},{35,39},{4,5},{36,... | collective-permute-start | bytes 1105928 | tf_op jit(solution)/shard_map/ppermute | solution.py:239
  76.6 11.3 %collective-permute-start.21 = (bf16[4,360,128]{2,1,0:T(8,128)(2,1)S(1)}, bf16[4,360,128]{2,1,0:T(8,128)(2,1)S(1)}, u32[]{:S(2)}, u32[]{:S(2)}) collective-permute-start(bf16[4,360,128]{2,1,0:T(8,128)(2,1)S(1)} %get-tuple-element.44), channel_id=1, source_target_pairs={{0,3},{32,44},{1,0},{33,45},{2,1},{34,46},{3,2},{35,47},{4,7},{36,... | collective-permute-start | bytes 1105928 | tf_op jit(solution)/shard_map/ppermute | solution.py:239
  88.3 6.0 %collective-permute-start.22 = (bf16[720,128]{1,0:T(8,128)(2,1)S(1)}, bf16[720,128]{1,0:T(8,128)(2,1)S(1)}, u32[]{:S(2)}, u32[]{:S(2)}) collective-permute-start(bf16[720,128]{1,0:T(8,128)(2,1)S(1)} %get-tuple-element.46), channel_id=1, source_target_pairs={{0,8},{32,34},{1,9},{33,35},{2,10},{34,32},{3,11},{35,33},{4,12},{... | collective-permute-start | bytes 552968 | tf_op jit(solution)/shard_map/ppermute | solution.py:242
  90.6 5.6 %collective-permute-start.23 = (bf16[720,128]{1,0:T(8,128)(2,1)S(1)}, bf16[720,128]{1,0:T(8,128)(2,1)S(1)}, u32[]{:S(2)}, u32[]{:S(2)}) collective-permute-start(bf16[720,128]{1,0:T(8,128)(2,1)S(1)} %get-tuple-element.47), channel_id=1, source_target_pairs={{0,4},{32,33},{1,5},{33,34},{2,6},{34,35},{3,7},{35,32},{4,8},{36,... | collective-permute-start | bytes 552968 | tf_op jit(solution)/shard_map/ppermute | solution.py:242
  91.2 5.0 %collective-permute-start.24 = (bf16[720,128]{1,0:T(8,128)(2,1)S(1)}, bf16[720,128]{1,0:T(8,128)(2,1)S(1)}, u32[]{:S(2)}, u32[]{:S(2)}) collective-permute-start(bf16[720,128]{1,0:T(8,128)(2,1)S(1)} %get-tuple-element.48), channel_id=1, source_target_pairs={{0,12},{32,35},{1,13},{33,32},{2,14},{34,33},{3,15},{35,34},{4,0},... | collective-permute-start | bytes 552968 | tf_op jit(solution)/shard_map/ppermute | solution.py:242
  96.5 10.9 %collective-permute-start.25 = (f32[3,72,128]{2,1,0:T(8,128)S(1)}, f32[3,72,128]{2,1,0:T(8,128)S(1)}, u32[]{:S(2)}, u32[]{:S(2)}) collective-permute-start(f32[3,72,128]{2,1,0:T(8,128)S(1)} %get-tuple-element.50), channel_id=1, source_target_pairs={{0,16},{16,0},{1,17},{17,1},{2,18},{18,2},{3,19},{19,3},{4,20},{20... | collective-permute-start | bytes 331784 | tf_op jit(solution)/shard_map/ppermute | solution.py:244
  98.4 9.9 %collective-permute-start.26 = (f32[3,72,128]{2,1,0:T(8,128)S(1)}, f32[3,72,128]{2,1,0:T(8,128)S(1)}, u32[]{:S(2)}, u32[]{:S(2)}) collective-permute-start(f32[3,72,128]{2,1,0:T(8,128)S(1)} %get-tuple-element.51), channel_id=1, source_target_pairs={{0,32},{32,0},{1,33},{33,1},{2,34},{34,2},{3,35},{35,3},{4,36},{36... | collective-permute-start | bytes 331784 | tf_op jit(solution)/shard_map/ppermute | solution.py:245
  107.4 4.7 %collective-permute-start.27 = (f32[3,72,128]{2,1,0:T(8,128)S(1)}, f32[3,72,128]{2,1,0:T(8,128)S(1)}, u32[]{:S(2)}, u32[]{:S(2)}) collective-permute-start(f32[3,72,128]{2,1,0:T(8,128)S(1)} %get-tuple-element.52), channel_id=1, source_target_pairs={{0,48},{16,32},{32,16},{48,0},{1,49},{17,33},{33,17},{49,1},{2,50}... | collective-permute-start | bytes 331784 | tf_op jit(solution)/shard_map/ppermute | solution.py:246

commit v3 on v2

--- a/solution.py
+++ b/solution.py
@@ -11,6 +11,7 @@
 UNITS = 1152
 CHIP_COLS = 72
 VMEM = pl.BlockSpec(memory_space=pltpu.VMEM)
+HBM = pl.BlockSpec(memory_space=pltpu.HBM)
 ANY = pl.BlockSpec(memory_space=pl.ANY)
 YX = ("c", "y", "x")
 STEPS = (0, 2, 1, 3)
@@ -51,10 +52,15 @@
     return jnp.dot(a, b, preferred_element_type=F32)
 
 
-def pack_codes(x_ref, o_ref):
-    o_ref[0:QT] = x_ref[:, 0:128]
-    o_ref[QT : 2 * QT] = x_ref[:, 128:256]
-    tail = x_ref[:, 256:288]
+def pack_codes(x_ref, e_ref, o_ref):
+    row = lax.broadcasted_iota(jnp.int32, (QT, QT), 0)
+    col = lax.broadcasted_iota(jnp.int32, (QT, QT), 1)
+    power = jnp.exp2(jnp.broadcast_to(e_ref[...], (QT, QT)).astype(F32))
+    scale = jnp.where(row == col, power, 0.0).astype(BF)
+    x = dot(scale, x_ref[...]).astype(BF)
+    o_ref[0:QT] = x[:, 0:128]
+    o_ref[QT : 2 * QT] = x[:, 128:256]
+    tail = x[:, 256:288]
     src = lax.broadcasted_iota(jnp.int32, (32, 128), 0)
     dst = lax.broadcasted_iota(jnp.int32, (32, 128), 1)
     total = jnp.zeros((40, 128), F32)
@@ -64,7 +70,8 @@
     o_ref[2 * QT : 360] = total.astype(BF)
 
 
-def merge_codes(a_ref, b_ref, c_ref, d_ref, *outs):
+def merge_codes(a_ref, b_ref, c_ref, d_ref, after1, after2, *outs):
+    del after1, after2
     pieces = (a_ref, b_ref, c_ref, d_ref)
     src = lax.broadcasted_iota(jnp.int32, (512, 128), 0)
     dst = lax.broadcasted_iota(jnp.int32, (512, 128), 1)
@@ -105,7 +112,14 @@
     pltpu.make_async_copy(w_ref, w_ref, sem).wait()
 
 
-def project_in(m0, m1, m2, m3, w_ref, o_ref, scale_ref, power_ref, x_ref):
+def stage_columns(own_ref, other_ref, after, w_ref, sem):
+    del after
+    for ref, at in ((own_ref, 0), (other_ref, 2 * UNITS)):
+        pltpu.make_async_copy(ref, w_ref.at[:, at : at + 2 * UNITS], sem).start()
+    pltpu.make_async_copy(w_ref, w_ref, sem).wait()
+
+
+def project_in(m0, m1, m2, m3, w_ref, o_ref, send_ref, x_ref):
     for i, m in enumerate((m0, m1, m2, m3)):
         x_ref[:, i * UNITS : (i + 1) * UNITS] = m[...]
     most = jnp.zeros((QT, 128), F32)
@@ -117,21 +131,20 @@
             most = jnp.maximum(most, jnp.abs(part[:, k : k + 128]))
     most = jnp.full((8, UNITS), jnp.max(most))
     power = 13.0 - jnp.ceil(jnp.log(jnp.maximum(most, 1e-30)) * 1.4426950408889634)
-    power_ref[...] = power
-    scale_ref[...] = jnp.exp2(power)
-
-
-def project_out(a_ref, own_ref, other_ref, o0, o1, o2, o3, t_ref, tail_ref):
+    send_ref[0:QT] = o_ref[...] * jnp.exp2(power)[:1]
+    send_ref[QT:] = power
+
+
+def project_out(a_ref, w_ref, o0, o1, o2, o3, t_ref, tail_ref):
     for g in range(4):
-        w_ref = own_ref if g < 2 else other_ref
         for n in range(0, UNITS, 256):
             to = min(n + 256, UNITS)
-            part = dot(a_ref[...], w_ref[:, g % 2 * UNITS + n : g % 2 * UNITS + to])
+            part = dot(a_ref[...], w_ref[:, g * UNITS + n : g * UNITS + to])
             t_ref[g, n:to] = part[:128].T
             tail_ref[32 * g : 32 * g + 32, n:to] = part[128:]
     t_ref[4] = tail_ref[...].T
     c, first, _ = own_place()
-    for rel, o in zip((0,) + STEPS[1:], (o0, o1, o2, o3)):
+    for rel, o in zip(STEPS, (o0, o1, o2, o3)):
         f = lax.rem(first + rel, 4)
         for s in range(4):
             at = pl.ds(pl.multiple_of(jnp.where(c == 0, s * 4 + f, f * 4 + s) * CHIP_COLS, 8), CHIP_COLS)
@@ -188,54 +201,66 @@
     z = ("zh", "zl")
     w_in_other = lax.ppermute(w_in, "c", swap)
     w_out_other = lax.ppermute(w_out, "c", swap)
-
-    packed = call(pack_codes, shape((360, 128), BF), [VMEM], name="pack_codes")(codes)
+    w_in, w_out = (pltpu.with_memory_space_constraint(w, pltpu.HBM) for w in (w_in, w_out))
+
+    packed = call(pack_codes, shape((360, 128), BF), [VMEM] * 2, name="pack_codes")(codes, exponents[None, :])
     one = lax.ppermute(packed, z, [(0, 1), (1, 2), (2, 0), (3, 3)])
     two = lax.ppermute(packed, z, [(2, 1), (3, 2), (1, 3), (0, 0)])
     piece = jnp.stack([jnp.where(zh == zl, two, one), jnp.where(zh == zl, one, two)])
 
     around = [lax.ppermute(piece, YX, first_axis(k)) for k in STEPS[1:]]
-    quarter = shape((QT, UNITS), BF)
-    merged = call(merge_codes, [quarter] * 2, [VMEM] * 4, name="merge_codes")(piece, *around)
-    around = [[lax.ppermute(m, YX, second_axis(k)) for k in STEPS[1:]] for m in merged]
     weights = call(
         arrange_rows,
-        shape((4 * UNITS, UNITS), BF),
-        [ANY] * 2,
+        pltpu.VMEM((4 * UNITS, UNITS), BF),
+        [HBM, ANY],
         [pltpu.SemaphoreType.DMA],
         nbytes=2 * 4608 * 1152 * 2,
+        vmem=8,
         name="arrange_rows",
     )(w_in, w_in_other)
-    other_exponents = lax.ppermute(exponents, "zh", swap)
-    powers = [jnp.where(zh == 0, exponents, other_exponents), jnp.where(zh == 0, other_exponents, exponents)]
-
-    scattered = []
-    for m, others, power in zip(merged, around, powers):
-        preact, scale, scale_power = call(
+    quarter = shape((QT, UNITS), BF)
+    merged = call(merge_codes, [quarter] * 2, [VMEM] * 4 + [ANY] * 2, name="merge_codes")(piece, *around, weights, w_out_other)
+    around = [[lax.ppermute(m, YX, second_axis(k)) for k in STEPS[1:]] for m in merged]
+
+    preacts, sends = [], []
+    for q in range(2):
+        preact, send = call(
             project_in,
-            [shape((QT, UNITS), F32)] + [shape((8, UNITS), F32)] * 2,
+            [shape((QT, UNITS), F32), shape((QT + 8, UNITS), F32)],
             [VMEM] * 5,
             [pltpu.VMEM((QT, 4 * UNITS), BF)],
             flops=2 * QT * 4608 * 1152,
             nbytes=4608 * 1152 * 2,
             name="project_in",
-        )(m, *others, weights)
-        sent = jnp.concatenate([(preact * scale[:1]).astype(jnp.float16), scale_power.astype(jnp.float16)])
-        got = lax.ppermute(sent, "zh", swap).astype(F32)
-        row_scale = jnp.exp2(power.astype(F32))[:, None]
-        summed = (preact + got[:QT] * jnp.exp2(-got[QT : QT + 1])) * row_scale
-        activ = jax.nn.gelu(summed, approximate=True).astype(BF)
+        )(merged[q], *around[q], weights)
+        preacts.append(preact)
+        sends.append(send.astype(jnp.float16))
+    gots = [lax.ppermute(send, "zh", swap) for send in sends]
+    weights = call(
+        stage_columns,
+        pltpu.VMEM((UNITS, 4 * UNITS), BF),
+        [HBM, ANY, ANY],
+        [pltpu.SemaphoreType.DMA],
+        nbytes=2 * 4608 * 1152 * 2,
+        vmem=8,
+        name="stage_columns",
+    )(w_out, w_out_other, preacts[1])
+
+    scattered = []
+    for preact, got in zip(preacts, gots):
+        other = got[:QT].astype(F32) * jnp.exp2(-got[QT : QT + 1].astype(F32))
+        activ = jax.nn.gelu(preact + other, approximate=True).astype(BF)
         part = (4, 360, 128)
         mine, *away = call(
             project_out,
             [shape(part, F32)] + [shape(part, BF)] * 3,
-            [VMEM] * 3,
+            [VMEM] * 2,
             [pltpu.VMEM((5, UNITS, 128), F32), pltpu.VMEM((128, UNITS), F32)],
             flops=2 * QT * 4608 * 1152,
             nbytes=4608 * 1152 * 2,
             vmem=12,
             name="project_out",
-        )(activ, w_out, w_out_other)
+        )(activ, weights)
         scattered += [mine] + [lax.ppermute(v, YX, first_axis(k)) for k, v in zip(STEPS[1:], away)]
     part = (720, 128)
     mine, *away = call(add_first, [shape(part, F32)] + [shape(part, BF)] * 3, [VMEM] * 8, name="add_first")(*scattered)

time: 113 us -> 97.5 us (0.86)
  starting transfers between devices: 51.7 us -> 47 us
  waiting for transfers between devices: 32.3 us -> 27.7 us
  local copies, waits for them, and re-layouts: 6.79 us -> 2.41 us
  other arithmetic: 2.78 us -> 0.84 us
    ppermute x3 -> x2, waiting for transfers between devices: 9.8 us -> 0.01 us  [shards(): gots = [lax.ppermute(send, 'zh', swap) for send in sends]]
    ppermute x6, waiting for transfers between devices: 1.08 us -> 6.93 us  [shards(): lax.ppermute(m, YX, second_axis(k))]
    unnamed x12 -> x4, local copies, waits for them, and re-layouts: 5.92 us -> 1.58 us
    ppermute x3, waiting for transfers between devices: 2.92 us -> 0.01 us  [shards(): around = [lax.ppermute(piece, YX, first_axis(k)) for k in STEPS[1:]]]
    ppermute x1, starting transfers between devices: 8.94 us -> 6.07 us  [shards(): from_c = lax.ppermute(to_c, 'c', swap)]
    ppermute x1, starting transfers between devices: 1.97 us -> 0.09 us  [shards(): from_zl = lax.ppermute(to_zl, 'zl', swap)]
    concatenate x2 -> x0, other arithmetic: 1.7 us -> none  [shards(): jnp.concatenate([(preact * scale[:1]).astype(jnp.float16), scale_power.as...]
    ppermute x6, waiting for transfers between devices: 9.14 us -> 10.7 us  [shards(): lax.ppermute(v, YX, first_axis(k))]
  transfers between devices with their start and end apart: 28 -> 27, of which waited for: 13 -> 13; matrix products, arithmetic and copies ran while one was open for 2% -> 1% of each run, Pallas kernels for 12% -> 19%
where the time goes in v3:
time: 97.5 us; the launch traced here: 97.3 us
  starting transfers between devices  47 us (48%)
  waiting for transfers between devices  27.7 us (28%)
  Pallas kernels  19.2 us (20%)
  local copies, waits for them, and re-layouts  2.41 us (2%)
    ppermute x6, waiting for transfers between devices, shards(): lax.ppermute(v, YX, first_axis(k))  10.7 us
    ppermute x6, starting transfers between devices, shards(): lax.ppermute(m, YX, second_axis(k))  8.56 us
    ppermute x1, starting transfers between devices, shards(): one = lax.ppermute(packed, z, [(0, 1), (1, 2), (2, 0), (3, 3)])  7.57 us
    ppermute x6, waiting for transfers between devices, shards(): lax.ppermute(m, YX, second_axis(k))  6.93 us
    ppermute x6, starting transfers between devices, shards(): lax.ppermute(v, YX, first_axis(k))  6.49 us
    ppermute x1, starting transfers between devices, shards(): from_c = lax.ppermute(to_c, 'c', swap)  6.07 us
    ppermute x3, starting transfers between devices, shards(): around = [lax.ppermute(piece, YX, first_axis(k)) for k in STEPS[1:]]  5.67 us
    pallas_call x2, Pallas kernels, shards(): call(project_out, [shape(part, F32)] + [shape(part, BF)] * 3, [VMEM] * 2,...  5.08 us
  transfers between devices with their start and end apart: 27, of which 13 were waited for; matrix products, arithmetic and copies ran while one was open for 1% of the time, Pallas kernels for 19%

profile of v3, /device:TPU:1, one launch (start us, length us, event | category | flops | bytes accessed | tf_op | source)
XLA Modules:
  0.0 97.3 jit_solution(2020252693926702710)
XLA Ops:
  0.0 1.4 %collective-permute-start.5 = (bf16[2304,1152]{1,0:T(8,128)(2,1)}, bf16[2304,1152]{1,0:T(8,128)(2,1)}, u32[]{:S(2)}, u32[]{:S(2)}) collective-permute-start(bf16[2304,1152]{1,0:T(8,128)(2,1)} %own_ref.2), channel_id=1, source_target_pairs={{0,32},{32,0},{1,33},{33,1},{2,34},{34,2},{3,35},{35,3},{4,36},{36... | collective-permute-start | bytes 15925256 | tf_op jit(solution)/shard_map/ppermute | solution.py:202
  1.4 0.0 collective-permute-start.6
  1.4 0.9 copy-done
  2.3 0.7 copy-done.1
  3.0 0.3 pack_codes.1
  3.3 0.7 collective-permute-start
  4.0 7.6 %collective-permute-start.1 = (bf16[360,128]{1,0:T(8,128)(2,1)S(1)}, bf16[360,128]{1,0:T(8,128)(2,1)S(1)}, u32[]{:S(2)}, u32[]{:S(2)}) collective-permute-start(bf16[360,128]{1,0:T(8,128)(2,1)S(1)} %pack_codes.1), channel_id=1, source_target_pairs={{0,16},{16,64},{64,0},{80,80},{1,17},{17,65},{65,1},{81,81},{2,18}... | collective-permute-start | bytes 276488 | tf_op jit(solution)/shard_map/ppermute | solution.py:207
  11.6 0.0 collective-permute-done
  11.6 1.7 %collective-permute-done.1 = bf16[360,128]{1,0:T(8,128)(2,1)S(1)} collective-permute-done((bf16[360,128]{1,0:T(8,128)(2,1)S(1)}, bf16[360,128]{1,0:T(8,128)(2,1)S(1)}, u32[]{:S(2)}, u32[]{:S(2)}) %collective-permute-start.1) | collective-permute-done | bytes 92192 | tf_op jit(solution)/shard_map/ppermute | solution.py:207
  13.4 3.0 %collective-permute-start.2 = (bf16[2,360,128]{2,1,0:T(8,128)(2,1)S(1)}, bf16[2,360,128]{2,1,0:T(8,128)(2,1)S(1)}, u32[]{:S(2)}, u32[]{:S(2)}) collective-permute-start(bf16[2,360,128]{2,1,0:T(8,128)(2,1)S(1)} %pad_maximum_fusion.a_ref), channel_id=1, source_target_pairs={{0,2},{32,40},{1,3},{33,41},{2,0},{34,42},{3,1},{35,43},{4,6},{36,... | collective-permute-start | bytes 552968 | tf_op jit(solution)/shard_map/ppermute | solution.py:211
  16.4 0.4 collective-permute-start.3
  16.8 2.3 %collective-permute-start.4 = (bf16[2,360,128]{2,1,0:T(8,128)(2,1)S(1)}, bf16[2,360,128]{2,1,0:T(8,128)(2,1)S(1)}, u32[]{:S(2)}, u32[]{:S(2)}) collective-permute-start(bf16[2,360,128]{2,1,0:T(8,128)(2,1)S(1)} %pad_maximum_fusion.a_ref), channel_id=1, source_target_pairs={{0,3},{32,44},{1,0},{33,45},{2,1},{34,46},{3,2},{35,47},{4,7},{36,... | collective-permute-start | bytes 552968 | tf_op jit(solution)/shard_map/ppermute | solution.py:211
  19.1 0.0 collective-permute-done.5.other_ref
  19.1 4.0 %arrange_rows.1.after1.w_ref = bf16[4608,1152]{1,0:T(8,128)(2,1)S(1)} custom-call(bf16[2304,1152]{1,0:T(8,128)(2,1)} %own_ref.2, bf16[2304,1152]{1,0:T(8,128)(2,1)} %collective-permute-done.5.other_ref), custom_call_target="tpu_custom_call" | custom-call | bytes 21233664 | tf_op jit(solution)/shard_map/arrange_rows/pallas_call | solution.py:212
  23.1 0.0 collective-permute-done.2.b_ref
  23.1 0.0 collective-permute-done.3.c_ref
  23.1 0.0 collective-permute-done.6.after2.other_ref
  23.1 0.4 merge_codes.1
  23.5 2.8 %collective-permute-start.7 = (bf16[160,1152]{1,0:T(8,128)(2,1)S(1)}, bf16[160,1152]{1,0:T(8,128)(2,1)S(1)}, u32[]{:S(2)}, u32[]{:S(2)}) collective-permute-start(bf16[160,1152]{1,0:T(8,128)(2,1)S(1)} %get-tuple-element.27.m0), channel_id=1, source_target_pairs={{0,8},{32,34},{1,9},{33,35},{2,10},{34,32},{3,11},{35,33},{4,12},{... | collective-permute-start | bytes 1105928 | tf_op jit(solution)/shard_map/ppermute | solution.py:223
  26.4 0.3 collective-permute-start.8
  26.7 2.4 %collective-permute-start.9 = (bf16[160,1152]{1,0:T(8,128)(2,1)S(1)}, bf16[160,1152]{1,0:T(8,128)(2,1)S(1)}, u32[]{:S(2)}, u32[]{:S(2)}) collective-permute-start(bf16[160,1152]{1,0:T(8,128)(2,1)S(1)} %get-tuple-element.27.m0), channel_id=1, source_target_pairs={{0,12},{32,35},{1,13},{33,32},{2,14},{34,33},{3,15},{35,34},{4,0},... | collective-permute-start | bytes 1105928 | tf_op jit(solution)/shard_map/ppermute | solution.py:223
  29.1 0.0 collective-permute-start.11
  29.1 0.6 collective-permute-start.12
  29.6 2.2 %collective-permute-done.7.m1 = bf16[160,1152]{1,0:T(8,128)(2,1)S(1)} collective-permute-done((bf16[160,1152]{1,0:T(8,128)(2,1)S(1)}, bf16[160,1152]{1,0:T(8,128)(2,1)S(1)}, u32[]{:S(2)}, u32[]{:S(2)}) %collective-permute-start.7) | collective-permute-done | bytes 368672 | tf_op jit(solution)/shard_map/ppermute | solution.py:223
  31.8 2.5 %collective-permute-start.13 = (bf16[160,1152]{1,0:T(8,128)(2,1)S(1)}, bf16[160,1152]{1,0:T(8,128)(2,1)S(1)}, u32[]{:S(2)}, u32[]{:S(2)}) collective-permute-start(bf16[160,1152]{1,0:T(8,128)(2,1)S(1)} %get-tuple-element.30.m0), channel_id=1, source_target_pairs={{0,12},{32,35},{1,13},{33,32},{2,14},{34,33},{3,15},{35,34},{4,0},... | collective-permute-start | bytes 1105928 | tf_op jit(solution)/shard_map/ppermute | solution.py:223
  34.3 1.5 %collective-permute-done.8.m2 = bf16[160,1152]{1,0:T(8,128)(2,1)S(1)} collective-permute-done((bf16[160,1152]{1,0:T(8,128)(2,1)S(1)}, bf16[160,1152]{1,0:T(8,128)(2,1)S(1)}, u32[]{:S(2)}, u32[]{:S(2)}) %collective-permute-start.8) | collective-permute-done | bytes 368672 | tf_op jit(solution)/shard_map/ppermute | solution.py:223
  35.7 0.1 collective-permute-done.9.m3
  35.8 2.3 %project_in.2 = (f32[160,1152]{1,0:T(8,128)S(1)}, f32[168,1152]{1,0:T(8,128)S(1)}) custom-call(bf16[160,1152]{1,0:T(8,128)(2,1)S(1)} %get-tuple-element.27.m0, bf16[160,1152]{1,0:T(8,128)(2,1)S(1)} %collective-permute-done.7.m1, bf16[160,1152]{1,0:T(8,128)(2,1)S(1)} %collective-permute-done.8.m2, bf16[160,1152]{1,0:T(8,128)(2,1)S(1)} %collective-permute-done.9.m3, ...), custom_call_target="tpu_custom_call" | custom-call | flops 1698693120 | bytes 10616832 | tf_op jit(solution)/shard_map/project_in/pallas_call | solution.py:227
  38.2 2.4 %collective-permute-start.10 = (f16[168,1152]{1,0:T(8,128)(2,1)S(1)}, f16[168,1152]{1,0:T(8,128)(2,1)S(1)}, u32[]{:S(2)}, u32[]{:S(2)}) collective-permute-start(f16[168,1152]{1,0:T(8,128)(2,1)S(1)} %convert_element_type.24), channel_id=1, source_target_pairs={{0,64},{64,0},{1,65},{65,1},{2,66},{66,2},{3,67},{67,3},{4,68},{68... | collective-permute-start | bytes 1161224 | tf_op jit(solution)/shard_map/ppermute | solution.py:238
  40.6 3.1 %collective-permute-done.12.m2 = bf16[160,1152]{1,0:T(8,128)(2,1)S(1)} collective-permute-done((bf16[160,1152]{1,0:T(8,128)(2,1)S(1)}, bf16[160,1152]{1,0:T(8,128)(2,1)S(1)}, u32[]{:S(2)}, u32[]{:S(2)}) %collective-permute-start.12) | collective-permute-done | bytes 368672 | tf_op jit(solution)/shard_map/ppermute | solution.py:223
  43.6 0.1 collective-permute-done.13.m3
  43.8 2.3 %project_in.3 = (f32[160,1152]{1,0:T(8,128)S(1)}, f32[168,1152]{1,0:T(8,128)S(1)}) custom-call(bf16[160,1152]{1,0:T(8,128)(2,1)S(1)} %get-tuple-element.30.m0, bf16[160,1152]{1,0:T(8,128)(2,1)S(1)} %collective-permute-done.11.m1, bf16[160,1152]{1,0:T(8,128)(2,1)S(1)} %collective-permute-done.12.m2, bf16[160,1152]{1,0:T(8,128)(2,1)S(1)} %collective-permute-done.13.m3, ...), custom_call_target="tpu_custom_call" | custom-call | flops 1698693120 | bytes 10616832 | tf_op jit(solution)/shard_map/project_in/pallas_call | solution.py:227
  46.1 2.4 %collective-permute-start.17 = (f16[168,1152]{1,0:T(8,128)(2,1)S(1)}, f16[168,1152]{1,0:T(8,128)(2,1)S(1)}, u32[]{:S(2)}, u32[]{:S(2)}) collective-permute-start(f16[168,1152]{1,0:T(8,128)(2,1)S(1)} %convert_element_type.28), channel_id=1, source_target_pairs={{0,64},{64,0},{1,65},{65,1},{2,66},{66,2},{3,67},{67,3},{4,68},{68... | collective-permute-start | bytes 1161224 | tf_op jit(solution)/shard_map/ppermute | solution.py:238
  48.5 4.1 %stage_columns.1.w_ref = bf16[1152,4608]{1,0:T(8,128)(2,1)S(1)} custom-call(bf16[1152,2304]{1,0:T(8,128)(2,1)} %own_ref.3, bf16[1152,2304]{1,0:T(8,128)(2,1)} %collective-permute-done.6.after2.other_ref, f32[160,1152]{1,0:T(8,128)S(1)} %get-tuple-element.31.after), custom_call_target="tpu_custom_call" | custom-call | bytes 21233664 | tf_op jit(solution)/shard_map/stage_columns/pallas_call | solution.py:239
  52.7 0.3 fusion.7.a_ref
  53.0 2.5 %project_out.2 = (f32[4,360,128]{2,1,0:T(8,128)S(1)}, bf16[4,360,128]{2,1,0:T(8,128)(2,1)S(1)}, bf16[4,360,128]{2,1,0:T(8,128)(2,1)S(1)}, bf16[4,360,128]{2,1,0:T(8,128)(2,1)S(1)}) custom-call(bf16[160,1152]{1,0:T(8,128)(2,1)S(1)} %fusion.7.a_ref, bf16[1152,4608]{1,0:T(8,128)(2,1)S(1)} %stage_columns.1.w_ref), custom_call_target="tpu_custom_call" | custom-call | flops 1698693120 | bytes 10616832 | tf_op jit(solution)/shard_map/project_out/pallas_call | solution.py:254
  55.5 0.7 collective-permute-start.14
  56.2 1.5 %collective-permute-start.15 = (bf16[4,360,128]{2,1,0:T(8,128)(2,1)S(1)}, bf16[4,360,128]{2,1,0:T(8,128)(2,1)S(1)}, u32[]{:S(2)}, u32[]{:S(2)}) collective-permute-start(bf16[4,360,128]{2,1,0:T(8,128)(2,1)S(1)} %get-tuple-element.34), channel_id=1, source_target_pairs={{0,1},{32,36},{1,2},{33,37},{2,3},{34,38},{3,0},{35,39},{4,5},{36,... | collective-permute-start | bytes 1105928 | tf_op jit(solution)/shard_map/ppermute | solution.py:264
  57.7 1.2 %collective-permute-start.16 = (bf16[4,360,128]{2,1,0:T(8,128)(2,1)S(1)}, bf16[4,360,128]{2,1,0:T(8,128)(2,1)S(1)}, u32[]{:S(2)}, u32[]{:S(2)}) collective-permute-start(bf16[4,360,128]{2,1,0:T(8,128)(2,1)S(1)} %get-tuple-element.35), channel_id=1, source_target_pairs={{0,3},{32,44},{1,0},{33,45},{2,1},{34,46},{3,2},{35,47},{4,7},{36,... | collective-permute-start | bytes 1105928 | tf_op jit(solution)/shard_map/ppermute | solution.py:264
  58.9 0.0 collective-permute-done.17
  59.0 0.3 fusion.15.a_ref
  59.3 2.5 %project_out.3 = (f32[4,360,128]{2,1,0:T(8,128)S(1)}, bf16[4,360,128]{2,1,0:T(8,128)(2,1)S(1)}, bf16[4,360,128]{2,1,0:T(8,128)(2,1)S(1)}, bf16[4,360,128]{2,1,0:T(8,128)(2,1)S(1)}) custom-call(bf16[160,1152]{1,0:T(8,128)(2,1)S(1)} %fusion.15.a_ref, bf16[1152,4608]{1,0:T(8,128)(2,1)S(1)} %stage_columns.1.w_ref), custom_call_target="tpu_custom_call" | custom-call | flops 1698693120 | bytes 10616832 | tf_op jit(solution)/shard_map/project_out/pallas_call | solution.py:254
  61.8 1.2 %collective-permute-start.18 = (bf16[4,360,128]{2,1,0:T(8,128)(2,1)S(1)}, bf16[4,360,128]{2,1,0:T(8,128)(2,1)S(1)}, u32[]{:S(2)}, u32[]{:S(2)}) collective-permute-start(bf16[4,360,128]{2,1,0:T(8,128)(2,1)S(1)} %get-tuple-element.38), channel_id=1, source_target_pairs={{0,2},{32,40},{1,3},{33,41},{2,0},{34,42},{3,1},{35,43},{4,6},{36,... | collective-permute-start | bytes 1105928 | tf_op jit(solution)/shard_map/ppermute | solution.py:264
  63.0 0.8 collective-permute-done.14.b0
  63.8 1.9 %collective-permute-start.20 = (bf16[4,360,128]{2,1,0:T(8,128)(2,1)S(1)}, bf16[4,360,128]{2,1,0:T(8,128)(2,1)S(1)}, u32[]{:S(2)}, u32[]{:S(2)}) collective-permute-start(bf16[4,360,128]{2,1,0:T(8,128)(2,1)S(1)} %get-tuple-element.40), channel_id=1, source_target_pairs={{0,3},{32,44},{1,0},{33,45},{2,1},{34,46},{3,2},{35,47},{4,7},{36,... | collective-permute-start | bytes 1105928 | tf_op jit(solution)/shard_map/ppermute | solution.py:264
  65.7 2.0 %collective-permute-done.15.c0 = bf16[4,360,128]{2,1,0:T(8,128)(2,1)S(1)} collective-permute-done((bf16[4,360,128]{2,1,0:T(8,128)(2,1)S(1)}, bf16[4,360,128]{2,1,0:T(8,128)(2,1)S(1)}, u32[]{:S(2)}, u32[]{:S(2)}) %collective-permute-start.15) | collective-permute-done | bytes 368672 | tf_op jit(solution)/shard_map/ppermute | solution.py:264
  67.7 0.0 collective-permute-done.16.d0
  67.7 4.0 %collective-permute-done.18.b1 = bf16[4,360,128]{2,1,0:T(8,128)(2,1)S(1)} collective-permute-done((bf16[4,360,128]{2,1,0:T(8,128)(2,1)S(1)}, bf16[4,360,128]{2,1,0:T(8,128)(2,1)S(1)}, u32[]{:S(2)}, u32[]{:S(2)}) %collective-permute-start.18) | collective-permute-done | bytes 368672 | tf_op jit(solution)/shard_map/ppermute | solution.py:264
  71.8 3.9 %collective-permute-done.19.c1 = bf16[4,360,128]{2,1,0:T(8,128)(2,1)S(1)} collective-permute-done((bf16[4,360,128]{2,1,0:T(8,128)(2,1)S(1)}, bf16[4,360,128]{2,1,0:T(8,128)(2,1)S(1)}, u32[]{:S(2)}, u32[]{:S(2)}) %collective-permute-start.19) | collective-permute-done | bytes 368672 | tf_op jit(solution)/shard_map/ppermute | solution.py:264
  75.6 0.0 collective-permute-done.20.d1
  75.6 0.3 add_first.1
  76.0 1.6 %collective-permute-start.21 = (bf16[720,128]{1,0:T(8,128)(2,1)S(1)}, bf16[720,128]{1,0:T(8,128)(2,1)S(1)}, u32[]{:S(2)}, u32[]{:S(2)}) collective-permute-start(bf16[720,128]{1,0:T(8,128)(2,1)S(1)} %get-tuple-element.42), channel_id=1, source_target_pairs={{0,8},{32,34},{1,9},{33,35},{2,10},{34,32},{3,11},{35,33},{4,12},{... | collective-permute-start | bytes 552968 | tf_op jit(solution)/shard_map/ppermute | solution.py:267
  77.5 1.4 %collective-permute-start.22 = (bf16[720,128]{1,0:T(8,128)(2,1)S(1)}, bf16[720,128]{1,0:T(8,128)(2,1)S(1)}, u32[]{:S(2)}, u32[]{:S(2)}) collective-permute-start(bf16[720,128]{1,0:T(8,128)(2,1)S(1)} %get-tuple-element.43), channel_id=1, source_target_pairs={{0,4},{32,33},{1,5},{33,34},{2,6},{34,35},{3,7},{35,32},{4,8},{36,... | collective-permute-start | bytes 552968 | tf_op jit(solution)/shard_map/ppermute | solution.py:267
  79.0 1.2 %collective-permute-start.23 = (bf16[720,128]{1,0:T(8,128)(2,1)S(1)}, bf16[720,128]{1,0:T(8,128)(2,1)S(1)}, u32[]{:S(2)}, u32[]{:S(2)}) collective-permute-start(bf16[720,128]{1,0:T(8,128)(2,1)S(1)} %get-tuple-element.44), channel_id=1, source_target_pairs={{0,12},{32,35},{1,13},{33,32},{2,14},{34,33},{3,15},{35,34},{4,0},... | collective-permute-start | bytes 552968 | tf_op jit(solution)/shard_map/ppermute | solution.py:267
  80.2 1.8 %collective-permute-done.21.b = bf16[720,128]{1,0:T(8,128)(2,1)S(1)} collective-permute-done((bf16[720,128]{1,0:T(8,128)(2,1)S(1)}, bf16[720,128]{1,0:T(8,128)(2,1)S(1)}, u32[]{:S(2)}, u32[]{:S(2)}) %collective-permute-start.21) | collective-permute-done | bytes 184352 | tf_op jit(solution)/shard_map/ppermute | solution.py:267
  82.0 1.9 %collective-permute-done.22.c = bf16[720,128]{1,0:T(8,128)(2,1)S(1)} collective-permute-done((bf16[720,128]{1,0:T(8,128)(2,1)S(1)}, bf16[720,128]{1,0:T(8,128)(2,1)S(1)}, u32[]{:S(2)}, u32[]{:S(2)}) %collective-permute-start.22) | collective-permute-done | bytes 184352 | tf_op jit(solution)/shard_map/ppermute | solution.py:267
  83.9 0.2 add_second.1
  84.1 0.1 collective-permute-start.24
  84.2 6.1 %collective-permute-start.25 = (f32[3,72,128]{2,1,0:T(8,128)S(1)}, f32[3,72,128]{2,1,0:T(8,128)S(1)}, u32[]{:S(2)}, u32[]{:S(2)}) collective-permute-start(f32[3,72,128]{2,1,0:T(8,128)S(1)} %get-tuple-element.47), channel_id=1, source_target_pairs={{0,32},{32,0},{1,33},{33,1},{2,34},{34,2},{3,35},{35,3},{4,36},{36... | collective-permute-start | bytes 331784 | tf_op jit(solution)/shard_map/ppermute | solution.py:270
  90.3 1.4 %collective-permute-start.26 = (f32[3,72,128]{2,1,0:T(8,128)S(1)}, f32[3,72,128]{2,1,0:T(8,128)S(1)}, u32[]{:S(2)}, u32[]{:S(2)}) collective-permute-start(f32[3,72,128]{2,1,0:T(8,128)S(1)} %get-tuple-element.48), channel_id=1, source_target_pairs={{0,48},{16,32},{32,16},{48,0},{1,49},{17,33},{33,17},{49,1},{2,50}... | collective-permute-start | bytes 331784 | tf_op jit(solution)/shard_map/ppermute | solution.py:271
  91.7 0.0 collective-permute-done.25.from_c
  91.7 4.6 %collective-permute-done.26.from_czl = f32[3,72,128]{2,1,0:T(8,128)S(1)} collective-permute-done((f32[3,72,128]{2,1,0:T(8,128)S(1)}, f32[3,72,128]{2,1,0:T(8,128)S(1)}, u32[]{:S(2)}, u32[]{:S(2)}) %collective-permute-start.26) | collective-permute-done | bytes 110624 | tf_op jit(solution)/shard_map/ppermute | solution.py:271
  96.3 0.2 finish.1
  96.5 0.8 copy.5
  (14 shorter events, 0.2 us)
Async XLA Ops:
  0.0 19.1 %collective-permute-start.5 = (bf16[2304,1152]{1,0:T(8,128)(2,1)}, bf16[2304,1152]{1,0:T(8,128)(2,1)}, u32[]{:S(2)}, u32[]{:S(2)}) collective-permute-start(bf16[2304,1152]{1,0:T(8,128)(2,1)} %own_ref.2), channel_id=1, source_target_pairs={{0,32},{32,0},{1,33},{33,1},{2,34},{34,2},{3,35},{35,3},{4,36},{36... | collective-permute-start | bytes 15925256 | tf_op jit(solution)/shard_map/ppermute | solution.py:202
  1.4 21.7 %collective-permute-start.6 = (bf16[1152,2304]{1,0:T(8,128)(2,1)}, bf16[1152,2304]{1,0:T(8,128)(2,1)}, u32[]{:S(2)}, u32[]{:S(2)}) collective-permute-start(bf16[1152,2304]{1,0:T(8,128)(2,1)} %own_ref.3), channel_id=1, source_target_pairs={{0,32},{32,0},{1,33},{33,1},{2,34},{34,2},{3,35},{35,3},{4,36},{36... | collective-permute-start | bytes 15925256 | tf_op jit(solution)/shard_map/ppermute | solution.py:203
  1.4 0.9 copy-start
  2.3 0.7 copy-start.1
  3.3 8.3 %collective-permute-start = (bf16[360,128]{1,0:T(8,128)(2,1)S(1)}, bf16[360,128]{1,0:T(8,128)(2,1)S(1)}, u32[]{:S(2)}, u32[]{:S(2)}) collective-permute-start(bf16[360,128]{1,0:T(8,128)(2,1)S(1)} %pack_codes.1), channel_id=1, source_target_pairs={{64,16},{80,64},{16,80},{0,0},{65,17},{81,65},{17,81},{1,1},{66,18... | collective-permute-start | bytes 276488 | tf_op jit(solution)/shard_map/ppermute | solution.py:208
  4.0 9.3 %collective-permute-start.1 = (bf16[360,128]{1,0:T(8,128)(2,1)S(1)}, bf16[360,128]{1,0:T(8,128)(2,1)S(1)}, u32[]{:S(2)}, u32[]{:S(2)}) collective-permute-start(bf16[360,128]{1,0:T(8,128)(2,1)S(1)} %pack_codes.1), channel_id=1, source_target_pairs={{0,16},{16,64},{64,0},{80,80},{1,17},{17,65},{65,1},{81,81},{2,18}... | collective-permute-start | bytes 276488 | tf_op jit(solution)/shard_map/ppermute | solution.py:207
  13.4 9.7 %collective-permute-start.2 = (bf16[2,360,128]{2,1,0:T(8,128)(2,1)S(1)}, bf16[2,360,128]{2,1,0:T(8,128)(2,1)S(1)}, u32[]{:S(2)}, u32[]{:S(2)}) collective-permute-start(bf16[2,360,128]{2,1,0:T(8,128)(2,1)S(1)} %pad_maximum_fusion.a_ref), channel_id=1, source_target_pairs={{0,2},{32,40},{1,3},{33,41},{2,0},{34,42},{3,1},{35,43},{4,6},{36,... | collective-permute-start | bytes 552968 | tf_op jit(solution)/shard_map/ppermute | solution.py:211
  16.4 6.7 %collective-permute-start.3 = (bf16[2,360,128]{2,1,0:T(8,128)(2,1)S(1)}, bf16[2,360,128]{2,1,0:T(8,128)(2,1)S(1)}, u32[]{:S(2)}, u32[]{:S(2)}) collective-permute-start(bf16[2,360,128]{2,1,0:T(8,128)(2,1)S(1)} %pad_maximum_fusion.a_ref), channel_id=1, source_target_pairs={{0,1},{32,36},{1,2},{33,37},{2,3},{34,38},{3,0},{35,39},{4,5},{36,... | collective-permute-start | bytes 552968 | tf_op jit(solution)/shard_map/ppermute | solution.py:211
  16.8 6.3 %collective-permute-start.4 = (bf16[2,360,128]{2,1,0:T(8,128)(2,1)S(1)}, bf16[2,360,128]{2,1,0:T(8,128)(2,1)S(1)}, u32[]{:S(2)}, u32[]{:S(2)}) collective-permute-start(bf16[2,360,128]{2,1,0:T(8,128)(2,1)S(1)} %pad_maximum_fusion.a_ref), channel_id=1, source_target_pairs={{0,3},{32,44},{1,0},{33,45},{2,1},{34,46},{3,2},{35,47},{4,7},{36,... | collective-permute-start | bytes 552968 | tf_op jit(solution)/shard_map/ppermute | solution.py:211
  23.5 8.2 %collective-permute-start.7 = (bf16[160,1152]{1,0:T(8,128)(2,1)S(1)}, bf16[160,1152]{1,0:T(8,128)(2,1)S(1)}, u32[]{:S(2)}, u32[]{:S(2)}) collective-permute-start(bf16[160,1152]{1,0:T(8,128)(2,1)S(1)} %get-tuple-element.27.m0), channel_id=1, source_target_pairs={{0,8},{32,34},{1,9},{33,35},{2,10},{34,32},{3,11},{35,33},{4,12},{... | collective-permute-start | bytes 1105928 | tf_op jit(solution)/shard_map/ppermute | solution.py:223
  26.4 9.4 %collective-permute-start.8 = (bf16[160,1152]{1,0:T(8,128)(2,1)S(1)}, bf16[160,1152]{1,0:T(8,128)(2,1)S(1)}, u32[]{:S(2)}, u32[]{:S(2)}) collective-permute-start(bf16[160,1152]{1,0:T(8,128)(2,1)S(1)} %get-tuple-element.27.m0), channel_id=1, source_target_pairs={{0,4},{32,33},{1,5},{33,34},{2,6},{34,35},{3,7},{35,32},{4,8},{36,... | collective-permute-start | bytes 1105928 | tf_op jit(solution)/shard_map/ppermute | solution.py:223
  26.7 9.1 %collective-permute-start.9 = (bf16[160,1152]{1,0:T(8,128)(2,1)S(1)}, bf16[160,1152]{1,0:T(8,128)(2,1)S(1)}, u32[]{:S(2)}, u32[]{:S(2)}) collective-permute-start(bf16[160,1152]{1,0:T(8,128)(2,1)S(1)} %get-tuple-element.27.m0), channel_id=1, source_target_pairs={{0,12},{32,35},{1,13},{33,32},{2,14},{34,33},{3,15},{35,34},{4,0},... | collective-permute-start | bytes 1105928 | tf_op jit(solution)/shard_map/ppermute | solution.py:223
  29.1 11.5 %collective-permute-start.11 = (bf16[160,1152]{1,0:T(8,128)(2,1)S(1)}, bf16[160,1152]{1,0:T(8,128)(2,1)S(1)}, u32[]{:S(2)}, u32[]{:S(2)}) collective-permute-start(bf16[160,1152]{1,0:T(8,128)(2,1)S(1)} %get-tuple-element.30.m0), channel_id=1, source_target_pairs={{0,8},{32,34},{1,9},{33,35},{2,10},{34,32},{3,11},{35,33},{4,12},{... | collective-permute-start | bytes 1105928 | tf_op jit(solution)/shard_map/ppermute | solution.py:223
  29.1 14.6 %collective-permute-start.12 = (bf16[160,1152]{1,0:T(8,128)(2,1)S(1)}, bf16[160,1152]{1,0:T(8,128)(2,1)S(1)}, u32[]{:S(2)}, u32[]{:S(2)}) collective-permute-start(bf16[160,1152]{1,0:T(8,128)(2,1)S(1)} %get-tuple-element.30.m0), channel_id=1, source_target_pairs={{0,4},{32,33},{1,5},{33,34},{2,6},{34,35},{3,7},{35,32},{4,8},{36,... | collective-permute-start | bytes 1105928 | tf_op jit(solution)/shard_map/ppermute | solution.py:223
  31.8 12.0 %collective-permute-start.13 = (bf16[160,1152]{1,0:T(8,128)(2,1)S(1)}, bf16[160,1152]{1,0:T(8,128)(2,1)S(1)}, u32[]{:S(2)}, u32[]{:S(2)}) collective-permute-start(bf16[160,1152]{1,0:T(8,128)(2,1)S(1)} %get-tuple-element.30.m0), channel_id=1, source_target_pairs={{0,12},{32,35},{1,13},{33,32},{2,14},{34,33},{3,15},{35,34},{4,0},... | collective-permute-start | bytes 1105928 | tf_op jit(solution)/shard_map/ppermute | solution.py:223
  38.2 14.5 %collective-permute-start.10 = (f16[168,1152]{1,0:T(8,128)(2,1)S(1)}, f16[168,1152]{1,0:T(8,128)(2,1)S(1)}, u32[]{:S(2)}, u32[]{:S(2)}) collective-permute-start(f16[168,1152]{1,0:T(8,128)(2,1)S(1)} %convert_element_type.24), channel_id=1, source_target_pairs={{0,64},{64,0},{1,65},{65,1},{2,66},{66,2},{3,67},{67,3},{4,68},{68... | collective-permute-start | bytes 1161224 | tf_op jit(solution)/shard_map/ppermute | solution.py:238
  46.1 12.8 %collective-permute-start.17 = (f16[168,1152]{1,0:T(8,128)(2,1)S(1)}, f16[168,1152]{1,0:T(8,128)(2,1)S(1)}, u32[]{:S(2)}, u32[]{:S(2)}) collective-permute-start(f16[168,1152]{1,0:T(8,128)(2,1)S(1)} %convert_element_type.28), channel_id=1, source_target_pairs={{0,64},{64,0},{1,65},{65,1},{2,66},{66,2},{3,67},{67,3},{4,68},{68... | collective-permute-start | bytes 1161224 | tf_op jit(solution)/shard_map/ppermute | solution.py:238
  55.5 8.3 %collective-permute-start.14 = (bf16[4,360,128]{2,1,0:T(8,128)(2,1)S(1)}, bf16[4,360,128]{2,1,0:T(8,128)(2,1)S(1)}, u32[]{:S(2)}, u32[]{:S(2)}) collective-permute-start(bf16[4,360,128]{2,1,0:T(8,128)(2,1)S(1)} %get-tuple-element.33), channel_id=1, source_target_pairs={{0,2},{32,40},{1,3},{33,41},{2,0},{34,42},{3,1},{35,43},{4,6},{36,... | collective-permute-start | bytes 1105928 | tf_op jit(solution)/shard_map/ppermute | solution.py:264
  56.2 11.5 %collective-permute-start.15 = (bf16[4,360,128]{2,1,0:T(8,128)(2,1)S(1)}, bf16[4,360,128]{2,1,0:T(8,128)(2,1)S(1)}, u32[]{:S(2)}, u32[]{:S(2)}) collective-permute-start(bf16[4,360,128]{2,1,0:T(8,128)(2,1)S(1)} %get-tuple-element.34), channel_id=1, source_target_pairs={{0,1},{32,36},{1,2},{33,37},{2,3},{34,38},{3,0},{35,39},{4,5},{36,... | collective-permute-start | bytes 1105928 | tf_op jit(solution)/shard_map/ppermute | solution.py:264
  57.7 10.0 %collective-permute-start.16 = (bf16[4,360,128]{2,1,0:T(8,128)(2,1)S(1)}, bf16[4,360,128]{2,1,0:T(8,128)(2,1)S(1)}, u32[]{:S(2)}, u32[]{:S(2)}) collective-permute-start(bf16[4,360,128]{2,1,0:T(8,128)(2,1)S(1)} %get-tuple-element.35), channel_id=1, source_target_pairs={{0,3},{32,44},{1,0},{33,45},{2,1},{34,46},{3,2},{35,47},{4,7},{36,... | collective-permute-start | bytes 1105928 | tf_op jit(solution)/shard_map/ppermute | solution.py:264
  61.8 9.9 %collective-permute-start.18 = (bf16[4,360,128]{2,1,0:T(8,128)(2,1)S(1)}, bf16[4,360,128]{2,1,0:T(8,128)(2,1)S(1)}, u32[]{:S(2)}, u32[]{:S(2)}) collective-permute-start(bf16[4,360,128]{2,1,0:T(8,128)(2,1)S(1)} %get-tuple-element.38), channel_id=1, source_target_pairs={{0,2},{32,40},{1,3},{33,41},{2,0},{34,42},{3,1},{35,43},{4,6},{36,... | collective-permute-start | bytes 1105928 | tf_op jit(solution)/shard_map/ppermute | solution.py:264
  63.0 12.6 %collective-permute-start.19 = (bf16[4,360,128]{2,1,0:T(8,128)(2,1)S(1)}, bf16[4,360,128]{2,1,0:T(8,128)(2,1)S(1)}, u32[]{:S(2)}, u32[]{:S(2)}) collective-permute-start(bf16[4,360,128]{2,1,0:T(8,128)(2,1)S(1)} %get-tuple-element.39), channel_id=1, source_target_pairs={{0,1},{32,36},{1,2},{33,37},{2,3},{34,38},{3,0},{35,39},{4,5},{36,... | collective-permute-start | bytes 1105928 | tf_op jit(solution)/shard_map/ppermute | solution.py:264
  63.8 11.8 %collective-permute-start.20 = (bf16[4,360,128]{2,1,0:T(8,128)(2,1)S(1)}, bf16[4,360,128]{2,1,0:T(8,128)(2,1)S(1)}, u32[]{:S(2)}, u32[]{:S(2)}) collective-permute-start(bf16[4,360,128]{2,1,0:T(8,128)(2,1)S(1)} %get-tuple-element.40), channel_id=1, source_target_pairs={{0,3},{32,44},{1,0},{33,45},{2,1},{34,46},{3,2},{35,47},{4,7},{36,... | collective-permute-start | bytes 1105928 | tf_op jit(solution)/shard_map/ppermute | solution.py:264
  76.0 6.1 %collective-permute-start.21 = (bf16[720,128]{1,0:T(8,128)(2,1)S(1)}, bf16[720,128]{1,0:T(8,128)(2,1)S(1)}, u32[]{:S(2)}, u32[]{:S(2)}) collective-permute-start(bf16[720,128]{1,0:T(8,128)(2,1)S(1)} %get-tuple-element.42), channel_id=1, source_target_pairs={{0,8},{32,34},{1,9},{33,35},{2,10},{34,32},{3,11},{35,33},{4,12},{... | collective-permute-start | bytes 552968 | tf_op jit(solution)/shard_map/ppermute | solution.py:267
  77.5 6.4 %collective-permute-start.22 = (bf16[720,128]{1,0:T(8,128)(2,1)S(1)}, bf16[720,128]{1,0:T(8,128)(2,1)S(1)}, u32[]{:S(2)}, u32[]{:S(2)}) collective-permute-start(bf16[720,128]{1,0:T(8,128)(2,1)S(1)} %get-tuple-element.43), channel_id=1, source_target_pairs={{0,4},{32,33},{1,5},{33,34},{2,6},{34,35},{3,7},{35,32},{4,8},{36,... | collective-permute-start | bytes 552968 | tf_op jit(solution)/shard_map/ppermute | solution.py:267
  79.0 4.9 %collective-permute-start.23 = (bf16[720,128]{1,0:T(8,128)(2,1)S(1)}, bf16[720,128]{1,0:T(8,128)(2,1)S(1)}, u32[]{:S(2)}, u32[]{:S(2)}) collective-permute-start(bf16[720,128]{1,0:T(8,128)(2,1)S(1)} %get-tuple-element.44), channel_id=1, source_target_pairs={{0,12},{32,35},{1,13},{33,32},{2,14},{34,33},{3,15},{35,34},{4,0},... | collective-permute-start | bytes 552968 | tf_op jit(solution)/shard_map/ppermute | solution.py:267
  84.1 7.6 %collective-permute-start.24 = (f32[3,72,128]{2,1,0:T(8,128)S(1)}, f32[3,72,128]{2,1,0:T(8,128)S(1)}, u32[]{:S(2)}, u32[]{:S(2)}) collective-permute-start(f32[3,72,128]{2,1,0:T(8,128)S(1)} %get-tuple-element.46), channel_id=1, source_target_pairs={{0,16},{16,0},{1,17},{17,1},{2,18},{18,2},{3,19},{19,3},{4,20},{20... | collective-permute-start | bytes 331784 | tf_op jit(solution)/shard_map/ppermute | solution.py:269
  84.2 7.5 %collective-permute-start.25 = (f32[3,72,128]{2,1,0:T(8,128)S(1)}, f32[3,72,128]{2,1,0:T(8,128)S(1)}, u32[]{:S(2)}, u32[]{:S(2)}) collective-permute-start(f32[3,72,128]{2,1,0:T(8,128)S(1)} %get-tuple-element.47), channel_id=1, source_target_pairs={{0,32},{32,0},{1,33},{33,1},{2,34},{34,2},{3,35},{35,3},{4,36},{36... | collective-permute-start | bytes 331784 | tf_op jit(solution)/shard_map/ppermute | solution.py:270
  90.3 6.0 %collective-permute-start.26 = (f32[3,72,128]{2,1,0:T(8,128)S(1)}, f32[3,72,128]{2,1,0:T(8,128)S(1)}, u32[]{:S(2)}, u32[]{:S(2)}) collective-permute-start(f32[3,72,128]{2,1,0:T(8,128)S(1)} %get-tuple-element.48), channel_id=1, source_target_pairs={{0,48},{16,32},{32,16},{48,0},{1,49},{17,33},{33,17},{49,1},{2,50}... | collective-permute-start | bytes 331784 | tf_op jit(solution)/shard_map/ppermute | solution.py:271

commit v4 on v3

--- a/solution.py
+++ b/solution.py
@@ -11,10 +11,10 @@
 UNITS = 1152
 CHIP_COLS = 72
 VMEM = pl.BlockSpec(memory_space=pltpu.VMEM)
-HBM = pl.BlockSpec(memory_space=pltpu.HBM)
 ANY = pl.BlockSpec(memory_space=pl.ANY)
 YX = ("c", "y", "x")
 STEPS = (0, 2, 1, 3)
+GATHER = (0, 3, 1, 2)
 
 
 def first_axis(step):
@@ -35,12 +35,13 @@
     return pairs
 
 
-def call(kernel, outs, ins, scratch=(), flops=0, nbytes=0, vmem=8, name=None):
+def call(kernel, outs, ins, scratch=(), flops=0, nbytes=0, vmem=8, alias={}, name=None):
     return pl.pallas_call(
         kernel,
         out_shape=outs,
         in_specs=ins,
         out_specs=jax.tree.map(lambda _: VMEM, outs),
+        input_output_aliases=alias,
         scratch_shapes=list(scratch),
         compiler_params=pltpu.CompilerParams(vmem_limit_bytes=vmem * 2**20),
         cost_estimate=pl.CostEstimate(flops=flops, bytes_accessed=nbytes, transcendentals=0),
@@ -52,9 +53,17 @@
     return jnp.dot(a, b, preferred_element_type=F32)
 
 
-def pack_codes(x_ref, e_ref, o_ref):
+def pack_codes(codes_ref, exponents_ref, o_ref, x_ref, e_ref, sems):
+    copies = [
+        pltpu.make_async_copy(codes_ref, x_ref, sems.at[0]),
+        pltpu.make_async_copy(exponents_ref, e_ref, sems.at[1]),
+    ]
+    for copy in copies:
+        copy.start()
     row = lax.broadcasted_iota(jnp.int32, (QT, QT), 0)
     col = lax.broadcasted_iota(jnp.int32, (QT, QT), 1)
+    for copy in copies:
+        copy.wait()
     power = jnp.exp2(jnp.broadcast_to(e_ref[...], (QT, QT)).astype(F32))
     scale = jnp.where(row == col, power, 0.0).astype(BF)
     x = dot(scale, x_ref[...]).astype(BF)
@@ -68,6 +77,13 @@
         place = jnp.where(dst == src + 32 * j, 1.0, 0.0).astype(BF)
         total += dot(tail, place)[40 * j : 40 * j + 40]
     o_ref[2 * QT : 360] = total.astype(BF)
+
+
+def order_quarters(one, two, after, o_ref):
+    del after
+    same = lax.axis_index("zh") == lax.axis_index("zl")
+    o_ref[0] = jnp.where(same, two[...], one[...])
+    o_ref[1] = jnp.where(same, one[...], two[...])
 
 
 def merge_codes(a_ref, b_ref, c_ref, d_ref, after1, after2, *outs):
@@ -92,47 +108,61 @@
     return c, jnp.where(c == 0, x, y), jnp.where(c == 0, y, x)
 
 
-def arrange_rows(own_ref, other_ref, w_ref, sem):
+def arrange_rows(own, ref, w_ref, sem):
     c, first, second = own_place()
     for i in range(4):
-        s = lax.rem(second + 4 - STEPS[i], 4)
+        s = lax.rem(second + 4 - GATHER[i], 4)
         for j in range(4):
-            f = lax.rem(first + 4 - STEPS[j], 4)
+            f = lax.rem(first + 4 - GATHER[j], 4)
             y, x = jnp.where(c == 0, s, f), jnp.where(c == 0, f, s)
             row = lax.rem(y, 2) * UNITS + x * PIECE
-            for ref, here in ((own_ref, lax.div(y, 2) == c), (other_ref, lax.div(y, 2) != c)):
-
-                @pl.when(here)
-                def _(ref=ref):
-                    for at, to, n in ((0, 256 * j, 256), (256, 1024 + 32 * j, 32)):
-                        pltpu.make_async_copy(
-                            ref.at[pl.ds(pl.multiple_of(row + at, 32), n)], w_ref.at[pl.ds(i * UNITS + to, n)], sem
-                        ).start()
-
-    pltpu.make_async_copy(w_ref, w_ref, sem).wait()
-
-
-def stage_columns(own_ref, other_ref, after, w_ref, sem):
+
+            @pl.when((lax.div(y, 2) == c) == own)
+            def _():
+                for at, to, n in ((0, 256 * j, 256), (256, 1024 + 32 * j, 32)):
+                    pltpu.make_async_copy(
+                        ref.at[pl.ds(pl.multiple_of(row + at, 32), n)], w_ref.at[pl.ds(i * UNITS + to, n)], sem
+                    ).start()
+
+    pltpu.make_async_copy(w_ref.at[: 2 * UNITS], w_ref.at[: 2 * UNITS], sem).wait()
+
+
+def arrange_own(ref, w_ref, sem):
+    arrange_rows(True, ref, w_ref, sem)
+
+
+def arrange_other(ref, half_ref, w_ref, sem):
+    del half_ref
+    arrange_rows(False, ref, w_ref, sem)
+
+
+def stage_own(ref, after, w_ref, sem):
     del after
-    for ref, at in ((own_ref, 0), (other_ref, 2 * UNITS)):
-        pltpu.make_async_copy(ref, w_ref.at[:, at : at + 2 * UNITS], sem).start()
-    pltpu.make_async_copy(w_ref, w_ref, sem).wait()
+    copy = pltpu.make_async_copy(ref, w_ref.at[:, : 2 * UNITS], sem)
+    copy.start()
+    copy.wait()
+
+
+def stage_other(ref, half_ref, w_ref, sem):
+    del half_ref
+    copy = pltpu.make_async_copy(ref, w_ref.at[:, 2 * UNITS :], sem)
+    copy.start()
+    copy.wait()
+
+
+def scaled(x):
+    most = jnp.full((8, x.shape[1]), jnp.max(jnp.abs(x)))
+    power = 13.0 - jnp.ceil(jnp.log(jnp.maximum(most, 1e-30)) * 1.4426950408889634)
+    return x * jnp.exp2(power)[:1], power
 
 
 def project_in(m0, m1, m2, m3, w_ref, o_ref, send_ref, x_ref):
     for i, m in enumerate((m0, m1, m2, m3)):
         x_ref[:, i * UNITS : (i + 1) * UNITS] = m[...]
-    most = jnp.zeros((QT, 128), F32)
     for n in range(0, UNITS, 256):
         to = min(n + 256, UNITS)
-        part = dot(x_ref[...], w_ref[:, n:to])
-        o_ref[:, n:to] = part
-        for k in range(0, to - n, 128):
-            most = jnp.maximum(most, jnp.abs(part[:, k : k + 128]))
-    most = jnp.full((8, UNITS), jnp.max(most))
-    power = 13.0 - jnp.ceil(jnp.log(jnp.maximum(most, 1e-30)) * 1.4426950408889634)
-    send_ref[0:QT] = o_ref[...] * jnp.exp2(power)[:1]
-    send_ref[QT:] = power
+        o_ref[:, n:to] = dot(x_ref[...], w_ref[:, n:to])
+    send_ref[0:QT], send_ref[QT:] = scaled(o_ref[...])
 
 
 def project_out(a_ref, w_ref, o0, o1, o2, o3, t_ref, tail_ref):
@@ -175,24 +205,33 @@
         tail = jnp.where(lane < 32, pltpu.roll(tiles[4], (128 - 32 * g) % 128, 1), pltpu.roll(tiles[9], (160 - 32 * g) % 128, 1))
         return tiles[g], tiles[5 + g], tail
 
-    for crel, same, swapped in ((0, keep, to_zl), (1, to_c, to_czl)):
-        for i, (lo, hi) in enumerate(zip(share(crel, 0), share(crel, 1))):
-            same[i] = jnp.where(zl == 0, lo, hi)
-            swapped[i] = jnp.where(zl == 0, hi, lo)
+    shares = []
+    for crel in range(2):
+        lo, hi = (jnp.concatenate(share(crel, z), axis=0) for z in range(2))
+        shares.append((jnp.where(zl == 0, lo, hi), jnp.where(zl == 0, hi, lo)))
+    keep[...] = shares[0][0]
+    to_c[...] = shares[1][0]
+    for ref, (_, value) in zip((to_zl, to_czl), shares):
+        ref[0:216], ref[216:] = scaled(value)
 
 
 def finish(keep, from_zl, from_c, from_czl, o_ref):
     c = lax.axis_index("c")
     for core, a, b in ((c, keep, from_zl), (1 - c, from_c, from_czl)):
-        tail = (a[2] + b[2]).T
+        total = a[...] + b[0:216] * jnp.exp2(-b[216:])[:1]
+        tail = total[144:].T
         for q in range(2):
             row = (2 * q + core) * QT
-            o_ref[pl.ds(pl.multiple_of(row, 8), 128)] = (a[q] + b[q]).T
+            o_ref[pl.ds(pl.multiple_of(row, 8), 128)] = total[72 * q : 72 * q + 72].T
             o_ref[pl.ds(pl.multiple_of(row + 128, 8), 32)] = tail[32 * q : 32 * q + 32]
 
 
 def shape(dims, dtype):
     return jax.ShapeDtypeStruct(dims, dtype)
+
+
+def in_hbm(x):
+    return pltpu.with_memory_space_constraint(x, pltpu.HBM)
 
 
 def shards(codes, exponents, w_in, w_out):
@@ -201,26 +240,27 @@
     z = ("zh", "zl")
     w_in_other = lax.ppermute(w_in, "c", swap)
     w_out_other = lax.ppermute(w_out, "c", swap)
-    w_in, w_out = (pltpu.with_memory_space_constraint(w, pltpu.HBM) for w in (w_in, w_out))
-
-    packed = call(pack_codes, shape((360, 128), BF), [VMEM] * 2, name="pack_codes")(codes, exponents[None, :])
+    w_in, w_out = in_hbm(w_in), in_hbm(w_out)
+
+    packed = call(
+        pack_codes,
+        shape((360, 128), BF),
+        [ANY] * 2,
+        [pltpu.VMEM((QT, PIECE), BF), pltpu.VMEM((1, QT), jnp.int32), pltpu.SemaphoreType.DMA((2,))],
+        name="pack_codes",
+    )(in_hbm(codes), in_hbm(exponents[None, :]))
     one = lax.ppermute(packed, z, [(0, 1), (1, 2), (2, 0), (3, 3)])
     two = lax.ppermute(packed, z, [(2, 1), (3, 2), (1, 3), (0, 0)])
-    piece = jnp.stack([jnp.where(zh == zl, two, one), jnp.where(zh == zl, one, two)])
-
-    around = [lax.ppermute(piece, YX, first_axis(k)) for k in STEPS[1:]]
-    weights = call(
-        arrange_rows,
-        pltpu.VMEM((4 * UNITS, UNITS), BF),
-        [HBM, ANY],
-        [pltpu.SemaphoreType.DMA],
-        nbytes=2 * 4608 * 1152 * 2,
-        vmem=8,
-        name="arrange_rows",
-    )(w_in, w_in_other)
+    dma, half = [pltpu.SemaphoreType.DMA], 4608 * 1152 * 2
+    rows = call(arrange_own, pltpu.VMEM((4 * UNITS, UNITS), BF), [ANY], dma, nbytes=half, name="arrange_own")(w_in)
+    piece = call(order_quarters, shape((2, 360, 128), BF), [VMEM, VMEM, ANY], name="order_quarters")(one, two, rows)
+    around = [lax.ppermute(piece, YX, first_axis(k)) for k in GATHER[1:]]
+    rows = call(
+        arrange_other, pltpu.VMEM((4 * UNITS, UNITS), BF), [ANY, VMEM], dma, nbytes=half, alias={1: 0}, name="arrange_other"
+    )(w_in_other, rows)
     quarter = shape((QT, UNITS), BF)
-    merged = call(merge_codes, [quarter] * 2, [VMEM] * 4 + [ANY] * 2, name="merge_codes")(piece, *around, weights, w_out_other)
-    around = [[lax.ppermute(m, YX, second_axis(k)) for k in STEPS[1:]] for m in merged]
+    merged = call(merge_codes, [quarter] * 2, [VMEM] * 4 + [ANY] * 2, name="merge_codes")(piece, *around, rows, w_out_other)
+    around = [[lax.ppermute(m, YX, second_axis(k)) for k in GATHER[1:]] for m in merged]
 
     preacts, sends = [], []
     for q in range(2):
@@ -232,19 +272,14 @@
             flops=2 * QT * 4608 * 1152,
             nbytes=4608 * 1152 * 2,
             name="project_in",
-        )(merged[q], *around[q], weights)
+        )(merged[q], *around[q], rows)
         preacts.append(preact)
         sends.append(send.astype(jnp.float16))
     gots = [lax.ppermute(send, "zh", swap) for send in sends]
-    weights = call(
-        stage_columns,
-        pltpu.VMEM((UNITS, 4 * UNITS), BF),
-        [HBM, ANY, ANY],
-        [pltpu.SemaphoreType.DMA],
-        nbytes=2 * 4608 * 1152 * 2,
-        vmem=8,
-        name="stage_columns",
-    )(w_out, w_out_other, preacts[1])
+    columns = call(stage_own, pltpu.VMEM((UNITS, 4 * UNITS), BF), [ANY] * 2, dma, nbytes=half, name="stage_own")(w_out, merged[0])
+    columns = call(
+        stage_other, pltpu.VMEM((UNITS, 4 * UNITS), BF), [ANY, VMEM], dma, nbytes=half, alias={1: 0}, name="stage_other"
+    )(w_out_other, columns)
 
     scattered = []
     for preact, got in zip(preacts, gots):
@@ -260,15 +295,16 @@
             nbytes=4608 * 1152 * 2,
             vmem=12,
             name="project_out",
-        )(activ, weights)
+        )(activ, columns)
         scattered += [mine] + [lax.ppermute(v, YX, first_axis(k)) for k, v in zip(STEPS[1:], away)]
     part = (720, 128)
     mine, *away = call(add_first, [shape(part, F32)] + [shape(part, BF)] * 3, [VMEM] * 8, name="add_first")(*scattered)
     away = [lax.ppermute(v, YX, second_axis(k)) for k, v in zip(STEPS[1:], away)]
-    keep, to_zl, to_c, to_czl = call(add_second, [shape((3, CHIP_COLS, 128), F32)] * 4, [VMEM] * 4, name="add_second")(mine, *away)
-    from_zl = lax.ppermute(to_zl, "zl", swap)
+    plain, with_power = shape((216, 128), F32), shape((224, 128), F32)
+    keep, to_zl, to_c, to_czl = call(add_second, [plain, with_power] * 2, [VMEM] * 4, name="add_second")(mine, *away)
+    from_zl = lax.ppermute(to_zl.astype(jnp.float16), "zl", swap).astype(F32)
+    from_czl = lax.ppermute(to_czl.astype(jnp.float16), ("c", "zl"), [(0, 3), (1, 2), (2, 1), (3, 0)]).astype(F32)
     from_c = lax.ppermute(to_c, "c", swap)
-    from_czl = lax.ppermute(to_czl, ("c", "zl"), [(0, 3), (1, 2), (2, 1), (3, 0)])
     return call(finish, shape((4 * QT, CHIP_COLS), F32), [VMEM] * 4, name="finish")(keep, from_zl, from_c, from_czl)
 
 

time: 97.5 us -> 94.7 us (0.971); the launches traced: 97.3 us -> 93.1 us
  waiting for transfers between devices: 27.7 us -> 21.7 us
  starting transfers between devices: 47 us -> 49.9 us
  local copies, waits for them, and re-layouts: 2.41 us -> 0.83 us
    ppermute x5, starting transfers between devices: 7.17 us -> 9.22 us  [the longest x3 5.65 us: shards(): around = [lax.ppermute(piece, YX, first_axis(k)) for k in GATHER[1:]]]
    ppermute x6, starting transfers between devices: 6.49 us -> 8.51 us  [shards(): lax.ppermute(v, YX, first_axis(k))]
    ppermute x6, waiting for transfers between devices: 10.7 us -> 8.7 us  [shards(): lax.ppermute(v, YX, first_axis(k))]
    ppermute x1, waiting for transfers between devices: 1.71 us -> 0.01 us  [shards(): one = lax.ppermute(packed, z, [(0, 1), (1, 2), (2, 0), (3, 3)])]
    ppermute x6, waiting for transfers between devices: 6.93 us -> 5.29 us  [shards(): lax.ppermute(m, YX, second_axis(k))]
    unnamed x4 -> x0, local copies, waits for them, and re-layouts: 1.58 us -> none
    ppermute x2, starting transfers between devices: 4.76 us -> 3.3 us  [shards(): gots = [lax.ppermute(send, 'zh', swap) for send in sends]]
    pallas_call x4 -> x7, Pallas kernels: 8.63 us -> 8.95 us  [the longest x1 2.54 us: shards(): call(arrange_own, pltpu.VMEM((4 * UNITS, UNITS), BF), [ANY], dma, nbytes=...]
  transfers between devices with their start and end apart: 27 -> 27, of which waited for: 13 -> 14; matrix products, arithmetic and copies ran while one was open for 1% -> 1% of each run, Pallas kernels for 19% -> 20%
where the time goes in v4:
time: 94.7 us; the launch traced here: 93.1 us
  starting transfers between devices  49.9 us (53%)
  waiting for transfers between devices  21.7 us (23%)
  Pallas kernels  19.5 us (21%)
    ppermute x6, waiting for transfers between devices, shards(): lax.ppermute(v, YX, first_axis(k))  8.7 us
    ppermute x6, starting transfers between devices, shards(): lax.ppermute(v, YX, first_axis(k))  8.51 us
    ppermute x6, starting transfers between devices, shards(): lax.ppermute(m, YX, second_axis(k))  7.93 us
    ppermute x1, starting transfers between devices, shards(): one = lax.ppermute(packed, z, [(0, 1), (1, 2), (2, 0), (3, 3)])  7.57 us
    ppermute x1, starting transfers between devices, shards(): from_c = lax.ppermute(to_c, 'c', swap)  6.56 us
    ppermute x3, starting transfers between devices, shards(): around = [lax.ppermute(piece, YX, first_axis(k)) for k in GATHER[1:]]  5.65 us
    ppermute x6, waiting for transfers between devices, shards(): lax.ppermute(m, YX, second_axis(k))  5.29 us
    pallas_call x2, Pallas kernels, shards(): call(project_out, [shape(part, F32)] + [shape(part, BF)] * 3, [VMEM] * 2,...  5.08 us
  transfers between devices with their start and end apart: 27, of which 14 were waited for; matrix products, arithmetic and copies ran while one was open for 1% of the time, Pallas kernels for 20%

profile of v4, /device:TPU:1, one launch (start us, length us, event | category | flops | bytes accessed | tf_op | source)
XLA Modules:
  0.0 93.1 jit_solution(2473135486138342135)
XLA Ops:
  0.0 1.4 %collective-permute-start.5 = (bf16[2304,1152]{1,0:T(8,128)(2,1)}, bf16[2304,1152]{1,0:T(8,128)(2,1)S(1)}, u32[]{:S(2)}, u32[]{:S(2)}) collective-permute-start(bf16[2304,1152]{1,0:T(8,128)(2,1)} %ref.2), channel_id=1, source_target_pairs={{0,32},{32,0},{1,33},{33,1},{2,34},{34,2},{3,35},{35,3},{4,36},{36... | collective-permute-start | bytes 15925256 | tf_op jit(solution)/shard_map/ppermute | solution.py:241
  1.4 0.0 collective-permute-start.6
  1.4 1.3 %pack_codes.1 = bf16[360,128]{1,0:T(8,128)(2,1)S(1)} custom-call(bf16[160,288]{1,0:T(8,128)(2,1)} %codes_ref.1, s32[1,160]{1,0:T(1,128)} %bitcast.1), custom_call_target="tpu_custom_call" | custom-call | tf_op jit(solution)/shard_map/pack_codes/pallas_call | solution.py:245
  2.7 0.7 collective-permute-start.1
  3.4 7.6 %collective-permute-start = (bf16[360,128]{1,0:T(8,128)(2,1)S(1)}, bf16[360,128]{1,0:T(8,128)(2,1)S(1)}, u32[]{:S(2)}, u32[]{:S(2)}) collective-permute-start(bf16[360,128]{1,0:T(8,128)(2,1)S(1)} %pack_codes.1), channel_id=1, source_target_pairs={{0,16},{16,64},{64,0},{80,80},{1,17},{17,65},{65,1},{81,81},{2,18}... | collective-permute-start | bytes 276488 | tf_op jit(solution)/shard_map/ppermute | solution.py:252
  10.9 2.5 %arrange_own.1.after.half_ref = bf16[4608,1152]{1,0:T(8,128)(2,1)S(1)} custom-call(bf16[2304,1152]{1,0:T(8,128)(2,1)} %ref.2), custom_call_target="tpu_custom_call" | custom-call | bytes 10616832 | tf_op jit(solution)/shard_map/arrange_own/pallas_call | solution.py:255
  13.5 0.0 collective-permute-done.1.two
  13.5 0.0 collective-permute-done.one
  13.6 3.0 %collective-permute-start.4 = (bf16[2,360,128]{2,1,0:T(8,128)(2,1)S(1)}, bf16[2,360,128]{2,1,0:T(8,128)(2,1)S(1)}, u32[]{:S(2)}, u32[]{:S(2)}) collective-permute-start(bf16[2,360,128]{2,1,0:T(8,128)(2,1)S(1)} %order_quarters.1.a_ref), channel_id=1, source_target_pairs={{0,2},{32,40},{1,3},{33,41},{2,0},{34,42},{3,1},{35,43},{4,6},{36,... | collective-permute-start | bytes 552968 | tf_op jit(solution)/shard_map/ppermute | solution.py:257
  16.5 0.4 collective-permute-start.3
  16.9 2.3 %collective-permute-start.2 = (bf16[2,360,128]{2,1,0:T(8,128)(2,1)S(1)}, bf16[2,360,128]{2,1,0:T(8,128)(2,1)S(1)}, u32[]{:S(2)}, u32[]{:S(2)}) collective-permute-start(bf16[2,360,128]{2,1,0:T(8,128)(2,1)S(1)} %order_quarters.1.a_ref), channel_id=1, source_target_pairs={{0,3},{32,44},{1,0},{33,45},{2,1},{34,46},{3,2},{35,47},{4,7},{36,... | collective-permute-start | bytes 552968 | tf_op jit(solution)/shard_map/ppermute | solution.py:257
  19.2 1.9 %arrange_other.1.after1.w_ref = bf16[4608,1152]{1,0:T(8,128)(2,1)S(1)} custom-call(bf16[2304,1152]{1,0:T(8,128)(2,1)S(1)} %collective-permute-done.5.ref, bf16[4608,1152]{1,0:T(8,128)(2,1)S(1)} %arrange_own.1.after.half_ref), custom_call_target="tpu_custom_call", output_to_operand_aliasing={{}: (1, {})} | custom-call | bytes 10616832 | tf_op jit(solution)/shard_map/arrange_other/pallas_call | solution.py:258
  21.1 1.3 %collective-permute-done.3.c_ref = bf16[2,360,128]{2,1,0:T(8,128)(2,1)S(1)} collective-permute-done((bf16[2,360,128]{2,1,0:T(8,128)(2,1)S(1)}, bf16[2,360,128]{2,1,0:T(8,128)(2,1)S(1)}, u32[]{:S(2)}, u32[]{:S(2)}) %collective-permute-start.3) | collective-permute-done | bytes 184352 | tf_op jit(solution)/shard_map/ppermute | solution.py:257
  22.4 0.0 collective-permute-done.2.b_ref
  22.4 0.0 collective-permute-done.6.after2.ref
  22.4 0.4 merge_codes.1
  22.8 2.5 %collective-permute-start.16 = (bf16[160,1152]{1,0:T(8,128)(2,1)S(1)}, bf16[160,1152]{1,0:T(8,128)(2,1)S(1)}, u32[]{:S(2)}, u32[]{:S(2)}) collective-permute-start(bf16[160,1152]{1,0:T(8,128)(2,1)S(1)} %get-tuple-element.34.m0), channel_id=1, source_target_pairs={{0,8},{32,34},{1,9},{33,35},{2,10},{34,32},{3,11},{35,33},{4,12},{... | collective-permute-start | bytes 1105928 | tf_op jit(solution)/shard_map/ppermute | solution.py:263
  25.4 0.3 collective-permute-start.15
  25.7 2.4 %collective-permute-start.14 = (bf16[160,1152]{1,0:T(8,128)(2,1)S(1)}, bf16[160,1152]{1,0:T(8,128)(2,1)S(1)}, u32[]{:S(2)}, u32[]{:S(2)}) collective-permute-start(bf16[160,1152]{1,0:T(8,128)(2,1)S(1)} %get-tuple-element.34.m0), channel_id=1, source_target_pairs={{0,12},{32,35},{1,13},{33,32},{2,14},{34,33},{3,15},{35,34},{4,0},... | collective-permute-start | bytes 1105928 | tf_op jit(solution)/shard_map/ppermute | solution.py:263
  28.0 0.0 collective-permute-start.9
  28.1 0.6 collective-permute-start.8
  28.6 2.5 %collective-permute-done.16.m3 = bf16[160,1152]{1,0:T(8,128)(2,1)S(1)} collective-permute-done((bf16[160,1152]{1,0:T(8,128)(2,1)S(1)}, bf16[160,1152]{1,0:T(8,128)(2,1)S(1)}, u32[]{:S(2)}, u32[]{:S(2)}) %collective-permute-start.16) | collective-permute-done | bytes 368672 | tf_op jit(solution)/shard_map/ppermute | solution.py:263
  31.1 2.2 %collective-permute-start.7 = (bf16[160,1152]{1,0:T(8,128)(2,1)S(1)}, bf16[160,1152]{1,0:T(8,128)(2,1)S(1)}, u32[]{:S(2)}, u32[]{:S(2)}) collective-permute-start(bf16[160,1152]{1,0:T(8,128)(2,1)S(1)} %get-tuple-element.27.m0.after), channel_id=1, source_target_pairs={{0,12},{32,35},{1,13},{33,32},{2,14},{34,33},{3,15},{35,34},{4,0},... | collective-permute-start | bytes 1105928 | tf_op jit(solution)/shard_map/ppermute | solution.py:263
  33.3 1.8 %collective-permute-done.15.m2 = bf16[160,1152]{1,0:T(8,128)(2,1)S(1)} collective-permute-done((bf16[160,1152]{1,0:T(8,128)(2,1)S(1)}, bf16[160,1152]{1,0:T(8,128)(2,1)S(1)}, u32[]{:S(2)}, u32[]{:S(2)}) %collective-permute-start.15) | collective-permute-done | bytes 368672 | tf_op jit(solution)/shard_map/ppermute | solution.py:263
  35.0 2.3 %project_in.3 = (f32[160,1152]{1,0:T(8,128)S(1)}, f32[168,1152]{1,0:T(8,128)S(1)}) custom-call(bf16[160,1152]{1,0:T(8,128)(2,1)S(1)} %get-tuple-element.34.m0, bf16[160,1152]{1,0:T(8,128)(2,1)S(1)} %collective-permute-done.14.m1, bf16[160,1152]{1,0:T(8,128)(2,1)S(1)} %collective-permute-done.15.m2, bf16[160,1152]{1,0:T(8,128)(2,1)S(1)} %collective-permute-done.16.m3, ...), custom_call_target="tpu_custom_call" | custom-call | flops 1698693120 | bytes 10616832 | tf_op jit(solution)/shard_map/project_in/pallas_call | solution.py:267
  37.4 1.6 %collective-permute-start.17 = (f16[168,1152]{1,0:T(8,128)(2,1)S(1)}, f16[168,1152]{1,0:T(8,128)(2,1)S(1)}, u32[]{:S(2)}, u32[]{:S(2)}) collective-permute-start(f16[168,1152]{1,0:T(8,128)(2,1)S(1)} %convert_element_type.40), channel_id=1, source_target_pairs={{0,64},{64,0},{1,65},{65,1},{2,66},{66,2},{3,67},{67,3},{4,68},{68... | collective-permute-start | bytes 1161224 | tf_op jit(solution)/shard_map/ppermute | solution.py:278
  38.9 2.5 %stage_own.1.half_ref = bf16[1152,4608]{1,0:T(8,128)(2,1)S(1)} custom-call(bf16[1152,2304]{1,0:T(8,128)(2,1)} %ref.3, bf16[160,1152]{1,0:T(8,128)(2,1)S(1)} %get-tuple-element.27.m0.after), custom_call_target="tpu_custom_call" | custom-call | bytes 10616832 | tf_op jit(solution)/shard_map/stage_own/pallas_call | solution.py:279
  41.5 0.4 stage_other.1.w_ref
  41.9 0.0 collective-permute-done.9.m3
  41.9 1.0 %collective-permute-done.8.m2 = bf16[160,1152]{1,0:T(8,128)(2,1)S(1)} collective-permute-done((bf16[160,1152]{1,0:T(8,128)(2,1)S(1)}, bf16[160,1152]{1,0:T(8,128)(2,1)S(1)}, u32[]{:S(2)}, u32[]{:S(2)}) %collective-permute-start.8) | collective-permute-done | bytes 368672 | tf_op jit(solution)/shard_map/ppermute | solution.py:263
  42.9 2.3 %project_in.2 = (f32[160,1152]{1,0:T(8,128)S(1)}, f32[168,1152]{1,0:T(8,128)S(1)}) custom-call(bf16[160,1152]{1,0:T(8,128)(2,1)S(1)} %get-tuple-element.27.m0.after, bf16[160,1152]{1,0:T(8,128)(2,1)S(1)} %collective-permute-done.7.m1, bf16[160,1152]{1,0:T(8,128)(2,1)S(1)} %collective-permute-done.8.m2, bf16[160,1152]{1,0:T(8,128)(2,1)S(1)} %collective-permute-done.9.m3, ...), custom_call_target="tpu_custom_call" | custom-call | flops 1698693120 | bytes 10616832 | tf_op jit(solution)/shard_map/project_in/pallas_call | solution.py:267
  45.3 1.7 %collective-permute-start.10 = (f16[168,1152]{1,0:T(8,128)(2,1)S(1)}, f16[168,1152]{1,0:T(8,128)(2,1)S(1)}, u32[]{:S(2)}, u32[]{:S(2)}) collective-permute-start(f16[168,1152]{1,0:T(8,128)(2,1)S(1)} %convert_element_type.36), channel_id=1, source_target_pairs={{0,64},{64,0},{1,65},{65,1},{2,66},{66,2},{3,67},{67,3},{4,68},{68... | collective-permute-start | bytes 1161224 | tf_op jit(solution)/shard_map/ppermute | solution.py:278
  47.0 0.0 collective-permute-done.17
  47.1 0.3 fusion.15.a_ref
  47.4 2.5 %project_out.3 = (f32[4,360,128]{2,1,0:T(8,128)S(1)}, bf16[4,360,128]{2,1,0:T(8,128)(2,1)S(1)}, bf16[4,360,128]{2,1,0:T(8,128)(2,1)S(1)}, bf16[4,360,128]{2,1,0:T(8,128)(2,1)S(1)}) custom-call(bf16[160,1152]{1,0:T(8,128)(2,1)S(1)} %fusion.15.a_ref, bf16[1152,4608]{1,0:T(8,128)(2,1)S(1)} %stage_other.1.w_ref), custom_call_target="tpu_custom_call" | custom-call | flops 1698693120 | bytes 10616832 | tf_op jit(solution)/shard_map/project_out/pallas_call | solution.py:289
  49.9 1.7 %collective-permute-start.18 = (bf16[4,360,128]{2,1,0:T(8,128)(2,1)S(1)}, bf16[4,360,128]{2,1,0:T(8,128)(2,1)S(1)}, u32[]{:S(2)}, u32[]{:S(2)}) collective-permute-start(bf16[4,360,128]{2,1,0:T(8,128)(2,1)S(1)} %get-tuple-element.38), channel_id=1, source_target_pairs={{0,2},{32,40},{1,3},{33,41},{2,0},{34,42},{3,1},{35,43},{4,6},{36,... | collective-permute-start | bytes 1105928 | tf_op jit(solution)/shard_map/ppermute | solution.py:299
  51.6 1.5 %collective-permute-start.19 = (bf16[4,360,128]{2,1,0:T(8,128)(2,1)S(1)}, bf16[4,360,128]{2,1,0:T(8,128)(2,1)S(1)}, u32[]{:S(2)}, u32[]{:S(2)}) collective-permute-start(bf16[4,360,128]{2,1,0:T(8,128)(2,1)S(1)} %get-tuple-element.39), channel_id=1, source_target_pairs={{0,1},{32,36},{1,2},{33,37},{2,3},{34,38},{3,0},{35,39},{4,5},{36,... | collective-permute-start | bytes 1105928 | tf_op jit(solution)/shard_map/ppermute | solution.py:299
  53.1 1.2 %collective-permute-start.20 = (bf16[4,360,128]{2,1,0:T(8,128)(2,1)S(1)}, bf16[4,360,128]{2,1,0:T(8,128)(2,1)S(1)}, u32[]{:S(2)}, u32[]{:S(2)}) collective-permute-start(bf16[4,360,128]{2,1,0:T(8,128)(2,1)S(1)} %get-tuple-element.40), channel_id=1, source_target_pairs={{0,3},{32,44},{1,0},{33,45},{2,1},{34,46},{3,2},{35,47},{4,7},{36,... | collective-permute-start | bytes 1105928 | tf_op jit(solution)/shard_map/ppermute | solution.py:299
  54.3 0.3 collective-permute-done.10
  54.7 0.3 fusion.7.a_ref
  55.0 2.5 %project_out.2 = (f32[4,360,128]{2,1,0:T(8,128)S(1)}, bf16[4,360,128]{2,1,0:T(8,128)(2,1)S(1)}, bf16[4,360,128]{2,1,0:T(8,128)(2,1)S(1)}, bf16[4,360,128]{2,1,0:T(8,128)(2,1)S(1)}) custom-call(bf16[160,1152]{1,0:T(8,128)(2,1)S(1)} %fusion.7.a_ref, bf16[1152,4608]{1,0:T(8,128)(2,1)S(1)} %stage_other.1.w_ref), custom_call_target="tpu_custom_call" | custom-call | flops 1698693120 | bytes 10616832 | tf_op jit(solution)/shard_map/project_out/pallas_call | solution.py:289
  57.5 1.5 %collective-permute-start.11 = (bf16[4,360,128]{2,1,0:T(8,128)(2,1)S(1)}, bf16[4,360,128]{2,1,0:T(8,128)(2,1)S(1)}, u32[]{:S(2)}, u32[]{:S(2)}) collective-permute-start(bf16[4,360,128]{2,1,0:T(8,128)(2,1)S(1)} %get-tuple-element.31), channel_id=1, source_target_pairs={{0,2},{32,40},{1,3},{33,41},{2,0},{34,42},{3,1},{35,43},{4,6},{36,... | collective-permute-start | bytes 1105928 | tf_op jit(solution)/shard_map/ppermute | solution.py:299
  59.0 2.2 %collective-permute-start.12 = (bf16[4,360,128]{2,1,0:T(8,128)(2,1)S(1)}, bf16[4,360,128]{2,1,0:T(8,128)(2,1)S(1)}, u32[]{:S(2)}, u32[]{:S(2)}) collective-permute-start(bf16[4,360,128]{2,1,0:T(8,128)(2,1)S(1)} %get-tuple-element.32), channel_id=1, source_target_pairs={{0,1},{32,36},{1,2},{33,37},{2,3},{34,38},{3,0},{35,39},{4,5},{36,... | collective-permute-start | bytes 1105928 | tf_op jit(solution)/shard_map/ppermute | solution.py:299
  61.2 0.0 collective-permute-done.18.b1
  61.2 0.5 collective-permute-start.13
  61.7 0.4 collective-permute-done.19.c1
  62.1 0.2 collective-permute-done.20.d1
  62.3 3.6 %collective-permute-done.11.b0 = bf16[4,360,128]{2,1,0:T(8,128)(2,1)S(1)} collective-permute-done((bf16[4,360,128]{2,1,0:T(8,128)(2,1)S(1)}, bf16[4,360,128]{2,1,0:T(8,128)(2,1)S(1)}, u32[]{:S(2)}, u32[]{:S(2)}) %collective-permute-start.11) | collective-permute-done | bytes 368672 | tf_op jit(solution)/shard_map/ppermute | solution.py:299
  65.9 4.1 %collective-permute-done.12.c0 = bf16[4,360,128]{2,1,0:T(8,128)(2,1)S(1)} collective-permute-done((bf16[4,360,128]{2,1,0:T(8,128)(2,1)S(1)}, bf16[4,360,128]{2,1,0:T(8,128)(2,1)S(1)}, u32[]{:S(2)}, u32[]{:S(2)}) %collective-permute-start.12) | collective-permute-done | bytes 368672 | tf_op jit(solution)/shard_map/ppermute | solution.py:299
  70.1 0.3 collective-permute-done.13.d0
  70.4 0.4 add_first.1
  70.7 2.1 %collective-permute-start.21 = (bf16[720,128]{1,0:T(8,128)(2,1)S(1)}, bf16[720,128]{1,0:T(8,128)(2,1)S(1)}, u32[]{:S(2)}, u32[]{:S(2)}) collective-permute-start(bf16[720,128]{1,0:T(8,128)(2,1)S(1)} %get-tuple-element.42), channel_id=1, source_target_pairs={{0,8},{32,34},{1,9},{33,35},{2,10},{34,32},{3,11},{35,33},{4,12},{... | collective-permute-start | bytes 552968 | tf_op jit(solution)/shard_map/ppermute | solution.py:302
  72.8 0.8 collective-permute-start.22
  73.6 1.9 %collective-permute-start.23 = (bf16[720,128]{1,0:T(8,128)(2,1)S(1)}, bf16[720,128]{1,0:T(8,128)(2,1)S(1)}, u32[]{:S(2)}, u32[]{:S(2)}) collective-permute-start(bf16[720,128]{1,0:T(8,128)(2,1)S(1)} %get-tuple-element.44), channel_id=1, source_target_pairs={{0,12},{32,35},{1,13},{33,32},{2,14},{34,33},{3,15},{35,34},{4,0},... | collective-permute-start | bytes 552968 | tf_op jit(solution)/shard_map/ppermute | solution.py:302
  75.5 1.3 %collective-permute-done.21.b = bf16[720,128]{1,0:T(8,128)(2,1)S(1)} collective-permute-done((bf16[720,128]{1,0:T(8,128)(2,1)S(1)}, bf16[720,128]{1,0:T(8,128)(2,1)S(1)}, u32[]{:S(2)}, u32[]{:S(2)}) %collective-permute-start.21) | collective-permute-done | bytes 184352 | tf_op jit(solution)/shard_map/ppermute | solution.py:302
  76.7 1.9 %collective-permute-done.22.c = bf16[720,128]{1,0:T(8,128)(2,1)S(1)} collective-permute-done((bf16[720,128]{1,0:T(8,128)(2,1)S(1)}, bf16[720,128]{1,0:T(8,128)(2,1)S(1)}, u32[]{:S(2)}, u32[]{:S(2)}) %collective-permute-start.22) | collective-permute-done | bytes 184352 | tf_op jit(solution)/shard_map/ppermute | solution.py:302
  78.7 0.3 add_second.1
  79.0 6.6 %collective-permute-start.25 = (f32[216,128]{1,0:T(8,128)S(1)}, f32[216,128]{1,0:T(8,128)S(1)}, u32[]{:S(2)}, u32[]{:S(2)}) collective-permute-start(f32[216,128]{1,0:T(8,128)S(1)} %get-tuple-element.47), channel_id=1, source_target_pairs={{0,32},{32,0},{1,33},{33,1},{2,34},{34,2},{3,35},{35,3},{4,36},{36... | collective-permute-start | bytes 331784 | tf_op jit(solution)/shard_map/ppermute | solution.py:307
  85.6 3.4 %collective-permute-start.26 = (f16[224,128]{1,0:T(8,128)(2,1)S(1)}, f16[224,128]{1,0:T(8,128)(2,1)S(1)}, u32[]{:S(2)}, u32[]{:S(2)}) collective-permute-start(f16[224,128]{1,0:T(8,128)(2,1)S(1)} %convert_element_type.46), channel_id=1, source_target_pairs={{0,48},{16,32},{32,16},{48,0},{1,49},{17,33},{33,17},{49,1},{2,50}... | collective-permute-start | bytes 172040 | tf_op jit(solution)/shard_map/ppermute | solution.py:306
  88.9 0.2 collective-permute-start.24
  89.1 2.2 %collective-permute-done.26 = f16[224,128]{1,0:T(8,128)(2,1)S(1)} collective-permute-done((f16[224,128]{1,0:T(8,128)(2,1)S(1)}, f16[224,128]{1,0:T(8,128)(2,1)S(1)}, u32[]{:S(2)}, u32[]{:S(2)}) %collective-permute-start.26) | collective-permute-done | bytes 57376 | tf_op jit(solution)/shard_map/ppermute | solution.py:306
  91.3 0.7 collective-permute-done.24
  92.1 0.2 finish.1
  92.3 0.8 copy.7
  (15 shorter events, 0.2 us)
Async XLA Ops:
  0.0 19.2 %collective-permute-start.5 = (bf16[2304,1152]{1,0:T(8,128)(2,1)}, bf16[2304,1152]{1,0:T(8,128)(2,1)S(1)}, u32[]{:S(2)}, u32[]{:S(2)}) collective-permute-start(bf16[2304,1152]{1,0:T(8,128)(2,1)} %ref.2), channel_id=1, source_target_pairs={{0,32},{32,0},{1,33},{33,1},{2,34},{34,2},{3,35},{35,3},{4,36},{36... | collective-permute-start | bytes 15925256 | tf_op jit(solution)/shard_map/ppermute | solution.py:241
  1.4 21.0 %collective-permute-start.6 = (bf16[1152,2304]{1,0:T(8,128)(2,1)}, bf16[1152,2304]{1,0:T(8,128)(2,1)S(1)}, u32[]{:S(2)}, u32[]{:S(2)}) collective-permute-start(bf16[1152,2304]{1,0:T(8,128)(2,1)} %ref.3), channel_id=1, source_target_pairs={{0,32},{32,0},{1,33},{33,1},{2,34},{34,2},{3,35},{35,3},{4,36},{36... | collective-permute-start | bytes 15925256 | tf_op jit(solution)/shard_map/ppermute | solution.py:242
  2.7 10.8 %collective-permute-start.1 = (bf16[360,128]{1,0:T(8,128)(2,1)S(1)}, bf16[360,128]{1,0:T(8,128)(2,1)S(1)}, u32[]{:S(2)}, u32[]{:S(2)}) collective-permute-start(bf16[360,128]{1,0:T(8,128)(2,1)S(1)} %pack_codes.1), channel_id=1, source_target_pairs={{64,16},{80,64},{16,80},{0,0},{65,17},{81,65},{17,81},{1,1},{66,18... | collective-permute-start | bytes 276488 | tf_op jit(solution)/shard_map/ppermute | solution.py:253
  3.4 10.1 %collective-permute-start = (bf16[360,128]{1,0:T(8,128)(2,1)S(1)}, bf16[360,128]{1,0:T(8,128)(2,1)S(1)}, u32[]{:S(2)}, u32[]{:S(2)}) collective-permute-start(bf16[360,128]{1,0:T(8,128)(2,1)S(1)} %pack_codes.1), channel_id=1, source_target_pairs={{0,16},{16,64},{64,0},{80,80},{1,17},{17,65},{65,1},{81,81},{2,18}... | collective-permute-start | bytes 276488 | tf_op jit(solution)/shard_map/ppermute | solution.py:252
  13.6 7.6 %collective-permute-start.4 = (bf16[2,360,128]{2,1,0:T(8,128)(2,1)S(1)}, bf16[2,360,128]{2,1,0:T(8,128)(2,1)S(1)}, u32[]{:S(2)}, u32[]{:S(2)}) collective-permute-start(bf16[2,360,128]{2,1,0:T(8,128)(2,1)S(1)} %order_quarters.1.a_ref), channel_id=1, source_target_pairs={{0,2},{32,40},{1,3},{33,41},{2,0},{34,42},{3,1},{35,43},{4,6},{36,... | collective-permute-start | bytes 552968 | tf_op jit(solution)/shard_map/ppermute | solution.py:257
  16.5 5.9 %collective-permute-start.3 = (bf16[2,360,128]{2,1,0:T(8,128)(2,1)S(1)}, bf16[2,360,128]{2,1,0:T(8,128)(2,1)S(1)}, u32[]{:S(2)}, u32[]{:S(2)}) collective-permute-start(bf16[2,360,128]{2,1,0:T(8,128)(2,1)S(1)} %order_quarters.1.a_ref), channel_id=1, source_target_pairs={{0,1},{32,36},{1,2},{33,37},{2,3},{34,38},{3,0},{35,39},{4,5},{36,... | collective-permute-start | bytes 552968 | tf_op jit(solution)/shard_map/ppermute | solution.py:257
  16.9 5.5 %collective-permute-start.2 = (bf16[2,360,128]{2,1,0:T(8,128)(2,1)S(1)}, bf16[2,360,128]{2,1,0:T(8,128)(2,1)S(1)}, u32[]{:S(2)}, u32[]{:S(2)}) collective-permute-start(bf16[2,360,128]{2,1,0:T(8,128)(2,1)S(1)} %order_quarters.1.a_ref), channel_id=1, source_target_pairs={{0,3},{32,44},{1,0},{33,45},{2,1},{34,46},{3,2},{35,47},{4,7},{36,... | collective-permute-start | bytes 552968 | tf_op jit(solution)/shard_map/ppermute | solution.py:257
  22.8 8.3 %collective-permute-start.16 = (bf16[160,1152]{1,0:T(8,128)(2,1)S(1)}, bf16[160,1152]{1,0:T(8,128)(2,1)S(1)}, u32[]{:S(2)}, u32[]{:S(2)}) collective-permute-start(bf16[160,1152]{1,0:T(8,128)(2,1)S(1)} %get-tuple-element.34.m0), channel_id=1, source_target_pairs={{0,8},{32,34},{1,9},{33,35},{2,10},{34,32},{3,11},{35,33},{4,12},{... | collective-permute-start | bytes 1105928 | tf_op jit(solution)/shard_map/ppermute | solution.py:263
  25.4 9.7 %collective-permute-start.15 = (bf16[160,1152]{1,0:T(8,128)(2,1)S(1)}, bf16[160,1152]{1,0:T(8,128)(2,1)S(1)}, u32[]{:S(2)}, u32[]{:S(2)}) collective-permute-start(bf16[160,1152]{1,0:T(8,128)(2,1)S(1)} %get-tuple-element.34.m0), channel_id=1, source_target_pairs={{0,4},{32,33},{1,5},{33,34},{2,6},{34,35},{3,7},{35,32},{4,8},{36,... | collective-permute-start | bytes 1105928 | tf_op jit(solution)/shard_map/ppermute | solution.py:263
  25.7 9.4 %collective-permute-start.14 = (bf16[160,1152]{1,0:T(8,128)(2,1)S(1)}, bf16[160,1152]{1,0:T(8,128)(2,1)S(1)}, u32[]{:S(2)}, u32[]{:S(2)}) collective-permute-start(bf16[160,1152]{1,0:T(8,128)(2,1)S(1)} %get-tuple-element.34.m0), channel_id=1, source_target_pairs={{0,12},{32,35},{1,13},{33,32},{2,14},{34,33},{3,15},{35,34},{4,0},... | collective-permute-start | bytes 1105928 | tf_op jit(solution)/shard_map/ppermute | solution.py:263
  28.0 13.9 %collective-permute-start.9 = (bf16[160,1152]{1,0:T(8,128)(2,1)S(1)}, bf16[160,1152]{1,0:T(8,128)(2,1)S(1)}, u32[]{:S(2)}, u32[]{:S(2)}) collective-permute-start(bf16[160,1152]{1,0:T(8,128)(2,1)S(1)} %get-tuple-element.27.m0.after), channel_id=1, source_target_pairs={{0,8},{32,34},{1,9},{33,35},{2,10},{34,32},{3,11},{35,33},{4,12},{... | collective-permute-start | bytes 1105928 | tf_op jit(solution)/shard_map/ppermute | solution.py:263
  28.1 14.9 %collective-permute-start.8 = (bf16[160,1152]{1,0:T(8,128)(2,1)S(1)}, bf16[160,1152]{1,0:T(8,128)(2,1)S(1)}, u32[]{:S(2)}, u32[]{:S(2)}) collective-permute-start(bf16[160,1152]{1,0:T(8,128)(2,1)S(1)} %get-tuple-element.27.m0.after), channel_id=1, source_target_pairs={{0,4},{32,33},{1,5},{33,34},{2,6},{34,35},{3,7},{35,32},{4,8},{36,... | collective-permute-start | bytes 1105928 | tf_op jit(solution)/shard_map/ppermute | solution.py:263
  31.1 11.8 %collective-permute-start.7 = (bf16[160,1152]{1,0:T(8,128)(2,1)S(1)}, bf16[160,1152]{1,0:T(8,128)(2,1)S(1)}, u32[]{:S(2)}, u32[]{:S(2)}) collective-permute-start(bf16[160,1152]{1,0:T(8,128)(2,1)S(1)} %get-tuple-element.27.m0.after), channel_id=1, source_target_pairs={{0,12},{32,35},{1,13},{33,32},{2,14},{34,33},{3,15},{35,34},{4,0},... | collective-permute-start | bytes 1105928 | tf_op jit(solution)/shard_map/ppermute | solution.py:263
  37.4 9.7 %collective-permute-start.17 = (f16[168,1152]{1,0:T(8,128)(2,1)S(1)}, f16[168,1152]{1,0:T(8,128)(2,1)S(1)}, u32[]{:S(2)}, u32[]{:S(2)}) collective-permute-start(f16[168,1152]{1,0:T(8,128)(2,1)S(1)} %convert_element_type.40), channel_id=1, source_target_pairs={{0,64},{64,0},{1,65},{65,1},{2,66},{66,2},{3,67},{67,3},{4,68},{68... | collective-permute-start | bytes 1161224 | tf_op jit(solution)/shard_map/ppermute | solution.py:278
  45.3 9.3 %collective-permute-start.10 = (f16[168,1152]{1,0:T(8,128)(2,1)S(1)}, f16[168,1152]{1,0:T(8,128)(2,1)S(1)}, u32[]{:S(2)}, u32[]{:S(2)}) collective-permute-start(f16[168,1152]{1,0:T(8,128)(2,1)S(1)} %convert_element_type.36), channel_id=1, source_target_pairs={{0,64},{64,0},{1,65},{65,1},{2,66},{66,2},{3,67},{67,3},{4,68},{68... | collective-permute-start | bytes 1161224 | tf_op jit(solution)/shard_map/ppermute | solution.py:278
  49.9 11.3 %collective-permute-start.18 = (bf16[4,360,128]{2,1,0:T(8,128)(2,1)S(1)}, bf16[4,360,128]{2,1,0:T(8,128)(2,1)S(1)}, u32[]{:S(2)}, u32[]{:S(2)}) collective-permute-start(bf16[4,360,128]{2,1,0:T(8,128)(2,1)S(1)} %get-tuple-element.38), channel_id=1, source_target_pairs={{0,2},{32,40},{1,3},{33,41},{2,0},{34,42},{3,1},{35,43},{4,6},{36,... | collective-permute-start | bytes 1105928 | tf_op jit(solution)/shard_map/ppermute | solution.py:299
  51.6 10.5 %collective-permute-start.19 = (bf16[4,360,128]{2,1,0:T(8,128)(2,1)S(1)}, bf16[4,360,128]{2,1,0:T(8,128)(2,1)S(1)}, u32[]{:S(2)}, u32[]{:S(2)}) collective-permute-start(bf16[4,360,128]{2,1,0:T(8,128)(2,1)S(1)} %get-tuple-element.39), channel_id=1, source_target_pairs={{0,1},{32,36},{1,2},{33,37},{2,3},{34,38},{3,0},{35,39},{4,5},{36,... | collective-permute-start | bytes 1105928 | tf_op jit(solution)/shard_map/ppermute | solution.py:299
  53.1 9.2 %collective-permute-start.20 = (bf16[4,360,128]{2,1,0:T(8,128)(2,1)S(1)}, bf16[4,360,128]{2,1,0:T(8,128)(2,1)S(1)}, u32[]{:S(2)}, u32[]{:S(2)}) collective-permute-start(bf16[4,360,128]{2,1,0:T(8,128)(2,1)S(1)} %get-tuple-element.40), channel_id=1, source_target_pairs={{0,3},{32,44},{1,0},{33,45},{2,1},{34,46},{3,2},{35,47},{4,7},{36,... | collective-permute-start | bytes 1105928 | tf_op jit(solution)/shard_map/ppermute | solution.py:299
  57.5 8.4 %collective-permute-start.11 = (bf16[4,360,128]{2,1,0:T(8,128)(2,1)S(1)}, bf16[4,360,128]{2,1,0:T(8,128)(2,1)S(1)}, u32[]{:S(2)}, u32[]{:S(2)}) collective-permute-start(bf16[4,360,128]{2,1,0:T(8,128)(2,1)S(1)} %get-tuple-element.31), channel_id=1, source_target_pairs={{0,2},{32,40},{1,3},{33,41},{2,0},{34,42},{3,1},{35,43},{4,6},{36,... | collective-permute-start | bytes 1105928 | tf_op jit(solution)/shard_map/ppermute | solution.py:299
  59.0 11.1 %collective-permute-start.12 = (bf16[4,360,128]{2,1,0:T(8,128)(2,1)S(1)}, bf16[4,360,128]{2,1,0:T(8,128)(2,1)S(1)}, u32[]{:S(2)}, u32[]{:S(2)}) collective-permute-start(bf16[4,360,128]{2,1,0:T(8,128)(2,1)S(1)} %get-tuple-element.32), channel_id=1, source_target_pairs={{0,1},{32,36},{1,2},{33,37},{2,3},{34,38},{3,0},{35,39},{4,5},{36,... | collective-permute-start | bytes 1105928 | tf_op jit(solution)/shard_map/ppermute | solution.py:299
  61.2 9.2 %collective-permute-start.13 = (bf16[4,360,128]{2,1,0:T(8,128)(2,1)S(1)}, bf16[4,360,128]{2,1,0:T(8,128)(2,1)S(1)}, u32[]{:S(2)}, u32[]{:S(2)}) collective-permute-start(bf16[4,360,128]{2,1,0:T(8,128)(2,1)S(1)} %get-tuple-element.33), channel_id=1, source_target_pairs={{0,3},{32,44},{1,0},{33,45},{2,1},{34,46},{3,2},{35,47},{4,7},{36,... | collective-permute-start | bytes 1105928 | tf_op jit(solution)/shard_map/ppermute | solution.py:299
  70.7 6.0 %collective-permute-start.21 = (bf16[720,128]{1,0:T(8,128)(2,1)S(1)}, bf16[720,128]{1,0:T(8,128)(2,1)S(1)}, u32[]{:S(2)}, u32[]{:S(2)}) collective-permute-start(bf16[720,128]{1,0:T(8,128)(2,1)S(1)} %get-tuple-element.42), channel_id=1, source_target_pairs={{0,8},{32,34},{1,9},{33,35},{2,10},{34,32},{3,11},{35,33},{4,12},{... | collective-permute-start | bytes 552968 | tf_op jit(solution)/shard_map/ppermute | solution.py:302
  72.8 5.9 %collective-permute-start.22 = (bf16[720,128]{1,0:T(8,128)(2,1)S(1)}, bf16[720,128]{1,0:T(8,128)(2,1)S(1)}, u32[]{:S(2)}, u32[]{:S(2)}) collective-permute-start(bf16[720,128]{1,0:T(8,128)(2,1)S(1)} %get-tuple-element.43), channel_id=1, source_target_pairs={{0,4},{32,33},{1,5},{33,34},{2,6},{34,35},{3,7},{35,32},{4,8},{36,... | collective-permute-start | bytes 552968 | tf_op jit(solution)/shard_map/ppermute | solution.py:302
  73.6 5.1 %collective-permute-start.23 = (bf16[720,128]{1,0:T(8,128)(2,1)S(1)}, bf16[720,128]{1,0:T(8,128)(2,1)S(1)}, u32[]{:S(2)}, u32[]{:S(2)}) collective-permute-start(bf16[720,128]{1,0:T(8,128)(2,1)S(1)} %get-tuple-element.44), channel_id=1, source_target_pairs={{0,12},{32,35},{1,13},{33,32},{2,14},{34,33},{3,15},{35,34},{4,0},... | collective-permute-start | bytes 552968 | tf_op jit(solution)/shard_map/ppermute | solution.py:302
  79.0 13.1 %collective-permute-start.25 = (f32[216,128]{1,0:T(8,128)S(1)}, f32[216,128]{1,0:T(8,128)S(1)}, u32[]{:S(2)}, u32[]{:S(2)}) collective-permute-start(f32[216,128]{1,0:T(8,128)S(1)} %get-tuple-element.47), channel_id=1, source_target_pairs={{0,32},{32,0},{1,33},{33,1},{2,34},{34,2},{3,35},{35,3},{4,36},{36... | collective-permute-start | bytes 331784 | tf_op jit(solution)/shard_map/ppermute | solution.py:307
  85.6 5.7 %collective-permute-start.26 = (f16[224,128]{1,0:T(8,128)(2,1)S(1)}, f16[224,128]{1,0:T(8,128)(2,1)S(1)}, u32[]{:S(2)}, u32[]{:S(2)}) collective-permute-start(f16[224,128]{1,0:T(8,128)(2,1)S(1)} %convert_element_type.46), channel_id=1, source_target_pairs={{0,48},{16,32},{32,16},{48,0},{1,49},{17,33},{33,17},{49,1},{2,50}... | collective-permute-start | bytes 172040 | tf_op jit(solution)/shard_map/ppermute | solution.py:306
  88.9 3.1 %collective-permute-start.24 = (f16[224,128]{1,0:T(8,128)(2,1)S(1)}, f16[224,128]{1,0:T(8,128)(2,1)S(1)}, u32[]{:S(2)}, u32[]{:S(2)}) collective-permute-start(f16[224,128]{1,0:T(8,128)(2,1)S(1)} %convert_element_type.44), channel_id=1, source_target_pairs={{0,16},{16,0},{1,17},{17,1},{2,18},{18,2},{3,19},{19,3},{4,20},{20... | collective-permute-start | bytes 172040 | tf_op jit(solution)/shard_map/ppermute | solution.py:305

commit v5 on v4

--- a/solution.py
+++ b/solution.py
@@ -15,6 +15,7 @@
 YX = ("c", "y", "x")
 STEPS = (0, 2, 1, 3)
 GATHER = (0, 3, 1, 2)
+ARRIVES = (0, 2, 3, 1)
 
 
 def first_axis(step):
@@ -35,12 +36,12 @@
     return pairs
 
 
-def call(kernel, outs, ins, scratch=(), flops=0, nbytes=0, vmem=8, alias={}, name=None):
+def call(kernel, outs, ins, scratch=(), flops=0, nbytes=0, vmem=8, alias={}, out_specs=None, name=None):
     return pl.pallas_call(
         kernel,
         out_shape=outs,
         in_specs=ins,
-        out_specs=jax.tree.map(lambda _: VMEM, outs),
+        out_specs=out_specs or jax.tree.map(lambda _: VMEM, outs),
         input_output_aliases=alias,
         scratch_shapes=list(scratch),
         compiler_params=pltpu.CompilerParams(vmem_limit_bytes=vmem * 2**20),
@@ -111,7 +112,7 @@
 def arrange_rows(own, ref, w_ref, sem):
     c, first, second = own_place()
     for i in range(4):
-        s = lax.rem(second + 4 - GATHER[i], 4)
+        s = lax.rem(second + 4 - ARRIVES[i], 4)
         for j in range(4):
             f = lax.rem(first + 4 - GATHER[j], 4)
             y, x = jnp.where(c == 0, s, f), jnp.where(c == 0, f, s)
@@ -156,12 +157,18 @@
     return x * jnp.exp2(power)[:1], power
 
 
-def project_in(m0, m1, m2, m3, w_ref, o_ref, send_ref, x_ref):
-    for i, m in enumerate((m0, m1, m2, m3)):
-        x_ref[:, i * UNITS : (i + 1) * UNITS] = m[...]
+def project_early(m0, m1, w_ref, o_ref):
     for n in range(0, UNITS, 256):
         to = min(n + 256, UNITS)
-        o_ref[:, n:to] = dot(x_ref[...], w_ref[:, n:to])
+        x = jnp.concatenate([m0[...], m1[...]], axis=1)
+        o_ref[:, n:to] = dot(x, w_ref[: 2 * UNITS, n:to])
+
+
+def project_in(m2, m3, w_ref, early_ref, o_ref, send_ref):
+    for n in range(0, UNITS, 256):
+        to = min(n + 256, UNITS)
+        x = jnp.concatenate([m2[...], m3[...]], axis=1)
+        o_ref[:, n:to] = early_ref[:, n:to] + dot(x, w_ref[2 * UNITS :, n:to])
     send_ref[0:QT], send_ref[QT:] = scaled(o_ref[...])
 
 
@@ -210,20 +217,23 @@
         lo, hi = (jnp.concatenate(share(crel, z), axis=0) for z in range(2))
         shares.append((jnp.where(zl == 0, lo, hi), jnp.where(zl == 0, hi, lo)))
     keep[...] = shares[0][0]
-    to_c[...] = shares[1][0]
-    for ref, (_, value) in zip((to_zl, to_czl), shares):
+    for ref, value in ((to_zl, shares[0][1]), (to_c, shares[1][0]), (to_czl, shares[1][1])):
         ref[0:216], ref[216:] = scaled(value)
 
 
-def finish(keep, from_zl, from_c, from_czl, o_ref):
+def finish(keep, from_c, from_czl, from_zl, out_ref, o_ref, sem):
     c = lax.axis_index("c")
-    for core, a, b in ((c, keep, from_zl), (1 - c, from_c, from_czl)):
-        total = a[...] + b[0:216] * jnp.exp2(-b[216:])[:1]
-        tail = total[144:].T
-        for q in range(2):
-            row = (2 * q + core) * QT
-            o_ref[pl.ds(pl.multiple_of(row, 8), 128)] = total[72 * q : 72 * q + 72].T
-            o_ref[pl.ds(pl.multiple_of(row + 128, 8), 32)] = tail[32 * q : 32 * q + 32]
+    whole = [ref[0:216] * jnp.exp2(-ref[216:])[:1] for ref in (from_zl, from_c, from_czl)]
+    own, other = keep[...] + whole[0], whole[1] + whole[2]
+    cores = jnp.where(c == 0, own, other), jnp.where(c == 0, other, own)
+    parts = []
+    for q in range(2):
+        for v in cores:
+            parts += [v[72 * q : 72 * q + 72], v[144:, 32 * q : 32 * q + 32]]
+    o_ref[...] = jnp.concatenate(parts, axis=1)
+    copy = pltpu.make_async_copy(o_ref, out_ref, sem)
+    copy.start()
+    copy.wait()
 
 
 def shape(dims, dtype):
@@ -264,15 +274,13 @@
 
     preacts, sends = [], []
     for q in range(2):
-        preact, send = call(
-            project_in,
-            [shape((QT, UNITS), F32), shape((QT + 8, UNITS), F32)],
-            [VMEM] * 5,
-            [pltpu.VMEM((QT, 4 * UNITS), BF)],
-            flops=2 * QT * 4608 * 1152,
-            nbytes=4608 * 1152 * 2,
-            name="project_in",
-        )(merged[q], *around[q], rows)
+        cost = dict(flops=QT * 4608 * 1152, nbytes=2304 * 1152 * 2)
+        early = call(project_early, shape((QT, UNITS), F32), [VMEM] * 3, name="project_early", **cost)(
+            merged[q], around[q][GATHER[1:].index(2)], rows
+        )
+        near = [v for k, v in zip(GATHER[1:], around[q]) if k != 2]
+        outs = [shape((QT, UNITS), F32), shape((QT + 8, UNITS), F32)]
+        preact, send = call(project_in, outs, [VMEM] * 4, name="project_in", **cost)(*near, rows, early)
         preacts.append(preact)
         sends.append(send.astype(jnp.float16))
     gots = [lax.ppermute(send, "zh", swap) for send in sends]
@@ -299,13 +307,17 @@
         scattered += [mine] + [lax.ppermute(v, YX, first_axis(k)) for k, v in zip(STEPS[1:], away)]
     part = (720, 128)
     mine, *away = call(add_first, [shape(part, F32)] + [shape(part, BF)] * 3, [VMEM] * 8, name="add_first")(*scattered)
-    away = [lax.ppermute(v, YX, second_axis(k)) for k, v in zip(STEPS[1:], away)]
-    plain, with_power = shape((216, 128), F32), shape((224, 128), F32)
-    keep, to_zl, to_c, to_czl = call(add_second, [plain, with_power] * 2, [VMEM] * 4, name="add_second")(mine, *away)
-    from_zl = lax.ppermute(to_zl.astype(jnp.float16), "zl", swap).astype(F32)
-    from_czl = lax.ppermute(to_czl.astype(jnp.float16), ("c", "zl"), [(0, 3), (1, 2), (2, 1), (3, 0)]).astype(F32)
+    around = [lax.ppermute(v, YX, second_axis(k)) for k, v in zip(STEPS[1:], away)]
+    away = [shape((224, 128), F32)] * 3
+    keep, *away = call(add_second, [shape((216, 128), F32)] + away, [VMEM] * 4, name="add_second")(mine, *around)
+    to_zl, to_c, to_czl = (v.astype(jnp.float16) for v in away)
     from_c = lax.ppermute(to_c, "c", swap)
-    return call(finish, shape((4 * QT, CHIP_COLS), F32), [VMEM] * 4, name="finish")(keep, from_zl, from_c, from_czl)
+    from_czl = lax.ppermute(to_czl, ("c", "zl"), [(0, 3), (1, 2), (2, 1), (3, 0)])
+    from_zl = lax.ppermute(to_zl, "zl", swap)
+    got = [v.astype(F32) for v in (from_c, from_czl, from_zl)]
+    whole = (CHIP_COLS, 4 * QT)
+    scratch = [pltpu.VMEM(whole, F32), pltpu.SemaphoreType.DMA]
+    return call(finish, pltpu.HBM(whole, F32), [VMEM] * 4, scratch, out_specs=ANY, name="finish")(keep, *got).T
 
 
 def solution(mesh):

time: 94.7 us -> 92.9 us (0.981)
  waiting for transfers between devices: 21.7 us -> 19.5 us
  Pallas kernels: 19.5 us -> 20.6 us
    ppermute x2, starting transfers between devices: 3.57 us -> 9.92 us  [the longest x1 7.93 us: shards(): lax.ppermute(to_czl, ('c', 'zl'), [(0, 3), (1, 2), (2, 1), (3, 0)])]
    ppermute x1, starting transfers between devices: 6.56 us -> 0.38 us  [shards(): from_c = lax.ppermute(to_c, 'c', swap)]
    ppermute x6, waiting for transfers between devices: 5.29 us -> 3.97 us  [shards(): lax.ppermute(m, YX, second_axis(k))]
    pallas_call x4 -> x6, Pallas kernels: 5.03 us -> 6.05 us  [the longest x2 2.68 us: shards(): call(project_in, outs, [VMEM] * 4, name='project_in', **cost)]
  transfers between devices with their start and end apart: 27 -> 27, of which waited for: 14 -> 13; matrix products, arithmetic and copies ran while one was open for 1% -> 1% of each run, Pallas kernels for 20% -> 20%
where the time goes in v5:
time: 92.9 us; the launch traced here: 91.4 us
  starting transfers between devices  50.1 us (54%)
  Pallas kernels  20.6 us (22%)
  waiting for transfers between devices  19.5 us (21%)
    ppermute x6, waiting for transfers between devices, shards(): lax.ppermute(v, YX, first_axis(k))  8.69 us
    ppermute x6, starting transfers between devices, shards(): lax.ppermute(v, YX, first_axis(k))  8.51 us
    ppermute x6, starting transfers between devices, shards(): lax.ppermute(m, YX, second_axis(k))  7.93 us
    ppermute x1, starting transfers between devices, shards(): lax.ppermute(to_czl, ('c', 'zl'), [(0, 3), (1, 2), (2, 1), (3, 0)])  7.93 us
    ppermute x1, starting transfers between devices, shards(): one = lax.ppermute(packed, z, [(0, 1), (1, 2), (2, 0), (3, 3)])  7.57 us
    ppermute x3, starting transfers between devices, shards(): around = [lax.ppermute(piece, YX, first_axis(k)) for k in GATHER[1:]]  5.65 us
    pallas_call x2, Pallas kernels, shards(): call(project_out, [shape(part, F32)] + [shape(part, BF)] * 3, [VMEM] * 2,...  5.08 us
    ppermute x3, starting transfers between devices, shards(): lax.ppermute(v, YX, second_axis(k))  4.75 us
  transfers between devices with their start and end apart: 27, of which 13 were waited for; matrix products, arithmetic and copies ran while one was open for 1% of the time, Pallas kernels for 20%

profile of v5, /device:TPU:1, one launch (start us, length us, event | category | flops | bytes accessed | tf_op | source)
XLA Modules:
  0.0 91.4 jit_solution(4286878478508883378)
XLA Ops:
  0.0 1.4 %collective-permute-start.5 = (bf16[2304,1152]{1,0:T(8,128)(2,1)}, bf16[2304,1152]{1,0:T(8,128)(2,1)S(1)}, u32[]{:S(2)}, u32[]{:S(2)}) collective-permute-start(bf16[2304,1152]{1,0:T(8,128)(2,1)} %ref.2), channel_id=1, source_target_pairs={{0,32},{32,0},{1,33},{33,1},{2,34},{34,2},{3,35},{35,3},{4,36},{36... | collective-permute-start | bytes 15925256 | tf_op jit(solution)/shard_map/ppermute | solution.py:251
  1.4 0.0 collective-permute-start.6
  1.4 1.3 %pack_codes.1 = bf16[360,128]{1,0:T(8,128)(2,1)S(1)} custom-call(bf16[160,288]{1,0:T(8,128)(2,1)} %codes_ref.1, s32[1,160]{1,0:T(1,128)} %bitcast.2), custom_call_target="tpu_custom_call" | custom-call | tf_op jit(solution)/shard_map/pack_codes/pallas_call | solution.py:255
  2.7 0.7 collective-permute-start.1
  3.4 7.6 %collective-permute-start = (bf16[360,128]{1,0:T(8,128)(2,1)S(1)}, bf16[360,128]{1,0:T(8,128)(2,1)S(1)}, u32[]{:S(2)}, u32[]{:S(2)}) collective-permute-start(bf16[360,128]{1,0:T(8,128)(2,1)S(1)} %pack_codes.1), channel_id=1, source_target_pairs={{0,16},{16,64},{64,0},{80,80},{1,17},{17,65},{65,1},{81,81},{2,18}... | collective-permute-start | bytes 276488 | tf_op jit(solution)/shard_map/ppermute | solution.py:262
  10.9 2.5 %arrange_own.1.after.half_ref = bf16[4608,1152]{1,0:T(8,128)(2,1)S(1)} custom-call(bf16[2304,1152]{1,0:T(8,128)(2,1)} %ref.2), custom_call_target="tpu_custom_call" | custom-call | bytes 10616832 | tf_op jit(solution)/shard_map/arrange_own/pallas_call | solution.py:265
  13.6 3.0 %collective-permute-start.4 = (bf16[2,360,128]{2,1,0:T(8,128)(2,1)S(1)}, bf16[2,360,128]{2,1,0:T(8,128)(2,1)S(1)}, u32[]{:S(2)}, u32[]{:S(2)}) collective-permute-start(bf16[2,360,128]{2,1,0:T(8,128)(2,1)S(1)} %order_quarters.1.a_ref), channel_id=1, source_target_pairs={{0,2},{32,40},{1,3},{33,41},{2,0},{34,42},{3,1},{35,43},{4,6},{36,... | collective-permute-start | bytes 552968 | tf_op jit(solution)/shard_map/ppermute | solution.py:267
  16.5 0.4 collective-permute-start.3
  16.9 2.3 %collective-permute-start.2 = (bf16[2,360,128]{2,1,0:T(8,128)(2,1)S(1)}, bf16[2,360,128]{2,1,0:T(8,128)(2,1)S(1)}, u32[]{:S(2)}, u32[]{:S(2)}) collective-permute-start(bf16[2,360,128]{2,1,0:T(8,128)(2,1)S(1)} %order_quarters.1.a_ref), channel_id=1, source_target_pairs={{0,3},{32,44},{1,0},{33,45},{2,1},{34,46},{3,2},{35,47},{4,7},{36,... | collective-permute-start | bytes 552968 | tf_op jit(solution)/shard_map/ppermute | solution.py:267
  19.2 0.0 collective-permute-done.5.ref
  19.2 1.9 %arrange_other.1.after1.w_ref = bf16[4608,1152]{1,0:T(8,128)(2,1)S(1)} custom-call(bf16[2304,1152]{1,0:T(8,128)(2,1)S(1)} %collective-permute-done.5.ref, bf16[4608,1152]{1,0:T(8,128)(2,1)S(1)} %arrange_own.1.after.half_ref), custom_call_target="tpu_custom_call", output_to_operand_aliasing={{}: (1, {})} | custom-call | bytes 10616832 | tf_op jit(solution)/shard_map/arrange_other/pallas_call | solution.py:268
  21.1 0.0 collective-permute-done.4.d_ref
  21.1 1.3 %collective-permute-done.3.c_ref = bf16[2,360,128]{2,1,0:T(8,128)(2,1)S(1)} collective-permute-done((bf16[2,360,128]{2,1,0:T(8,128)(2,1)S(1)}, bf16[2,360,128]{2,1,0:T(8,128)(2,1)S(1)}, u32[]{:S(2)}, u32[]{:S(2)}) %collective-permute-start.3) | collective-permute-done | bytes 184352 | tf_op jit(solution)/shard_map/ppermute | solution.py:267
  22.4 0.4 merge_codes.1
  22.9 2.5 %collective-permute-start.16 = (bf16[160,1152]{1,0:T(8,128)(2,1)S(1)}, bf16[160,1152]{1,0:T(8,128)(2,1)S(1)}, u32[]{:S(2)}, u32[]{:S(2)}) collective-permute-start(bf16[160,1152]{1,0:T(8,128)(2,1)S(1)} %get-tuple-element.34.m0), channel_id=1, source_target_pairs={{0,8},{32,34},{1,9},{33,35},{2,10},{34,32},{3,11},{35,33},{4,12},{... | collective-permute-start | bytes 1105928 | tf_op jit(solution)/shard_map/ppermute | solution.py:273
  25.4 0.3 collective-permute-start.15
  25.7 2.4 %collective-permute-start.14 = (bf16[160,1152]{1,0:T(8,128)(2,1)S(1)}, bf16[160,1152]{1,0:T(8,128)(2,1)S(1)}, u32[]{:S(2)}, u32[]{:S(2)}) collective-permute-start(bf16[160,1152]{1,0:T(8,128)(2,1)S(1)} %get-tuple-element.34.m0), channel_id=1, source_target_pairs={{0,12},{32,35},{1,13},{33,32},{2,14},{34,33},{3,15},{35,34},{4,0},... | collective-permute-start | bytes 1105928 | tf_op jit(solution)/shard_map/ppermute | solution.py:273
  28.1 0.6 collective-permute-start.8
  28.6 2.5 %collective-permute-done.16.m1 = bf16[160,1152]{1,0:T(8,128)(2,1)S(1)} collective-permute-done((bf16[160,1152]{1,0:T(8,128)(2,1)S(1)}, bf16[160,1152]{1,0:T(8,128)(2,1)S(1)}, u32[]{:S(2)}, u32[]{:S(2)}) %collective-permute-start.16) | collective-permute-done | bytes 368672 | tf_op jit(solution)/shard_map/ppermute | solution.py:273
  31.1 2.2 %collective-permute-start.7 = (bf16[160,1152]{1,0:T(8,128)(2,1)S(1)}, bf16[160,1152]{1,0:T(8,128)(2,1)S(1)}, u32[]{:S(2)}, u32[]{:S(2)}) collective-permute-start(bf16[160,1152]{1,0:T(8,128)(2,1)S(1)} %get-tuple-element.27.m0.after), channel_id=1, source_target_pairs={{0,12},{32,35},{1,13},{33,32},{2,14},{34,33},{3,15},{35,34},{4,0},... | collective-permute-start | bytes 1105928 | tf_op jit(solution)/shard_map/ppermute | solution.py:273
  33.3 1.1 %project_early.3.early_ref = f32[160,1152]{1,0:T(8,128)S(1)} custom-call(bf16[160,1152]{1,0:T(8,128)(2,1)S(1)} %get-tuple-element.34.m0, bf16[160,1152]{1,0:T(8,128)(2,1)S(1)} %collective-permute-done.16.m1, bf16[4608,1152]{1,0:T(8,128)(2,1)S(1)} %arrange_other.1.after1.w_ref), custom_call_target="tpu_custom_call" | custom-call | flops 849346560 | bytes 5308416 | tf_op jit(solution)/shard_map/project_early/pallas_call | solution.py:278
  34.4 0.6 collective-permute-done.15.m3
  35.0 0.0 collective-permute-done.14.m2
  35.0 1.3 %project_in.3 = (f32[160,1152]{1,0:T(8,128)S(1)}, f32[168,1152]{1,0:T(8,128)S(1)}) custom-call(bf16[160,1152]{1,0:T(8,128)(2,1)S(1)} %collective-permute-done.14.m2, bf16[160,1152]{1,0:T(8,128)(2,1)S(1)} %collective-permute-done.15.m3, bf16[4608,1152]{1,0:T(8,128)(2,1)S(1)} %arrange_other.1.after1.w_ref, f32[160,1152]{1,0:T(8,128)S(1)} %project_early.3.early_ref), custom_call_target="tpu_custom_call" | custom-call | flops 849346560 | bytes 5308416 | tf_op jit(solution)/shard_map/project_in/pallas_call | solution.py:283
  36.4 1.6 %collective-permute-start.17 = (f16[168,1152]{1,0:T(8,128)(2,1)S(1)}, f16[168,1152]{1,0:T(8,128)(2,1)S(1)}, u32[]{:S(2)}, u32[]{:S(2)}) collective-permute-start(f16[168,1152]{1,0:T(8,128)(2,1)S(1)} %convert_element_type.46), channel_id=1, source_target_pairs={{0,64},{64,0},{1,65},{65,1},{2,66},{66,2},{3,67},{67,3},{4,68},{68... | collective-permute-start | bytes 1161224 | tf_op jit(solution)/shard_map/ppermute | solution.py:286
  38.0 2.5 %stage_own.1.half_ref = bf16[1152,4608]{1,0:T(8,128)(2,1)S(1)} custom-call(bf16[1152,2304]{1,0:T(8,128)(2,1)} %ref.3, bf16[160,1152]{1,0:T(8,128)(2,1)S(1)} %get-tuple-element.27.m0.after), custom_call_target="tpu_custom_call" | custom-call | bytes 10616832 | tf_op jit(solution)/shard_map/stage_own/pallas_call | solution.py:287
  40.5 0.4 stage_other.1.w_ref
  41.0 0.0 collective-permute-done.9.m1
  41.0 1.1 %project_early.2.early_ref = f32[160,1152]{1,0:T(8,128)S(1)} custom-call(bf16[160,1152]{1,0:T(8,128)(2,1)S(1)} %get-tuple-element.27.m0.after, bf16[160,1152]{1,0:T(8,128)(2,1)S(1)} %collective-permute-done.9.m1, bf16[4608,1152]{1,0:T(8,128)(2,1)S(1)} %arrange_other.1.after1.w_ref), custom_call_target="tpu_custom_call" | custom-call | flops 849346560 | bytes 5308416 | tf_op jit(solution)/shard_map/project_early/pallas_call | solution.py:278
  42.1 0.8 collective-permute-done.8.m3
  42.9 0.0 collective-permute-done.7.m2
  42.9 1.3 %project_in.2 = (f32[160,1152]{1,0:T(8,128)S(1)}, f32[168,1152]{1,0:T(8,128)S(1)}) custom-call(bf16[160,1152]{1,0:T(8,128)(2,1)S(1)} %collective-permute-done.7.m2, bf16[160,1152]{1,0:T(8,128)(2,1)S(1)} %collective-permute-done.8.m3, bf16[4608,1152]{1,0:T(8,128)(2,1)S(1)} %arrange_other.1.after1.w_ref, f32[160,1152]{1,0:T(8,128)S(1)} %project_early.2.early_ref), custom_call_target="tpu_custom_call" | custom-call | flops 849346560 | bytes 5308416 | tf_op jit(solution)/shard_map/project_in/pallas_call | solution.py:283
  44.3 1.7 %collective-permute-start.10 = (f16[168,1152]{1,0:T(8,128)(2,1)S(1)}, f16[168,1152]{1,0:T(8,128)(2,1)S(1)}, u32[]{:S(2)}, u32[]{:S(2)}) collective-permute-start(f16[168,1152]{1,0:T(8,128)(2,1)S(1)} %convert_element_type.42), channel_id=1, source_target_pairs={{0,64},{64,0},{1,65},{65,1},{2,66},{66,2},{3,67},{67,3},{4,68},{68... | collective-permute-start | bytes 1161224 | tf_op jit(solution)/shard_map/ppermute | solution.py:286
  46.1 0.0 collective-permute-done.17
  46.1 0.3 fusion.15.a_ref
  46.4 2.5 %project_out.3 = (f32[4,360,128]{2,1,0:T(8,128)S(1)}, bf16[4,360,128]{2,1,0:T(8,128)(2,1)S(1)}, bf16[4,360,128]{2,1,0:T(8,128)(2,1)S(1)}, bf16[4,360,128]{2,1,0:T(8,128)(2,1)S(1)}) custom-call(bf16[160,1152]{1,0:T(8,128)(2,1)S(1)} %fusion.15.a_ref, bf16[1152,4608]{1,0:T(8,128)(2,1)S(1)} %stage_other.1.w_ref), custom_call_target="tpu_custom_call" | custom-call | flops 1698693120 | bytes 10616832 | tf_op jit(solution)/shard_map/project_out/pallas_call | solution.py:297
  49.0 1.7 %collective-permute-start.18 = (bf16[4,360,128]{2,1,0:T(8,128)(2,1)S(1)}, bf16[4,360,128]{2,1,0:T(8,128)(2,1)S(1)}, u32[]{:S(2)}, u32[]{:S(2)}) collective-permute-start(bf16[4,360,128]{2,1,0:T(8,128)(2,1)S(1)} %get-tuple-element.38), channel_id=1, source_target_pairs={{0,2},{32,40},{1,3},{33,41},{2,0},{34,42},{3,1},{35,43},{4,6},{36,... | collective-permute-start | bytes 1105928 | tf_op jit(solution)/shard_map/ppermute | solution.py:307
  50.7 1.5 %collective-permute-start.19 = (bf16[4,360,128]{2,1,0:T(8,128)(2,1)S(1)}, bf16[4,360,128]{2,1,0:T(8,128)(2,1)S(1)}, u32[]{:S(2)}, u32[]{:S(2)}) collective-permute-start(bf16[4,360,128]{2,1,0:T(8,128)(2,1)S(1)} %get-tuple-element.39), channel_id=1, source_target_pairs={{0,1},{32,36},{1,2},{33,37},{2,3},{34,38},{3,0},{35,39},{4,5},{36,... | collective-permute-start | bytes 1105928 | tf_op jit(solution)/shard_map/ppermute | solution.py:307
  52.1 1.2 %collective-permute-start.20 = (bf16[4,360,128]{2,1,0:T(8,128)(2,1)S(1)}, bf16[4,360,128]{2,1,0:T(8,128)(2,1)S(1)}, u32[]{:S(2)}, u32[]{:S(2)}) collective-permute-start(bf16[4,360,128]{2,1,0:T(8,128)(2,1)S(1)} %get-tuple-element.40), channel_id=1, source_target_pairs={{0,3},{32,44},{1,0},{33,45},{2,1},{34,46},{3,2},{35,47},{4,7},{36,... | collective-permute-start | bytes 1105928 | tf_op jit(solution)/shard_map/ppermute | solution.py:307
  53.4 0.4 collective-permute-done.10
  53.8 0.3 fusion.7.a_ref
  54.1 2.5 %project_out.2 = (f32[4,360,128]{2,1,0:T(8,128)S(1)}, bf16[4,360,128]{2,1,0:T(8,128)(2,1)S(1)}, bf16[4,360,128]{2,1,0:T(8,128)(2,1)S(1)}, bf16[4,360,128]{2,1,0:T(8,128)(2,1)S(1)}) custom-call(bf16[160,1152]{1,0:T(8,128)(2,1)S(1)} %fusion.7.a_ref, bf16[1152,4608]{1,0:T(8,128)(2,1)S(1)} %stage_other.1.w_ref), custom_call_target="tpu_custom_call" | custom-call | flops 1698693120 | bytes 10616832 | tf_op jit(solution)/shard_map/project_out/pallas_call | solution.py:297
  56.6 1.5 %collective-permute-start.11 = (bf16[4,360,128]{2,1,0:T(8,128)(2,1)S(1)}, bf16[4,360,128]{2,1,0:T(8,128)(2,1)S(1)}, u32[]{:S(2)}, u32[]{:S(2)}) collective-permute-start(bf16[4,360,128]{2,1,0:T(8,128)(2,1)S(1)} %get-tuple-element.31), channel_id=1, source_target_pairs={{0,2},{32,40},{1,3},{33,41},{2,0},{34,42},{3,1},{35,43},{4,6},{36,... | collective-permute-start | bytes 1105928 | tf_op jit(solution)/shard_map/ppermute | solution.py:307
  58.1 2.2 %collective-permute-start.12 = (bf16[4,360,128]{2,1,0:T(8,128)(2,1)S(1)}, bf16[4,360,128]{2,1,0:T(8,128)(2,1)S(1)}, u32[]{:S(2)}, u32[]{:S(2)}) collective-permute-start(bf16[4,360,128]{2,1,0:T(8,128)(2,1)S(1)} %get-tuple-element.32), channel_id=1, source_target_pairs={{0,1},{32,36},{1,2},{33,37},{2,3},{34,38},{3,0},{35,39},{4,5},{36,... | collective-permute-start | bytes 1105928 | tf_op jit(solution)/shard_map/ppermute | solution.py:307
  60.3 0.5 collective-permute-start.13
  60.8 0.4 collective-permute-done.19.c1
  61.2 0.2 collective-permute-done.20.d1
  61.3 3.6 %collective-permute-done.11.b0 = bf16[4,360,128]{2,1,0:T(8,128)(2,1)S(1)} collective-permute-done((bf16[4,360,128]{2,1,0:T(8,128)(2,1)S(1)}, bf16[4,360,128]{2,1,0:T(8,128)(2,1)S(1)}, u32[]{:S(2)}, u32[]{:S(2)}) %collective-permute-start.11) | collective-permute-done | bytes 368672 | tf_op jit(solution)/shard_map/ppermute | solution.py:307
  65.0 4.1 %collective-permute-done.12.c0 = bf16[4,360,128]{2,1,0:T(8,128)(2,1)S(1)} collective-permute-done((bf16[4,360,128]{2,1,0:T(8,128)(2,1)S(1)}, bf16[4,360,128]{2,1,0:T(8,128)(2,1)S(1)}, u32[]{:S(2)}, u32[]{:S(2)}) %collective-permute-start.12) | collective-permute-done | bytes 368672 | tf_op jit(solution)/shard_map/ppermute | solution.py:307
  69.1 0.3 collective-permute-done.13.d0
  69.5 0.4 add_first.1
  69.8 2.1 %collective-permute-start.21 = (bf16[720,128]{1,0:T(8,128)(2,1)S(1)}, bf16[720,128]{1,0:T(8,128)(2,1)S(1)}, u32[]{:S(2)}, u32[]{:S(2)}) collective-permute-start(bf16[720,128]{1,0:T(8,128)(2,1)S(1)} %get-tuple-element.42), channel_id=1, source_target_pairs={{0,8},{32,34},{1,9},{33,35},{2,10},{34,32},{3,11},{35,33},{4,12},{... | collective-permute-start | bytes 552968 | tf_op jit(solution)/shard_map/ppermute | solution.py:310
  71.9 0.8 collective-permute-start.22
  72.6 1.9 %collective-permute-start.23 = (bf16[720,128]{1,0:T(8,128)(2,1)S(1)}, bf16[720,128]{1,0:T(8,128)(2,1)S(1)}, u32[]{:S(2)}, u32[]{:S(2)}) collective-permute-start(bf16[720,128]{1,0:T(8,128)(2,1)S(1)} %get-tuple-element.44), channel_id=1, source_target_pairs={{0,12},{32,35},{1,13},{33,32},{2,14},{34,33},{3,15},{35,34},{4,0},... | collective-permute-start | bytes 552968 | tf_op jit(solution)/shard_map/ppermute | solution.py:310
  74.6 1.3 %collective-permute-done.21.b = bf16[720,128]{1,0:T(8,128)(2,1)S(1)} collective-permute-done((bf16[720,128]{1,0:T(8,128)(2,1)S(1)}, bf16[720,128]{1,0:T(8,128)(2,1)S(1)}, u32[]{:S(2)}, u32[]{:S(2)}) %collective-permute-start.21) | collective-permute-done | bytes 184352 | tf_op jit(solution)/shard_map/ppermute | solution.py:310
  75.8 1.9 %collective-permute-done.22.c = bf16[720,128]{1,0:T(8,128)(2,1)S(1)} collective-permute-done((bf16[720,128]{1,0:T(8,128)(2,1)S(1)}, bf16[720,128]{1,0:T(8,128)(2,1)S(1)}, u32[]{:S(2)}, u32[]{:S(2)}) %collective-permute-start.22) | collective-permute-done | bytes 184352 | tf_op jit(solution)/shard_map/ppermute | solution.py:310
  77.8 0.0 collective-permute-done.23.d
  77.8 0.3 add_second.1
  78.1 2.0 %collective-permute-start.26 = (f16[224,128]{1,0:T(8,128)(2,1)S(1)}, f16[224,128]{1,0:T(8,128)(2,1)S(1)}, u32[]{:S(2)}, u32[]{:S(2)}) collective-permute-start(f16[224,128]{1,0:T(8,128)(2,1)S(1)} %convert_element_type.54), channel_id=1, source_target_pairs={{0,16},{16,0},{1,17},{17,1},{2,18},{18,2},{3,19},{19,3},{4,20},{20... | collective-permute-start | bytes 172040 | tf_op jit(solution)/shard_map/ppermute | solution.py:316
  80.1 7.9 %collective-permute-start.25 = (f16[224,128]{1,0:T(8,128)(2,1)S(1)}, f16[224,128]{1,0:T(8,128)(2,1)S(1)}, u32[]{:S(2)}, u32[]{:S(2)}) collective-permute-start(f16[224,128]{1,0:T(8,128)(2,1)S(1)} %convert_element_type.52), channel_id=1, source_target_pairs={{0,48},{16,32},{32,16},{48,0},{1,49},{17,33},{33,17},{49,1},{2,50}... | collective-permute-start | bytes 172040 | tf_op jit(solution)/shard_map/ppermute | solution.py:315
  88.0 0.4 collective-permute-start.24
  88.4 0.0 collective-permute-done.26
  88.4 2.0 %collective-permute-done.25 = f16[224,128]{1,0:T(8,128)(2,1)S(1)} collective-permute-done((f16[224,128]{1,0:T(8,128)(2,1)S(1)}, f16[224,128]{1,0:T(8,128)(2,1)S(1)}, u32[]{:S(2)}, u32[]{:S(2)}) %collective-permute-start.25) | collective-permute-done | bytes 57376 | tf_op jit(solution)/shard_map/ppermute | solution.py:315
  90.5 0.8 finish.1
  (18 shorter events, 0.3 us)
Async XLA Ops:
  0.0 19.2 %collective-permute-start.5 = (bf16[2304,1152]{1,0:T(8,128)(2,1)}, bf16[2304,1152]{1,0:T(8,128)(2,1)S(1)}, u32[]{:S(2)}, u32[]{:S(2)}) collective-permute-start(bf16[2304,1152]{1,0:T(8,128)(2,1)} %ref.2), channel_id=1, source_target_pairs={{0,32},{32,0},{1,33},{33,1},{2,34},{34,2},{3,35},{35,3},{4,36},{36... | collective-permute-start | bytes 15925256 | tf_op jit(solution)/shard_map/ppermute | solution.py:251
  1.4 21.0 %collective-permute-start.6 = (bf16[1152,2304]{1,0:T(8,128)(2,1)}, bf16[1152,2304]{1,0:T(8,128)(2,1)S(1)}, u32[]{:S(2)}, u32[]{:S(2)}) collective-permute-start(bf16[1152,2304]{1,0:T(8,128)(2,1)} %ref.3), channel_id=1, source_target_pairs={{0,32},{32,0},{1,33},{33,1},{2,34},{34,2},{3,35},{35,3},{4,36},{36... | collective-permute-start | bytes 15925256 | tf_op jit(solution)/shard_map/ppermute | solution.py:252
  2.7 10.8 %collective-permute-start.1 = (bf16[360,128]{1,0:T(8,128)(2,1)S(1)}, bf16[360,128]{1,0:T(8,128)(2,1)S(1)}, u32[]{:S(2)}, u32[]{:S(2)}) collective-permute-start(bf16[360,128]{1,0:T(8,128)(2,1)S(1)} %pack_codes.1), channel_id=1, source_target_pairs={{64,16},{80,64},{16,80},{0,0},{65,17},{81,65},{17,81},{1,1},{66,18... | collective-permute-start | bytes 276488 | tf_op jit(solution)/shard_map/ppermute | solution.py:263
  3.4 10.1 %collective-permute-start = (bf16[360,128]{1,0:T(8,128)(2,1)S(1)}, bf16[360,128]{1,0:T(8,128)(2,1)S(1)}, u32[]{:S(2)}, u32[]{:S(2)}) collective-permute-start(bf16[360,128]{1,0:T(8,128)(2,1)S(1)} %pack_codes.1), channel_id=1, source_target_pairs={{0,16},{16,64},{64,0},{80,80},{1,17},{17,65},{65,1},{81,81},{2,18}... | collective-permute-start | bytes 276488 | tf_op jit(solution)/shard_map/ppermute | solution.py:262
  13.6 7.6 %collective-permute-start.4 = (bf16[2,360,128]{2,1,0:T(8,128)(2,1)S(1)}, bf16[2,360,128]{2,1,0:T(8,128)(2,1)S(1)}, u32[]{:S(2)}, u32[]{:S(2)}) collective-permute-start(bf16[2,360,128]{2,1,0:T(8,128)(2,1)S(1)} %order_quarters.1.a_ref), channel_id=1, source_target_pairs={{0,2},{32,40},{1,3},{33,41},{2,0},{34,42},{3,1},{35,43},{4,6},{36,... | collective-permute-start | bytes 552968 | tf_op jit(solution)/shard_map/ppermute | solution.py:267
  16.5 5.9 %collective-permute-start.3 = (bf16[2,360,128]{2,1,0:T(8,128)(2,1)S(1)}, bf16[2,360,128]{2,1,0:T(8,128)(2,1)S(1)}, u32[]{:S(2)}, u32[]{:S(2)}) collective-permute-start(bf16[2,360,128]{2,1,0:T(8,128)(2,1)S(1)} %order_quarters.1.a_ref), channel_id=1, source_target_pairs={{0,1},{32,36},{1,2},{33,37},{2,3},{34,38},{3,0},{35,39},{4,5},{36,... | collective-permute-start | bytes 552968 | tf_op jit(solution)/shard_map/ppermute | solution.py:267
  16.9 5.5 %collective-permute-start.2 = (bf16[2,360,128]{2,1,0:T(8,128)(2,1)S(1)}, bf16[2,360,128]{2,1,0:T(8,128)(2,1)S(1)}, u32[]{:S(2)}, u32[]{:S(2)}) collective-permute-start(bf16[2,360,128]{2,1,0:T(8,128)(2,1)S(1)} %order_quarters.1.a_ref), channel_id=1, source_target_pairs={{0,3},{32,44},{1,0},{33,45},{2,1},{34,46},{3,2},{35,47},{4,7},{36,... | collective-permute-start | bytes 552968 | tf_op jit(solution)/shard_map/ppermute | solution.py:267
  22.9 8.3 %collective-permute-start.16 = (bf16[160,1152]{1,0:T(8,128)(2,1)S(1)}, bf16[160,1152]{1,0:T(8,128)(2,1)S(1)}, u32[]{:S(2)}, u32[]{:S(2)}) collective-permute-start(bf16[160,1152]{1,0:T(8,128)(2,1)S(1)} %get-tuple-element.34.m0), channel_id=1, source_target_pairs={{0,8},{32,34},{1,9},{33,35},{2,10},{34,32},{3,11},{35,33},{4,12},{... | collective-permute-start | bytes 1105928 | tf_op jit(solution)/shard_map/ppermute | solution.py:273
  25.4 9.7 %collective-permute-start.15 = (bf16[160,1152]{1,0:T(8,128)(2,1)S(1)}, bf16[160,1152]{1,0:T(8,128)(2,1)S(1)}, u32[]{:S(2)}, u32[]{:S(2)}) collective-permute-start(bf16[160,1152]{1,0:T(8,128)(2,1)S(1)} %get-tuple-element.34.m0), channel_id=1, source_target_pairs={{0,4},{32,33},{1,5},{33,34},{2,6},{34,35},{3,7},{35,32},{4,8},{36,... | collective-permute-start | bytes 1105928 | tf_op jit(solution)/shard_map/ppermute | solution.py:273
  25.7 9.4 %collective-permute-start.14 = (bf16[160,1152]{1,0:T(8,128)(2,1)S(1)}, bf16[160,1152]{1,0:T(8,128)(2,1)S(1)}, u32[]{:S(2)}, u32[]{:S(2)}) collective-permute-start(bf16[160,1152]{1,0:T(8,128)(2,1)S(1)} %get-tuple-element.34.m0), channel_id=1, source_target_pairs={{0,12},{32,35},{1,13},{33,32},{2,14},{34,33},{3,15},{35,34},{4,0},... | collective-permute-start | bytes 1105928 | tf_op jit(solution)/shard_map/ppermute | solution.py:273
  28.1 12.9 %collective-permute-start.9 = (bf16[160,1152]{1,0:T(8,128)(2,1)S(1)}, bf16[160,1152]{1,0:T(8,128)(2,1)S(1)}, u32[]{:S(2)}, u32[]{:S(2)}) collective-permute-start(bf16[160,1152]{1,0:T(8,128)(2,1)S(1)} %get-tuple-element.27.m0.after), channel_id=1, source_target_pairs={{0,8},{32,34},{1,9},{33,35},{2,10},{34,32},{3,11},{35,33},{4,12},{... | collective-permute-start | bytes 1105928 | tf_op jit(solution)/shard_map/ppermute | solution.py:273
  28.1 14.9 %collective-permute-start.8 = (bf16[160,1152]{1,0:T(8,128)(2,1)S(1)}, bf16[160,1152]{1,0:T(8,128)(2,1)S(1)}, u32[]{:S(2)}, u32[]{:S(2)}) collective-permute-start(bf16[160,1152]{1,0:T(8,128)(2,1)S(1)} %get-tuple-element.27.m0.after), channel_id=1, source_target_pairs={{0,4},{32,33},{1,5},{33,34},{2,6},{34,35},{3,7},{35,32},{4,8},{36,... | collective-permute-start | bytes 1105928 | tf_op jit(solution)/shard_map/ppermute | solution.py:273
  31.1 11.8 %collective-permute-start.7 = (bf16[160,1152]{1,0:T(8,128)(2,1)S(1)}, bf16[160,1152]{1,0:T(8,128)(2,1)S(1)}, u32[]{:S(2)}, u32[]{:S(2)}) collective-permute-start(bf16[160,1152]{1,0:T(8,128)(2,1)S(1)} %get-tuple-element.27.m0.after), channel_id=1, source_target_pairs={{0,12},{32,35},{1,13},{33,32},{2,14},{34,33},{3,15},{35,34},{4,0},... | collective-permute-start | bytes 1105928 | tf_op jit(solution)/shard_map/ppermute | solution.py:273
  36.4 9.6 %collective-permute-start.17 = (f16[168,1152]{1,0:T(8,128)(2,1)S(1)}, f16[168,1152]{1,0:T(8,128)(2,1)S(1)}, u32[]{:S(2)}, u32[]{:S(2)}) collective-permute-start(f16[168,1152]{1,0:T(8,128)(2,1)S(1)} %convert_element_type.46), channel_id=1, source_target_pairs={{0,64},{64,0},{1,65},{65,1},{2,66},{66,2},{3,67},{67,3},{4,68},{68... | collective-permute-start | bytes 1161224 | tf_op jit(solution)/shard_map/ppermute | solution.py:286
  44.3 9.4 %collective-permute-start.10 = (f16[168,1152]{1,0:T(8,128)(2,1)S(1)}, f16[168,1152]{1,0:T(8,128)(2,1)S(1)}, u32[]{:S(2)}, u32[]{:S(2)}) collective-permute-start(f16[168,1152]{1,0:T(8,128)(2,1)S(1)} %convert_element_type.42), channel_id=1, source_target_pairs={{0,64},{64,0},{1,65},{65,1},{2,66},{66,2},{3,67},{67,3},{4,68},{68... | collective-permute-start | bytes 1161224 | tf_op jit(solution)/shard_map/ppermute | solution.py:286
  49.0 11.3 %collective-permute-start.18 = (bf16[4,360,128]{2,1,0:T(8,128)(2,1)S(1)}, bf16[4,360,128]{2,1,0:T(8,128)(2,1)S(1)}, u32[]{:S(2)}, u32[]{:S(2)}) collective-permute-start(bf16[4,360,128]{2,1,0:T(8,128)(2,1)S(1)} %get-tuple-element.38), channel_id=1, source_target_pairs={{0,2},{32,40},{1,3},{33,41},{2,0},{34,42},{3,1},{35,43},{4,6},{36,... | collective-permute-start | bytes 1105928 | tf_op jit(solution)/shard_map/ppermute | solution.py:307
  50.7 10.5 %collective-permute-start.19 = (bf16[4,360,128]{2,1,0:T(8,128)(2,1)S(1)}, bf16[4,360,128]{2,1,0:T(8,128)(2,1)S(1)}, u32[]{:S(2)}, u32[]{:S(2)}) collective-permute-start(bf16[4,360,128]{2,1,0:T(8,128)(2,1)S(1)} %get-tuple-element.39), channel_id=1, source_target_pairs={{0,1},{32,36},{1,2},{33,37},{2,3},{34,38},{3,0},{35,39},{4,5},{36,... | collective-permute-start | bytes 1105928 | tf_op jit(solution)/shard_map/ppermute | solution.py:307
  52.1 9.2 %collective-permute-start.20 = (bf16[4,360,128]{2,1,0:T(8,128)(2,1)S(1)}, bf16[4,360,128]{2,1,0:T(8,128)(2,1)S(1)}, u32[]{:S(2)}, u32[]{:S(2)}) collective-permute-start(bf16[4,360,128]{2,1,0:T(8,128)(2,1)S(1)} %get-tuple-element.40), channel_id=1, source_target_pairs={{0,3},{32,44},{1,0},{33,45},{2,1},{34,46},{3,2},{35,47},{4,7},{36,... | collective-permute-start | bytes 1105928 | tf_op jit(solution)/shard_map/ppermute | solution.py:307
  56.6 8.4 %collective-permute-start.11 = (bf16[4,360,128]{2,1,0:T(8,128)(2,1)S(1)}, bf16[4,360,128]{2,1,0:T(8,128)(2,1)S(1)}, u32[]{:S(2)}, u32[]{:S(2)}) collective-permute-start(bf16[4,360,128]{2,1,0:T(8,128)(2,1)S(1)} %get-tuple-element.31), channel_id=1, source_target_pairs={{0,2},{32,40},{1,3},{33,41},{2,0},{34,42},{3,1},{35,43},{4,6},{36,... | collective-permute-start | bytes 1105928 | tf_op jit(solution)/shard_map/ppermute | solution.py:307
  58.1 11.0 %collective-permute-start.12 = (bf16[4,360,128]{2,1,0:T(8,128)(2,1)S(1)}, bf16[4,360,128]{2,1,0:T(8,128)(2,1)S(1)}, u32[]{:S(2)}, u32[]{:S(2)}) collective-permute-start(bf16[4,360,128]{2,1,0:T(8,128)(2,1)S(1)} %get-tuple-element.32), channel_id=1, source_target_pairs={{0,1},{32,36},{1,2},{33,37},{2,3},{34,38},{3,0},{35,39},{4,5},{36,... | collective-permute-start | bytes 1105928 | tf_op jit(solution)/shard_map/ppermute | solution.py:307
  60.3 9.2 %collective-permute-start.13 = (bf16[4,360,128]{2,1,0:T(8,128)(2,1)S(1)}, bf16[4,360,128]{2,1,0:T(8,128)(2,1)S(1)}, u32[]{:S(2)}, u32[]{:S(2)}) collective-permute-start(bf16[4,360,128]{2,1,0:T(8,128)(2,1)S(1)} %get-tuple-element.33), channel_id=1, source_target_pairs={{0,3},{32,44},{1,0},{33,45},{2,1},{34,46},{3,2},{35,47},{4,7},{36,... | collective-permute-start | bytes 1105928 | tf_op jit(solution)/shard_map/ppermute | solution.py:307
  69.8 6.0 %collective-permute-start.21 = (bf16[720,128]{1,0:T(8,128)(2,1)S(1)}, bf16[720,128]{1,0:T(8,128)(2,1)S(1)}, u32[]{:S(2)}, u32[]{:S(2)}) collective-permute-start(bf16[720,128]{1,0:T(8,128)(2,1)S(1)} %get-tuple-element.42), channel_id=1, source_target_pairs={{0,8},{32,34},{1,9},{33,35},{2,10},{34,32},{3,11},{35,33},{4,12},{... | collective-permute-start | bytes 552968 | tf_op jit(solution)/shard_map/ppermute | solution.py:310
  71.9 5.9 %collective-permute-start.22 = (bf16[720,128]{1,0:T(8,128)(2,1)S(1)}, bf16[720,128]{1,0:T(8,128)(2,1)S(1)}, u32[]{:S(2)}, u32[]{:S(2)}) collective-permute-start(bf16[720,128]{1,0:T(8,128)(2,1)S(1)} %get-tuple-element.43), channel_id=1, source_target_pairs={{0,4},{32,33},{1,5},{33,34},{2,6},{34,35},{3,7},{35,32},{4,8},{36,... | collective-permute-start | bytes 552968 | tf_op jit(solution)/shard_map/ppermute | solution.py:310
  72.6 5.1 %collective-permute-start.23 = (bf16[720,128]{1,0:T(8,128)(2,1)S(1)}, bf16[720,128]{1,0:T(8,128)(2,1)S(1)}, u32[]{:S(2)}, u32[]{:S(2)}) collective-permute-start(bf16[720,128]{1,0:T(8,128)(2,1)S(1)} %get-tuple-element.44), channel_id=1, source_target_pairs={{0,12},{32,35},{1,13},{33,32},{2,14},{34,33},{3,15},{35,34},{4,0},... | collective-permute-start | bytes 552968 | tf_op jit(solution)/shard_map/ppermute | solution.py:310
  78.1 10.3 %collective-permute-start.26 = (f16[224,128]{1,0:T(8,128)(2,1)S(1)}, f16[224,128]{1,0:T(8,128)(2,1)S(1)}, u32[]{:S(2)}, u32[]{:S(2)}) collective-permute-start(f16[224,128]{1,0:T(8,128)(2,1)S(1)} %convert_element_type.54), channel_id=1, source_target_pairs={{0,16},{16,0},{1,17},{17,1},{2,18},{18,2},{3,19},{19,3},{4,20},{20... | collective-permute-start | bytes 172040 | tf_op jit(solution)/shard_map/ppermute | solution.py:316
  80.1 10.3 %collective-permute-start.25 = (f16[224,128]{1,0:T(8,128)(2,1)S(1)}, f16[224,128]{1,0:T(8,128)(2,1)S(1)}, u32[]{:S(2)}, u32[]{:S(2)}) collective-permute-start(f16[224,128]{1,0:T(8,128)(2,1)S(1)} %convert_element_type.52), channel_id=1, source_target_pairs={{0,48},{16,32},{32,16},{48,0},{1,49},{17,33},{33,17},{49,1},{2,50}... | collective-permute-start | bytes 172040 | tf_op jit(solution)/shard_map/ppermute | solution.py:315
  88.0 2.4 %collective-permute-start.24 = (f16[224,128]{1,0:T(8,128)(2,1)S(1)}, f16[224,128]{1,0:T(8,128)(2,1)S(1)}, u32[]{:S(2)}, u32[]{:S(2)}) collective-permute-start(f16[224,128]{1,0:T(8,128)(2,1)S(1)} %convert_element_type.50), channel_id=1, source_target_pairs={{0,32},{32,0},{1,33},{33,1},{2,34},{34,2},{3,35},{35,3},{4,36},{36... | collective-permute-start | bytes 172040 | tf_op jit(solution)/shard_map/ppermute | solution.py:314

commit v6 on v5

--- a/solution.py
+++ b/solution.py
@@ -82,9 +82,9 @@
 
 def order_quarters(one, two, after, o_ref):
     del after
-    same = lax.axis_index("zh") == lax.axis_index("zl")
-    o_ref[0] = jnp.where(same, two[...], one[...])
-    o_ref[1] = jnp.where(same, one[...], two[...])
+    swapped = lax.axis_index("zl") == 1
+    o_ref[0] = jnp.where(swapped, one[...], two[...])
+    o_ref[1] = jnp.where(swapped, two[...], one[...])
 
 
 def merge_codes(a_ref, b_ref, c_ref, d_ref, after1, after2, *outs):
@@ -259,8 +259,8 @@
         [pltpu.VMEM((QT, PIECE), BF), pltpu.VMEM((1, QT), jnp.int32), pltpu.SemaphoreType.DMA((2,))],
         name="pack_codes",
     )(in_hbm(codes), in_hbm(exponents[None, :]))
-    one = lax.ppermute(packed, z, [(0, 1), (1, 2), (2, 0), (3, 3)])
-    two = lax.ppermute(packed, z, [(2, 1), (3, 2), (1, 3), (0, 0)])
+    one = lax.ppermute(packed, z, [(0, 1), (3, 2), (2, 0), (1, 3)])
+    two = lax.ppermute(packed, z, [(2, 1), (1, 2), (0, 0), (3, 3)])
     dma, half = [pltpu.SemaphoreType.DMA], 4608 * 1152 * 2
     rows = call(arrange_own, pltpu.VMEM((4 * UNITS, UNITS), BF), [ANY], dma, nbytes=half, name="arrange_own")(w_in)
     piece = call(order_quarters, shape((2, 360, 128), BF), [VMEM, VMEM, ANY], name="order_quarters")(one, two, rows)

time: 92.9 us -> 89 us (0.958)
  starting transfers between devices: 50.1 us -> 46.2 us
    ppermute x2, starting transfers between devices: 8.23 us -> 5.34 us  [the longest x1 4.67 us: shards(): one = lax.ppermute(packed, z, [(0, 1), (3, 2), (2, 0), (1, 3)])]
    ppermute x1, starting transfers between devices: 7.93 us -> 6.9 us  [shards(): lax.ppermute(to_czl, ('c', 'zl'), [(0, 3), (1, 2), (2, 1), (3, 0)])]
    ppermute x6, starting transfers between devices: 8.51 us -> 9.51 us  [shards(): lax.ppermute(v, YX, first_axis(k))]
  transfers between devices with their start and end apart: 27 -> 27, of which waited for: 13 -> 11; matrix products, arithmetic and copies ran while one was open for 1% -> 1% of each run, Pallas kernels for 20% -> 21%
where the time goes in v6:
time: 89 us; the launch traced here: 87.5 us
  starting transfers between devices  46.2 us (52%)
  Pallas kernels  20.5 us (23%)
  waiting for transfers between devices  19.5 us (22%)
    ppermute x6, starting transfers between devices, shards(): lax.ppermute(v, YX, first_axis(k))  9.51 us
    ppermute x6, waiting for transfers between devices, shards(): lax.ppermute(v, YX, first_axis(k))  8.36 us
    ppermute x6, starting transfers between devices, shards(): lax.ppermute(m, YX, second_axis(k))  7.94 us
    ppermute x1, starting transfers between devices, shards(): lax.ppermute(to_czl, ('c', 'zl'), [(0, 3), (1, 2), (2, 1), (3, 0)])  6.9 us
    ppermute x3, starting transfers between devices, shards(): around = [lax.ppermute(piece, YX, first_axis(k)) for k in GATHER[1:]]  5.66 us
    pallas_call x2, Pallas kernels, shards(): call(project_out, [shape(part, F32)] + [shape(part, BF)] * 3, [VMEM] * 2,...  5.08 us
    ppermute x1, starting transfers between devices, shards(): one = lax.ppermute(packed, z, [(0, 1), (3, 2), (2, 0), (1, 3)])  4.67 us
    ppermute x3, starting transfers between devices, shards(): lax.ppermute(v, YX, second_axis(k))  4.23 us
  transfers between devices with their start and end apart: 27, of which 11 were waited for; matrix products, arithmetic and copies ran while one was open for 1% of the time, Pallas kernels for 21%

profile of v6, /device:TPU:1, one launch (start us, length us, event | category | flops | bytes accessed | tf_op | source)
XLA Modules:
  0.0 87.5 jit_solution(6622256057413367945)
XLA Ops:
  0.0 1.4 %collective-permute-start.5 = (bf16[2304,1152]{1,0:T(8,128)(2,1)}, bf16[2304,1152]{1,0:T(8,128)(2,1)S(1)}, u32[]{:S(2)}, u32[]{:S(2)}) collective-permute-start(bf16[2304,1152]{1,0:T(8,128)(2,1)} %ref.2), channel_id=1, source_target_pairs={{0,32},{32,0},{1,33},{33,1},{2,34},{34,2},{3,35},{35,3},{4,36},{36... | collective-permute-start | bytes 15925256 | tf_op jit(solution)/shard_map/ppermute | solution.py:251
  1.4 0.0 collective-permute-start.6
  1.4 1.3 %pack_codes.1 = bf16[360,128]{1,0:T(8,128)(2,1)S(1)} custom-call(bf16[160,288]{1,0:T(8,128)(2,1)} %codes_ref.1, s32[1,160]{1,0:T(1,128)} %bitcast.2), custom_call_target="tpu_custom_call" | custom-call | tf_op jit(solution)/shard_map/pack_codes/pallas_call | solution.py:255
  2.7 0.7 collective-permute-start.1
  3.4 4.7 %collective-permute-start = (bf16[360,128]{1,0:T(8,128)(2,1)S(1)}, bf16[360,128]{1,0:T(8,128)(2,1)S(1)}, u32[]{:S(2)}, u32[]{:S(2)}) collective-permute-start(bf16[360,128]{1,0:T(8,128)(2,1)S(1)} %pack_codes.1), channel_id=1, source_target_pairs={{0,16},{80,64},{64,0},{16,80},{1,17},{81,65},{65,1},{17,81},{2,18}... | collective-permute-start | bytes 276488 | tf_op jit(solution)/shard_map/ppermute | solution.py:262
  8.0 2.5 %arrange_own.1.after.half_ref = bf16[4608,1152]{1,0:T(8,128)(2,1)S(1)} custom-call(bf16[2304,1152]{1,0:T(8,128)(2,1)} %ref.2), custom_call_target="tpu_custom_call" | custom-call | bytes 10616832 | tf_op jit(solution)/shard_map/arrange_own/pallas_call | solution.py:265
  10.5 0.3 collective-permute-done.one
  10.9 3.0 %collective-permute-start.4 = (bf16[2,360,128]{2,1,0:T(8,128)(2,1)S(1)}, bf16[2,360,128]{2,1,0:T(8,128)(2,1)S(1)}, u32[]{:S(2)}, u32[]{:S(2)}) collective-permute-start(bf16[2,360,128]{2,1,0:T(8,128)(2,1)S(1)} %order_quarters.1.a_ref), channel_id=1, source_target_pairs={{0,2},{32,40},{1,3},{33,41},{2,0},{34,42},{3,1},{35,43},{4,6},{36,... | collective-permute-start | bytes 552968 | tf_op jit(solution)/shard_map/ppermute | solution.py:267
  13.9 0.4 collective-permute-start.3
  14.3 2.3 %collective-permute-start.2 = (bf16[2,360,128]{2,1,0:T(8,128)(2,1)S(1)}, bf16[2,360,128]{2,1,0:T(8,128)(2,1)S(1)}, u32[]{:S(2)}, u32[]{:S(2)}) collective-permute-start(bf16[2,360,128]{2,1,0:T(8,128)(2,1)S(1)} %order_quarters.1.a_ref), channel_id=1, source_target_pairs={{0,3},{32,44},{1,0},{33,45},{2,1},{34,46},{3,2},{35,47},{4,7},{36,... | collective-permute-start | bytes 552968 | tf_op jit(solution)/shard_map/ppermute | solution.py:267
  16.5 0.0 collective-permute-done.5.ref
  16.6 1.9 %arrange_other.1.after1.w_ref = bf16[4608,1152]{1,0:T(8,128)(2,1)S(1)} custom-call(bf16[2304,1152]{1,0:T(8,128)(2,1)S(1)} %collective-permute-done.5.ref, bf16[4608,1152]{1,0:T(8,128)(2,1)S(1)} %arrange_own.1.after.half_ref), custom_call_target="tpu_custom_call", output_to_operand_aliasing={{}: (1, {})} | custom-call | bytes 10616832 | tf_op jit(solution)/shard_map/arrange_other/pallas_call | solution.py:268
  18.5 1.3 %collective-permute-done.3.c_ref = bf16[2,360,128]{2,1,0:T(8,128)(2,1)S(1)} collective-permute-done((bf16[2,360,128]{2,1,0:T(8,128)(2,1)S(1)}, bf16[2,360,128]{2,1,0:T(8,128)(2,1)S(1)}, u32[]{:S(2)}, u32[]{:S(2)}) %collective-permute-start.3) | collective-permute-done | bytes 184352 | tf_op jit(solution)/shard_map/ppermute | solution.py:267
  19.8 0.0 collective-permute-done.6.after2.ref
  19.8 0.4 merge_codes.1
  20.2 2.5 %collective-permute-start.16 = (bf16[160,1152]{1,0:T(8,128)(2,1)S(1)}, bf16[160,1152]{1,0:T(8,128)(2,1)S(1)}, u32[]{:S(2)}, u32[]{:S(2)}) collective-permute-start(bf16[160,1152]{1,0:T(8,128)(2,1)S(1)} %get-tuple-element.34.m0), channel_id=1, source_target_pairs={{0,8},{32,34},{1,9},{33,35},{2,10},{34,32},{3,11},{35,33},{4,12},{... | collective-permute-start | bytes 1105928 | tf_op jit(solution)/shard_map/ppermute | solution.py:273
  22.7 0.3 collective-permute-start.15
  23.0 2.4 %collective-permute-start.14 = (bf16[160,1152]{1,0:T(8,128)(2,1)S(1)}, bf16[160,1152]{1,0:T(8,128)(2,1)S(1)}, u32[]{:S(2)}, u32[]{:S(2)}) collective-permute-start(bf16[160,1152]{1,0:T(8,128)(2,1)S(1)} %get-tuple-element.34.m0), channel_id=1, source_target_pairs={{0,12},{32,35},{1,13},{33,32},{2,14},{34,33},{3,15},{35,34},{4,0},... | collective-permute-start | bytes 1105928 | tf_op jit(solution)/shard_map/ppermute | solution.py:273
  25.4 0.0 collective-permute-start.9
  25.4 0.6 collective-permute-start.8
  26.0 2.5 %collective-permute-done.16.m1 = bf16[160,1152]{1,0:T(8,128)(2,1)S(1)} collective-permute-done((bf16[160,1152]{1,0:T(8,128)(2,1)S(1)}, bf16[160,1152]{1,0:T(8,128)(2,1)S(1)}, u32[]{:S(2)}, u32[]{:S(2)}) %collective-permute-start.16) | collective-permute-done | bytes 368672 | tf_op jit(solution)/shard_map/ppermute | solution.py:273
  28.5 2.2 %collective-permute-start.7 = (bf16[160,1152]{1,0:T(8,128)(2,1)S(1)}, bf16[160,1152]{1,0:T(8,128)(2,1)S(1)}, u32[]{:S(2)}, u32[]{:S(2)}) collective-permute-start(bf16[160,1152]{1,0:T(8,128)(2,1)S(1)} %get-tuple-element.27.m0.after), channel_id=1, source_target_pairs={{0,12},{32,35},{1,13},{33,32},{2,14},{34,33},{3,15},{35,34},{4,0},... | collective-permute-start | bytes 1105928 | tf_op jit(solution)/shard_map/ppermute | solution.py:273
  30.6 1.1 %project_early.3.early_ref = f32[160,1152]{1,0:T(8,128)S(1)} custom-call(bf16[160,1152]{1,0:T(8,128)(2,1)S(1)} %get-tuple-element.34.m0, bf16[160,1152]{1,0:T(8,128)(2,1)S(1)} %collective-permute-done.16.m1, bf16[4608,1152]{1,0:T(8,128)(2,1)S(1)} %arrange_other.1.after1.w_ref), custom_call_target="tpu_custom_call" | custom-call | flops 849346560 | bytes 5308416 | tf_op jit(solution)/shard_map/project_early/pallas_call | solution.py:278
  31.7 0.6 collective-permute-done.15.m3
  32.4 0.0 collective-permute-done.14.m2
  32.4 1.3 %project_in.3 = (f32[160,1152]{1,0:T(8,128)S(1)}, f32[168,1152]{1,0:T(8,128)S(1)}) custom-call(bf16[160,1152]{1,0:T(8,128)(2,1)S(1)} %collective-permute-done.14.m2, bf16[160,1152]{1,0:T(8,128)(2,1)S(1)} %collective-permute-done.15.m3, bf16[4608,1152]{1,0:T(8,128)(2,1)S(1)} %arrange_other.1.after1.w_ref, f32[160,1152]{1,0:T(8,128)S(1)} %project_early.3.early_ref), custom_call_target="tpu_custom_call" | custom-call | flops 849346560 | bytes 5308416 | tf_op jit(solution)/shard_map/project_in/pallas_call | solution.py:283
  33.8 1.7 %collective-permute-start.17 = (f16[168,1152]{1,0:T(8,128)(2,1)S(1)}, f16[168,1152]{1,0:T(8,128)(2,1)S(1)}, u32[]{:S(2)}, u32[]{:S(2)}) collective-permute-start(f16[168,1152]{1,0:T(8,128)(2,1)S(1)} %convert_element_type.46), channel_id=1, source_target_pairs={{0,64},{64,0},{1,65},{65,1},{2,66},{66,2},{3,67},{67,3},{4,68},{68... | collective-permute-start | bytes 1161224 | tf_op jit(solution)/shard_map/ppermute | solution.py:286
  35.5 2.5 %stage_own.1.half_ref = bf16[1152,4608]{1,0:T(8,128)(2,1)S(1)} custom-call(bf16[1152,2304]{1,0:T(8,128)(2,1)} %ref.3, bf16[160,1152]{1,0:T(8,128)(2,1)S(1)} %get-tuple-element.27.m0.after), custom_call_target="tpu_custom_call" | custom-call | bytes 10616832 | tf_op jit(solution)/shard_map/stage_own/pallas_call | solution.py:287
  38.0 0.4 stage_other.1.w_ref
  38.4 0.0 collective-permute-done.9.m1
  38.4 1.1 %project_early.2.early_ref = f32[160,1152]{1,0:T(8,128)S(1)} custom-call(bf16[160,1152]{1,0:T(8,128)(2,1)S(1)} %get-tuple-element.27.m0.after, bf16[160,1152]{1,0:T(8,128)(2,1)S(1)} %collective-permute-done.9.m1, bf16[4608,1152]{1,0:T(8,128)(2,1)S(1)} %arrange_other.1.after1.w_ref), custom_call_target="tpu_custom_call" | custom-call | flops 849346560 | bytes 5308416 | tf_op jit(solution)/shard_map/project_early/pallas_call | solution.py:278
  39.6 0.7 collective-permute-done.8.m3
  40.3 0.0 collective-permute-done.7.m2
  40.3 1.3 %project_in.2 = (f32[160,1152]{1,0:T(8,128)S(1)}, f32[168,1152]{1,0:T(8,128)S(1)}) custom-call(bf16[160,1152]{1,0:T(8,128)(2,1)S(1)} %collective-permute-done.7.m2, bf16[160,1152]{1,0:T(8,128)(2,1)S(1)} %collective-permute-done.8.m3, bf16[4608,1152]{1,0:T(8,128)(2,1)S(1)} %arrange_other.1.after1.w_ref, f32[160,1152]{1,0:T(8,128)S(1)} %project_early.2.early_ref), custom_call_target="tpu_custom_call" | custom-call | flops 849346560 | bytes 5308416 | tf_op jit(solution)/shard_map/project_in/pallas_call | solution.py:283
  41.7 1.9 %collective-permute-start.10 = (f16[168,1152]{1,0:T(8,128)(2,1)S(1)}, f16[168,1152]{1,0:T(8,128)(2,1)S(1)}, u32[]{:S(2)}, u32[]{:S(2)}) collective-permute-start(f16[168,1152]{1,0:T(8,128)(2,1)S(1)} %convert_element_type.42), channel_id=1, source_target_pairs={{0,64},{64,0},{1,65},{65,1},{2,66},{66,2},{3,67},{67,3},{4,68},{68... | collective-permute-start | bytes 1161224 | tf_op jit(solution)/shard_map/ppermute | solution.py:286
  43.6 0.3 fusion.15.a_ref
  43.9 2.5 %project_out.3 = (f32[4,360,128]{2,1,0:T(8,128)S(1)}, bf16[4,360,128]{2,1,0:T(8,128)(2,1)S(1)}, bf16[4,360,128]{2,1,0:T(8,128)(2,1)S(1)}, bf16[4,360,128]{2,1,0:T(8,128)(2,1)S(1)}) custom-call(bf16[160,1152]{1,0:T(8,128)(2,1)S(1)} %fusion.15.a_ref, bf16[1152,4608]{1,0:T(8,128)(2,1)S(1)} %stage_other.1.w_ref), custom_call_target="tpu_custom_call" | custom-call | flops 1698693120 | bytes 10616832 | tf_op jit(solution)/shard_map/project_out/pallas_call | solution.py:297
  46.5 3.0 %collective-permute-start.18 = (bf16[4,360,128]{2,1,0:T(8,128)(2,1)S(1)}, bf16[4,360,128]{2,1,0:T(8,128)(2,1)S(1)}, u32[]{:S(2)}, u32[]{:S(2)}) collective-permute-start(bf16[4,360,128]{2,1,0:T(8,128)(2,1)S(1)} %get-tuple-element.38), channel_id=1, source_target_pairs={{0,2},{32,40},{1,3},{33,41},{2,0},{34,42},{3,1},{35,43},{4,6},{36,... | collective-permute-start | bytes 1105928 | tf_op jit(solution)/shard_map/ppermute | solution.py:307
  49.5 0.4 collective-permute-start.19
  49.9 2.3 %collective-permute-start.20 = (bf16[4,360,128]{2,1,0:T(8,128)(2,1)S(1)}, bf16[4,360,128]{2,1,0:T(8,128)(2,1)S(1)}, u32[]{:S(2)}, u32[]{:S(2)}) collective-permute-start(bf16[4,360,128]{2,1,0:T(8,128)(2,1)S(1)} %get-tuple-element.40), channel_id=1, source_target_pairs={{0,3},{32,44},{1,0},{33,45},{2,1},{34,46},{3,2},{35,47},{4,7},{36,... | collective-permute-start | bytes 1105928 | tf_op jit(solution)/shard_map/ppermute | solution.py:307
  52.2 0.0 collective-permute-done.10
  52.2 0.3 fusion.7.a_ref
  52.5 2.5 %project_out.2 = (f32[4,360,128]{2,1,0:T(8,128)S(1)}, bf16[4,360,128]{2,1,0:T(8,128)(2,1)S(1)}, bf16[4,360,128]{2,1,0:T(8,128)(2,1)S(1)}, bf16[4,360,128]{2,1,0:T(8,128)(2,1)S(1)}) custom-call(bf16[160,1152]{1,0:T(8,128)(2,1)S(1)} %fusion.7.a_ref, bf16[1152,4608]{1,0:T(8,128)(2,1)S(1)} %stage_other.1.w_ref), custom_call_target="tpu_custom_call" | custom-call | flops 1698693120 | bytes 10616832 | tf_op jit(solution)/shard_map/project_out/pallas_call | solution.py:297
  55.1 1.2 %collective-permute-start.11 = (bf16[4,360,128]{2,1,0:T(8,128)(2,1)S(1)}, bf16[4,360,128]{2,1,0:T(8,128)(2,1)S(1)}, u32[]{:S(2)}, u32[]{:S(2)}) collective-permute-start(bf16[4,360,128]{2,1,0:T(8,128)(2,1)S(1)} %get-tuple-element.31), channel_id=1, source_target_pairs={{0,2},{32,40},{1,3},{33,41},{2,0},{34,42},{3,1},{35,43},{4,6},{36,... | collective-permute-start | bytes 1105928 | tf_op jit(solution)/shard_map/ppermute | solution.py:307
  56.2 1.3 %collective-permute-start.12 = (bf16[4,360,128]{2,1,0:T(8,128)(2,1)S(1)}, bf16[4,360,128]{2,1,0:T(8,128)(2,1)S(1)}, u32[]{:S(2)}, u32[]{:S(2)}) collective-permute-start(bf16[4,360,128]{2,1,0:T(8,128)(2,1)S(1)} %get-tuple-element.32), channel_id=1, source_target_pairs={{0,1},{32,36},{1,2},{33,37},{2,3},{34,38},{3,0},{35,39},{4,5},{36,... | collective-permute-start | bytes 1105928 | tf_op jit(solution)/shard_map/ppermute | solution.py:307
  57.6 0.0 collective-permute-done.18.b1
  57.6 1.3 %collective-permute-start.13 = (bf16[4,360,128]{2,1,0:T(8,128)(2,1)S(1)}, bf16[4,360,128]{2,1,0:T(8,128)(2,1)S(1)}, u32[]{:S(2)}, u32[]{:S(2)}) collective-permute-start(bf16[4,360,128]{2,1,0:T(8,128)(2,1)S(1)} %get-tuple-element.33), channel_id=1, source_target_pairs={{0,3},{32,44},{1,0},{33,45},{2,1},{34,46},{3,2},{35,47},{4,7},{36,... | collective-permute-start | bytes 1105928 | tf_op jit(solution)/shard_map/ppermute | solution.py:307
  58.9 0.1 collective-permute-done.20.d1
  59.0 4.3 %collective-permute-done.11.b0 = bf16[4,360,128]{2,1,0:T(8,128)(2,1)S(1)} collective-permute-done((bf16[4,360,128]{2,1,0:T(8,128)(2,1)S(1)}, bf16[4,360,128]{2,1,0:T(8,128)(2,1)S(1)}, u32[]{:S(2)}, u32[]{:S(2)}) %collective-permute-start.11) | collective-permute-done | bytes 368672 | tf_op jit(solution)/shard_map/ppermute | solution.py:307
  63.4 3.9 %collective-permute-done.12.c0 = bf16[4,360,128]{2,1,0:T(8,128)(2,1)S(1)} collective-permute-done((bf16[4,360,128]{2,1,0:T(8,128)(2,1)S(1)}, bf16[4,360,128]{2,1,0:T(8,128)(2,1)S(1)}, u32[]{:S(2)}, u32[]{:S(2)}) %collective-permute-start.12) | collective-permute-done | bytes 368672 | tf_op jit(solution)/shard_map/ppermute | solution.py:307
  67.3 0.4 add_first.1
  67.6 1.6 %collective-permute-start.21 = (bf16[720,128]{1,0:T(8,128)(2,1)S(1)}, bf16[720,128]{1,0:T(8,128)(2,1)S(1)}, u32[]{:S(2)}, u32[]{:S(2)}) collective-permute-start(bf16[720,128]{1,0:T(8,128)(2,1)S(1)} %get-tuple-element.42), channel_id=1, source_target_pairs={{0,8},{32,34},{1,9},{33,35},{2,10},{34,32},{3,11},{35,33},{4,12},{... | collective-permute-start | bytes 552968 | tf_op jit(solution)/shard_map/ppermute | solution.py:310
  69.2 1.2 %collective-permute-start.22 = (bf16[720,128]{1,0:T(8,128)(2,1)S(1)}, bf16[720,128]{1,0:T(8,128)(2,1)S(1)}, u32[]{:S(2)}, u32[]{:S(2)}) collective-permute-start(bf16[720,128]{1,0:T(8,128)(2,1)S(1)} %get-tuple-element.43), channel_id=1, source_target_pairs={{0,4},{32,33},{1,5},{33,34},{2,6},{34,35},{3,7},{35,32},{4,8},{36,... | collective-permute-start | bytes 552968 | tf_op jit(solution)/shard_map/ppermute | solution.py:310
  70.3 1.5 %collective-permute-start.23 = (bf16[720,128]{1,0:T(8,128)(2,1)S(1)}, bf16[720,128]{1,0:T(8,128)(2,1)S(1)}, u32[]{:S(2)}, u32[]{:S(2)}) collective-permute-start(bf16[720,128]{1,0:T(8,128)(2,1)S(1)} %get-tuple-element.44), channel_id=1, source_target_pairs={{0,12},{32,35},{1,13},{33,32},{2,14},{34,33},{3,15},{35,34},{4,0},... | collective-permute-start | bytes 552968 | tf_op jit(solution)/shard_map/ppermute | solution.py:310
  71.9 1.8 %collective-permute-done.21.b = bf16[720,128]{1,0:T(8,128)(2,1)S(1)} collective-permute-done((bf16[720,128]{1,0:T(8,128)(2,1)S(1)}, bf16[720,128]{1,0:T(8,128)(2,1)S(1)}, u32[]{:S(2)}, u32[]{:S(2)}) %collective-permute-start.21) | collective-permute-done | bytes 184352 | tf_op jit(solution)/shard_map/ppermute | solution.py:310
  73.7 1.9 %collective-permute-done.22.c = bf16[720,128]{1,0:T(8,128)(2,1)S(1)} collective-permute-done((bf16[720,128]{1,0:T(8,128)(2,1)S(1)}, bf16[720,128]{1,0:T(8,128)(2,1)S(1)}, u32[]{:S(2)}, u32[]{:S(2)}) %collective-permute-start.22) | collective-permute-done | bytes 184352 | tf_op jit(solution)/shard_map/ppermute | solution.py:310
  75.6 0.0 collective-permute-done.23.d
  75.6 0.3 add_second.1
  75.9 1.3 %collective-permute-start.26 = (f16[224,128]{1,0:T(8,128)(2,1)S(1)}, f16[224,128]{1,0:T(8,128)(2,1)S(1)}, u32[]{:S(2)}, u32[]{:S(2)}) collective-permute-start(f16[224,128]{1,0:T(8,128)(2,1)S(1)} %convert_element_type.54), channel_id=1, source_target_pairs={{0,16},{16,0},{1,17},{17,1},{2,18},{18,2},{3,19},{19,3},{4,20},{20... | collective-permute-start | bytes 172040 | tf_op jit(solution)/shard_map/ppermute | solution.py:316
  77.2 6.9 %collective-permute-start.25 = (f16[224,128]{1,0:T(8,128)(2,1)S(1)}, f16[224,128]{1,0:T(8,128)(2,1)S(1)}, u32[]{:S(2)}, u32[]{:S(2)}) collective-permute-start(f16[224,128]{1,0:T(8,128)(2,1)S(1)} %convert_element_type.52), channel_id=1, source_target_pairs={{0,48},{16,32},{32,16},{48,0},{1,49},{17,33},{33,17},{49,1},{2,50}... | collective-permute-start | bytes 172040 | tf_op jit(solution)/shard_map/ppermute | solution.py:315
  84.1 0.4 collective-permute-start.24
  84.5 0.0 collective-permute-done.26
  84.5 2.0 %collective-permute-done.25 = f16[224,128]{1,0:T(8,128)(2,1)S(1)} collective-permute-done((f16[224,128]{1,0:T(8,128)(2,1)S(1)}, f16[224,128]{1,0:T(8,128)(2,1)S(1)}, u32[]{:S(2)}, u32[]{:S(2)}) %collective-permute-start.25) | collective-permute-done | bytes 57376 | tf_op jit(solution)/shard_map/ppermute | solution.py:315
  86.5 0.8 finish.1
  (18 shorter events, 0.3 us)
Async XLA Ops:
  0.0 16.6 %collective-permute-start.5 = (bf16[2304,1152]{1,0:T(8,128)(2,1)}, bf16[2304,1152]{1,0:T(8,128)(2,1)S(1)}, u32[]{:S(2)}, u32[]{:S(2)}) collective-permute-start(bf16[2304,1152]{1,0:T(8,128)(2,1)} %ref.2), channel_id=1, source_target_pairs={{0,32},{32,0},{1,33},{33,1},{2,34},{34,2},{3,35},{35,3},{4,36},{36... | collective-permute-start | bytes 15925256 | tf_op jit(solution)/shard_map/ppermute | solution.py:251
  1.4 18.3 %collective-permute-start.6 = (bf16[1152,2304]{1,0:T(8,128)(2,1)}, bf16[1152,2304]{1,0:T(8,128)(2,1)S(1)}, u32[]{:S(2)}, u32[]{:S(2)}) collective-permute-start(bf16[1152,2304]{1,0:T(8,128)(2,1)} %ref.3), channel_id=1, source_target_pairs={{0,32},{32,0},{1,33},{33,1},{2,34},{34,2},{3,35},{35,3},{4,36},{36... | collective-permute-start | bytes 15925256 | tf_op jit(solution)/shard_map/ppermute | solution.py:252
  2.7 7.8 %collective-permute-start.1 = (bf16[360,128]{1,0:T(8,128)(2,1)S(1)}, bf16[360,128]{1,0:T(8,128)(2,1)S(1)}, u32[]{:S(2)}, u32[]{:S(2)}) collective-permute-start(bf16[360,128]{1,0:T(8,128)(2,1)S(1)} %pack_codes.1), channel_id=1, source_target_pairs={{64,16},{16,64},{0,0},{80,80},{65,17},{17,65},{1,1},{81,81},{66,18... | collective-permute-start | bytes 276488 | tf_op jit(solution)/shard_map/ppermute | solution.py:263
  3.4 7.5 %collective-permute-start = (bf16[360,128]{1,0:T(8,128)(2,1)S(1)}, bf16[360,128]{1,0:T(8,128)(2,1)S(1)}, u32[]{:S(2)}, u32[]{:S(2)}) collective-permute-start(bf16[360,128]{1,0:T(8,128)(2,1)S(1)} %pack_codes.1), channel_id=1, source_target_pairs={{0,16},{80,64},{64,0},{16,80},{1,17},{81,65},{65,1},{17,81},{2,18}... | collective-permute-start | bytes 276488 | tf_op jit(solution)/shard_map/ppermute | solution.py:262
  10.9 7.6 %collective-permute-start.4 = (bf16[2,360,128]{2,1,0:T(8,128)(2,1)S(1)}, bf16[2,360,128]{2,1,0:T(8,128)(2,1)S(1)}, u32[]{:S(2)}, u32[]{:S(2)}) collective-permute-start(bf16[2,360,128]{2,1,0:T(8,128)(2,1)S(1)} %order_quarters.1.a_ref), channel_id=1, source_target_pairs={{0,2},{32,40},{1,3},{33,41},{2,0},{34,42},{3,1},{35,43},{4,6},{36,... | collective-permute-start | bytes 552968 | tf_op jit(solution)/shard_map/ppermute | solution.py:267
  13.9 5.9 %collective-permute-start.3 = (bf16[2,360,128]{2,1,0:T(8,128)(2,1)S(1)}, bf16[2,360,128]{2,1,0:T(8,128)(2,1)S(1)}, u32[]{:S(2)}, u32[]{:S(2)}) collective-permute-start(bf16[2,360,128]{2,1,0:T(8,128)(2,1)S(1)} %order_quarters.1.a_ref), channel_id=1, source_target_pairs={{0,1},{32,36},{1,2},{33,37},{2,3},{34,38},{3,0},{35,39},{4,5},{36,... | collective-permute-start | bytes 552968 | tf_op jit(solution)/shard_map/ppermute | solution.py:267
  14.3 5.5 %collective-permute-start.2 = (bf16[2,360,128]{2,1,0:T(8,128)(2,1)S(1)}, bf16[2,360,128]{2,1,0:T(8,128)(2,1)S(1)}, u32[]{:S(2)}, u32[]{:S(2)}) collective-permute-start(bf16[2,360,128]{2,1,0:T(8,128)(2,1)S(1)} %order_quarters.1.a_ref), channel_id=1, source_target_pairs={{0,3},{32,44},{1,0},{33,45},{2,1},{34,46},{3,2},{35,47},{4,7},{36,... | collective-permute-start | bytes 552968 | tf_op jit(solution)/shard_map/ppermute | solution.py:267
  20.2 8.3 %collective-permute-start.16 = (bf16[160,1152]{1,0:T(8,128)(2,1)S(1)}, bf16[160,1152]{1,0:T(8,128)(2,1)S(1)}, u32[]{:S(2)}, u32[]{:S(2)}) collective-permute-start(bf16[160,1152]{1,0:T(8,128)(2,1)S(1)} %get-tuple-element.34.m0), channel_id=1, source_target_pairs={{0,8},{32,34},{1,9},{33,35},{2,10},{34,32},{3,11},{35,33},{4,12},{... | collective-permute-start | bytes 1105928 | tf_op jit(solution)/shard_map/ppermute | solution.py:273
  22.7 9.7 %collective-permute-start.15 = (bf16[160,1152]{1,0:T(8,128)(2,1)S(1)}, bf16[160,1152]{1,0:T(8,128)(2,1)S(1)}, u32[]{:S(2)}, u32[]{:S(2)}) collective-permute-start(bf16[160,1152]{1,0:T(8,128)(2,1)S(1)} %get-tuple-element.34.m0), channel_id=1, source_target_pairs={{0,4},{32,33},{1,5},{33,34},{2,6},{34,35},{3,7},{35,32},{4,8},{36,... | collective-permute-start | bytes 1105928 | tf_op jit(solution)/shard_map/ppermute | solution.py:273
  23.0 9.4 %collective-permute-start.14 = (bf16[160,1152]{1,0:T(8,128)(2,1)S(1)}, bf16[160,1152]{1,0:T(8,128)(2,1)S(1)}, u32[]{:S(2)}, u32[]{:S(2)}) collective-permute-start(bf16[160,1152]{1,0:T(8,128)(2,1)S(1)} %get-tuple-element.34.m0), channel_id=1, source_target_pairs={{0,12},{32,35},{1,13},{33,32},{2,14},{34,33},{3,15},{35,34},{4,0},... | collective-permute-start | bytes 1105928 | tf_op jit(solution)/shard_map/ppermute | solution.py:273
  25.4 13.0 %collective-permute-start.9 = (bf16[160,1152]{1,0:T(8,128)(2,1)S(1)}, bf16[160,1152]{1,0:T(8,128)(2,1)S(1)}, u32[]{:S(2)}, u32[]{:S(2)}) collective-permute-start(bf16[160,1152]{1,0:T(8,128)(2,1)S(1)} %get-tuple-element.27.m0.after), channel_id=1, source_target_pairs={{0,8},{32,34},{1,9},{33,35},{2,10},{34,32},{3,11},{35,33},{4,12},{... | collective-permute-start | bytes 1105928 | tf_op jit(solution)/shard_map/ppermute | solution.py:273
  25.4 14.9 %collective-permute-start.8 = (bf16[160,1152]{1,0:T(8,128)(2,1)S(1)}, bf16[160,1152]{1,0:T(8,128)(2,1)S(1)}, u32[]{:S(2)}, u32[]{:S(2)}) collective-permute-start(bf16[160,1152]{1,0:T(8,128)(2,1)S(1)} %get-tuple-element.27.m0.after), channel_id=1, source_target_pairs={{0,4},{32,33},{1,5},{33,34},{2,6},{34,35},{3,7},{35,32},{4,8},{36,... | collective-permute-start | bytes 1105928 | tf_op jit(solution)/shard_map/ppermute | solution.py:273
  28.5 11.8 %collective-permute-start.7 = (bf16[160,1152]{1,0:T(8,128)(2,1)S(1)}, bf16[160,1152]{1,0:T(8,128)(2,1)S(1)}, u32[]{:S(2)}, u32[]{:S(2)}) collective-permute-start(bf16[160,1152]{1,0:T(8,128)(2,1)S(1)} %get-tuple-element.27.m0.after), channel_id=1, source_target_pairs={{0,12},{32,35},{1,13},{33,32},{2,14},{34,33},{3,15},{35,34},{4,0},... | collective-permute-start | bytes 1105928 | tf_op jit(solution)/shard_map/ppermute | solution.py:273
  33.8 9.8 %collective-permute-start.17 = (f16[168,1152]{1,0:T(8,128)(2,1)S(1)}, f16[168,1152]{1,0:T(8,128)(2,1)S(1)}, u32[]{:S(2)}, u32[]{:S(2)}) collective-permute-start(f16[168,1152]{1,0:T(8,128)(2,1)S(1)} %convert_element_type.46), channel_id=1, source_target_pairs={{0,64},{64,0},{1,65},{65,1},{2,66},{66,2},{3,67},{67,3},{4,68},{68... | collective-permute-start | bytes 1161224 | tf_op jit(solution)/shard_map/ppermute | solution.py:286
  41.7 10.5 %collective-permute-start.10 = (f16[168,1152]{1,0:T(8,128)(2,1)S(1)}, f16[168,1152]{1,0:T(8,128)(2,1)S(1)}, u32[]{:S(2)}, u32[]{:S(2)}) collective-permute-start(f16[168,1152]{1,0:T(8,128)(2,1)S(1)} %convert_element_type.42), channel_id=1, source_target_pairs={{0,64},{64,0},{1,65},{65,1},{2,66},{66,2},{3,67},{67,3},{4,68},{68... | collective-permute-start | bytes 1161224 | tf_op jit(solution)/shard_map/ppermute | solution.py:286
  46.5 11.1 %collective-permute-start.18 = (bf16[4,360,128]{2,1,0:T(8,128)(2,1)S(1)}, bf16[4,360,128]{2,1,0:T(8,128)(2,1)S(1)}, u32[]{:S(2)}, u32[]{:S(2)}) collective-permute-start(bf16[4,360,128]{2,1,0:T(8,128)(2,1)S(1)} %get-tuple-element.38), channel_id=1, source_target_pairs={{0,2},{32,40},{1,3},{33,41},{2,0},{34,42},{3,1},{35,43},{4,6},{36,... | collective-permute-start | bytes 1105928 | tf_op jit(solution)/shard_map/ppermute | solution.py:307
  49.5 9.4 %collective-permute-start.19 = (bf16[4,360,128]{2,1,0:T(8,128)(2,1)S(1)}, bf16[4,360,128]{2,1,0:T(8,128)(2,1)S(1)}, u32[]{:S(2)}, u32[]{:S(2)}) collective-permute-start(bf16[4,360,128]{2,1,0:T(8,128)(2,1)S(1)} %get-tuple-element.39), channel_id=1, source_target_pairs={{0,1},{32,36},{1,2},{33,37},{2,3},{34,38},{3,0},{35,39},{4,5},{36,... | collective-permute-start | bytes 1105928 | tf_op jit(solution)/shard_map/ppermute | solution.py:307
  49.9 9.1 %collective-permute-start.20 = (bf16[4,360,128]{2,1,0:T(8,128)(2,1)S(1)}, bf16[4,360,128]{2,1,0:T(8,128)(2,1)S(1)}, u32[]{:S(2)}, u32[]{:S(2)}) collective-permute-start(bf16[4,360,128]{2,1,0:T(8,128)(2,1)S(1)} %get-tuple-element.40), channel_id=1, source_target_pairs={{0,3},{32,44},{1,0},{33,45},{2,1},{34,46},{3,2},{35,47},{4,7},{36,... | collective-permute-start | bytes 1105928 | tf_op jit(solution)/shard_map/ppermute | solution.py:307
  55.1 8.3 %collective-permute-start.11 = (bf16[4,360,128]{2,1,0:T(8,128)(2,1)S(1)}, bf16[4,360,128]{2,1,0:T(8,128)(2,1)S(1)}, u32[]{:S(2)}, u32[]{:S(2)}) collective-permute-start(bf16[4,360,128]{2,1,0:T(8,128)(2,1)S(1)} %get-tuple-element.31), channel_id=1, source_target_pairs={{0,2},{32,40},{1,3},{33,41},{2,0},{34,42},{3,1},{35,43},{4,6},{36,... | collective-permute-start | bytes 1105928 | tf_op jit(solution)/shard_map/ppermute | solution.py:307
  56.2 11.0 %collective-permute-start.12 = (bf16[4,360,128]{2,1,0:T(8,128)(2,1)S(1)}, bf16[4,360,128]{2,1,0:T(8,128)(2,1)S(1)}, u32[]{:S(2)}, u32[]{:S(2)}) collective-permute-start(bf16[4,360,128]{2,1,0:T(8,128)(2,1)S(1)} %get-tuple-element.32), channel_id=1, source_target_pairs={{0,1},{32,36},{1,2},{33,37},{2,3},{34,38},{3,0},{35,39},{4,5},{36,... | collective-permute-start | bytes 1105928 | tf_op jit(solution)/shard_map/ppermute | solution.py:307
  57.6 9.7 %collective-permute-start.13 = (bf16[4,360,128]{2,1,0:T(8,128)(2,1)S(1)}, bf16[4,360,128]{2,1,0:T(8,128)(2,1)S(1)}, u32[]{:S(2)}, u32[]{:S(2)}) collective-permute-start(bf16[4,360,128]{2,1,0:T(8,128)(2,1)S(1)} %get-tuple-element.33), channel_id=1, source_target_pairs={{0,3},{32,44},{1,0},{33,45},{2,1},{34,46},{3,2},{35,47},{4,7},{36,... | collective-permute-start | bytes 1105928 | tf_op jit(solution)/shard_map/ppermute | solution.py:307
  67.6 6.1 %collective-permute-start.21 = (bf16[720,128]{1,0:T(8,128)(2,1)S(1)}, bf16[720,128]{1,0:T(8,128)(2,1)S(1)}, u32[]{:S(2)}, u32[]{:S(2)}) collective-permute-start(bf16[720,128]{1,0:T(8,128)(2,1)S(1)} %get-tuple-element.42), channel_id=1, source_target_pairs={{0,8},{32,34},{1,9},{33,35},{2,10},{34,32},{3,11},{35,33},{4,12},{... | collective-permute-start | bytes 552968 | tf_op jit(solution)/shard_map/ppermute | solution.py:310
  69.2 6.4 %collective-permute-start.22 = (bf16[720,128]{1,0:T(8,128)(2,1)S(1)}, bf16[720,128]{1,0:T(8,128)(2,1)S(1)}, u32[]{:S(2)}, u32[]{:S(2)}) collective-permute-start(bf16[720,128]{1,0:T(8,128)(2,1)S(1)} %get-tuple-element.43), channel_id=1, source_target_pairs={{0,4},{32,33},{1,5},{33,34},{2,6},{34,35},{3,7},{35,32},{4,8},{36,... | collective-permute-start | bytes 552968 | tf_op jit(solution)/shard_map/ppermute | solution.py:310
  70.3 5.2 %collective-permute-start.23 = (bf16[720,128]{1,0:T(8,128)(2,1)S(1)}, bf16[720,128]{1,0:T(8,128)(2,1)S(1)}, u32[]{:S(2)}, u32[]{:S(2)}) collective-permute-start(bf16[720,128]{1,0:T(8,128)(2,1)S(1)} %get-tuple-element.44), channel_id=1, source_target_pairs={{0,12},{32,35},{1,13},{33,32},{2,14},{34,33},{3,15},{35,34},{4,0},... | collective-permute-start | bytes 552968 | tf_op jit(solution)/shard_map/ppermute | solution.py:310
  75.9 8.6 %collective-permute-start.26 = (f16[224,128]{1,0:T(8,128)(2,1)S(1)}, f16[224,128]{1,0:T(8,128)(2,1)S(1)}, u32[]{:S(2)}, u32[]{:S(2)}) collective-permute-start(f16[224,128]{1,0:T(8,128)(2,1)S(1)} %convert_element_type.54), channel_id=1, source_target_pairs={{0,16},{16,0},{1,17},{17,1},{2,18},{18,2},{3,19},{19,3},{4,20},{20... | collective-permute-start | bytes 172040 | tf_op jit(solution)/shard_map/ppermute | solution.py:316
  77.2 9.3 %collective-permute-start.25 = (f16[224,128]{1,0:T(8,128)(2,1)S(1)}, f16[224,128]{1,0:T(8,128)(2,1)S(1)}, u32[]{:S(2)}, u32[]{:S(2)}) collective-permute-start(f16[224,128]{1,0:T(8,128)(2,1)S(1)} %convert_element_type.52), channel_id=1, source_target_pairs={{0,48},{16,32},{32,16},{48,0},{1,49},{17,33},{33,17},{49,1},{2,50}... | collective-permute-start | bytes 172040 | tf_op jit(solution)/shard_map/ppermute | solution.py:315
  84.1 2.4 %collective-permute-start.24 = (f16[224,128]{1,0:T(8,128)(2,1)S(1)}, f16[224,128]{1,0:T(8,128)(2,1)S(1)}, u32[]{:S(2)}, u32[]{:S(2)}) collective-permute-start(f16[224,128]{1,0:T(8,128)(2,1)S(1)} %convert_element_type.50), channel_id=1, source_target_pairs={{0,32},{32,0},{1,33},{33,1},{2,34},{34,2},{3,35},{35,3},{4,36},{36... | collective-permute-start | bytes 172040 | tf_op jit(solution)/shard_map/ppermute | solution.py:314

commit v7 on v6

--- a/solution.py
+++ b/solution.py
@@ -18,7 +18,7 @@
 ARRIVES = (0, 2, 3, 1)
 
 
-def first_axis(step):
+def second_axis(step):
     pairs = []
     for y in range(4):
         for x in range(4):
@@ -27,7 +27,7 @@
     return pairs
 
 
-def second_axis(step):
+def first_axis(step):
     pairs = []
     for y in range(4):
         for x in range(4):
@@ -90,23 +90,18 @@
 def merge_codes(a_ref, b_ref, c_ref, d_ref, after1, after2, *outs):
     del after1, after2
     pieces = (a_ref, b_ref, c_ref, d_ref)
-    src = lax.broadcasted_iota(jnp.int32, (512, 128), 0)
-    dst = lax.broadcasted_iota(jnp.int32, (512, 128), 1)
     for q, o_ref in enumerate(outs):
         for j, ref in enumerate(pieces):
             o_ref[:, 256 * j : 256 * j + 128] = ref[q, 0:QT]
             o_ref[:, 256 * j + 128 : 256 * j + 256] = ref[q, QT : 2 * QT]
-        tails = jnp.concatenate([ref[q, 2 * QT : 360] for ref in pieces], axis=1)
-        groups = []
-        for j in range(4):
-            place = (src // 128 == dst // 32) & (src % 128 == 32 * j + dst % 32)
-            groups.append(dot(tails, jnp.where(place, 1.0, 0.0).astype(BF)))
+        tails = [ref[q, 2 * QT : 360].astype(F32) for ref in pieces]
+        groups = [jnp.concatenate([t[:, 32 * j : 32 * j + 32] for t in tails], axis=1) for j in range(4)]
         o_ref[:, 1024:1152] = jnp.concatenate(groups, axis=0).astype(BF)
 
 
 def own_place():
     c, y, x = lax.axis_index("c"), lax.axis_index("y"), lax.axis_index("x")
-    return c, jnp.where(c == 0, x, y), jnp.where(c == 0, y, x)
+    return c, jnp.where(c == 0, y, x), jnp.where(c == 0, x, y)
 
 
 def arrange_rows(own, ref, w_ref, sem):
@@ -115,7 +110,7 @@
         s = lax.rem(second + 4 - ARRIVES[i], 4)
         for j in range(4):
             f = lax.rem(first + 4 - GATHER[j], 4)
-            y, x = jnp.where(c == 0, s, f), jnp.where(c == 0, f, s)
+            y, x = jnp.where(c == 0, f, s), jnp.where(c == 0, s, f)
             row = lax.rem(y, 2) * UNITS + x * PIECE
 
             @pl.when((lax.div(y, 2) == c) == own)
@@ -184,7 +179,7 @@
     for rel, o in zip(STEPS, (o0, o1, o2, o3)):
         f = lax.rem(first + rel, 4)
         for s in range(4):
-            at = pl.ds(pl.multiple_of(jnp.where(c == 0, s * 4 + f, f * 4 + s) * CHIP_COLS, 8), CHIP_COLS)
+            at = pl.ds(pl.multiple_of(jnp.where(c == 0, f * 4 + s, s * 4 + f) * CHIP_COLS, 8), CHIP_COLS)
             for p in range(2):
                 both = jnp.concatenate([t_ref[2 * p, at], t_ref[2 * p + 1, at]], axis=0)
                 o[s, 144 * p : 144 * p + 144] = both.astype(o.dtype)
@@ -284,7 +279,7 @@
         preacts.append(preact)
         sends.append(send.astype(jnp.float16))
     gots = [lax.ppermute(send, "zh", swap) for send in sends]
-    columns = call(stage_own, pltpu.VMEM((UNITS, 4 * UNITS), BF), [ANY] * 2, dma, nbytes=half, name="stage_own")(w_out, merged[0])
+    columns = call(stage_own, pltpu.VMEM((UNITS, 4 * UNITS), BF), [ANY] * 2, dma, nbytes=half, name="stage_own")(w_out, rows)
     columns = call(
         stage_other, pltpu.VMEM((UNITS, 4 * UNITS), BF), [ANY, VMEM], dma, nbytes=half, alias={1: 0}, name="stage_other"
     )(w_out_other, columns)

time: 89 us -> 87.9 us (0.988)
  waiting for transfers between devices: 19.5 us -> 18 us
    ppermute x6, starting transfers between devices: 7.94 us -> 8.99 us  [shards(): lax.ppermute(m, YX, second_axis(k))]
    ppermute x6, waiting for transfers between devices: 3.84 us -> 2.82 us  [shards(): lax.ppermute(m, YX, second_axis(k))]
  transfers between devices with their start and end apart: 27 -> 27, of which waited for: 11 -> 11; matrix products, arithmetic and copies ran while one was open for 1% -> 1% of each run, Pallas kernels for 21% -> 22%
where the time goes in v7:
time: 87.9 us; the launch traced here: 86.4 us
  starting transfers between devices  46.8 us (53%)
  Pallas kernels  20.3 us (23%)
  waiting for transfers between devices  18 us (20%)
    ppermute x6, starting transfers between devices, shards(): lax.ppermute(v, YX, first_axis(k))  9.43 us
    ppermute x6, starting transfers between devices, shards(): lax.ppermute(m, YX, second_axis(k))  8.99 us
    ppermute x6, waiting for transfers between devices, shards(): lax.ppermute(v, YX, first_axis(k))  8.26 us
    ppermute x1, starting transfers between devices, shards(): lax.ppermute(to_czl, ('c', 'zl'), [(0, 3), (1, 2), (2, 1), (3, 0)])  6.32 us
    ppermute x3, starting transfers between devices, shards(): around = [lax.ppermute(piece, YX, first_axis(k)) for k in GATHER[1:]]  5.49 us
    pallas_call x2, Pallas kernels, shards(): call(project_out, [shape(part, F32)] + [shape(part, BF)] * 3, [VMEM] * 2,...  5.08 us
    ppermute x1, starting transfers between devices, shards(): one = lax.ppermute(packed, z, [(0, 1), (3, 2), (2, 0), (1, 3)])  4.67 us
    ppermute x3, starting transfers between devices, shards(): lax.ppermute(v, YX, second_axis(k))  4.34 us
  transfers between devices with their start and end apart: 27, of which 11 were waited for; matrix products, arithmetic and copies ran while one was open for 1% of the time, Pallas kernels for 22%

profile of v7, /device:TPU:1, one launch (start us, length us, event | category | flops | bytes accessed | tf_op | source)
XLA Modules:
  0.0 86.4 jit_solution(2938718893640028923)
XLA Ops:
  0.0 1.4 %collective-permute-start.5 = (bf16[2304,1152]{1,0:T(8,128)(2,1)}, bf16[2304,1152]{1,0:T(8,128)(2,1)S(1)}, u32[]{:S(2)}, u32[]{:S(2)}) collective-permute-start(bf16[2304,1152]{1,0:T(8,128)(2,1)} %ref.2), channel_id=1, source_target_pairs={{0,32},{32,0},{1,33},{33,1},{2,34},{34,2},{3,35},{35,3},{4,36},{36... | collective-permute-start | bytes 15925256 | tf_op jit(solution)/shard_map/ppermute | solution.py:246
  1.4 0.0 collective-permute-start.6
  1.4 1.3 %pack_codes.1 = bf16[360,128]{1,0:T(8,128)(2,1)S(1)} custom-call(bf16[160,288]{1,0:T(8,128)(2,1)} %codes_ref.1, s32[1,160]{1,0:T(1,128)} %bitcast.2), custom_call_target="tpu_custom_call" | custom-call | tf_op jit(solution)/shard_map/pack_codes/pallas_call | solution.py:250
  2.7 0.7 collective-permute-start.1
  3.4 4.7 %collective-permute-start = (bf16[360,128]{1,0:T(8,128)(2,1)S(1)}, bf16[360,128]{1,0:T(8,128)(2,1)S(1)}, u32[]{:S(2)}, u32[]{:S(2)}) collective-permute-start(bf16[360,128]{1,0:T(8,128)(2,1)S(1)} %pack_codes.1), channel_id=1, source_target_pairs={{0,16},{80,64},{64,0},{16,80},{1,17},{81,65},{65,1},{17,81},{2,18}... | collective-permute-start | bytes 276488 | tf_op jit(solution)/shard_map/ppermute | solution.py:257
  8.0 2.5 %arrange_own.1.after.half_ref = bf16[4608,1152]{1,0:T(8,128)(2,1)S(1)} custom-call(bf16[2304,1152]{1,0:T(8,128)(2,1)} %ref.2), custom_call_target="tpu_custom_call" | custom-call | bytes 10616832 | tf_op jit(solution)/shard_map/arrange_own/pallas_call | solution.py:260
  10.5 0.0 collective-permute-done.1.two
  10.5 0.3 collective-permute-done.one
  10.9 2.8 %collective-permute-start.4 = (bf16[2,360,128]{2,1,0:T(8,128)(2,1)S(1)}, bf16[2,360,128]{2,1,0:T(8,128)(2,1)S(1)}, u32[]{:S(2)}, u32[]{:S(2)}) collective-permute-start(bf16[2,360,128]{2,1,0:T(8,128)(2,1)S(1)} %order_quarters.1.a_ref), channel_id=1, source_target_pairs={{0,8},{32,34},{1,9},{33,35},{2,10},{34,32},{3,11},{35,33},{4,12},{... | collective-permute-start | bytes 552968 | tf_op jit(solution)/shard_map/ppermute | solution.py:262
  13.7 0.3 collective-permute-start.3
  14.0 2.3 %collective-permute-start.2 = (bf16[2,360,128]{2,1,0:T(8,128)(2,1)S(1)}, bf16[2,360,128]{2,1,0:T(8,128)(2,1)S(1)}, u32[]{:S(2)}, u32[]{:S(2)}) collective-permute-start(bf16[2,360,128]{2,1,0:T(8,128)(2,1)S(1)} %order_quarters.1.a_ref), channel_id=1, source_target_pairs={{0,12},{32,35},{1,13},{33,32},{2,14},{34,33},{3,15},{35,34},{4,0},... | collective-permute-start | bytes 552968 | tf_op jit(solution)/shard_map/ppermute | solution.py:262
  16.4 0.0 collective-permute-done.5.ref
  16.4 1.9 %arrange_other.1.after1.w_ref.after = bf16[4608,1152]{1,0:T(8,128)(2,1)S(1)} custom-call(bf16[2304,1152]{1,0:T(8,128)(2,1)S(1)} %collective-permute-done.5.ref, bf16[4608,1152]{1,0:T(8,128)(2,1)S(1)} %arrange_own.1.after.half_ref), custom_call_target="tpu_custom_call", output_to_operand_aliasing={{}: (1, {})} | custom-call | bytes 10616832 | tf_op jit(solution)/shard_map/arrange_other/pallas_call | solution.py:263
  18.3 0.0 collective-permute-done.4.d_ref
  18.3 1.0 %collective-permute-done.3.c_ref = bf16[2,360,128]{2,1,0:T(8,128)(2,1)S(1)} collective-permute-done((bf16[2,360,128]{2,1,0:T(8,128)(2,1)S(1)}, bf16[2,360,128]{2,1,0:T(8,128)(2,1)S(1)}, u32[]{:S(2)}, u32[]{:S(2)}) %collective-permute-start.3) | collective-permute-done | bytes 184352 | tf_op jit(solution)/shard_map/ppermute | solution.py:262
  19.3 0.2 merge_codes.1
  19.6 3.0 %collective-permute-start.16 = (bf16[160,1152]{1,0:T(8,128)(2,1)S(1)}, bf16[160,1152]{1,0:T(8,128)(2,1)S(1)}, u32[]{:S(2)}, u32[]{:S(2)}) collective-permute-start(bf16[160,1152]{1,0:T(8,128)(2,1)S(1)} %get-tuple-element.34.m0), channel_id=1, source_target_pairs={{0,2},{32,40},{1,3},{33,41},{2,0},{34,42},{3,1},{35,43},{4,6},{36,... | collective-permute-start | bytes 1105928 | tf_op jit(solution)/shard_map/ppermute | solution.py:268
  22.5 0.4 collective-permute-start.15
  22.9 2.3 %collective-permute-start.14 = (bf16[160,1152]{1,0:T(8,128)(2,1)S(1)}, bf16[160,1152]{1,0:T(8,128)(2,1)S(1)}, u32[]{:S(2)}, u32[]{:S(2)}) collective-permute-start(bf16[160,1152]{1,0:T(8,128)(2,1)S(1)} %get-tuple-element.34.m0), channel_id=1, source_target_pairs={{0,3},{32,44},{1,0},{33,45},{2,1},{34,46},{3,2},{35,47},{4,7},{36,... | collective-permute-start | bytes 1105928 | tf_op jit(solution)/shard_map/ppermute | solution.py:268
  25.2 0.0 collective-permute-start.9
  25.2 0.6 collective-permute-start.8
  25.8 2.0 %collective-permute-done.16.m1 = bf16[160,1152]{1,0:T(8,128)(2,1)S(1)} collective-permute-done((bf16[160,1152]{1,0:T(8,128)(2,1)S(1)}, bf16[160,1152]{1,0:T(8,128)(2,1)S(1)}, u32[]{:S(2)}, u32[]{:S(2)}) %collective-permute-start.16) | collective-permute-done | bytes 368672 | tf_op jit(solution)/shard_map/ppermute | solution.py:268
  27.8 2.7 %collective-permute-start.7 = (bf16[160,1152]{1,0:T(8,128)(2,1)S(1)}, bf16[160,1152]{1,0:T(8,128)(2,1)S(1)}, u32[]{:S(2)}, u32[]{:S(2)}) collective-permute-start(bf16[160,1152]{1,0:T(8,128)(2,1)S(1)} %get-tuple-element.27.m0), channel_id=1, source_target_pairs={{0,3},{32,44},{1,0},{33,45},{2,1},{34,46},{3,2},{35,47},{4,7},{36,... | collective-permute-start | bytes 1105928 | tf_op jit(solution)/shard_map/ppermute | solution.py:268
  30.5 1.1 %project_early.3.early_ref = f32[160,1152]{1,0:T(8,128)S(1)} custom-call(bf16[160,1152]{1,0:T(8,128)(2,1)S(1)} %get-tuple-element.34.m0, bf16[160,1152]{1,0:T(8,128)(2,1)S(1)} %collective-permute-done.16.m1, bf16[4608,1152]{1,0:T(8,128)(2,1)S(1)} %arrange_other.1.after1.w_ref.after), custom_call_target="tpu_custom_call" | custom-call | flops 849346560 | bytes 5308416 | tf_op jit(solution)/shard_map/project_early/pallas_call | solution.py:273
  31.7 0.1 collective-permute-done.15.m3
  31.7 0.3 collective-permute-done.14.m2
  32.1 1.3 %project_in.3 = (f32[160,1152]{1,0:T(8,128)S(1)}, f32[168,1152]{1,0:T(8,128)S(1)}) custom-call(bf16[160,1152]{1,0:T(8,128)(2,1)S(1)} %collective-permute-done.14.m2, bf16[160,1152]{1,0:T(8,128)(2,1)S(1)} %collective-permute-done.15.m3, bf16[4608,1152]{1,0:T(8,128)(2,1)S(1)} %arrange_other.1.after1.w_ref.after, f32[160,1152]{1,0:T(8,128)S(1)} %project_early.3.early_ref), custom_call_target="tpu_custom_call" | custom-call | flops 849346560 | bytes 5308416 | tf_op jit(solution)/shard_map/project_in/pallas_call | solution.py:278
  33.5 2.1 %collective-permute-start.17 = (f16[168,1152]{1,0:T(8,128)(2,1)S(1)}, f16[168,1152]{1,0:T(8,128)(2,1)S(1)}, u32[]{:S(2)}, u32[]{:S(2)}) collective-permute-start(f16[168,1152]{1,0:T(8,128)(2,1)S(1)} %convert_element_type.46), channel_id=1, source_target_pairs={{0,64},{64,0},{1,65},{65,1},{2,66},{66,2},{3,67},{67,3},{4,68},{68... | collective-permute-start | bytes 1161224 | tf_op jit(solution)/shard_map/ppermute | solution.py:281
  35.5 2.5 %stage_own.1.half_ref = bf16[1152,4608]{1,0:T(8,128)(2,1)S(1)} custom-call(bf16[1152,2304]{1,0:T(8,128)(2,1)} %ref.3, bf16[4608,1152]{1,0:T(8,128)(2,1)S(1)} %arrange_other.1.after1.w_ref.after), custom_call_target="tpu_custom_call" | custom-call | bytes 10616832 | tf_op jit(solution)/shard_map/stage_own/pallas_call | solution.py:282
  38.0 0.4 stage_other.1.w_ref
  38.5 0.0 collective-permute-done.9.m1
  38.5 1.1 %project_early.2.early_ref = f32[160,1152]{1,0:T(8,128)S(1)} custom-call(bf16[160,1152]{1,0:T(8,128)(2,1)S(1)} %get-tuple-element.27.m0, bf16[160,1152]{1,0:T(8,128)(2,1)S(1)} %collective-permute-done.9.m1, bf16[4608,1152]{1,0:T(8,128)(2,1)S(1)} %arrange_other.1.after1.w_ref.after), custom_call_target="tpu_custom_call" | custom-call | flops 849346560 | bytes 5308416 | tf_op jit(solution)/shard_map/project_early/pallas_call | solution.py:273
  39.6 0.0 collective-permute-done.8.m3
  39.6 0.4 collective-permute-done.7.m2
  40.0 1.3 %project_in.2 = (f32[160,1152]{1,0:T(8,128)S(1)}, f32[168,1152]{1,0:T(8,128)S(1)}) custom-call(bf16[160,1152]{1,0:T(8,128)(2,1)S(1)} %collective-permute-done.7.m2, bf16[160,1152]{1,0:T(8,128)(2,1)S(1)} %collective-permute-done.8.m3, bf16[4608,1152]{1,0:T(8,128)(2,1)S(1)} %arrange_other.1.after1.w_ref.after, f32[160,1152]{1,0:T(8,128)S(1)} %project_early.2.early_ref), custom_call_target="tpu_custom_call" | custom-call | flops 849346560 | bytes 5308416 | tf_op jit(solution)/shard_map/project_in/pallas_call | solution.py:278
  41.4 2.2 %collective-permute-start.10 = (f16[168,1152]{1,0:T(8,128)(2,1)S(1)}, f16[168,1152]{1,0:T(8,128)(2,1)S(1)}, u32[]{:S(2)}, u32[]{:S(2)}) collective-permute-start(f16[168,1152]{1,0:T(8,128)(2,1)S(1)} %convert_element_type.42), channel_id=1, source_target_pairs={{0,64},{64,0},{1,65},{65,1},{2,66},{66,2},{3,67},{67,3},{4,68},{68... | collective-permute-start | bytes 1161224 | tf_op jit(solution)/shard_map/ppermute | solution.py:281
  43.7 0.3 fusion.15.a_ref
  44.0 2.5 %project_out.3 = (f32[4,360,128]{2,1,0:T(8,128)S(1)}, bf16[4,360,128]{2,1,0:T(8,128)(2,1)S(1)}, bf16[4,360,128]{2,1,0:T(8,128)(2,1)S(1)}, bf16[4,360,128]{2,1,0:T(8,128)(2,1)S(1)}) custom-call(bf16[160,1152]{1,0:T(8,128)(2,1)S(1)} %fusion.15.a_ref, bf16[1152,4608]{1,0:T(8,128)(2,1)S(1)} %stage_other.1.w_ref), custom_call_target="tpu_custom_call" | custom-call | flops 1698693120 | bytes 10616832 | tf_op jit(solution)/shard_map/project_out/pallas_call | solution.py:292
  46.6 2.8 %collective-permute-start.18 = (bf16[4,360,128]{2,1,0:T(8,128)(2,1)S(1)}, bf16[4,360,128]{2,1,0:T(8,128)(2,1)S(1)}, u32[]{:S(2)}, u32[]{:S(2)}) collective-permute-start(bf16[4,360,128]{2,1,0:T(8,128)(2,1)S(1)} %get-tuple-element.38), channel_id=1, source_target_pairs={{0,8},{32,34},{1,9},{33,35},{2,10},{34,32},{3,11},{35,33},{4,12},{... | collective-permute-start | bytes 1105928 | tf_op jit(solution)/shard_map/ppermute | solution.py:302
  49.4 0.3 collective-permute-start.19
  49.7 2.4 %collective-permute-start.20 = (bf16[4,360,128]{2,1,0:T(8,128)(2,1)S(1)}, bf16[4,360,128]{2,1,0:T(8,128)(2,1)S(1)}, u32[]{:S(2)}, u32[]{:S(2)}) collective-permute-start(bf16[4,360,128]{2,1,0:T(8,128)(2,1)S(1)} %get-tuple-element.40), channel_id=1, source_target_pairs={{0,12},{32,35},{1,13},{33,32},{2,14},{34,33},{3,15},{35,34},{4,0},... | collective-permute-start | bytes 1105928 | tf_op jit(solution)/shard_map/ppermute | solution.py:302
  52.1 0.0 collective-permute-done.10
  52.1 0.3 fusion.7.a_ref
  52.4 2.5 %project_out.2 = (f32[4,360,128]{2,1,0:T(8,128)S(1)}, bf16[4,360,128]{2,1,0:T(8,128)(2,1)S(1)}, bf16[4,360,128]{2,1,0:T(8,128)(2,1)S(1)}, bf16[4,360,128]{2,1,0:T(8,128)(2,1)S(1)}) custom-call(bf16[160,1152]{1,0:T(8,128)(2,1)S(1)} %fusion.7.a_ref, bf16[1152,4608]{1,0:T(8,128)(2,1)S(1)} %stage_other.1.w_ref), custom_call_target="tpu_custom_call" | custom-call | flops 1698693120 | bytes 10616832 | tf_op jit(solution)/shard_map/project_out/pallas_call | solution.py:292
  55.0 1.3 %collective-permute-start.11 = (bf16[4,360,128]{2,1,0:T(8,128)(2,1)S(1)}, bf16[4,360,128]{2,1,0:T(8,128)(2,1)S(1)}, u32[]{:S(2)}, u32[]{:S(2)}) collective-permute-start(bf16[4,360,128]{2,1,0:T(8,128)(2,1)S(1)} %get-tuple-element.31), channel_id=1, source_target_pairs={{0,8},{32,34},{1,9},{33,35},{2,10},{34,32},{3,11},{35,33},{4,12},{... | collective-permute-start | bytes 1105928 | tf_op jit(solution)/shard_map/ppermute | solution.py:302
  56.2 0.9 %collective-permute-start.12 = (bf16[4,360,128]{2,1,0:T(8,128)(2,1)S(1)}, bf16[4,360,128]{2,1,0:T(8,128)(2,1)S(1)}, u32[]{:S(2)}, u32[]{:S(2)}) collective-permute-start(bf16[4,360,128]{2,1,0:T(8,128)(2,1)S(1)} %get-tuple-element.32), channel_id=1, source_target_pairs={{0,4},{32,33},{1,5},{33,34},{2,6},{34,35},{3,7},{35,32},{4,8},{36,... | collective-permute-start | bytes 1105928 | tf_op jit(solution)/shard_map/ppermute | solution.py:302
  57.2 1.7 %collective-permute-start.13 = (bf16[4,360,128]{2,1,0:T(8,128)(2,1)S(1)}, bf16[4,360,128]{2,1,0:T(8,128)(2,1)S(1)}, u32[]{:S(2)}, u32[]{:S(2)}) collective-permute-start(bf16[4,360,128]{2,1,0:T(8,128)(2,1)S(1)} %get-tuple-element.33), channel_id=1, source_target_pairs={{0,12},{32,35},{1,13},{33,32},{2,14},{34,33},{3,15},{35,34},{4,0},... | collective-permute-start | bytes 1105928 | tf_op jit(solution)/shard_map/ppermute | solution.py:302
  58.9 0.0 collective-permute-done.19.c1
  58.9 4.3 %collective-permute-done.11.b0 = bf16[4,360,128]{2,1,0:T(8,128)(2,1)S(1)} collective-permute-done((bf16[4,360,128]{2,1,0:T(8,128)(2,1)S(1)}, bf16[4,360,128]{2,1,0:T(8,128)(2,1)S(1)}, u32[]{:S(2)}, u32[]{:S(2)}) %collective-permute-start.11) | collective-permute-done | bytes 368672 | tf_op jit(solution)/shard_map/ppermute | solution.py:302
  63.3 3.9 %collective-permute-done.12.c0 = bf16[4,360,128]{2,1,0:T(8,128)(2,1)S(1)} collective-permute-done((bf16[4,360,128]{2,1,0:T(8,128)(2,1)S(1)}, bf16[4,360,128]{2,1,0:T(8,128)(2,1)S(1)}, u32[]{:S(2)}, u32[]{:S(2)}) %collective-permute-start.12) | collective-permute-done | bytes 368672 | tf_op jit(solution)/shard_map/ppermute | solution.py:302
  67.2 0.0 collective-permute-done.13.d0
  67.2 0.4 add_first.1
  67.5 1.7 %collective-permute-start.21 = (bf16[720,128]{1,0:T(8,128)(2,1)S(1)}, bf16[720,128]{1,0:T(8,128)(2,1)S(1)}, u32[]{:S(2)}, u32[]{:S(2)}) collective-permute-start(bf16[720,128]{1,0:T(8,128)(2,1)S(1)} %get-tuple-element.42), channel_id=1, source_target_pairs={{0,2},{32,40},{1,3},{33,41},{2,0},{34,42},{3,1},{35,43},{4,6},{36,... | collective-permute-start | bytes 552968 | tf_op jit(solution)/shard_map/ppermute | solution.py:305
  69.2 1.1 %collective-permute-start.22 = (bf16[720,128]{1,0:T(8,128)(2,1)S(1)}, bf16[720,128]{1,0:T(8,128)(2,1)S(1)}, u32[]{:S(2)}, u32[]{:S(2)}) collective-permute-start(bf16[720,128]{1,0:T(8,128)(2,1)S(1)} %get-tuple-element.43), channel_id=1, source_target_pairs={{0,1},{32,36},{1,2},{33,37},{2,3},{34,38},{3,0},{35,39},{4,5},{36,... | collective-permute-start | bytes 552968 | tf_op jit(solution)/shard_map/ppermute | solution.py:305
  70.2 1.6 %collective-permute-start.23 = (bf16[720,128]{1,0:T(8,128)(2,1)S(1)}, bf16[720,128]{1,0:T(8,128)(2,1)S(1)}, u32[]{:S(2)}, u32[]{:S(2)}) collective-permute-start(bf16[720,128]{1,0:T(8,128)(2,1)S(1)} %get-tuple-element.44), channel_id=1, source_target_pairs={{0,3},{32,44},{1,0},{33,45},{2,1},{34,46},{3,2},{35,47},{4,7},{36,... | collective-permute-start | bytes 552968 | tf_op jit(solution)/shard_map/ppermute | solution.py:305
  71.9 1.7 %collective-permute-done.21.b = bf16[720,128]{1,0:T(8,128)(2,1)S(1)} collective-permute-done((bf16[720,128]{1,0:T(8,128)(2,1)S(1)}, bf16[720,128]{1,0:T(8,128)(2,1)S(1)}, u32[]{:S(2)}, u32[]{:S(2)}) %collective-permute-start.21) | collective-permute-done | bytes 184352 | tf_op jit(solution)/shard_map/ppermute | solution.py:305
  73.6 1.9 %collective-permute-done.22.c = bf16[720,128]{1,0:T(8,128)(2,1)S(1)} collective-permute-done((bf16[720,128]{1,0:T(8,128)(2,1)S(1)}, bf16[720,128]{1,0:T(8,128)(2,1)S(1)}, u32[]{:S(2)}, u32[]{:S(2)}) %collective-permute-start.22) | collective-permute-done | bytes 184352 | tf_op jit(solution)/shard_map/ppermute | solution.py:305
  75.5 0.3 add_second.1
  75.8 0.8 collective-permute-start.26
  76.6 6.3 %collective-permute-start.25 = (f16[224,128]{1,0:T(8,128)(2,1)S(1)}, f16[224,128]{1,0:T(8,128)(2,1)S(1)}, u32[]{:S(2)}, u32[]{:S(2)}) collective-permute-start(f16[224,128]{1,0:T(8,128)(2,1)S(1)} %convert_element_type.52), channel_id=1, source_target_pairs={{0,48},{16,32},{32,16},{48,0},{1,49},{17,33},{33,17},{49,1},{2,50}... | collective-permute-start | bytes 172040 | tf_op jit(solution)/shard_map/ppermute | solution.py:310
  83.0 0.4 collective-permute-start.24
  83.4 0.0 collective-permute-done.26
  83.4 2.0 %collective-permute-done.25 = f16[224,128]{1,0:T(8,128)(2,1)S(1)} collective-permute-done((f16[224,128]{1,0:T(8,128)(2,1)S(1)}, f16[224,128]{1,0:T(8,128)(2,1)S(1)}, u32[]{:S(2)}, u32[]{:S(2)}) %collective-permute-start.25) | collective-permute-done | bytes 57376 | tf_op jit(solution)/shard_map/ppermute | solution.py:310
  85.4 0.8 finish.1
  (18 shorter events, 0.3 us)
Async XLA Ops:
  0.0 16.4 %collective-permute-start.5 = (bf16[2304,1152]{1,0:T(8,128)(2,1)}, bf16[2304,1152]{1,0:T(8,128)(2,1)S(1)}, u32[]{:S(2)}, u32[]{:S(2)}) collective-permute-start(bf16[2304,1152]{1,0:T(8,128)(2,1)} %ref.2), channel_id=1, source_target_pairs={{0,32},{32,0},{1,33},{33,1},{2,34},{34,2},{3,35},{35,3},{4,36},{36... | collective-permute-start | bytes 15925256 | tf_op jit(solution)/shard_map/ppermute | solution.py:246
  1.4 17.9 %collective-permute-start.6 = (bf16[1152,2304]{1,0:T(8,128)(2,1)}, bf16[1152,2304]{1,0:T(8,128)(2,1)S(1)}, u32[]{:S(2)}, u32[]{:S(2)}) collective-permute-start(bf16[1152,2304]{1,0:T(8,128)(2,1)} %ref.3), channel_id=1, source_target_pairs={{0,32},{32,0},{1,33},{33,1},{2,34},{34,2},{3,35},{35,3},{4,36},{36... | collective-permute-start | bytes 15925256 | tf_op jit(solution)/shard_map/ppermute | solution.py:247
  2.7 7.8 %collective-permute-start.1 = (bf16[360,128]{1,0:T(8,128)(2,1)S(1)}, bf16[360,128]{1,0:T(8,128)(2,1)S(1)}, u32[]{:S(2)}, u32[]{:S(2)}) collective-permute-start(bf16[360,128]{1,0:T(8,128)(2,1)S(1)} %pack_codes.1), channel_id=1, source_target_pairs={{64,16},{16,64},{0,0},{80,80},{65,17},{17,65},{1,1},{81,81},{66,18... | collective-permute-start | bytes 276488 | tf_op jit(solution)/shard_map/ppermute | solution.py:258
  3.4 7.5 %collective-permute-start = (bf16[360,128]{1,0:T(8,128)(2,1)S(1)}, bf16[360,128]{1,0:T(8,128)(2,1)S(1)}, u32[]{:S(2)}, u32[]{:S(2)}) collective-permute-start(bf16[360,128]{1,0:T(8,128)(2,1)S(1)} %pack_codes.1), channel_id=1, source_target_pairs={{0,16},{80,64},{64,0},{16,80},{1,17},{81,65},{65,1},{17,81},{2,18}... | collective-permute-start | bytes 276488 | tf_op jit(solution)/shard_map/ppermute | solution.py:257
  10.9 7.4 %collective-permute-start.4 = (bf16[2,360,128]{2,1,0:T(8,128)(2,1)S(1)}, bf16[2,360,128]{2,1,0:T(8,128)(2,1)S(1)}, u32[]{:S(2)}, u32[]{:S(2)}) collective-permute-start(bf16[2,360,128]{2,1,0:T(8,128)(2,1)S(1)} %order_quarters.1.a_ref), channel_id=1, source_target_pairs={{0,8},{32,34},{1,9},{33,35},{2,10},{34,32},{3,11},{35,33},{4,12},{... | collective-permute-start | bytes 552968 | tf_op jit(solution)/shard_map/ppermute | solution.py:262
  13.7 5.6 %collective-permute-start.3 = (bf16[2,360,128]{2,1,0:T(8,128)(2,1)S(1)}, bf16[2,360,128]{2,1,0:T(8,128)(2,1)S(1)}, u32[]{:S(2)}, u32[]{:S(2)}) collective-permute-start(bf16[2,360,128]{2,1,0:T(8,128)(2,1)S(1)} %order_quarters.1.a_ref), channel_id=1, source_target_pairs={{0,4},{32,33},{1,5},{33,34},{2,6},{34,35},{3,7},{35,32},{4,8},{36,... | collective-permute-start | bytes 552968 | tf_op jit(solution)/shard_map/ppermute | solution.py:262
  14.0 5.3 %collective-permute-start.2 = (bf16[2,360,128]{2,1,0:T(8,128)(2,1)S(1)}, bf16[2,360,128]{2,1,0:T(8,128)(2,1)S(1)}, u32[]{:S(2)}, u32[]{:S(2)}) collective-permute-start(bf16[2,360,128]{2,1,0:T(8,128)(2,1)S(1)} %order_quarters.1.a_ref), channel_id=1, source_target_pairs={{0,12},{32,35},{1,13},{33,32},{2,14},{34,33},{3,15},{35,34},{4,0},... | collective-permute-start | bytes 552968 | tf_op jit(solution)/shard_map/ppermute | solution.py:262
  19.6 8.2 %collective-permute-start.16 = (bf16[160,1152]{1,0:T(8,128)(2,1)S(1)}, bf16[160,1152]{1,0:T(8,128)(2,1)S(1)}, u32[]{:S(2)}, u32[]{:S(2)}) collective-permute-start(bf16[160,1152]{1,0:T(8,128)(2,1)S(1)} %get-tuple-element.34.m0), channel_id=1, source_target_pairs={{0,2},{32,40},{1,3},{33,41},{2,0},{34,42},{3,1},{35,43},{4,6},{36,... | collective-permute-start | bytes 1105928 | tf_op jit(solution)/shard_map/ppermute | solution.py:268
  22.5 9.2 %collective-permute-start.15 = (bf16[160,1152]{1,0:T(8,128)(2,1)S(1)}, bf16[160,1152]{1,0:T(8,128)(2,1)S(1)}, u32[]{:S(2)}, u32[]{:S(2)}) collective-permute-start(bf16[160,1152]{1,0:T(8,128)(2,1)S(1)} %get-tuple-element.34.m0), channel_id=1, source_target_pairs={{0,1},{32,36},{1,2},{33,37},{2,3},{34,38},{3,0},{35,39},{4,5},{36,... | collective-permute-start | bytes 1105928 | tf_op jit(solution)/shard_map/ppermute | solution.py:268
  22.9 9.1 %collective-permute-start.14 = (bf16[160,1152]{1,0:T(8,128)(2,1)S(1)}, bf16[160,1152]{1,0:T(8,128)(2,1)S(1)}, u32[]{:S(2)}, u32[]{:S(2)}) collective-permute-start(bf16[160,1152]{1,0:T(8,128)(2,1)S(1)} %get-tuple-element.34.m0), channel_id=1, source_target_pairs={{0,3},{32,44},{1,0},{33,45},{2,1},{34,46},{3,2},{35,47},{4,7},{36,... | collective-permute-start | bytes 1105928 | tf_op jit(solution)/shard_map/ppermute | solution.py:268
  25.2 13.3 %collective-permute-start.9 = (bf16[160,1152]{1,0:T(8,128)(2,1)S(1)}, bf16[160,1152]{1,0:T(8,128)(2,1)S(1)}, u32[]{:S(2)}, u32[]{:S(2)}) collective-permute-start(bf16[160,1152]{1,0:T(8,128)(2,1)S(1)} %get-tuple-element.27.m0), channel_id=1, source_target_pairs={{0,2},{32,40},{1,3},{33,41},{2,0},{34,42},{3,1},{35,43},{4,6},{36,... | collective-permute-start | bytes 1105928 | tf_op jit(solution)/shard_map/ppermute | solution.py:268
  25.2 14.4 %collective-permute-start.8 = (bf16[160,1152]{1,0:T(8,128)(2,1)S(1)}, bf16[160,1152]{1,0:T(8,128)(2,1)S(1)}, u32[]{:S(2)}, u32[]{:S(2)}) collective-permute-start(bf16[160,1152]{1,0:T(8,128)(2,1)S(1)} %get-tuple-element.27.m0), channel_id=1, source_target_pairs={{0,1},{32,36},{1,2},{33,37},{2,3},{34,38},{3,0},{35,39},{4,5},{36,... | collective-permute-start | bytes 1105928 | tf_op jit(solution)/shard_map/ppermute | solution.py:268
  27.8 12.2 %collective-permute-start.7 = (bf16[160,1152]{1,0:T(8,128)(2,1)S(1)}, bf16[160,1152]{1,0:T(8,128)(2,1)S(1)}, u32[]{:S(2)}, u32[]{:S(2)}) collective-permute-start(bf16[160,1152]{1,0:T(8,128)(2,1)S(1)} %get-tuple-element.27.m0), channel_id=1, source_target_pairs={{0,3},{32,44},{1,0},{33,45},{2,1},{34,46},{3,2},{35,47},{4,7},{36,... | collective-permute-start | bytes 1105928 | tf_op jit(solution)/shard_map/ppermute | solution.py:268
  33.5 10.2 %collective-permute-start.17 = (f16[168,1152]{1,0:T(8,128)(2,1)S(1)}, f16[168,1152]{1,0:T(8,128)(2,1)S(1)}, u32[]{:S(2)}, u32[]{:S(2)}) collective-permute-start(f16[168,1152]{1,0:T(8,128)(2,1)S(1)} %convert_element_type.46), channel_id=1, source_target_pairs={{0,64},{64,0},{1,65},{65,1},{2,66},{66,2},{3,67},{67,3},{4,68},{68... | collective-permute-start | bytes 1161224 | tf_op jit(solution)/shard_map/ppermute | solution.py:281
  41.4 10.6 %collective-permute-start.10 = (f16[168,1152]{1,0:T(8,128)(2,1)S(1)}, f16[168,1152]{1,0:T(8,128)(2,1)S(1)}, u32[]{:S(2)}, u32[]{:S(2)}) collective-permute-start(f16[168,1152]{1,0:T(8,128)(2,1)S(1)} %convert_element_type.42), channel_id=1, source_target_pairs={{0,64},{64,0},{1,65},{65,1},{2,66},{66,2},{3,67},{67,3},{4,68},{68... | collective-permute-start | bytes 1161224 | tf_op jit(solution)/shard_map/ppermute | solution.py:281
  46.6 10.6 %collective-permute-start.18 = (bf16[4,360,128]{2,1,0:T(8,128)(2,1)S(1)}, bf16[4,360,128]{2,1,0:T(8,128)(2,1)S(1)}, u32[]{:S(2)}, u32[]{:S(2)}) collective-permute-start(bf16[4,360,128]{2,1,0:T(8,128)(2,1)S(1)} %get-tuple-element.38), channel_id=1, source_target_pairs={{0,8},{32,34},{1,9},{33,35},{2,10},{34,32},{3,11},{35,33},{4,12},{... | collective-permute-start | bytes 1105928 | tf_op jit(solution)/shard_map/ppermute | solution.py:302
  49.4 9.5 %collective-permute-start.19 = (bf16[4,360,128]{2,1,0:T(8,128)(2,1)S(1)}, bf16[4,360,128]{2,1,0:T(8,128)(2,1)S(1)}, u32[]{:S(2)}, u32[]{:S(2)}) collective-permute-start(bf16[4,360,128]{2,1,0:T(8,128)(2,1)S(1)} %get-tuple-element.39), channel_id=1, source_target_pairs={{0,4},{32,33},{1,5},{33,34},{2,6},{34,35},{3,7},{35,32},{4,8},{36,... | collective-permute-start | bytes 1105928 | tf_op jit(solution)/shard_map/ppermute | solution.py:302
  49.7 9.2 %collective-permute-start.20 = (bf16[4,360,128]{2,1,0:T(8,128)(2,1)S(1)}, bf16[4,360,128]{2,1,0:T(8,128)(2,1)S(1)}, u32[]{:S(2)}, u32[]{:S(2)}) collective-permute-start(bf16[4,360,128]{2,1,0:T(8,128)(2,1)S(1)} %get-tuple-element.40), channel_id=1, source_target_pairs={{0,12},{32,35},{1,13},{33,32},{2,14},{34,33},{3,15},{35,34},{4,0},... | collective-permute-start | bytes 1105928 | tf_op jit(solution)/shard_map/ppermute | solution.py:302
  55.0 8.3 %collective-permute-start.11 = (bf16[4,360,128]{2,1,0:T(8,128)(2,1)S(1)}, bf16[4,360,128]{2,1,0:T(8,128)(2,1)S(1)}, u32[]{:S(2)}, u32[]{:S(2)}) collective-permute-start(bf16[4,360,128]{2,1,0:T(8,128)(2,1)S(1)} %get-tuple-element.31), channel_id=1, source_target_pairs={{0,8},{32,34},{1,9},{33,35},{2,10},{34,32},{3,11},{35,33},{4,12},{... | collective-permute-start | bytes 1105928 | tf_op jit(solution)/shard_map/ppermute | solution.py:302
  56.2 10.9 %collective-permute-start.12 = (bf16[4,360,128]{2,1,0:T(8,128)(2,1)S(1)}, bf16[4,360,128]{2,1,0:T(8,128)(2,1)S(1)}, u32[]{:S(2)}, u32[]{:S(2)}) collective-permute-start(bf16[4,360,128]{2,1,0:T(8,128)(2,1)S(1)} %get-tuple-element.32), channel_id=1, source_target_pairs={{0,4},{32,33},{1,5},{33,34},{2,6},{34,35},{3,7},{35,32},{4,8},{36,... | collective-permute-start | bytes 1105928 | tf_op jit(solution)/shard_map/ppermute | solution.py:302
  57.2 10.0 %collective-permute-start.13 = (bf16[4,360,128]{2,1,0:T(8,128)(2,1)S(1)}, bf16[4,360,128]{2,1,0:T(8,128)(2,1)S(1)}, u32[]{:S(2)}, u32[]{:S(2)}) collective-permute-start(bf16[4,360,128]{2,1,0:T(8,128)(2,1)S(1)} %get-tuple-element.33), channel_id=1, source_target_pairs={{0,12},{32,35},{1,13},{33,32},{2,14},{34,33},{3,15},{35,34},{4,0},... | collective-permute-start | bytes 1105928 | tf_op jit(solution)/shard_map/ppermute | solution.py:302
  67.5 6.0 %collective-permute-start.21 = (bf16[720,128]{1,0:T(8,128)(2,1)S(1)}, bf16[720,128]{1,0:T(8,128)(2,1)S(1)}, u32[]{:S(2)}, u32[]{:S(2)}) collective-permute-start(bf16[720,128]{1,0:T(8,128)(2,1)S(1)} %get-tuple-element.42), channel_id=1, source_target_pairs={{0,2},{32,40},{1,3},{33,41},{2,0},{34,42},{3,1},{35,43},{4,6},{36,... | collective-permute-start | bytes 552968 | tf_op jit(solution)/shard_map/ppermute | solution.py:305
  69.2 6.3 %collective-permute-start.22 = (bf16[720,128]{1,0:T(8,128)(2,1)S(1)}, bf16[720,128]{1,0:T(8,128)(2,1)S(1)}, u32[]{:S(2)}, u32[]{:S(2)}) collective-permute-start(bf16[720,128]{1,0:T(8,128)(2,1)S(1)} %get-tuple-element.43), channel_id=1, source_target_pairs={{0,1},{32,36},{1,2},{33,37},{2,3},{34,38},{3,0},{35,39},{4,5},{36,... | collective-permute-start | bytes 552968 | tf_op jit(solution)/shard_map/ppermute | solution.py:305
  70.2 5.2 %collective-permute-start.23 = (bf16[720,128]{1,0:T(8,128)(2,1)S(1)}, bf16[720,128]{1,0:T(8,128)(2,1)S(1)}, u32[]{:S(2)}, u32[]{:S(2)}) collective-permute-start(bf16[720,128]{1,0:T(8,128)(2,1)S(1)} %get-tuple-element.44), channel_id=1, source_target_pairs={{0,3},{32,44},{1,0},{33,45},{2,1},{34,46},{3,2},{35,47},{4,7},{36,... | collective-permute-start | bytes 552968 | tf_op jit(solution)/shard_map/ppermute | solution.py:305
  75.8 7.5 %collective-permute-start.26 = (f16[224,128]{1,0:T(8,128)(2,1)S(1)}, f16[224,128]{1,0:T(8,128)(2,1)S(1)}, u32[]{:S(2)}, u32[]{:S(2)}) collective-permute-start(f16[224,128]{1,0:T(8,128)(2,1)S(1)} %convert_element_type.54), channel_id=1, source_target_pairs={{0,16},{16,0},{1,17},{17,1},{2,18},{18,2},{3,19},{19,3},{4,20},{20... | collective-permute-start | bytes 172040 | tf_op jit(solution)/shard_map/ppermute | solution.py:311
  76.6 8.7 %collective-permute-start.25 = (f16[224,128]{1,0:T(8,128)(2,1)S(1)}, f16[224,128]{1,0:T(8,128)(2,1)S(1)}, u32[]{:S(2)}, u32[]{:S(2)}) collective-permute-start(f16[224,128]{1,0:T(8,128)(2,1)S(1)} %convert_element_type.52), channel_id=1, source_target_pairs={{0,48},{16,32},{32,16},{48,0},{1,49},{17,33},{33,17},{49,1},{2,50}... | collective-permute-start | bytes 172040 | tf_op jit(solution)/shard_map/ppermute | solution.py:310
  83.0 2.4 %collective-permute-start.24 = (f16[224,128]{1,0:T(8,128)(2,1)S(1)}, f16[224,128]{1,0:T(8,128)(2,1)S(1)}, u32[]{:S(2)}, u32[]{:S(2)}) collective-permute-start(f16[224,128]{1,0:T(8,128)(2,1)S(1)} %convert_element_type.50), channel_id=1, source_target_pairs={{0,32},{32,0},{1,33},{33,1},{2,34},{34,2},{3,35},{35,3},{4,36},{36... | collective-permute-start | bytes 172040 | tf_op jit(solution)/shard_map/ppermute | solution.py:309

commit v8 on v7

--- a/solution.py
+++ b/solution.py
@@ -70,14 +70,8 @@
     x = dot(scale, x_ref[...]).astype(BF)
     o_ref[0:QT] = x[:, 0:128]
     o_ref[QT : 2 * QT] = x[:, 128:256]
-    tail = x[:, 256:288]
-    src = lax.broadcasted_iota(jnp.int32, (32, 128), 0)
-    dst = lax.broadcasted_iota(jnp.int32, (32, 128), 1)
-    total = jnp.zeros((40, 128), F32)
-    for j in range(4):
-        place = jnp.where(dst == src + 32 * j, 1.0, 0.0).astype(BF)
-        total += dot(tail, place)[40 * j : 40 * j + 40]
-    o_ref[2 * QT : 360] = total.astype(BF)
+    tail = x[:, 256:288].astype(F32)
+    o_ref[2 * QT : 360] = jnp.concatenate([tail[40 * j : 40 * j + 40] for j in range(4)], axis=1).astype(BF)
 
 
 def order_quarters(one, two, after, o_ref):

time: 87.9 us -> 87.7 us (level)
  transfers between devices with their start and end apart: 27 -> 27, of which waited for: 11 -> 11; matrix products, arithmetic and copies ran while one was open for 1% -> 1% of each run, Pallas kernels for 22% -> 21%
where the time goes in v8:
time: 87.7 us; the launch traced here: 86.3 us
  starting transfers between devices  46.8 us (53%)
  Pallas kernels  20.2 us (23%)
  waiting for transfers between devices  18.1 us (21%)
    ppermute x6, starting transfers between devices, shards(): lax.ppermute(v, YX, first_axis(k))  9.5 us
    ppermute x6, starting transfers between devices, shards(): lax.ppermute(m, YX, second_axis(k))  8.98 us
    ppermute x6, waiting for transfers between devices, shards(): lax.ppermute(v, YX, first_axis(k))  8.19 us
    ppermute x1, starting transfers between devices, shards(): lax.ppermute(to_czl, ('c', 'zl'), [(0, 3), (1, 2), (2, 1), (3, 0)])  6.16 us
    ppermute x3, starting transfers between devices, shards(): around = [lax.ppermute(piece, YX, first_axis(k)) for k in GATHER[1:]]  5.5 us
    pallas_call x2, Pallas kernels, shards(): call(project_out, [shape(part, F32)] + [shape(part, BF)] * 3, [VMEM] * 2,...  5.08 us
    ppermute x1, starting transfers between devices, shards(): one = lax.ppermute(packed, z, [(0, 1), (3, 2), (2, 0), (1, 3)])  4.67 us
    ppermute x2, starting transfers between devices, shards(): gots = [lax.ppermute(send, 'zh', swap) for send in sends]  4.43 us
  transfers between devices with their start and end apart: 27, of which 11 were waited for; matrix products, arithmetic and copies ran while one was open for 1% of the time, Pallas kernels for 21%

profile of v8, /device:TPU:1, one launch (start us, length us, event | category | flops | bytes accessed | tf_op | source)
XLA Modules:
  0.0 86.3 jit_solution(12933408835577699925)
XLA Ops:
  0.0 1.4 %collective-permute-start.5 = (bf16[2304,1152]{1,0:T(8,128)(2,1)}, bf16[2304,1152]{1,0:T(8,128)(2,1)S(1)}, u32[]{:S(2)}, u32[]{:S(2)}) collective-permute-start(bf16[2304,1152]{1,0:T(8,128)(2,1)} %ref.2), channel_id=1, source_target_pairs={{0,32},{32,0},{1,33},{33,1},{2,34},{34,2},{3,35},{35,3},{4,36},{36... | collective-permute-start | bytes 15925256 | tf_op jit(solution)/shard_map/ppermute | solution.py:240
  1.4 0.0 collective-permute-start.6
  1.4 1.2 %pack_codes.1 = bf16[360,128]{1,0:T(8,128)(2,1)S(1)} custom-call(bf16[160,288]{1,0:T(8,128)(2,1)} %codes_ref.1, s32[1,160]{1,0:T(1,128)} %bitcast.2), custom_call_target="tpu_custom_call" | custom-call | tf_op jit(solution)/shard_map/pack_codes/pallas_call | solution.py:244
  2.6 0.7 collective-permute-start.1
  3.3 4.7 %collective-permute-start = (bf16[360,128]{1,0:T(8,128)(2,1)S(1)}, bf16[360,128]{1,0:T(8,128)(2,1)S(1)}, u32[]{:S(2)}, u32[]{:S(2)}) collective-permute-start(bf16[360,128]{1,0:T(8,128)(2,1)S(1)} %pack_codes.1), channel_id=1, source_target_pairs={{0,16},{80,64},{64,0},{16,80},{1,17},{81,65},{65,1},{17,81},{2,18}... | collective-permute-start | bytes 276488 | tf_op jit(solution)/shard_map/ppermute | solution.py:251
  8.0 2.5 %arrange_own.1.after.half_ref = bf16[4608,1152]{1,0:T(8,128)(2,1)S(1)} custom-call(bf16[2304,1152]{1,0:T(8,128)(2,1)} %ref.2), custom_call_target="tpu_custom_call" | custom-call | bytes 10616832 | tf_op jit(solution)/shard_map/arrange_own/pallas_call | solution.py:254
  10.4 0.0 collective-permute-done.1.two
  10.4 0.3 collective-permute-done.one
  10.8 2.8 %collective-permute-start.4 = (bf16[2,360,128]{2,1,0:T(8,128)(2,1)S(1)}, bf16[2,360,128]{2,1,0:T(8,128)(2,1)S(1)}, u32[]{:S(2)}, u32[]{:S(2)}) collective-permute-start(bf16[2,360,128]{2,1,0:T(8,128)(2,1)S(1)} %order_quarters.1.a_ref), channel_id=1, source_target_pairs={{0,8},{32,34},{1,9},{33,35},{2,10},{34,32},{3,11},{35,33},{4,12},{... | collective-permute-start | bytes 552968 | tf_op jit(solution)/shard_map/ppermute | solution.py:256
  13.6 0.3 collective-permute-start.3
  13.9 2.4 %collective-permute-start.2 = (bf16[2,360,128]{2,1,0:T(8,128)(2,1)S(1)}, bf16[2,360,128]{2,1,0:T(8,128)(2,1)S(1)}, u32[]{:S(2)}, u32[]{:S(2)}) collective-permute-start(bf16[2,360,128]{2,1,0:T(8,128)(2,1)S(1)} %order_quarters.1.a_ref), channel_id=1, source_target_pairs={{0,12},{32,35},{1,13},{33,32},{2,14},{34,33},{3,15},{35,34},{4,0},... | collective-permute-start | bytes 552968 | tf_op jit(solution)/shard_map/ppermute | solution.py:256
  16.3 1.9 %arrange_other.1.after1.w_ref.after = bf16[4608,1152]{1,0:T(8,128)(2,1)S(1)} custom-call(bf16[2304,1152]{1,0:T(8,128)(2,1)S(1)} %collective-permute-done.5.ref, bf16[4608,1152]{1,0:T(8,128)(2,1)S(1)} %arrange_own.1.after.half_ref), custom_call_target="tpu_custom_call", output_to_operand_aliasing={{}: (1, {})} | custom-call | bytes 10616832 | tf_op jit(solution)/shard_map/arrange_other/pallas_call | solution.py:257
  18.2 0.0 collective-permute-done.4.d_ref
  18.2 1.0 %collective-permute-done.3.c_ref = bf16[2,360,128]{2,1,0:T(8,128)(2,1)S(1)} collective-permute-done((bf16[2,360,128]{2,1,0:T(8,128)(2,1)S(1)}, bf16[2,360,128]{2,1,0:T(8,128)(2,1)S(1)}, u32[]{:S(2)}, u32[]{:S(2)}) %collective-permute-start.3) | collective-permute-done | bytes 184352 | tf_op jit(solution)/shard_map/ppermute | solution.py:256
  19.2 0.0 collective-permute-done.2.b_ref
  19.2 0.0 collective-permute-done.6.after2.ref
  19.2 0.2 merge_codes.1
  19.5 3.0 %collective-permute-start.16 = (bf16[160,1152]{1,0:T(8,128)(2,1)S(1)}, bf16[160,1152]{1,0:T(8,128)(2,1)S(1)}, u32[]{:S(2)}, u32[]{:S(2)}) collective-permute-start(bf16[160,1152]{1,0:T(8,128)(2,1)S(1)} %get-tuple-element.34.m0), channel_id=1, source_target_pairs={{0,2},{32,40},{1,3},{33,41},{2,0},{34,42},{3,1},{35,43},{4,6},{36,... | collective-permute-start | bytes 1105928 | tf_op jit(solution)/shard_map/ppermute | solution.py:262
  22.5 0.4 collective-permute-start.15
  22.9 2.3 %collective-permute-start.14 = (bf16[160,1152]{1,0:T(8,128)(2,1)S(1)}, bf16[160,1152]{1,0:T(8,128)(2,1)S(1)}, u32[]{:S(2)}, u32[]{:S(2)}) collective-permute-start(bf16[160,1152]{1,0:T(8,128)(2,1)S(1)} %get-tuple-element.34.m0), channel_id=1, source_target_pairs={{0,3},{32,44},{1,0},{33,45},{2,1},{34,46},{3,2},{35,47},{4,7},{36,... | collective-permute-start | bytes 1105928 | tf_op jit(solution)/shard_map/ppermute | solution.py:262
  25.2 0.0 collective-permute-start.9
  25.2 0.6 collective-permute-start.8
  25.7 2.0 %collective-permute-done.16.m1 = bf16[160,1152]{1,0:T(8,128)(2,1)S(1)} collective-permute-done((bf16[160,1152]{1,0:T(8,128)(2,1)S(1)}, bf16[160,1152]{1,0:T(8,128)(2,1)S(1)}, u32[]{:S(2)}, u32[]{:S(2)}) %collective-permute-start.16) | collective-permute-done | bytes 368672 | tf_op jit(solution)/shard_map/ppermute | solution.py:262
  27.7 2.7 %collective-permute-start.7 = (bf16[160,1152]{1,0:T(8,128)(2,1)S(1)}, bf16[160,1152]{1,0:T(8,128)(2,1)S(1)}, u32[]{:S(2)}, u32[]{:S(2)}) collective-permute-start(bf16[160,1152]{1,0:T(8,128)(2,1)S(1)} %get-tuple-element.27.m0), channel_id=1, source_target_pairs={{0,3},{32,44},{1,0},{33,45},{2,1},{34,46},{3,2},{35,47},{4,7},{36,... | collective-permute-start | bytes 1105928 | tf_op jit(solution)/shard_map/ppermute | solution.py:262
  30.5 1.1 %project_early.3.early_ref = f32[160,1152]{1,0:T(8,128)S(1)} custom-call(bf16[160,1152]{1,0:T(8,128)(2,1)S(1)} %get-tuple-element.34.m0, bf16[160,1152]{1,0:T(8,128)(2,1)S(1)} %collective-permute-done.16.m1, bf16[4608,1152]{1,0:T(8,128)(2,1)S(1)} %arrange_other.1.after1.w_ref.after), custom_call_target="tpu_custom_call" | custom-call | flops 849346560 | bytes 5308416 | tf_op jit(solution)/shard_map/project_early/pallas_call | solution.py:267
  31.6 0.1 collective-permute-done.15.m3
  31.7 0.3 collective-permute-done.14.m2
  32.0 1.3 %project_in.3 = (f32[160,1152]{1,0:T(8,128)S(1)}, f32[168,1152]{1,0:T(8,128)S(1)}) custom-call(bf16[160,1152]{1,0:T(8,128)(2,1)S(1)} %collective-permute-done.14.m2, bf16[160,1152]{1,0:T(8,128)(2,1)S(1)} %collective-permute-done.15.m3, bf16[4608,1152]{1,0:T(8,128)(2,1)S(1)} %arrange_other.1.after1.w_ref.after, f32[160,1152]{1,0:T(8,128)S(1)} %project_early.3.early_ref), custom_call_target="tpu_custom_call" | custom-call | flops 849346560 | bytes 5308416 | tf_op jit(solution)/shard_map/project_in/pallas_call | solution.py:272
  33.4 2.1 %collective-permute-start.17 = (f16[168,1152]{1,0:T(8,128)(2,1)S(1)}, f16[168,1152]{1,0:T(8,128)(2,1)S(1)}, u32[]{:S(2)}, u32[]{:S(2)}) collective-permute-start(f16[168,1152]{1,0:T(8,128)(2,1)S(1)} %convert_element_type.46), channel_id=1, source_target_pairs={{0,64},{64,0},{1,65},{65,1},{2,66},{66,2},{3,67},{67,3},{4,68},{68... | collective-permute-start | bytes 1161224 | tf_op jit(solution)/shard_map/ppermute | solution.py:275
  35.5 2.5 %stage_own.1.half_ref = bf16[1152,4608]{1,0:T(8,128)(2,1)S(1)} custom-call(bf16[1152,2304]{1,0:T(8,128)(2,1)} %ref.3, bf16[4608,1152]{1,0:T(8,128)(2,1)S(1)} %arrange_other.1.after1.w_ref.after), custom_call_target="tpu_custom_call" | custom-call | bytes 10616832 | tf_op jit(solution)/shard_map/stage_own/pallas_call | solution.py:276
  38.0 0.4 stage_other.1.w_ref
  38.5 1.1 %project_early.2.early_ref = f32[160,1152]{1,0:T(8,128)S(1)} custom-call(bf16[160,1152]{1,0:T(8,128)(2,1)S(1)} %get-tuple-element.27.m0, bf16[160,1152]{1,0:T(8,128)(2,1)S(1)} %collective-permute-done.9.m1, bf16[4608,1152]{1,0:T(8,128)(2,1)S(1)} %arrange_other.1.after1.w_ref.after), custom_call_target="tpu_custom_call" | custom-call | flops 849346560 | bytes 5308416 | tf_op jit(solution)/shard_map/project_early/pallas_call | solution.py:267
  39.6 0.3 collective-permute-done.7.m2
  40.0 1.3 %project_in.2 = (f32[160,1152]{1,0:T(8,128)S(1)}, f32[168,1152]{1,0:T(8,128)S(1)}) custom-call(bf16[160,1152]{1,0:T(8,128)(2,1)S(1)} %collective-permute-done.7.m2, bf16[160,1152]{1,0:T(8,128)(2,1)S(1)} %collective-permute-done.8.m3, bf16[4608,1152]{1,0:T(8,128)(2,1)S(1)} %arrange_other.1.after1.w_ref.after, f32[160,1152]{1,0:T(8,128)S(1)} %project_early.2.early_ref), custom_call_target="tpu_custom_call" | custom-call | flops 849346560 | bytes 5308416 | tf_op jit(solution)/shard_map/project_in/pallas_call | solution.py:272
  41.4 2.3 %collective-permute-start.10 = (f16[168,1152]{1,0:T(8,128)(2,1)S(1)}, f16[168,1152]{1,0:T(8,128)(2,1)S(1)}, u32[]{:S(2)}, u32[]{:S(2)}) collective-permute-start(f16[168,1152]{1,0:T(8,128)(2,1)S(1)} %convert_element_type.42), channel_id=1, source_target_pairs={{0,64},{64,0},{1,65},{65,1},{2,66},{66,2},{3,67},{67,3},{4,68},{68... | collective-permute-start | bytes 1161224 | tf_op jit(solution)/shard_map/ppermute | solution.py:275
  43.7 0.0 collective-permute-done.17
  43.7 0.3 fusion.15.a_ref
  44.0 2.5 %project_out.3 = (f32[4,360,128]{2,1,0:T(8,128)S(1)}, bf16[4,360,128]{2,1,0:T(8,128)(2,1)S(1)}, bf16[4,360,128]{2,1,0:T(8,128)(2,1)S(1)}, bf16[4,360,128]{2,1,0:T(8,128)(2,1)S(1)}) custom-call(bf16[160,1152]{1,0:T(8,128)(2,1)S(1)} %fusion.15.a_ref, bf16[1152,4608]{1,0:T(8,128)(2,1)S(1)} %stage_other.1.w_ref), custom_call_target="tpu_custom_call" | custom-call | flops 1698693120 | bytes 10616832 | tf_op jit(solution)/shard_map/project_out/pallas_call | solution.py:286
  46.6 2.8 %collective-permute-start.18 = (bf16[4,360,128]{2,1,0:T(8,128)(2,1)S(1)}, bf16[4,360,128]{2,1,0:T(8,128)(2,1)S(1)}, u32[]{:S(2)}, u32[]{:S(2)}) collective-permute-start(bf16[4,360,128]{2,1,0:T(8,128)(2,1)S(1)} %get-tuple-element.38), channel_id=1, source_target_pairs={{0,8},{32,34},{1,9},{33,35},{2,10},{34,32},{3,11},{35,33},{4,12},{... | collective-permute-start | bytes 1105928 | tf_op jit(solution)/shard_map/ppermute | solution.py:296
  49.4 0.3 collective-permute-start.19
  49.7 2.4 %collective-permute-start.20 = (bf16[4,360,128]{2,1,0:T(8,128)(2,1)S(1)}, bf16[4,360,128]{2,1,0:T(8,128)(2,1)S(1)}, u32[]{:S(2)}, u32[]{:S(2)}) collective-permute-start(bf16[4,360,128]{2,1,0:T(8,128)(2,1)S(1)} %get-tuple-element.40), channel_id=1, source_target_pairs={{0,12},{32,35},{1,13},{33,32},{2,14},{34,33},{3,15},{35,34},{4,0},... | collective-permute-start | bytes 1105928 | tf_op jit(solution)/shard_map/ppermute | solution.py:296
  52.1 0.0 collective-permute-done.10
  52.1 0.3 fusion.7.a_ref
  52.4 2.5 %project_out.2 = (f32[4,360,128]{2,1,0:T(8,128)S(1)}, bf16[4,360,128]{2,1,0:T(8,128)(2,1)S(1)}, bf16[4,360,128]{2,1,0:T(8,128)(2,1)S(1)}, bf16[4,360,128]{2,1,0:T(8,128)(2,1)S(1)}) custom-call(bf16[160,1152]{1,0:T(8,128)(2,1)S(1)} %fusion.7.a_ref, bf16[1152,4608]{1,0:T(8,128)(2,1)S(1)} %stage_other.1.w_ref), custom_call_target="tpu_custom_call" | custom-call | flops 1698693120 | bytes 10616832 | tf_op jit(solution)/shard_map/project_out/pallas_call | solution.py:286
  55.0 1.3 %collective-permute-start.11 = (bf16[4,360,128]{2,1,0:T(8,128)(2,1)S(1)}, bf16[4,360,128]{2,1,0:T(8,128)(2,1)S(1)}, u32[]{:S(2)}, u32[]{:S(2)}) collective-permute-start(bf16[4,360,128]{2,1,0:T(8,128)(2,1)S(1)} %get-tuple-element.31), channel_id=1, source_target_pairs={{0,8},{32,34},{1,9},{33,35},{2,10},{34,32},{3,11},{35,33},{4,12},{... | collective-permute-start | bytes 1105928 | tf_op jit(solution)/shard_map/ppermute | solution.py:296
  56.3 0.8 collective-permute-start.12
  57.1 0.0 collective-permute-done.18.b1
  57.1 1.9 %collective-permute-start.13 = (bf16[4,360,128]{2,1,0:T(8,128)(2,1)S(1)}, bf16[4,360,128]{2,1,0:T(8,128)(2,1)S(1)}, u32[]{:S(2)}, u32[]{:S(2)}) collective-permute-start(bf16[4,360,128]{2,1,0:T(8,128)(2,1)S(1)} %get-tuple-element.33), channel_id=1, source_target_pairs={{0,12},{32,35},{1,13},{33,32},{2,14},{34,33},{3,15},{35,34},{4,0},... | collective-permute-start | bytes 1105928 | tf_op jit(solution)/shard_map/ppermute | solution.py:296
  59.0 0.0 collective-permute-done.19.c1
  59.0 0.0 collective-permute-done.20.d1
  59.0 4.3 %collective-permute-done.11.b0 = bf16[4,360,128]{2,1,0:T(8,128)(2,1)S(1)} collective-permute-done((bf16[4,360,128]{2,1,0:T(8,128)(2,1)S(1)}, bf16[4,360,128]{2,1,0:T(8,128)(2,1)S(1)}, u32[]{:S(2)}, u32[]{:S(2)}) %collective-permute-start.11) | collective-permute-done | bytes 368672 | tf_op jit(solution)/shard_map/ppermute | solution.py:296
  63.3 3.9 %collective-permute-done.12.c0 = bf16[4,360,128]{2,1,0:T(8,128)(2,1)S(1)} collective-permute-done((bf16[4,360,128]{2,1,0:T(8,128)(2,1)S(1)}, bf16[4,360,128]{2,1,0:T(8,128)(2,1)S(1)}, u32[]{:S(2)}, u32[]{:S(2)}) %collective-permute-start.12) | collective-permute-done | bytes 368672 | tf_op jit(solution)/shard_map/ppermute | solution.py:296
  67.2 0.4 add_first.1
  67.5 1.6 %collective-permute-start.21 = (bf16[720,128]{1,0:T(8,128)(2,1)S(1)}, bf16[720,128]{1,0:T(8,128)(2,1)S(1)}, u32[]{:S(2)}, u32[]{:S(2)}) collective-permute-start(bf16[720,128]{1,0:T(8,128)(2,1)S(1)} %get-tuple-element.42), channel_id=1, source_target_pairs={{0,2},{32,40},{1,3},{33,41},{2,0},{34,42},{3,1},{35,43},{4,6},{36,... | collective-permute-start | bytes 552968 | tf_op jit(solution)/shard_map/ppermute | solution.py:299
  69.1 1.1 %collective-permute-start.22 = (bf16[720,128]{1,0:T(8,128)(2,1)S(1)}, bf16[720,128]{1,0:T(8,128)(2,1)S(1)}, u32[]{:S(2)}, u32[]{:S(2)}) collective-permute-start(bf16[720,128]{1,0:T(8,128)(2,1)S(1)} %get-tuple-element.43), channel_id=1, source_target_pairs={{0,1},{32,36},{1,2},{33,37},{2,3},{34,38},{3,0},{35,39},{4,5},{36,... | collective-permute-start | bytes 552968 | tf_op jit(solution)/shard_map/ppermute | solution.py:299
  70.2 1.5 %collective-permute-start.23 = (bf16[720,128]{1,0:T(8,128)(2,1)S(1)}, bf16[720,128]{1,0:T(8,128)(2,1)S(1)}, u32[]{:S(2)}, u32[]{:S(2)}) collective-permute-start(bf16[720,128]{1,0:T(8,128)(2,1)S(1)} %get-tuple-element.44), channel_id=1, source_target_pairs={{0,3},{32,44},{1,0},{33,45},{2,1},{34,46},{3,2},{35,47},{4,7},{36,... | collective-permute-start | bytes 552968 | tf_op jit(solution)/shard_map/ppermute | solution.py:299
  71.8 1.8 %collective-permute-done.21.b = bf16[720,128]{1,0:T(8,128)(2,1)S(1)} collective-permute-done((bf16[720,128]{1,0:T(8,128)(2,1)S(1)}, bf16[720,128]{1,0:T(8,128)(2,1)S(1)}, u32[]{:S(2)}, u32[]{:S(2)}) %collective-permute-start.21) | collective-permute-done | bytes 184352 | tf_op jit(solution)/shard_map/ppermute | solution.py:299
  73.6 1.9 %collective-permute-done.22.c = bf16[720,128]{1,0:T(8,128)(2,1)S(1)} collective-permute-done((bf16[720,128]{1,0:T(8,128)(2,1)S(1)}, bf16[720,128]{1,0:T(8,128)(2,1)S(1)}, u32[]{:S(2)}, u32[]{:S(2)}) %collective-permute-start.22) | collective-permute-done | bytes 184352 | tf_op jit(solution)/shard_map/ppermute | solution.py:299
  75.5 0.3 add_second.1
  75.8 0.8 collective-permute-start.26
  76.6 6.2 %collective-permute-start.25 = (f16[224,128]{1,0:T(8,128)(2,1)S(1)}, f16[224,128]{1,0:T(8,128)(2,1)S(1)}, u32[]{:S(2)}, u32[]{:S(2)}) collective-permute-start(f16[224,128]{1,0:T(8,128)(2,1)S(1)} %convert_element_type.52), channel_id=1, source_target_pairs={{0,48},{16,32},{32,16},{48,0},{1,49},{17,33},{33,17},{49,1},{2,50}... | collective-permute-start | bytes 172040 | tf_op jit(solution)/shard_map/ppermute | solution.py:304
  82.8 0.4 collective-permute-start.24
  83.2 2.1 %collective-permute-done.25 = f16[224,128]{1,0:T(8,128)(2,1)S(1)} collective-permute-done((f16[224,128]{1,0:T(8,128)(2,1)S(1)}, f16[224,128]{1,0:T(8,128)(2,1)S(1)}, u32[]{:S(2)}, u32[]{:S(2)}) %collective-permute-start.25) | collective-permute-done | bytes 57376 | tf_op jit(solution)/shard_map/ppermute | solution.py:304
  85.3 0.8 finish.1
  (18 shorter events, 0.3 us)
Async XLA Ops:
  0.0 16.3 %collective-permute-start.5 = (bf16[2304,1152]{1,0:T(8,128)(2,1)}, bf16[2304,1152]{1,0:T(8,128)(2,1)S(1)}, u32[]{:S(2)}, u32[]{:S(2)}) collective-permute-start(bf16[2304,1152]{1,0:T(8,128)(2,1)} %ref.2), channel_id=1, source_target_pairs={{0,32},{32,0},{1,33},{33,1},{2,34},{34,2},{3,35},{35,3},{4,36},{36... | collective-permute-start | bytes 15925256 | tf_op jit(solution)/shard_map/ppermute | solution.py:240
  1.4 17.8 %collective-permute-start.6 = (bf16[1152,2304]{1,0:T(8,128)(2,1)}, bf16[1152,2304]{1,0:T(8,128)(2,1)S(1)}, u32[]{:S(2)}, u32[]{:S(2)}) collective-permute-start(bf16[1152,2304]{1,0:T(8,128)(2,1)} %ref.3), channel_id=1, source_target_pairs={{0,32},{32,0},{1,33},{33,1},{2,34},{34,2},{3,35},{35,3},{4,36},{36... | collective-permute-start | bytes 15925256 | tf_op jit(solution)/shard_map/ppermute | solution.py:241
  2.6 7.8 %collective-permute-start.1 = (bf16[360,128]{1,0:T(8,128)(2,1)S(1)}, bf16[360,128]{1,0:T(8,128)(2,1)S(1)}, u32[]{:S(2)}, u32[]{:S(2)}) collective-permute-start(bf16[360,128]{1,0:T(8,128)(2,1)S(1)} %pack_codes.1), channel_id=1, source_target_pairs={{64,16},{16,64},{0,0},{80,80},{65,17},{17,65},{1,1},{81,81},{66,18... | collective-permute-start | bytes 276488 | tf_op jit(solution)/shard_map/ppermute | solution.py:252
  3.3 7.5 %collective-permute-start = (bf16[360,128]{1,0:T(8,128)(2,1)S(1)}, bf16[360,128]{1,0:T(8,128)(2,1)S(1)}, u32[]{:S(2)}, u32[]{:S(2)}) collective-permute-start(bf16[360,128]{1,0:T(8,128)(2,1)S(1)} %pack_codes.1), channel_id=1, source_target_pairs={{0,16},{80,64},{64,0},{16,80},{1,17},{81,65},{65,1},{17,81},{2,18}... | collective-permute-start | bytes 276488 | tf_op jit(solution)/shard_map/ppermute | solution.py:251
  10.8 7.4 %collective-permute-start.4 = (bf16[2,360,128]{2,1,0:T(8,128)(2,1)S(1)}, bf16[2,360,128]{2,1,0:T(8,128)(2,1)S(1)}, u32[]{:S(2)}, u32[]{:S(2)}) collective-permute-start(bf16[2,360,128]{2,1,0:T(8,128)(2,1)S(1)} %order_quarters.1.a_ref), channel_id=1, source_target_pairs={{0,8},{32,34},{1,9},{33,35},{2,10},{34,32},{3,11},{35,33},{4,12},{... | collective-permute-start | bytes 552968 | tf_op jit(solution)/shard_map/ppermute | solution.py:256
  13.6 5.6 %collective-permute-start.3 = (bf16[2,360,128]{2,1,0:T(8,128)(2,1)S(1)}, bf16[2,360,128]{2,1,0:T(8,128)(2,1)S(1)}, u32[]{:S(2)}, u32[]{:S(2)}) collective-permute-start(bf16[2,360,128]{2,1,0:T(8,128)(2,1)S(1)} %order_quarters.1.a_ref), channel_id=1, source_target_pairs={{0,4},{32,33},{1,5},{33,34},{2,6},{34,35},{3,7},{35,32},{4,8},{36,... | collective-permute-start | bytes 552968 | tf_op jit(solution)/shard_map/ppermute | solution.py:256
  13.9 5.3 %collective-permute-start.2 = (bf16[2,360,128]{2,1,0:T(8,128)(2,1)S(1)}, bf16[2,360,128]{2,1,0:T(8,128)(2,1)S(1)}, u32[]{:S(2)}, u32[]{:S(2)}) collective-permute-start(bf16[2,360,128]{2,1,0:T(8,128)(2,1)S(1)} %order_quarters.1.a_ref), channel_id=1, source_target_pairs={{0,12},{32,35},{1,13},{33,32},{2,14},{34,33},{3,15},{35,34},{4,0},... | collective-permute-start | bytes 552968 | tf_op jit(solution)/shard_map/ppermute | solution.py:256
  19.5 8.2 %collective-permute-start.16 = (bf16[160,1152]{1,0:T(8,128)(2,1)S(1)}, bf16[160,1152]{1,0:T(8,128)(2,1)S(1)}, u32[]{:S(2)}, u32[]{:S(2)}) collective-permute-start(bf16[160,1152]{1,0:T(8,128)(2,1)S(1)} %get-tuple-element.34.m0), channel_id=1, source_target_pairs={{0,2},{32,40},{1,3},{33,41},{2,0},{34,42},{3,1},{35,43},{4,6},{36,... | collective-permute-start | bytes 1105928 | tf_op jit(solution)/shard_map/ppermute | solution.py:262
  22.5 9.2 %collective-permute-start.15 = (bf16[160,1152]{1,0:T(8,128)(2,1)S(1)}, bf16[160,1152]{1,0:T(8,128)(2,1)S(1)}, u32[]{:S(2)}, u32[]{:S(2)}) collective-permute-start(bf16[160,1152]{1,0:T(8,128)(2,1)S(1)} %get-tuple-element.34.m0), channel_id=1, source_target_pairs={{0,1},{32,36},{1,2},{33,37},{2,3},{34,38},{3,0},{35,39},{4,5},{36,... | collective-permute-start | bytes 1105928 | tf_op jit(solution)/shard_map/ppermute | solution.py:262
  22.9 9.1 %collective-permute-start.14 = (bf16[160,1152]{1,0:T(8,128)(2,1)S(1)}, bf16[160,1152]{1,0:T(8,128)(2,1)S(1)}, u32[]{:S(2)}, u32[]{:S(2)}) collective-permute-start(bf16[160,1152]{1,0:T(8,128)(2,1)S(1)} %get-tuple-element.34.m0), channel_id=1, source_target_pairs={{0,3},{32,44},{1,0},{33,45},{2,1},{34,46},{3,2},{35,47},{4,7},{36,... | collective-permute-start | bytes 1105928 | tf_op jit(solution)/shard_map/ppermute | solution.py:262
  25.2 13.3 %collective-permute-start.9 = (bf16[160,1152]{1,0:T(8,128)(2,1)S(1)}, bf16[160,1152]{1,0:T(8,128)(2,1)S(1)}, u32[]{:S(2)}, u32[]{:S(2)}) collective-permute-start(bf16[160,1152]{1,0:T(8,128)(2,1)S(1)} %get-tuple-element.27.m0), channel_id=1, source_target_pairs={{0,2},{32,40},{1,3},{33,41},{2,0},{34,42},{3,1},{35,43},{4,6},{36,... | collective-permute-start | bytes 1105928 | tf_op jit(solution)/shard_map/ppermute | solution.py:262
  25.2 14.5 %collective-permute-start.8 = (bf16[160,1152]{1,0:T(8,128)(2,1)S(1)}, bf16[160,1152]{1,0:T(8,128)(2,1)S(1)}, u32[]{:S(2)}, u32[]{:S(2)}) collective-permute-start(bf16[160,1152]{1,0:T(8,128)(2,1)S(1)} %get-tuple-element.27.m0), channel_id=1, source_target_pairs={{0,1},{32,36},{1,2},{33,37},{2,3},{34,38},{3,0},{35,39},{4,5},{36,... | collective-permute-start | bytes 1105928 | tf_op jit(solution)/shard_map/ppermute | solution.py:262
  27.7 12.2 %collective-permute-start.7 = (bf16[160,1152]{1,0:T(8,128)(2,1)S(1)}, bf16[160,1152]{1,0:T(8,128)(2,1)S(1)}, u32[]{:S(2)}, u32[]{:S(2)}) collective-permute-start(bf16[160,1152]{1,0:T(8,128)(2,1)S(1)} %get-tuple-element.27.m0), channel_id=1, source_target_pairs={{0,3},{32,44},{1,0},{33,45},{2,1},{34,46},{3,2},{35,47},{4,7},{36,... | collective-permute-start | bytes 1105928 | tf_op jit(solution)/shard_map/ppermute | solution.py:262
  33.4 10.3 %collective-permute-start.17 = (f16[168,1152]{1,0:T(8,128)(2,1)S(1)}, f16[168,1152]{1,0:T(8,128)(2,1)S(1)}, u32[]{:S(2)}, u32[]{:S(2)}) collective-permute-start(f16[168,1152]{1,0:T(8,128)(2,1)S(1)} %convert_element_type.46), channel_id=1, source_target_pairs={{0,64},{64,0},{1,65},{65,1},{2,66},{66,2},{3,67},{67,3},{4,68},{68... | collective-permute-start | bytes 1161224 | tf_op jit(solution)/shard_map/ppermute | solution.py:275
  41.4 10.7 %collective-permute-start.10 = (f16[168,1152]{1,0:T(8,128)(2,1)S(1)}, f16[168,1152]{1,0:T(8,128)(2,1)S(1)}, u32[]{:S(2)}, u32[]{:S(2)}) collective-permute-start(f16[168,1152]{1,0:T(8,128)(2,1)S(1)} %convert_element_type.42), channel_id=1, source_target_pairs={{0,64},{64,0},{1,65},{65,1},{2,66},{66,2},{3,67},{67,3},{4,68},{68... | collective-permute-start | bytes 1161224 | tf_op jit(solution)/shard_map/ppermute | solution.py:275
  46.6 10.5 %collective-permute-start.18 = (bf16[4,360,128]{2,1,0:T(8,128)(2,1)S(1)}, bf16[4,360,128]{2,1,0:T(8,128)(2,1)S(1)}, u32[]{:S(2)}, u32[]{:S(2)}) collective-permute-start(bf16[4,360,128]{2,1,0:T(8,128)(2,1)S(1)} %get-tuple-element.38), channel_id=1, source_target_pairs={{0,8},{32,34},{1,9},{33,35},{2,10},{34,32},{3,11},{35,33},{4,12},{... | collective-permute-start | bytes 1105928 | tf_op jit(solution)/shard_map/ppermute | solution.py:296
  49.4 9.6 %collective-permute-start.19 = (bf16[4,360,128]{2,1,0:T(8,128)(2,1)S(1)}, bf16[4,360,128]{2,1,0:T(8,128)(2,1)S(1)}, u32[]{:S(2)}, u32[]{:S(2)}) collective-permute-start(bf16[4,360,128]{2,1,0:T(8,128)(2,1)S(1)} %get-tuple-element.39), channel_id=1, source_target_pairs={{0,4},{32,33},{1,5},{33,34},{2,6},{34,35},{3,7},{35,32},{4,8},{36,... | collective-permute-start | bytes 1105928 | tf_op jit(solution)/shard_map/ppermute | solution.py:296
  49.7 9.3 %collective-permute-start.20 = (bf16[4,360,128]{2,1,0:T(8,128)(2,1)S(1)}, bf16[4,360,128]{2,1,0:T(8,128)(2,1)S(1)}, u32[]{:S(2)}, u32[]{:S(2)}) collective-permute-start(bf16[4,360,128]{2,1,0:T(8,128)(2,1)S(1)} %get-tuple-element.40), channel_id=1, source_target_pairs={{0,12},{32,35},{1,13},{33,32},{2,14},{34,33},{3,15},{35,34},{4,0},... | collective-permute-start | bytes 1105928 | tf_op jit(solution)/shard_map/ppermute | solution.py:296
  55.0 8.3 %collective-permute-start.11 = (bf16[4,360,128]{2,1,0:T(8,128)(2,1)S(1)}, bf16[4,360,128]{2,1,0:T(8,128)(2,1)S(1)}, u32[]{:S(2)}, u32[]{:S(2)}) collective-permute-start(bf16[4,360,128]{2,1,0:T(8,128)(2,1)S(1)} %get-tuple-element.31), channel_id=1, source_target_pairs={{0,8},{32,34},{1,9},{33,35},{2,10},{34,32},{3,11},{35,33},{4,12},{... | collective-permute-start | bytes 1105928 | tf_op jit(solution)/shard_map/ppermute | solution.py:296
  56.3 10.9 %collective-permute-start.12 = (bf16[4,360,128]{2,1,0:T(8,128)(2,1)S(1)}, bf16[4,360,128]{2,1,0:T(8,128)(2,1)S(1)}, u32[]{:S(2)}, u32[]{:S(2)}) collective-permute-start(bf16[4,360,128]{2,1,0:T(8,128)(2,1)S(1)} %get-tuple-element.32), channel_id=1, source_target_pairs={{0,4},{32,33},{1,5},{33,34},{2,6},{34,35},{3,7},{35,32},{4,8},{36,... | collective-permute-start | bytes 1105928 | tf_op jit(solution)/shard_map/ppermute | solution.py:296
  57.1 10.1 %collective-permute-start.13 = (bf16[4,360,128]{2,1,0:T(8,128)(2,1)S(1)}, bf16[4,360,128]{2,1,0:T(8,128)(2,1)S(1)}, u32[]{:S(2)}, u32[]{:S(2)}) collective-permute-start(bf16[4,360,128]{2,1,0:T(8,128)(2,1)S(1)} %get-tuple-element.33), channel_id=1, source_target_pairs={{0,12},{32,35},{1,13},{33,32},{2,14},{34,33},{3,15},{35,34},{4,0},... | collective-permute-start | bytes 1105928 | tf_op jit(solution)/shard_map/ppermute | solution.py:296
  67.5 6.1 %collective-permute-start.21 = (bf16[720,128]{1,0:T(8,128)(2,1)S(1)}, bf16[720,128]{1,0:T(8,128)(2,1)S(1)}, u32[]{:S(2)}, u32[]{:S(2)}) collective-permute-start(bf16[720,128]{1,0:T(8,128)(2,1)S(1)} %get-tuple-element.42), channel_id=1, source_target_pairs={{0,2},{32,40},{1,3},{33,41},{2,0},{34,42},{3,1},{35,43},{4,6},{36,... | collective-permute-start | bytes 552968 | tf_op jit(solution)/shard_map/ppermute | solution.py:299
  69.1 6.4 %collective-permute-start.22 = (bf16[720,128]{1,0:T(8,128)(2,1)S(1)}, bf16[720,128]{1,0:T(8,128)(2,1)S(1)}, u32[]{:S(2)}, u32[]{:S(2)}) collective-permute-start(bf16[720,128]{1,0:T(8,128)(2,1)S(1)} %get-tuple-element.43), channel_id=1, source_target_pairs={{0,1},{32,36},{1,2},{33,37},{2,3},{34,38},{3,0},{35,39},{4,5},{36,... | collective-permute-start | bytes 552968 | tf_op jit(solution)/shard_map/ppermute | solution.py:299
  70.2 5.2 %collective-permute-start.23 = (bf16[720,128]{1,0:T(8,128)(2,1)S(1)}, bf16[720,128]{1,0:T(8,128)(2,1)S(1)}, u32[]{:S(2)}, u32[]{:S(2)}) collective-permute-start(bf16[720,128]{1,0:T(8,128)(2,1)S(1)} %get-tuple-element.44), channel_id=1, source_target_pairs={{0,3},{32,44},{1,0},{33,45},{2,1},{34,46},{3,2},{35,47},{4,7},{36,... | collective-permute-start | bytes 552968 | tf_op jit(solution)/shard_map/ppermute | solution.py:299
  75.8 7.4 %collective-permute-start.26 = (f16[224,128]{1,0:T(8,128)(2,1)S(1)}, f16[224,128]{1,0:T(8,128)(2,1)S(1)}, u32[]{:S(2)}, u32[]{:S(2)}) collective-permute-start(f16[224,128]{1,0:T(8,128)(2,1)S(1)} %convert_element_type.54), channel_id=1, source_target_pairs={{0,16},{16,0},{1,17},{17,1},{2,18},{18,2},{3,19},{19,3},{4,20},{20... | collective-permute-start | bytes 172040 | tf_op jit(solution)/shard_map/ppermute | solution.py:305
  76.6 8.6 %collective-permute-start.25 = (f16[224,128]{1,0:T(8,128)(2,1)S(1)}, f16[224,128]{1,0:T(8,128)(2,1)S(1)}, u32[]{:S(2)}, u32[]{:S(2)}) collective-permute-start(f16[224,128]{1,0:T(8,128)(2,1)S(1)} %convert_element_type.52), channel_id=1, source_target_pairs={{0,48},{16,32},{32,16},{48,0},{1,49},{17,33},{33,17},{49,1},{2,50}... | collective-permute-start | bytes 172040 | tf_op jit(solution)/shard_map/ppermute | solution.py:304
  82.8 2.5 %collective-permute-start.24 = (f16[224,128]{1,0:T(8,128)(2,1)S(1)}, f16[224,128]{1,0:T(8,128)(2,1)S(1)}, u32[]{:S(2)}, u32[]{:S(2)}) collective-permute-start(f16[224,128]{1,0:T(8,128)(2,1)S(1)} %convert_element_type.50), channel_id=1, source_target_pairs={{0,32},{32,0},{1,33},{33,1},{2,34},{34,2},{3,35},{35,3},{4,36},{36... | collective-permute-start | bytes 172040 | tf_op jit(solution)/shard_map/ppermute | solution.py:303

commit v9 on v8

--- a/solution.py
+++ b/solution.py
@@ -140,8 +140,8 @@
     copy.wait()
 
 
-def scaled(x):
-    most = jnp.full((8, x.shape[1]), jnp.max(jnp.abs(x)))
+def scaled(x, most=None):
+    most = jnp.full((8, x.shape[1]), jnp.max(jnp.abs(x) if most is None else most))
     power = 13.0 - jnp.ceil(jnp.log(jnp.maximum(most, 1e-30)) * 1.4426950408889634)
     return x * jnp.exp2(power)[:1], power
 
@@ -154,11 +154,15 @@
 
 
 def project_in(m2, m3, w_ref, early_ref, o_ref, send_ref):
+    most = jnp.zeros((QT, 128), F32)
     for n in range(0, UNITS, 256):
         to = min(n + 256, UNITS)
         x = jnp.concatenate([m2[...], m3[...]], axis=1)
-        o_ref[:, n:to] = early_ref[:, n:to] + dot(x, w_ref[2 * UNITS :, n:to])
-    send_ref[0:QT], send_ref[QT:] = scaled(o_ref[...])
+        part = early_ref[:, n:to] + dot(x, w_ref[2 * UNITS :, n:to])
+        o_ref[:, n:to] = part
+        for k in range(0, to - n, 128):
+            most = jnp.maximum(most, jnp.abs(part[:, k : k + 128]))
+    send_ref[0:QT], send_ref[QT:] = scaled(o_ref[...], most)
 
 
 def project_out(a_ref, w_ref, o0, o1, o2, o3, t_ref, tail_ref):

time: 87.7 us -> 87.7 us (level)
  no operation moved by 1% of the time
where the time goes in v9:
time: 87.7 us; the launch traced here: 86.3 us
  starting transfers between devices  46.8 us (53%)
  Pallas kernels  20.2 us (23%)
  waiting for transfers between devices  18.1 us (21%)
    ppermute x6, starting transfers between devices, shards(): lax.ppermute(v, YX, first_axis(k))  9.51 us
    ppermute x6, starting transfers between devices, shards(): lax.ppermute(m, YX, second_axis(k))  8.98 us
    ppermute x6, waiting for transfers between devices, shards(): lax.ppermute(v, YX, first_axis(k))  8.19 us
    ppermute x1, starting transfers between devices, shards(): lax.ppermute(to_czl, ('c', 'zl'), [(0, 3), (1, 2), (2, 1), (3, 0)])  6.16 us
    ppermute x3, starting transfers between devices, shards(): around = [lax.ppermute(piece, YX, first_axis(k)) for k in GATHER[1:]]  5.5 us
    pallas_call x2, Pallas kernels, shards(): call(project_out, [shape(part, F32)] + [shape(part, BF)] * 3, [VMEM] * 2,...  5.08 us
    ppermute x1, starting transfers between devices, shards(): one = lax.ppermute(packed, z, [(0, 1), (3, 2), (2, 0), (1, 3)])  4.67 us
    ppermute x2, starting transfers between devices, shards(): gots = [lax.ppermute(send, 'zh', swap) for send in sends]  4.43 us
  transfers between devices with their start and end apart: 27, of which 11 were waited for; matrix products, arithmetic and copies ran while one was open for 1% of the time, Pallas kernels for 21%

profile of v9, /device:TPU:1, one launch (start us, length us, event | category | flops | bytes accessed | tf_op | source)
XLA Modules:
  0.0 86.3 jit_solution(8733970893085180909)
XLA Ops:
  0.0 1.4 %collective-permute-start.5 = (bf16[2304,1152]{1,0:T(8,128)(2,1)}, bf16[2304,1152]{1,0:T(8,128)(2,1)S(1)}, u32[]{:S(2)}, u32[]{:S(2)}) collective-permute-start(bf16[2304,1152]{1,0:T(8,128)(2,1)} %ref.2), channel_id=1, source_target_pairs={{0,32},{32,0},{1,33},{33,1},{2,34},{34,2},{3,35},{35,3},{4,36},{36... | collective-permute-start | bytes 15925256 | tf_op jit(solution)/shard_map/ppermute | solution.py:244
  1.4 0.0 collective-permute-start.6
  1.4 1.2 %pack_codes.1 = bf16[360,128]{1,0:T(8,128)(2,1)S(1)} custom-call(bf16[160,288]{1,0:T(8,128)(2,1)} %codes_ref.1, s32[1,160]{1,0:T(1,128)} %bitcast.2), custom_call_target="tpu_custom_call" | custom-call | tf_op jit(solution)/shard_map/pack_codes/pallas_call | solution.py:248
  2.6 0.7 collective-permute-start.1
  3.3 4.7 %collective-permute-start = (bf16[360,128]{1,0:T(8,128)(2,1)S(1)}, bf16[360,128]{1,0:T(8,128)(2,1)S(1)}, u32[]{:S(2)}, u32[]{:S(2)}) collective-permute-start(bf16[360,128]{1,0:T(8,128)(2,1)S(1)} %pack_codes.1), channel_id=1, source_target_pairs={{0,16},{80,64},{64,0},{16,80},{1,17},{81,65},{65,1},{17,81},{2,18}... | collective-permute-start | bytes 276488 | tf_op jit(solution)/shard_map/ppermute | solution.py:255
  8.0 2.5 %arrange_own.1.after.half_ref = bf16[4608,1152]{1,0:T(8,128)(2,1)S(1)} custom-call(bf16[2304,1152]{1,0:T(8,128)(2,1)} %ref.2), custom_call_target="tpu_custom_call" | custom-call | bytes 10616832 | tf_op jit(solution)/shard_map/arrange_own/pallas_call | solution.py:258
  10.4 0.0 collective-permute-done.1.two
  10.4 0.3 collective-permute-done.one
  10.8 2.8 %collective-permute-start.4 = (bf16[2,360,128]{2,1,0:T(8,128)(2,1)S(1)}, bf16[2,360,128]{2,1,0:T(8,128)(2,1)S(1)}, u32[]{:S(2)}, u32[]{:S(2)}) collective-permute-start(bf16[2,360,128]{2,1,0:T(8,128)(2,1)S(1)} %order_quarters.1.a_ref), channel_id=1, source_target_pairs={{0,8},{32,34},{1,9},{33,35},{2,10},{34,32},{3,11},{35,33},{4,12},{... | collective-permute-start | bytes 552968 | tf_op jit(solution)/shard_map/ppermute | solution.py:260
  13.6 0.3 collective-permute-start.3
  13.9 2.4 %collective-permute-start.2 = (bf16[2,360,128]{2,1,0:T(8,128)(2,1)S(1)}, bf16[2,360,128]{2,1,0:T(8,128)(2,1)S(1)}, u32[]{:S(2)}, u32[]{:S(2)}) collective-permute-start(bf16[2,360,128]{2,1,0:T(8,128)(2,1)S(1)} %order_quarters.1.a_ref), channel_id=1, source_target_pairs={{0,12},{32,35},{1,13},{33,32},{2,14},{34,33},{3,15},{35,34},{4,0},... | collective-permute-start | bytes 552968 | tf_op jit(solution)/shard_map/ppermute | solution.py:260
  16.3 0.0 collective-permute-done.5.ref
  16.3 1.9 %arrange_other.1.after1.w_ref.after = bf16[4608,1152]{1,0:T(8,128)(2,1)S(1)} custom-call(bf16[2304,1152]{1,0:T(8,128)(2,1)S(1)} %collective-permute-done.5.ref, bf16[4608,1152]{1,0:T(8,128)(2,1)S(1)} %arrange_own.1.after.half_ref), custom_call_target="tpu_custom_call", output_to_operand_aliasing={{}: (1, {})} | custom-call | bytes 10616832 | tf_op jit(solution)/shard_map/arrange_other/pallas_call | solution.py:261
  18.2 0.0 collective-permute-done.4.d_ref
  18.2 1.0 %collective-permute-done.3.c_ref = bf16[2,360,128]{2,1,0:T(8,128)(2,1)S(1)} collective-permute-done((bf16[2,360,128]{2,1,0:T(8,128)(2,1)S(1)}, bf16[2,360,128]{2,1,0:T(8,128)(2,1)S(1)}, u32[]{:S(2)}, u32[]{:S(2)}) %collective-permute-start.3) | collective-permute-done | bytes 184352 | tf_op jit(solution)/shard_map/ppermute | solution.py:260
  19.2 0.0 collective-permute-done.2.b_ref
  19.2 0.0 collective-permute-done.6.after2.ref
  19.2 0.2 merge_codes.1
  19.5 3.0 %collective-permute-start.16 = (bf16[160,1152]{1,0:T(8,128)(2,1)S(1)}, bf16[160,1152]{1,0:T(8,128)(2,1)S(1)}, u32[]{:S(2)}, u32[]{:S(2)}) collective-permute-start(bf16[160,1152]{1,0:T(8,128)(2,1)S(1)} %get-tuple-element.34.m0), channel_id=1, source_target_pairs={{0,2},{32,40},{1,3},{33,41},{2,0},{34,42},{3,1},{35,43},{4,6},{36,... | collective-permute-start | bytes 1105928 | tf_op jit(solution)/shard_map/ppermute | solution.py:266
  22.5 0.4 collective-permute-start.15
  22.9 2.3 %collective-permute-start.14 = (bf16[160,1152]{1,0:T(8,128)(2,1)S(1)}, bf16[160,1152]{1,0:T(8,128)(2,1)S(1)}, u32[]{:S(2)}, u32[]{:S(2)}) collective-permute-start(bf16[160,1152]{1,0:T(8,128)(2,1)S(1)} %get-tuple-element.34.m0), channel_id=1, source_target_pairs={{0,3},{32,44},{1,0},{33,45},{2,1},{34,46},{3,2},{35,47},{4,7},{36,... | collective-permute-start | bytes 1105928 | tf_op jit(solution)/shard_map/ppermute | solution.py:266
  25.2 0.0 collective-permute-start.9
  25.2 0.6 collective-permute-start.8
  25.7 2.0 %collective-permute-done.16.m1 = bf16[160,1152]{1,0:T(8,128)(2,1)S(1)} collective-permute-done((bf16[160,1152]{1,0:T(8,128)(2,1)S(1)}, bf16[160,1152]{1,0:T(8,128)(2,1)S(1)}, u32[]{:S(2)}, u32[]{:S(2)}) %collective-permute-start.16) | collective-permute-done | bytes 368672 | tf_op jit(solution)/shard_map/ppermute | solution.py:266
  27.7 2.7 %collective-permute-start.7 = (bf16[160,1152]{1,0:T(8,128)(2,1)S(1)}, bf16[160,1152]{1,0:T(8,128)(2,1)S(1)}, u32[]{:S(2)}, u32[]{:S(2)}) collective-permute-start(bf16[160,1152]{1,0:T(8,128)(2,1)S(1)} %get-tuple-element.27.m0), channel_id=1, source_target_pairs={{0,3},{32,44},{1,0},{33,45},{2,1},{34,46},{3,2},{35,47},{4,7},{36,... | collective-permute-start | bytes 1105928 | tf_op jit(solution)/shard_map/ppermute | solution.py:266
  30.5 1.1 %project_early.3.early_ref = f32[160,1152]{1,0:T(8,128)S(1)} custom-call(bf16[160,1152]{1,0:T(8,128)(2,1)S(1)} %get-tuple-element.34.m0, bf16[160,1152]{1,0:T(8,128)(2,1)S(1)} %collective-permute-done.16.m1, bf16[4608,1152]{1,0:T(8,128)(2,1)S(1)} %arrange_other.1.after1.w_ref.after), custom_call_target="tpu_custom_call" | custom-call | flops 849346560 | bytes 5308416 | tf_op jit(solution)/shard_map/project_early/pallas_call | solution.py:271
  31.6 0.1 collective-permute-done.15.m3
  31.7 0.3 collective-permute-done.14.m2
  32.0 1.3 %project_in.3 = (f32[160,1152]{1,0:T(8,128)S(1)}, f32[168,1152]{1,0:T(8,128)S(1)}) custom-call(bf16[160,1152]{1,0:T(8,128)(2,1)S(1)} %collective-permute-done.14.m2, bf16[160,1152]{1,0:T(8,128)(2,1)S(1)} %collective-permute-done.15.m3, bf16[4608,1152]{1,0:T(8,128)(2,1)S(1)} %arrange_other.1.after1.w_ref.after, f32[160,1152]{1,0:T(8,128)S(1)} %project_early.3.early_ref), custom_call_target="tpu_custom_call" | custom-call | flops 849346560 | bytes 5308416 | tf_op jit(solution)/shard_map/project_in/pallas_call | solution.py:276
  33.4 2.1 %collective-permute-start.17 = (f16[168,1152]{1,0:T(8,128)(2,1)S(1)}, f16[168,1152]{1,0:T(8,128)(2,1)S(1)}, u32[]{:S(2)}, u32[]{:S(2)}) collective-permute-start(f16[168,1152]{1,0:T(8,128)(2,1)S(1)} %convert_element_type.46), channel_id=1, source_target_pairs={{0,64},{64,0},{1,65},{65,1},{2,66},{66,2},{3,67},{67,3},{4,68},{68... | collective-permute-start | bytes 1161224 | tf_op jit(solution)/shard_map/ppermute | solution.py:279
  35.5 2.5 %stage_own.1.half_ref = bf16[1152,4608]{1,0:T(8,128)(2,1)S(1)} custom-call(bf16[1152,2304]{1,0:T(8,128)(2,1)} %ref.3, bf16[4608,1152]{1,0:T(8,128)(2,1)S(1)} %arrange_other.1.after1.w_ref.after), custom_call_target="tpu_custom_call" | custom-call | bytes 10616832 | tf_op jit(solution)/shard_map/stage_own/pallas_call | solution.py:280
  38.0 0.4 stage_other.1.w_ref
  38.5 1.1 %project_early.2.early_ref = f32[160,1152]{1,0:T(8,128)S(1)} custom-call(bf16[160,1152]{1,0:T(8,128)(2,1)S(1)} %get-tuple-element.27.m0, bf16[160,1152]{1,0:T(8,128)(2,1)S(1)} %collective-permute-done.9.m1, bf16[4608,1152]{1,0:T(8,128)(2,1)S(1)} %arrange_other.1.after1.w_ref.after), custom_call_target="tpu_custom_call" | custom-call | flops 849346560 | bytes 5308416 | tf_op jit(solution)/shard_map/project_early/pallas_call | solution.py:271
  39.6 0.3 collective-permute-done.7.m2
  40.0 1.3 %project_in.2 = (f32[160,1152]{1,0:T(8,128)S(1)}, f32[168,1152]{1,0:T(8,128)S(1)}) custom-call(bf16[160,1152]{1,0:T(8,128)(2,1)S(1)} %collective-permute-done.7.m2, bf16[160,1152]{1,0:T(8,128)(2,1)S(1)} %collective-permute-done.8.m3, bf16[4608,1152]{1,0:T(8,128)(2,1)S(1)} %arrange_other.1.after1.w_ref.after, f32[160,1152]{1,0:T(8,128)S(1)} %project_early.2.early_ref), custom_call_target="tpu_custom_call" | custom-call | flops 849346560 | bytes 5308416 | tf_op jit(solution)/shard_map/project_in/pallas_call | solution.py:276
  41.4 2.3 %collective-permute-start.10 = (f16[168,1152]{1,0:T(8,128)(2,1)S(1)}, f16[168,1152]{1,0:T(8,128)(2,1)S(1)}, u32[]{:S(2)}, u32[]{:S(2)}) collective-permute-start(f16[168,1152]{1,0:T(8,128)(2,1)S(1)} %convert_element_type.42), channel_id=1, source_target_pairs={{0,64},{64,0},{1,65},{65,1},{2,66},{66,2},{3,67},{67,3},{4,68},{68... | collective-permute-start | bytes 1161224 | tf_op jit(solution)/shard_map/ppermute | solution.py:279
  43.7 0.0 collective-permute-done.17
  43.7 0.3 fusion.15.a_ref
  44.0 2.5 %project_out.3 = (f32[4,360,128]{2,1,0:T(8,128)S(1)}, bf16[4,360,128]{2,1,0:T(8,128)(2,1)S(1)}, bf16[4,360,128]{2,1,0:T(8,128)(2,1)S(1)}, bf16[4,360,128]{2,1,0:T(8,128)(2,1)S(1)}) custom-call(bf16[160,1152]{1,0:T(8,128)(2,1)S(1)} %fusion.15.a_ref, bf16[1152,4608]{1,0:T(8,128)(2,1)S(1)} %stage_other.1.w_ref), custom_call_target="tpu_custom_call" | custom-call | flops 1698693120 | bytes 10616832 | tf_op jit(solution)/shard_map/project_out/pallas_call | solution.py:290
  46.6 2.8 %collective-permute-start.18 = (bf16[4,360,128]{2,1,0:T(8,128)(2,1)S(1)}, bf16[4,360,128]{2,1,0:T(8,128)(2,1)S(1)}, u32[]{:S(2)}, u32[]{:S(2)}) collective-permute-start(bf16[4,360,128]{2,1,0:T(8,128)(2,1)S(1)} %get-tuple-element.38), channel_id=1, source_target_pairs={{0,8},{32,34},{1,9},{33,35},{2,10},{34,32},{3,11},{35,33},{4,12},{... | collective-permute-start | bytes 1105928 | tf_op jit(solution)/shard_map/ppermute | solution.py:300
  49.4 0.3 collective-permute-start.19
  49.7 2.4 %collective-permute-start.20 = (bf16[4,360,128]{2,1,0:T(8,128)(2,1)S(1)}, bf16[4,360,128]{2,1,0:T(8,128)(2,1)S(1)}, u32[]{:S(2)}, u32[]{:S(2)}) collective-permute-start(bf16[4,360,128]{2,1,0:T(8,128)(2,1)S(1)} %get-tuple-element.40), channel_id=1, source_target_pairs={{0,12},{32,35},{1,13},{33,32},{2,14},{34,33},{3,15},{35,34},{4,0},... | collective-permute-start | bytes 1105928 | tf_op jit(solution)/shard_map/ppermute | solution.py:300
  52.1 0.3 fusion.7.a_ref
  52.4 2.5 %project_out.2 = (f32[4,360,128]{2,1,0:T(8,128)S(1)}, bf16[4,360,128]{2,1,0:T(8,128)(2,1)S(1)}, bf16[4,360,128]{2,1,0:T(8,128)(2,1)S(1)}, bf16[4,360,128]{2,1,0:T(8,128)(2,1)S(1)}) custom-call(bf16[160,1152]{1,0:T(8,128)(2,1)S(1)} %fusion.7.a_ref, bf16[1152,4608]{1,0:T(8,128)(2,1)S(1)} %stage_other.1.w_ref), custom_call_target="tpu_custom_call" | custom-call | flops 1698693120 | bytes 10616832 | tf_op jit(solution)/shard_map/project_out/pallas_call | solution.py:290
  55.0 1.3 %collective-permute-start.11 = (bf16[4,360,128]{2,1,0:T(8,128)(2,1)S(1)}, bf16[4,360,128]{2,1,0:T(8,128)(2,1)S(1)}, u32[]{:S(2)}, u32[]{:S(2)}) collective-permute-start(bf16[4,360,128]{2,1,0:T(8,128)(2,1)S(1)} %get-tuple-element.31), channel_id=1, source_target_pairs={{0,8},{32,34},{1,9},{33,35},{2,10},{34,32},{3,11},{35,33},{4,12},{... | collective-permute-start | bytes 1105928 | tf_op jit(solution)/shard_map/ppermute | solution.py:300
  56.3 0.8 collective-permute-start.12
  57.1 1.9 %collective-permute-start.13 = (bf16[4,360,128]{2,1,0:T(8,128)(2,1)S(1)}, bf16[4,360,128]{2,1,0:T(8,128)(2,1)S(1)}, u32[]{:S(2)}, u32[]{:S(2)}) collective-permute-start(bf16[4,360,128]{2,1,0:T(8,128)(2,1)S(1)} %get-tuple-element.33), channel_id=1, source_target_pairs={{0,12},{32,35},{1,13},{33,32},{2,14},{34,33},{3,15},{35,34},{4,0},... | collective-permute-start | bytes 1105928 | tf_op jit(solution)/shard_map/ppermute | solution.py:300
  59.0 4.3 %collective-permute-done.11.b0 = bf16[4,360,128]{2,1,0:T(8,128)(2,1)S(1)} collective-permute-done((bf16[4,360,128]{2,1,0:T(8,128)(2,1)S(1)}, bf16[4,360,128]{2,1,0:T(8,128)(2,1)S(1)}, u32[]{:S(2)}, u32[]{:S(2)}) %collective-permute-start.11) | collective-permute-done | bytes 368672 | tf_op jit(solution)/shard_map/ppermute | solution.py:300
  63.3 3.9 %collective-permute-done.12.c0 = bf16[4,360,128]{2,1,0:T(8,128)(2,1)S(1)} collective-permute-done((bf16[4,360,128]{2,1,0:T(8,128)(2,1)S(1)}, bf16[4,360,128]{2,1,0:T(8,128)(2,1)S(1)}, u32[]{:S(2)}, u32[]{:S(2)}) %collective-permute-start.12) | collective-permute-done | bytes 368672 | tf_op jit(solution)/shard_map/ppermute | solution.py:300
  67.2 0.0 collective-permute-done.13.d0
  67.2 0.4 add_first.1
  67.5 1.6 %collective-permute-start.21 = (bf16[720,128]{1,0:T(8,128)(2,1)S(1)}, bf16[720,128]{1,0:T(8,128)(2,1)S(1)}, u32[]{:S(2)}, u32[]{:S(2)}) collective-permute-start(bf16[720,128]{1,0:T(8,128)(2,1)S(1)} %get-tuple-element.42), channel_id=1, source_target_pairs={{0,2},{32,40},{1,3},{33,41},{2,0},{34,42},{3,1},{35,43},{4,6},{36,... | collective-permute-start | bytes 552968 | tf_op jit(solution)/shard_map/ppermute | solution.py:303
  69.1 1.1 %collective-permute-start.22 = (bf16[720,128]{1,0:T(8,128)(2,1)S(1)}, bf16[720,128]{1,0:T(8,128)(2,1)S(1)}, u32[]{:S(2)}, u32[]{:S(2)}) collective-permute-start(bf16[720,128]{1,0:T(8,128)(2,1)S(1)} %get-tuple-element.43), channel_id=1, source_target_pairs={{0,1},{32,36},{1,2},{33,37},{2,3},{34,38},{3,0},{35,39},{4,5},{36,... | collective-permute-start | bytes 552968 | tf_op jit(solution)/shard_map/ppermute | solution.py:303
  70.3 1.5 %collective-permute-start.23 = (bf16[720,128]{1,0:T(8,128)(2,1)S(1)}, bf16[720,128]{1,0:T(8,128)(2,1)S(1)}, u32[]{:S(2)}, u32[]{:S(2)}) collective-permute-start(bf16[720,128]{1,0:T(8,128)(2,1)S(1)} %get-tuple-element.44), channel_id=1, source_target_pairs={{0,3},{32,44},{1,0},{33,45},{2,1},{34,46},{3,2},{35,47},{4,7},{36,... | collective-permute-start | bytes 552968 | tf_op jit(solution)/shard_map/ppermute | solution.py:303
  71.8 1.8 %collective-permute-done.21.b = bf16[720,128]{1,0:T(8,128)(2,1)S(1)} collective-permute-done((bf16[720,128]{1,0:T(8,128)(2,1)S(1)}, bf16[720,128]{1,0:T(8,128)(2,1)S(1)}, u32[]{:S(2)}, u32[]{:S(2)}) %collective-permute-start.21) | collective-permute-done | bytes 184352 | tf_op jit(solution)/shard_map/ppermute | solution.py:303
  73.6 1.9 %collective-permute-done.22.c = bf16[720,128]{1,0:T(8,128)(2,1)S(1)} collective-permute-done((bf16[720,128]{1,0:T(8,128)(2,1)S(1)}, bf16[720,128]{1,0:T(8,128)(2,1)S(1)}, u32[]{:S(2)}, u32[]{:S(2)}) %collective-permute-start.22) | collective-permute-done | bytes 184352 | tf_op jit(solution)/shard_map/ppermute | solution.py:303
  75.5 0.3 add_second.1
  75.8 0.8 collective-permute-start.26
  76.6 6.2 %collective-permute-start.25 = (f16[224,128]{1,0:T(8,128)(2,1)S(1)}, f16[224,128]{1,0:T(8,128)(2,1)S(1)}, u32[]{:S(2)}, u32[]{:S(2)}) collective-permute-start(f16[224,128]{1,0:T(8,128)(2,1)S(1)} %convert_element_type.52), channel_id=1, source_target_pairs={{0,48},{16,32},{32,16},{48,0},{1,49},{17,33},{33,17},{49,1},{2,50}... | collective-permute-start | bytes 172040 | tf_op jit(solution)/shard_map/ppermute | solution.py:308
  82.8 0.4 collective-permute-start.24
  83.2 0.0 collective-permute-done.26
  83.2 2.1 %collective-permute-done.25 = f16[224,128]{1,0:T(8,128)(2,1)S(1)} collective-permute-done((f16[224,128]{1,0:T(8,128)(2,1)S(1)}, f16[224,128]{1,0:T(8,128)(2,1)S(1)}, u32[]{:S(2)}, u32[]{:S(2)}) %collective-permute-start.25) | collective-permute-done | bytes 57376 | tf_op jit(solution)/shard_map/ppermute | solution.py:308
  85.3 0.0 collective-permute-done.24
  85.3 0.8 finish.1
  (18 shorter events, 0.3 us)
Async XLA Ops:
  0.0 16.3 %collective-permute-start.5 = (bf16[2304,1152]{1,0:T(8,128)(2,1)}, bf16[2304,1152]{1,0:T(8,128)(2,1)S(1)}, u32[]{:S(2)}, u32[]{:S(2)}) collective-permute-start(bf16[2304,1152]{1,0:T(8,128)(2,1)} %ref.2), channel_id=1, source_target_pairs={{0,32},{32,0},{1,33},{33,1},{2,34},{34,2},{3,35},{35,3},{4,36},{36... | collective-permute-start | bytes 15925256 | tf_op jit(solution)/shard_map/ppermute | solution.py:244
  1.4 17.8 %collective-permute-start.6 = (bf16[1152,2304]{1,0:T(8,128)(2,1)}, bf16[1152,2304]{1,0:T(8,128)(2,1)S(1)}, u32[]{:S(2)}, u32[]{:S(2)}) collective-permute-start(bf16[1152,2304]{1,0:T(8,128)(2,1)} %ref.3), channel_id=1, source_target_pairs={{0,32},{32,0},{1,33},{33,1},{2,34},{34,2},{3,35},{35,3},{4,36},{36... | collective-permute-start | bytes 15925256 | tf_op jit(solution)/shard_map/ppermute | solution.py:245
  2.6 7.8 %collective-permute-start.1 = (bf16[360,128]{1,0:T(8,128)(2,1)S(1)}, bf16[360,128]{1,0:T(8,128)(2,1)S(1)}, u32[]{:S(2)}, u32[]{:S(2)}) collective-permute-start(bf16[360,128]{1,0:T(8,128)(2,1)S(1)} %pack_codes.1), channel_id=1, source_target_pairs={{64,16},{16,64},{0,0},{80,80},{65,17},{17,65},{1,1},{81,81},{66,18... | collective-permute-start | bytes 276488 | tf_op jit(solution)/shard_map/ppermute | solution.py:256
  3.3 7.5 %collective-permute-start = (bf16[360,128]{1,0:T(8,128)(2,1)S(1)}, bf16[360,128]{1,0:T(8,128)(2,1)S(1)}, u32[]{:S(2)}, u32[]{:S(2)}) collective-permute-start(bf16[360,128]{1,0:T(8,128)(2,1)S(1)} %pack_codes.1), channel_id=1, source_target_pairs={{0,16},{80,64},{64,0},{16,80},{1,17},{81,65},{65,1},{17,81},{2,18}... | collective-permute-start | bytes 276488 | tf_op jit(solution)/shard_map/ppermute | solution.py:255
  10.8 7.4 %collective-permute-start.4 = (bf16[2,360,128]{2,1,0:T(8,128)(2,1)S(1)}, bf16[2,360,128]{2,1,0:T(8,128)(2,1)S(1)}, u32[]{:S(2)}, u32[]{:S(2)}) collective-permute-start(bf16[2,360,128]{2,1,0:T(8,128)(2,1)S(1)} %order_quarters.1.a_ref), channel_id=1, source_target_pairs={{0,8},{32,34},{1,9},{33,35},{2,10},{34,32},{3,11},{35,33},{4,12},{... | collective-permute-start | bytes 552968 | tf_op jit(solution)/shard_map/ppermute | solution.py:260
  13.6 5.6 %collective-permute-start.3 = (bf16[2,360,128]{2,1,0:T(8,128)(2,1)S(1)}, bf16[2,360,128]{2,1,0:T(8,128)(2,1)S(1)}, u32[]{:S(2)}, u32[]{:S(2)}) collective-permute-start(bf16[2,360,128]{2,1,0:T(8,128)(2,1)S(1)} %order_quarters.1.a_ref), channel_id=1, source_target_pairs={{0,4},{32,33},{1,5},{33,34},{2,6},{34,35},{3,7},{35,32},{4,8},{36,... | collective-permute-start | bytes 552968 | tf_op jit(solution)/shard_map/ppermute | solution.py:260
  13.9 5.3 %collective-permute-start.2 = (bf16[2,360,128]{2,1,0:T(8,128)(2,1)S(1)}, bf16[2,360,128]{2,1,0:T(8,128)(2,1)S(1)}, u32[]{:S(2)}, u32[]{:S(2)}) collective-permute-start(bf16[2,360,128]{2,1,0:T(8,128)(2,1)S(1)} %order_quarters.1.a_ref), channel_id=1, source_target_pairs={{0,12},{32,35},{1,13},{33,32},{2,14},{34,33},{3,15},{35,34},{4,0},... | collective-permute-start | bytes 552968 | tf_op jit(solution)/shard_map/ppermute | solution.py:260
  19.5 8.2 %collective-permute-start.16 = (bf16[160,1152]{1,0:T(8,128)(2,1)S(1)}, bf16[160,1152]{1,0:T(8,128)(2,1)S(1)}, u32[]{:S(2)}, u32[]{:S(2)}) collective-permute-start(bf16[160,1152]{1,0:T(8,128)(2,1)S(1)} %get-tuple-element.34.m0), channel_id=1, source_target_pairs={{0,2},{32,40},{1,3},{33,41},{2,0},{34,42},{3,1},{35,43},{4,6},{36,... | collective-permute-start | bytes 1105928 | tf_op jit(solution)/shard_map/ppermute | solution.py:266
  22.5 9.2 %collective-permute-start.15 = (bf16[160,1152]{1,0:T(8,128)(2,1)S(1)}, bf16[160,1152]{1,0:T(8,128)(2,1)S(1)}, u32[]{:S(2)}, u32[]{:S(2)}) collective-permute-start(bf16[160,1152]{1,0:T(8,128)(2,1)S(1)} %get-tuple-element.34.m0), channel_id=1, source_target_pairs={{0,1},{32,36},{1,2},{33,37},{2,3},{34,38},{3,0},{35,39},{4,5},{36,... | collective-permute-start | bytes 1105928 | tf_op jit(solution)/shard_map/ppermute | solution.py:266
  22.9 9.1 %collective-permute-start.14 = (bf16[160,1152]{1,0:T(8,128)(2,1)S(1)}, bf16[160,1152]{1,0:T(8,128)(2,1)S(1)}, u32[]{:S(2)}, u32[]{:S(2)}) collective-permute-start(bf16[160,1152]{1,0:T(8,128)(2,1)S(1)} %get-tuple-element.34.m0), channel_id=1, source_target_pairs={{0,3},{32,44},{1,0},{33,45},{2,1},{34,46},{3,2},{35,47},{4,7},{36,... | collective-permute-start | bytes 1105928 | tf_op jit(solution)/shard_map/ppermute | solution.py:266
  25.2 13.3 %collective-permute-start.9 = (bf16[160,1152]{1,0:T(8,128)(2,1)S(1)}, bf16[160,1152]{1,0:T(8,128)(2,1)S(1)}, u32[]{:S(2)}, u32[]{:S(2)}) collective-permute-start(bf16[160,1152]{1,0:T(8,128)(2,1)S(1)} %get-tuple-element.27.m0), channel_id=1, source_target_pairs={{0,2},{32,40},{1,3},{33,41},{2,0},{34,42},{3,1},{35,43},{4,6},{36,... | collective-permute-start | bytes 1105928 | tf_op jit(solution)/shard_map/ppermute | solution.py:266
  25.2 14.5 %collective-permute-start.8 = (bf16[160,1152]{1,0:T(8,128)(2,1)S(1)}, bf16[160,1152]{1,0:T(8,128)(2,1)S(1)}, u32[]{:S(2)}, u32[]{:S(2)}) collective-permute-start(bf16[160,1152]{1,0:T(8,128)(2,1)S(1)} %get-tuple-element.27.m0), channel_id=1, source_target_pairs={{0,1},{32,36},{1,2},{33,37},{2,3},{34,38},{3,0},{35,39},{4,5},{36,... | collective-permute-start | bytes 1105928 | tf_op jit(solution)/shard_map/ppermute | solution.py:266
  27.7 12.2 %collective-permute-start.7 = (bf16[160,1152]{1,0:T(8,128)(2,1)S(1)}, bf16[160,1152]{1,0:T(8,128)(2,1)S(1)}, u32[]{:S(2)}, u32[]{:S(2)}) collective-permute-start(bf16[160,1152]{1,0:T(8,128)(2,1)S(1)} %get-tuple-element.27.m0), channel_id=1, source_target_pairs={{0,3},{32,44},{1,0},{33,45},{2,1},{34,46},{3,2},{35,47},{4,7},{36,... | collective-permute-start | bytes 1105928 | tf_op jit(solution)/shard_map/ppermute | solution.py:266
  33.4 10.3 %collective-permute-start.17 = (f16[168,1152]{1,0:T(8,128)(2,1)S(1)}, f16[168,1152]{1,0:T(8,128)(2,1)S(1)}, u32[]{:S(2)}, u32[]{:S(2)}) collective-permute-start(f16[168,1152]{1,0:T(8,128)(2,1)S(1)} %convert_element_type.46), channel_id=1, source_target_pairs={{0,64},{64,0},{1,65},{65,1},{2,66},{66,2},{3,67},{67,3},{4,68},{68... | collective-permute-start | bytes 1161224 | tf_op jit(solution)/shard_map/ppermute | solution.py:279
  41.4 10.7 %collective-permute-start.10 = (f16[168,1152]{1,0:T(8,128)(2,1)S(1)}, f16[168,1152]{1,0:T(8,128)(2,1)S(1)}, u32[]{:S(2)}, u32[]{:S(2)}) collective-permute-start(f16[168,1152]{1,0:T(8,128)(2,1)S(1)} %convert_element_type.42), channel_id=1, source_target_pairs={{0,64},{64,0},{1,65},{65,1},{2,66},{66,2},{3,67},{67,3},{4,68},{68... | collective-permute-start | bytes 1161224 | tf_op jit(solution)/shard_map/ppermute | solution.py:279
  46.6 10.5 %collective-permute-start.18 = (bf16[4,360,128]{2,1,0:T(8,128)(2,1)S(1)}, bf16[4,360,128]{2,1,0:T(8,128)(2,1)S(1)}, u32[]{:S(2)}, u32[]{:S(2)}) collective-permute-start(bf16[4,360,128]{2,1,0:T(8,128)(2,1)S(1)} %get-tuple-element.38), channel_id=1, source_target_pairs={{0,8},{32,34},{1,9},{33,35},{2,10},{34,32},{3,11},{35,33},{4,12},{... | collective-permute-start | bytes 1105928 | tf_op jit(solution)/shard_map/ppermute | solution.py:300
  49.4 9.6 %collective-permute-start.19 = (bf16[4,360,128]{2,1,0:T(8,128)(2,1)S(1)}, bf16[4,360,128]{2,1,0:T(8,128)(2,1)S(1)}, u32[]{:S(2)}, u32[]{:S(2)}) collective-permute-start(bf16[4,360,128]{2,1,0:T(8,128)(2,1)S(1)} %get-tuple-element.39), channel_id=1, source_target_pairs={{0,4},{32,33},{1,5},{33,34},{2,6},{34,35},{3,7},{35,32},{4,8},{36,... | collective-permute-start | bytes 1105928 | tf_op jit(solution)/shard_map/ppermute | solution.py:300
  49.7 9.3 %collective-permute-start.20 = (bf16[4,360,128]{2,1,0:T(8,128)(2,1)S(1)}, bf16[4,360,128]{2,1,0:T(8,128)(2,1)S(1)}, u32[]{:S(2)}, u32[]{:S(2)}) collective-permute-start(bf16[4,360,128]{2,1,0:T(8,128)(2,1)S(1)} %get-tuple-element.40), channel_id=1, source_target_pairs={{0,12},{32,35},{1,13},{33,32},{2,14},{34,33},{3,15},{35,34},{4,0},... | collective-permute-start | bytes 1105928 | tf_op jit(solution)/shard_map/ppermute | solution.py:300
  55.0 8.3 %collective-permute-start.11 = (bf16[4,360,128]{2,1,0:T(8,128)(2,1)S(1)}, bf16[4,360,128]{2,1,0:T(8,128)(2,1)S(1)}, u32[]{:S(2)}, u32[]{:S(2)}) collective-permute-start(bf16[4,360,128]{2,1,0:T(8,128)(2,1)S(1)} %get-tuple-element.31), channel_id=1, source_target_pairs={{0,8},{32,34},{1,9},{33,35},{2,10},{34,32},{3,11},{35,33},{4,12},{... | collective-permute-start | bytes 1105928 | tf_op jit(solution)/shard_map/ppermute | solution.py:300
  56.3 10.9 %collective-permute-start.12 = (bf16[4,360,128]{2,1,0:T(8,128)(2,1)S(1)}, bf16[4,360,128]{2,1,0:T(8,128)(2,1)S(1)}, u32[]{:S(2)}, u32[]{:S(2)}) collective-permute-start(bf16[4,360,128]{2,1,0:T(8,128)(2,1)S(1)} %get-tuple-element.32), channel_id=1, source_target_pairs={{0,4},{32,33},{1,5},{33,34},{2,6},{34,35},{3,7},{35,32},{4,8},{36,... | collective-permute-start | bytes 1105928 | tf_op jit(solution)/shard_map/ppermute | solution.py:300
  57.1 10.1 %collective-permute-start.13 = (bf16[4,360,128]{2,1,0:T(8,128)(2,1)S(1)}, bf16[4,360,128]{2,1,0:T(8,128)(2,1)S(1)}, u32[]{:S(2)}, u32[]{:S(2)}) collective-permute-start(bf16[4,360,128]{2,1,0:T(8,128)(2,1)S(1)} %get-tuple-element.33), channel_id=1, source_target_pairs={{0,12},{32,35},{1,13},{33,32},{2,14},{34,33},{3,15},{35,34},{4,0},... | collective-permute-start | bytes 1105928 | tf_op jit(solution)/shard_map/ppermute | solution.py:300
  67.5 6.1 %collective-permute-start.21 = (bf16[720,128]{1,0:T(8,128)(2,1)S(1)}, bf16[720,128]{1,0:T(8,128)(2,1)S(1)}, u32[]{:S(2)}, u32[]{:S(2)}) collective-permute-start(bf16[720,128]{1,0:T(8,128)(2,1)S(1)} %get-tuple-element.42), channel_id=1, source_target_pairs={{0,2},{32,40},{1,3},{33,41},{2,0},{34,42},{3,1},{35,43},{4,6},{36,... | collective-permute-start | bytes 552968 | tf_op jit(solution)/shard_map/ppermute | solution.py:303
  69.1 6.4 %collective-permute-start.22 = (bf16[720,128]{1,0:T(8,128)(2,1)S(1)}, bf16[720,128]{1,0:T(8,128)(2,1)S(1)}, u32[]{:S(2)}, u32[]{:S(2)}) collective-permute-start(bf16[720,128]{1,0:T(8,128)(2,1)S(1)} %get-tuple-element.43), channel_id=1, source_target_pairs={{0,1},{32,36},{1,2},{33,37},{2,3},{34,38},{3,0},{35,39},{4,5},{36,... | collective-permute-start | bytes 552968 | tf_op jit(solution)/shard_map/ppermute | solution.py:303
  70.3 5.2 %collective-permute-start.23 = (bf16[720,128]{1,0:T(8,128)(2,1)S(1)}, bf16[720,128]{1,0:T(8,128)(2,1)S(1)}, u32[]{:S(2)}, u32[]{:S(2)}) collective-permute-start(bf16[720,128]{1,0:T(8,128)(2,1)S(1)} %get-tuple-element.44), channel_id=1, source_target_pairs={{0,3},{32,44},{1,0},{33,45},{2,1},{34,46},{3,2},{35,47},{4,7},{36,... | collective-permute-start | bytes 552968 | tf_op jit(solution)/shard_map/ppermute | solution.py:303
  75.8 7.4 %collective-permute-start.26 = (f16[224,128]{1,0:T(8,128)(2,1)S(1)}, f16[224,128]{1,0:T(8,128)(2,1)S(1)}, u32[]{:S(2)}, u32[]{:S(2)}) collective-permute-start(f16[224,128]{1,0:T(8,128)(2,1)S(1)} %convert_element_type.54), channel_id=1, source_target_pairs={{0,16},{16,0},{1,17},{17,1},{2,18},{18,2},{3,19},{19,3},{4,20},{20... | collective-permute-start | bytes 172040 | tf_op jit(solution)/shard_map/ppermute | solution.py:309
  76.6 8.6 %collective-permute-start.25 = (f16[224,128]{1,0:T(8,128)(2,1)S(1)}, f16[224,128]{1,0:T(8,128)(2,1)S(1)}, u32[]{:S(2)}, u32[]{:S(2)}) collective-permute-start(f16[224,128]{1,0:T(8,128)(2,1)S(1)} %convert_element_type.52), channel_id=1, source_target_pairs={{0,48},{16,32},{32,16},{48,0},{1,49},{17,33},{33,17},{49,1},{2,50}... | collective-permute-start | bytes 172040 | tf_op jit(solution)/shard_map/ppermute | solution.py:308
  82.8 2.5 %collective-permute-start.24 = (f16[224,128]{1,0:T(8,128)(2,1)S(1)}, f16[224,128]{1,0:T(8,128)(2,1)S(1)}, u32[]{:S(2)}, u32[]{:S(2)}) collective-permute-start(f16[224,128]{1,0:T(8,128)(2,1)S(1)} %convert_element_type.50), channel_id=1, source_target_pairs={{0,32},{32,0},{1,33},{33,1},{2,34},{34,2},{3,35},{35,3},{4,36},{36... | collective-permute-start | bytes 172040 | tf_op jit(solution)/shard_map/ppermute | solution.py:307
